TPU v7x, 32 devices: a whole 2x2x4 slice. The times are simulated.
32 devices in a mesh: dp: 8 (over y, x, core), tensor: 4 (over z).
Axes of the slice: x: 2, y: 2, z: 4, core: 2. Of those that a mesh axis runs over, the one named last changes fastest.
Arguments:
- inputs: bfloat16 [16384, 1536], P('dp'), may hold values from -6 to 6
- gain_attn: float32 [1536], replicated, may hold values from 0.5 to 1.5
- w_query: bfloat16 [1536, 1536], P(None, 'tensor'), may hold values from -0.15625 to 0.15625
- w_key: bfloat16 [1536, 1536], P(None, 'tensor'), may hold values from -0.15625 to 0.15625
- w_value: bfloat16 [1536, 1536], P(None, 'tensor'), may hold values from -0.15625 to 0.15625
- w_outgate: bfloat16 [1536, 1536], P(None, 'tensor'), may hold values from -0.15625 to 0.15625
- w_forget: bfloat16 [1536, 24], P(None, 'tensor'), may hold values from -0.15625 to 0.15625
- forget_bias: float32 [24], P('tensor'), may hold values from 2 to 8
- w_out: bfloat16 [1536, 1536], P(None, 'tensor'), may hold values from -0.625 to 0.625
- gain_mlp: float32 [1536], replicated, may hold values from 0.5 to 1.5
- w_gate: bfloat16 [1536, 4096], P(None, 'tensor'), may hold values from -0.15625 to 0.15625
- w_up: bfloat16 [1536, 4096], P(None, 'tensor'), may hold values from -0.15625 to 0.15625
- w_down: bfloat16 [1536, 4096], P(None, 'tensor'), may hold values from -0.09375 to 0.09375
- segment_ids: int32 [16, 1024], P('dp'), may hold values from 0 to 2, never falling along the last dimension, each value on 1 to 768 neighbouring positions
- cotangent: bfloat16 [16384, 1536], P('dp'), may hold values from -6 to 6
Outputs:
- output: float32 [16384, 1536], P(('dp', 'tensor'))
- grad_inputs: float32 [16384, 1536], P(('dp', 'tensor'))
- grad_gain_attn: float32 [1536], replicated
- grad_w_query: float32 [1536, 1536], P('dp', 'tensor')
- grad_w_key: float32 [1536, 1536], P('dp', 'tensor')
- grad_w_value: float32 [1536, 1536], P('dp', 'tensor')
- grad_w_outgate: float32 [1536, 1536], P('dp', 'tensor')
- grad_w_forget: float32 [1536, 24], P('dp', 'tensor')
- grad_forget_bias: float32 [24], P('tensor')
- grad_w_out: float32 [1536, 1536], P('dp', 'tensor')
- grad_gain_mlp: float32 [1536], replicated
- grad_w_gate: float32 [1536, 4096], P('dp', 'tensor')
- grad_w_up: float32 [1536, 4096], P('dp', 'tensor')
- grad_w_down: float32 [1536, 4096], P('dp', 'tensor')
Inputs may be any that keep to these rules, and one draw needn't show every extreme that they name: `segment_ids`: within each packed row the document numbers never fall; attention stays inside a document.
All inputs are finite; a program needn't handle non-finite values.
Results may differ from a plain program's by a relative error of at most 0.035.
Values may be sent and summed in bfloat16 or wider, within the bound.
No kernel may reach another device: no remote copies, remote signals or barrier semaphores. Data moves between devices by JAX's collectives and lax.ppermute only.
A program may use at most 320 MiB of HBM per device.

v0:
```python
import jax
import jax.numpy as jnp
from jax import lax
from jax.sharding import PartitionSpec as P

eps = 1e-06


def contract_last(left, right):
    return lax.dot_general(
        left, right, (((1,), (1,)), ((), ())), preferred_element_type=jnp.float32
    )


def contract_first(left, right):
    return lax.dot_general(
        left, right, (((0,), (0,)), ((), ())), preferred_element_type=jnp.float32
    )


def product(left, right):
    return jnp.dot(left, right, preferred_element_type=jnp.float32)


def normalize(values, scale_gain):
    inverse = lax.rsqrt(jnp.mean(values * values, axis=-1, keepdims=True) + eps)
    return (values * inverse * scale_gain, inverse)


def norm_back(values, inverse, scale_gain, upstream):
    unit_rows = values * inverse
    scaled = upstream * scale_gain
    return inverse * (scaled - unit_rows * jnp.mean(scaled * unit_rows, axis=-1, keepdims=True))


def gain_part(values, inverse, upstream):
    return jnp.sum(upstream * (values * inverse), axis=0)


def log_keep(values):
    return jnp.minimum(values, 0.0) - jnp.log1p(jnp.exp(-jnp.abs(values)))


def row_scores(queries, key_rows, running, segment):
    length = queries.shape[0]
    scores = jnp.einsum(
        "qhd,khd->hqk", queries, key_rows, preferred_element_type=jnp.float32
    ) * queries.shape[-1] ** (-0.5)
    scores = scores + running.T[:, :, None] - running.T[:, None, :]
    causal = lax.broadcasted_iota(jnp.int32, (length, length), 0) >= lax.broadcasted_iota(
        jnp.int32, (length, length), 1
    )
    allowed = causal & (segment[:, None] == segment[None, :])
    return jnp.where(allowed[None], scores, -1e30)


def attend_forward(pieces):
    queries, key_rows, value_rows, running, segment = pieces
    scores = row_scores(queries, key_rows, running, segment)
    row_peak = jnp.max(scores, axis=-1, keepdims=True)
    numerators = jnp.exp(scores - row_peak)
    totals = jnp.sum(numerators, axis=-1, keepdims=True)
    weights_low = (numerators / totals).astype(jnp.bfloat16)
    attended = jnp.einsum(
        "hqk,khd->qhd", weights_low, value_rows, preferred_element_type=jnp.float32
    )
    return (attended, row_peak + jnp.log(totals))


def attend_backward(pieces):
    queries, key_rows, value_rows, running, segment, log_total, grad_attended = pieces
    scores = row_scores(queries, key_rows, running, segment)
    weights_full = jnp.exp(scores - log_total)
    weights_low = weights_full.astype(jnp.bfloat16)
    grad_values = jnp.einsum(
        "hqk,qhd->khd", weights_low, grad_attended, preferred_element_type=jnp.float32
    )
    grad_weights = jnp.einsum(
        "qhd,khd->hqk", grad_attended, value_rows, preferred_element_type=jnp.float32
    )
    centre = jnp.sum(weights_full * grad_weights, axis=-1, keepdims=True)
    score_full = weights_full * (grad_weights - centre)
    grad_scores = score_full.astype(jnp.bfloat16)
    factor = queries.shape[-1] ** (-0.5)
    grad_queries = (
        jnp.einsum("hqk,khd->qhd", grad_scores, key_rows, preferred_element_type=jnp.float32)
        * factor
    )
    grad_keys = (
        jnp.einsum("hqk,qhd->khd", grad_scores, queries, preferred_element_type=jnp.float32)
        * factor
    )
    grad_running = (jnp.sum(score_full, axis=2) - jnp.sum(score_full, axis=1)).T
    return (grad_queries, grad_keys, grad_values, grad_running)


def on_device(
    inputs,
    gain_attn,
    w_query,
    w_key,
    w_value,
    w_outgate,
    w_forget,
    forget_bias,
    w_out,
    gain_mlp,
    w_gate,
    w_up,
    w_down,
    segment_ids,
    cotangent,
):
    row_count, length = segment_ids.shape
    tokens_local = inputs.shape[0]
    head_local = w_forget.shape[1]
    width_local = w_query.shape[1]
    head_width = width_local // head_local
    groups = lax.axis_size("tensor")
    own_count = tokens_local // groups
    own_start = lax.axis_index("tensor") * own_count

    def own_rows(array):
        return lax.dynamic_slice_in_dim(array, own_start, own_count, 0)

    inputs_full = inputs.astype(jnp.float32)
    inputs_own = own_rows(inputs_full)
    normed, inverse_attn = normalize(inputs_full, gain_attn)
    normed_low = normed.astype(jnp.bfloat16)
    queries = product(normed_low, w_query).astype(jnp.bfloat16)
    key_rows = product(normed_low, w_key).astype(jnp.bfloat16)
    value_rows = product(normed_low, w_value).astype(jnp.bfloat16)
    outgate = product(normed_low, w_outgate)
    forget = product(normed_low, w_forget) + forget_bias
    running = jnp.cumsum(log_keep(forget).reshape(row_count, length, head_local), axis=1)
    row_shape = (row_count, length, head_local, head_width)
    query_blocks = queries.reshape(row_shape)
    key_blocks = key_rows.reshape(row_shape)
    value_blocks = value_rows.reshape(row_shape)
    attended, log_total = lax.map(
        attend_forward, (query_blocks, key_blocks, value_blocks, running, segment_ids)
    )
    attended = attended.reshape(tokens_local, width_local)
    gate_open = jax.nn.sigmoid(outgate)
    gated_low = (attended * gate_open).astype(jnp.bfloat16)
    branch_part = contract_last(gated_low, w_out)
    hidden_full = inputs_full + lax.psum(branch_part.astype(jnp.bfloat16), "tensor").astype(
        jnp.float32
    )
    normed_full, inverse_full = normalize(hidden_full, gain_mlp)
    mlp_low = normed_full.astype(jnp.bfloat16)
    hidden_own = own_rows(hidden_full)
    inverse_mlp = own_rows(inverse_full)
    gate_pre = product(mlp_low, w_gate)
    up_pre = product(mlp_low, w_up)
    gate_sig = jax.nn.sigmoid(gate_pre)
    hidden_low = (gate_pre * gate_sig * up_pre).astype(jnp.bfloat16)
    ffn_part = contract_last(hidden_low, w_down)
    output_own = hidden_own + own_rows(
        lax.psum(ffn_part.astype(jnp.bfloat16), "tensor").astype(jnp.float32)
    )
    grad_hidden = product(cotangent, w_down)
    grad_gate = (grad_hidden * up_pre * gate_sig * (1.0 + gate_pre * (1.0 - gate_sig))).astype(
        jnp.bfloat16
    )
    grad_up = (grad_hidden * gate_pre * gate_sig).astype(jnp.bfloat16)
    grad_down_w = contract_first(cotangent, hidden_low)
    grad_gate_w = contract_first(mlp_low, grad_gate)
    grad_up_w = contract_first(mlp_low, grad_up)
    mlp_grad_part = contract_last(grad_gate, w_gate) + contract_last(grad_up, w_up)
    cotangent_full = cotangent.astype(jnp.float32)
    mlp_grad_full = lax.psum(mlp_grad_part.astype(jnp.bfloat16), "tensor").astype(jnp.float32)
    residual_full = cotangent_full + norm_back(hidden_full, inverse_full, gain_mlp, mlp_grad_full)
    residual_low = residual_full.astype(jnp.bfloat16)
    residual_own = own_rows(residual_full)
    mlp_grad_own = own_rows(mlp_grad_full)
    mlp_gain_part = gain_part(hidden_own, inverse_mlp, mlp_grad_own)
    grad_gated = product(residual_low, w_out)
    grad_out_w = contract_first(residual_low, gated_low)
    grad_attended = (grad_gated * gate_open).astype(jnp.bfloat16)
    grad_outgate = (grad_gated * attended * gate_open * (1.0 - gate_open)).astype(jnp.bfloat16)
    query_back, key_back, value_back, running_back = lax.map(
        attend_backward,
        (
            query_blocks,
            key_blocks,
            value_blocks,
            running,
            segment_ids,
            log_total,
            grad_attended.reshape(row_shape),
        ),
    )
    grad_queries = query_back.reshape(tokens_local, width_local).astype(jnp.bfloat16)
    grad_keys = key_back.reshape(tokens_local, width_local).astype(jnp.bfloat16)
    grad_values = value_back.reshape(tokens_local, width_local).astype(jnp.bfloat16)
    rate_back = lax.cumsum(running_back, axis=1, reverse=True).reshape(tokens_local, head_local)
    grad_forget = (rate_back * jax.nn.sigmoid(-forget)).astype(jnp.bfloat16)
    grad_query_w = contract_first(normed_low, grad_queries)
    grad_key_w = contract_first(normed_low, grad_keys)
    grad_value_w = contract_first(normed_low, grad_values)
    grad_outgate_w = contract_first(normed_low, grad_outgate)
    grad_forget_w = contract_first(normed_low, grad_forget)
    bias_part = jnp.sum(grad_forget.astype(jnp.float32), axis=0)
    attn_grad_part = contract_last(grad_queries, w_query) + contract_last(grad_keys, w_key)
    attn_grad_part = (
        attn_grad_part
        + contract_last(grad_values, w_value)
        + contract_last(grad_outgate, w_outgate)
    )
    attn_grad_part = attn_grad_part + contract_last(grad_forget, w_forget)
    attn_grad_own = own_rows(
        lax.psum(attn_grad_part.astype(jnp.bfloat16), "tensor").astype(jnp.float32)
    )
    inverse_own = own_rows(inverse_attn)
    grad_inputs = residual_own + norm_back(inputs_own, inverse_own, gain_attn, attn_grad_own)
    attn_gain_part = gain_part(inputs_own, inverse_own, attn_grad_own)
    head_start = lax.axis_index("tensor") * head_local
    bias_full = lax.dynamic_update_slice(
        jnp.zeros((head_local * groups,), jnp.float32), bias_part, (head_start,)
    )
    small_sums = lax.psum((attn_gain_part, mlp_gain_part, bias_full), ("dp", "tensor"))
    bias_own = lax.dynamic_slice_in_dim(small_sums[2], head_start, head_local, 0)
    summed = (
        lax.psum_scatter(
            grad_query_w.astype(jnp.bfloat16), "dp", scatter_dimension=0, tiled=True
        ).astype(jnp.float32),
        lax.psum_scatter(
            grad_key_w.astype(jnp.bfloat16), "dp", scatter_dimension=0, tiled=True
        ).astype(jnp.float32),
        lax.psum_scatter(
            grad_value_w.astype(jnp.bfloat16), "dp", scatter_dimension=0, tiled=True
        ).astype(jnp.float32),
        lax.psum_scatter(
            grad_outgate_w.astype(jnp.bfloat16), "dp", scatter_dimension=0, tiled=True
        ).astype(jnp.float32),
        lax.psum_scatter(
            grad_forget_w.astype(jnp.bfloat16), "dp", scatter_dimension=0, tiled=True
        ).astype(jnp.float32),
        lax.psum_scatter(
            grad_out_w.astype(jnp.bfloat16), "dp", scatter_dimension=0, tiled=True
        ).astype(jnp.float32),
        lax.psum_scatter(
            grad_gate_w.astype(jnp.bfloat16), "dp", scatter_dimension=0, tiled=True
        ).astype(jnp.float32),
        lax.psum_scatter(
            grad_up_w.astype(jnp.bfloat16), "dp", scatter_dimension=0, tiled=True
        ).astype(jnp.float32),
        lax.psum_scatter(
            grad_down_w.astype(jnp.bfloat16), "dp", scatter_dimension=0, tiled=True
        ).astype(jnp.float32),
    )
    return (
        output_own,
        grad_inputs,
        small_sums[0],
        summed[0],
        summed[1],
        summed[2],
        summed[3],
        summed[4],
        bias_own,
        summed[5],
        small_sums[1],
        summed[6],
        summed[7],
        summed[8],
    )


def solution(mesh):
    placed = (
        P("dp", None),
        P(),
        P(None, "tensor"),
        P(None, "tensor"),
        P(None, "tensor"),
        P(None, "tensor"),
        P(None, "tensor"),
        P("tensor"),
        P(None, "tensor"),
        P(),
        P(None, "tensor"),
        P(None, "tensor"),
        P(None, "tensor"),
        P("dp", None),
        P("dp", None),
    )
    return jax.shard_map(
        on_device,
        mesh=mesh,
        in_specs=placed,
        out_specs=(
            P(("dp", "tensor"), None),
            P(("dp", "tensor"), None),
            P(),
            P("dp", "tensor"),
            P("dp", "tensor"),
            P("dp", "tensor"),
            P("dp", "tensor"),
            P("dp", "tensor"),
            P("tensor"),
            P("dp", "tensor"),
            P(),
            P("dp", "tensor"),
            P("dp", "tensor"),
            P("dp", "tensor"),
        ),
        check_vma=False,
    )
```

profile of v0, /device:TPU:0, one launch (start us, length us, event | category | flops | bytes accessed | tf_op | source)
XLA Modules:
  0.0 1729.5 jit_solution(7672722581979576592)
XLA Ops:
  75.2 139.1 %while.28 = (s32[]{:T(128)}, f32[2,1024,6,64]{1,0,3,2:T(2,128)}, f32[2,6,1024,1]{2,1,3,0:T(8,128)S(1)}, bf16[2,1024,6,64]{1,3,2,0:T(8,128)(2,1)}, s32[2,1024]{1,...) while((s32[]{:T(128)}, f32[2,1024,6,64]{1,0,3,2:T(2,128)}, ...), condition=%wide.region_6.7_spmd, body=%wide.region_3.6_spmd.sunk | while | flops 1726998528 | bytes 96662664 | solution.py:140
  76.1 12.8 fusion.143
  88.9 12.7 fusion.144
  101.6 12.8 fusion.145
  117.1 27.8 %dynamic_update_slice.37 = f32[2,1024,6,64]{1,0,3,2:T(2,128)} dynamic-update-slice(f32[2,1024,6,64]{1,0,3,2:T(2,128)} %get-tuple-element.483, f32[1,1024,6,64]{1,0,3,2:T(1,128)} %copy.174, s32[]{:T(128)} %get-tuple-element.482, s32[]{:T(128)} %constant.59.clone.1..sunk, s32[]{:T(128)} %constant.59.clone.1..sunk, s32[]{:T(128)} %constant.59.clone.1..sunk) | dynamic-update-slice | bytes 3145732 | tf_op jit(solution)/shard_map/while/body/jit(dynamic_update_index_in_dim)/dynamic_update_slice | solution.py:140
  145.5 12.8 fusion.143
  158.3 12.7 fusion.144
  171.0 12.8 fusion.145
  186.6 27.8 %dynamic_update_slice.37 = f32[2,1024,6,64]{1,0,3,2:T(2,128)} dynamic-update-slice(f32[2,1024,6,64]{1,0,3,2:T(2,128)} %get-tuple-element.483, f32[1,1024,6,64]{1,0,3,2:T(1,128)} %copy.174, s32[]{:T(128)} %get-tuple-element.482, s32[]{:T(128)} %constant.59.clone.1..sunk, s32[]{:T(128)} %constant.59.clone.1..sunk, s32[]{:T(128)} %constant.59.clone.1..sunk) | dynamic-update-slice | bytes 3145732 | tf_op jit(solution)/shard_map/while/body/jit(dynamic_update_index_in_dim)/dynamic_update_slice | solution.py:140
  223.3 9.5 multiply_convert_fusion.7
  239.5 225.6 %all-reduce.6.cloned.1.call-done = bf16[2048,1536]{1,0:T(8,128)(2,1)} async-done(((bf16[2048,1536]{1,0:T(8,128)(2,1)}), bf16[2048,1536]{1,0:T(8,128)(2,1)}) %all-reduce.6.cloned.1.call-update) | async-done | bytes 6291472 | tf_op jit(solution)/shard_map/psum | solution.py:147
  477.6 8.8 fusion.64
  486.5 8.8 fusion.65
  495.3 15.7 multiply_convert_fusion.2
  511.0 12.5 fusion.66
  523.5 12.3 add_convert_fusion.1
  535.8 11.4 fusion.51
  552.0 11.4 convolution_convert_fusion.4
  563.5 11.3 convolution_convert_fusion.3
  574.9 182.9 %all-reduce.8.cloned.1.call-done = bf16[2048,1536]{1,0:T(8,128)(2,1)} async-done(((bf16[2048,1536]{1,0:T(8,128)(2,1)}), bf16[2048,1536]{1,0:T(8,128)(2,1)}) %all-reduce.8.cloned.1.call-update) | async-done | bytes 6291472 | tf_op jit(solution)/shard_map/psum | solution.py:172
  757.8 8.5 multiply_reduce_fusion.1
  766.4 14.8 multiply_add_fusion
  781.2 10.8 multiply_convert_fusion.6
  801.5 178.7 %while.29 = (s32[]{:T(128)}, bf16[2,1024,6,64]{1,3,2,0:T(8,128)(2,1)}, bf16[2,1024,6,64]{1,3,2,0:T(8,128)(2,1)}, bf16[2,1024,6,64]{1,3,2,0:T(8,128)(2,1)}, f32[2...) while((s32[]{:T(128)}, ...), condition=%wide.region_16.17_spmd, body=%wide.region_12.16_spmd.sunk | while | flops 4112240640 | bytes 239224112 | solution.py:182
  801.7 13.4 fusion.154
  816.7 20.8 %multiply_reduce_fusion.6 = (f32[6,1024]{1,0:T(8,128)S(1)}, f32[6,1024,1024]{1,2,0:T(8,128)}) fusion(f32[6,1024,1024]{1,2,0:T(8,128)} %fusion.154, f32[6,1024]{1,0:T(8,128)S(1)} %dynamic-slice_bitcast_fusion.7, f32[6,1024]{1,0:T(8,128)S(1)} %dynamic-slice_bitcast_fusion.8, bf16[2,1024,6,64]{1,3,2,0:T(8,128)(2,1)} %get-tuple-element.533, ...), kind=kOutput, calls=%fused_computation.24.clone.1 | convolution fusion | flops 849340416 | bytes 53076992 | tf_op jit(solution)/shard_map/while/body/eval_jaxpr/qhd,khd->hqk/dot_general | solution.py:46
  837.5 22.8 %fusion.156 = (f32[6,1024]{1,0:T(8,128)S(1)}, f32[6,1024]{1,0:T(8,128)S(1)}, bf16[6,1024,1024]{1,2,0:T(8,128)(2,1)}) fusion(f32[6,1024,1024]{1,2,0:T(8,128)} %get-tuple-element.467, f32[6,1024,1024]{1,2,0:T(8,128)} %fusion.154, f32[6,1024]{1,0:T(8,128)S(1)} %get-tuple-element.468), kind=kLoop, calls=%fused_computation.118.clone.1 | loop fusion | flops 31444992 | bytes 62988288 | tf_op jit(solution)/shard_map/while/body/eval_jaxpr/reduce_sum | solution.py:93
  860.3 8.8 bitcast_dynamic-update-slice_fusion.12
  869.1 7.9 bitcast_dynamic-update-slice_fusion.11
  878.2 13.8 bitcast_dynamic-update-slice_fusion.13
  892.0 13.6 fusion.154
  907.2 19.7 %multiply_reduce_fusion.6 = (f32[6,1024]{1,0:T(8,128)S(1)}, f32[6,1024,1024]{1,2,0:T(8,128)}) fusion(f32[6,1024,1024]{1,2,0:T(8,128)} %fusion.154, f32[6,1024]{1,0:T(8,128)S(1)} %dynamic-slice_bitcast_fusion.7, f32[6,1024]{1,0:T(8,128)S(1)} %dynamic-slice_bitcast_fusion.8, bf16[2,1024,6,64]{1,3,2,0:T(8,128)(2,1)} %get-tuple-element.533, ...), kind=kOutput, calls=%fused_computation.24.clone.1 | convolution fusion | flops 849340416 | bytes 53076992 | tf_op jit(solution)/shard_map/while/body/eval_jaxpr/qhd,khd->hqk/dot_general | solution.py:46
  926.9 22.4 %fusion.156 = (f32[6,1024]{1,0:T(8,128)S(1)}, f32[6,1024]{1,0:T(8,128)S(1)}, bf16[6,1024,1024]{1,2,0:T(8,128)(2,1)}) fusion(f32[6,1024,1024]{1,2,0:T(8,128)} %get-tuple-element.467, f32[6,1024,1024]{1,2,0:T(8,128)} %fusion.154, f32[6,1024]{1,0:T(8,128)S(1)} %get-tuple-element.468), kind=kLoop, calls=%fused_computation.118.clone.1 | loop fusion | flops 31444992 | bytes 62988288 | tf_op jit(solution)/shard_map/while/body/eval_jaxpr/reduce_sum | solution.py:93
  949.3 8.7 bitcast_dynamic-update-slice_fusion.12
  966.6 13.2 bitcast_dynamic-update-slice_fusion.13
  980.2 14.9 reduce-window.16
  1003.5 7.7 convolution_convert_fusion.8
  1023.4 11.1 convolution_convert_fusion
  1045.3 10.0 fusion.67
  1067.0 10.0 fusion.69
  1088.3 20.1 %add_convert_fusion = bf16[2048,1536]{1,0:T(8,128)(2,1)} fusion(f32[2048,1536]{1,0:T(8,128)} %fusion.70, f32[2048,1536]{1,0:T(8,128)} %fusion.69, f32[2048,1536]{1,0:T(8,128)} %fusion.67, f32[2048,1536]{1,0:T(8,128)} %fusion.68, bf16[2048,6]{0,1:T(8,128)(2,1)S(1)} %get-tuple-element.315, bf16[1536,6]{0,1:T(8,128)(2,1)S(1)} %copy-done.32), kind=kOutput, calls=%fused_computation.61 | convolution fusion | flops 53477376 | bytes 56666112 | tf_op jit(solution)/shard_map/dot_general | solution.py:10
  1108.5 9.1 convert_element_type.156
  1127.3 9.3 convert_element_type.172
  1141.4 15.7 reduce-scatter.18.cloned.1.call-done
  1158.7 38.8 %reduce-scatter.22.cloned.1.call-done = bf16[192,384]{1,0:T(8,128)(2,1)} async-done(((bf16[1536,384]{1,0:T(8,128)(2,1)}), bf16[192,384]{1,0:T(8,128)(2,1)}) %reduce-scatter.22.cloned.1.call-update) | async-done | bytes 147472 | tf_op jit(solution)/shard_map/reduce_scatter | solution.py:240
  1199.2 39.3 %reduce-scatter.20.cloned.1.call-done = bf16[192,384]{1,0:T(8,128)(2,1)} async-done(((bf16[1536,384]{1,0:T(8,128)(2,1)}), bf16[192,384]{1,0:T(8,128)(2,1)}) %reduce-scatter.20.cloned.1.call-update) | async-done | bytes 147472 | tf_op jit(solution)/shard_map/reduce_scatter | solution.py:234
  1240.1 427.6 %all-reduce.10.cloned.1.call-done = (bf16[2048,1536]{1,0:T(8,128)(2,1)}, bf16[2048,1536]{1,0:T(8,128)(2,1)}) async-done(((bf16[2048,1536]{1,0:T(8,128)(2,1)}, bf16[2048,1536]{1,0:T(8,128)(2,1)}), (bf16[2048,1536]{1,0:T(8,128)(2,1)}, bf16[2048,1536]{1,0:T(8,128)(2,1)})) %all-reduce.10.cloned.1.call-update) | async-done | bytes 12582928 | tf_op jit(solution)/shard_map/psum | solution.py:160
  1676.5 39.4 %all-reduce = (f32[1536]{0:T(1024)}, f32[24]{0:T(128)S(1)}, f32[1536]{0:T(1024)}) all-reduce(f32[1536]{0:T(1024)S(1)} %get-tuple-element.266, f32[24]{0:T(128)S(1)} %dynamic_update_slice.24, f32[1536]{0:T(1024)S(1)} %get-tuple-element.323), channel_id=1, replica_groups=mesh['dp'=8,'tensor'=4] {'dp','tensor'}, use_global_device_ids=true, to_apply=%region_22.23 | all-reduce | flops 3096 | bytes 24768 | tf_op jit(solution)/shard_map/psum | solution.py:222
  (259 shorter events, 218.9 us)
Async XLA Ops:
  7.2 488.1 %copy-start = (bf16[1536,1024]{1,0:T(8,128)(2,1)S(1)}, bf16[1536,1024]{1,0:T(8,128)(2,1)}, u32[]{:S(2)}) copy-start(bf16[1536,1024]{1,0:T(8,128)(2,1)} %param.31) | copy-start | bytes 9437188
  7.2 457.9 %all-reduce.6.cloned.1.call-start = ((), (), s32[]{:S(2)}) async-start(), calls=%async_computation.9 | async-start | bytes 12582912 | tf_op jit(solution)/shard_map/psum | solution.py:147
  65.7 9.5 copy-start.28
  88.9 12.7 copy-start.7
  158.3 12.7 copy-start.7
  214.3 9.0 copy-start.15
  214.3 9.0 copy-start.25
  223.3 10.7 copy-start.22
  239.4 232.6 %copy-start.33 = (f32[1536]{0:T(1024)S(1)}, f32[1536]{0:T(1024)}, u32[]{:S(2)}) copy-start(f32[1536]{0:T(1024)} %param.28) | copy-start | bytes 18436
  239.4 518.3 %all-reduce.8.cloned.1.call-start = ((), (), s32[]{:S(2)}) async-start(), calls=%async_computation.10 | async-start | bytes 12582912 | tf_op jit(solution)/shard_map/psum | solution.py:172
  472.0 294.3 %copy-start.30 = (f32[2048]{0:T(1024)}, f32[2048]{0:T(1024)S(1)}, u32[]{:S(2)}) copy-start(f32[2048]{0:T(1024)S(1)} %add_rsqrt_fusion) | copy-start | bytes 24580
  477.6 8.9 copy-start.14
  477.6 8.9 copy-start.39
  477.6 17.7 %slice-start.5 = ((s8[6291456]{0:T(1024)(128)(4,1)}), s8[4194304]{0:T(1024)(128)(4,1)S(1)}, s32[]{:S(2)}) async-start(s8[6291456]{0:T(1024)(128)(4,1)} %bitcast.230), calls=%async_computation.26 | async-start | bytes 8388608
  486.5 8.8 slice-start.6
  511.0 12.5 copy-start.40
  511.0 12.5 copy-start.43
  535.8 583.3 %reduce-scatter.30.cloned.1.call-start = ((), (), s32[]{:S(2)}) async-start(), calls=%async_computation.19 | async-start | bytes 3538944
  552.0 571.2 %reduce-scatter.24.cloned.1.call-start = ((), (), s32[]{:S(2)}) async-start(), calls=%async_computation.16 | async-start | bytes 3538944 | tf_op jit(solution)/shard_map/reduce_scatter | solution.py:243
  563.4 561.7 %reduce-scatter.26.cloned.1.call-start = ((), (), s32[]{:S(2)}) async-start(), calls=%async_computation.17 | async-start | bytes 3538944 | tf_op jit(solution)/shard_map/reduce_scatter | solution.py:246
  574.8 561.8 %reduce-scatter.28.cloned.1.call-start = ((), (), s32[]{:S(2)}) async-start(), calls=%async_computation.18 | async-start | bytes 442368
  781.2 10.8 copy-start.2
  792.0 9.6 copy-start.16
  792.0 9.6 copy-start.26
  792.0 9.6 copy-start.29
  837.5 22.8 %copy-start.8 = (bf16[2,1024,6,64]{1,3,2,0:T(8,128)(2,1)S(1)}, bf16[2,1024,6,64]{1,3,2,0:T(8,128)(2,1)}, u32[]{:S(2)}) copy-start(bf16[2,1024,6,64]{1,3,2,0:T(8,128)(2,1)} %get-tuple-element.535) | copy-start | bytes 4718596 | tf_op jit(solution)/shard_map/while
  837.5 22.8 %copy-start.19 = (bf16[2,1024,6,64]{1,3,2,0:T(8,128)(2,1)S(1)}, bf16[2,1024,6,64]{1,3,2,0:T(8,128)(2,1)}, u32[]{:S(2)}) copy-start(bf16[2,1024,6,64]{1,3,2,0:T(8,128)(2,1)} %get-tuple-element.517) | copy-start | bytes 4718596 | tf_op jit(solution)/shard_map/while
  860.3 8.8 copy-start.9
  860.3 8.8 copy-start.17
  926.9 22.4 %copy-start.8 = (bf16[2,1024,6,64]{1,3,2,0:T(8,128)(2,1)S(1)}, bf16[2,1024,6,64]{1,3,2,0:T(8,128)(2,1)}, u32[]{:S(2)}) copy-start(bf16[2,1024,6,64]{1,3,2,0:T(8,128)(2,1)} %get-tuple-element.535) | copy-start | bytes 4718596 | tf_op jit(solution)/shard_map/while
  926.9 22.4 %copy-start.19 = (bf16[2,1024,6,64]{1,3,2,0:T(8,128)(2,1)S(1)}, bf16[2,1024,6,64]{1,3,2,0:T(8,128)(2,1)}, u32[]{:S(2)}) copy-start(bf16[2,1024,6,64]{1,3,2,0:T(8,128)(2,1)} %get-tuple-element.517) | copy-start | bytes 4718596 | tf_op jit(solution)/shard_map/while
  949.3 8.7 copy-start.9
  980.2 21.1 %copy-start.27 = (f32[2048,6]{0,1:T(8,128)S(1)}, f32[2048,6]{0,1:T(8,128)}, u32[]{:S(2)}) copy-start(f32[2048,6]{0,1:T(8,128)} %get-tuple-element.330) | copy-start | bytes 147460
  1003.4 134.6 %reduce-scatter.14.cloned.1.call-start = ((), (), s32[]{:S(2)}) async-start(), calls=%async_computation.11 | async-start | bytes 1327104 | tf_op jit(solution)/shard_map/reduce_scatter | solution.py:225
  1011.2 128.5 %reduce-scatter.16.cloned.1.call-start = ((), (), s32[]{:S(2)}) async-start(), calls=%async_computation.12 | async-start | bytes 1327104 | tf_op jit(solution)/shard_map/reduce_scatter | solution.py:228
  1023.2 133.9 %reduce-scatter.18.cloned.1.call-start = ((), (), s32[]{:S(2)}) async-start(), calls=%async_computation.13 | async-start | bytes 1327104 | tf_op jit(solution)/shard_map/reduce_scatter | solution.py:231
  1023.4 11.1 copy-start.21
  1045.0 152.5 %reduce-scatter.22.cloned.1.call-start = ((), (), s32[]{:S(2)}) async-start(), calls=%async_computation.15 | async-start | bytes 1327104 | tf_op jit(solution)/shard_map/reduce_scatter | solution.py:240
  1045.3 10.0 copy-start.12
  1045.3 10.0 copy-start.24
  1045.3 16.7 slice-start
  1045.3 16.7 slice-start.1
  1066.7 171.8 %reduce-scatter.20.cloned.1.call-start = ((), (), s32[]{:S(2)}) async-start(), calls=%async_computation.14 | async-start | bytes 1327104 | tf_op jit(solution)/shard_map/reduce_scatter | solution.py:234
  1067.0 10.0 copy-start.10
  1067.0 10.0 copy-start.23
  1067.0 16.5 slice-start.3
  1088.0 579.8 %all-reduce.10.cloned.1.call-start = ((), (), s32[]{:S(2)}) async-start(), calls=%async_computation.20 | async-start | bytes 25165824 | tf_op jit(solution)/shard_map/psum | solution.py:160
  1127.3 540.5 %copy-start.35 = (f32[1536]{0:T(1024)S(1)}, f32[1536]{0:T(1024)}, u32[]{:S(2)}) copy-start(f32[1536]{0:T(1024)} %param.20) | copy-start | bytes 18436
  (22 other events, 102.0 us)
Sparse Core Ops, SparseCore 0:
  239.5 225.5 all-reduce.5
  535.9 221.8 all-reduce.7
  761.1 45.1 reduce-scatter.29
  810.0 46.1 reduce-scatter.23
  859.4 46.3 reduce-scatter.25
  1003.5 32.6 reduce-scatter.27
  1039.8 36.7 reduce-scatter.13
  1079.8 36.7 reduce-scatter.15
  1120.2 36.8 reduce-scatter.17
  1160.7 36.7 reduce-scatter.21
  1201.7 36.7 reduce-scatter.19
  1240.9 426.7 all-reduce.9
where the time goes:
time: 1740 us; the launch traced here: 1730 us
  waiting for transfers between devices  930 us (53%)
  matrix products  418 us (24%)
  other arithmetic  183 us (11%)
  local copies, waits for them, and re-layouts  141 us (8%)
  blocking collectives  39.4 us (2%)
    psum x1, waiting for transfers between devices, on_device(): lax.psum(ffn_part.astype(jnp.bfloat16), 'tensor').astype(jnp.float32)  428 us
    psum x1, waiting for transfers between devices, on_device(): lax.psum(branch_part.astype(jnp.bfloat16), 'tensor').astype(jnp.float32)  226 us
    psum x1, waiting for transfers between devices, on_device(): lax.psum(mlp_grad_part.astype(jnp.bfloat16), 'tensor').astype(jnp.float32)  183 us
    dot_general x9, matrix products, contract_last(): lax.dot_general(left, right, (((1,), (1,)), ((), ())), preferred_element_...  94.5 us
    dot_general x9, matrix products, product(): return jnp.dot(left, right, preferred_element_type=jnp.float32)  78.9 us
    dot_general x9, matrix products, contract_first(): lax.dot_general(left, right, (((0,), (0,)), ((), ())), preferred_element_...  66.4 us
    dot_general x4, matrix products, row_scores(): jnp.einsum('qhd,khd->hqk', queries, key_rows, preferred_element_type=jnp....  66.1 us
    dynamic_update_slice x4, local copies, waits for them, and re-layouts, on_device(): lax.map(attend_forward, (query_blocks, key_blocks, value_blocks, running,...  61 us
  transfers between devices with their start and end apart: 12, of which 6 were waited for; matrix products, arithmetic and copies ran while one was open for 24% of the time, Pallas kernels for 0%

commit v1 on v0

v1 whole, which is shorter than its diff:
```python
import jax
import jax.numpy as jnp
from jax import lax
from jax.sharding import PartitionSpec as P
from jax.experimental import pallas as pl
from jax.experimental.pallas import tpu as pltpu

LOG2E = 1.4426950408889634
LN2 = 0.6931471805599453
HEAD = 64
BLK = 256

def last(a, b):
    return lax.dot_general(a, b, (((1,), (1,)), ((), ())), preferred_element_type=jnp.float32)
def first(a, b):
    return lax.dot_general(a, b, (((0,), (0,)), ((), ())), preferred_element_type=jnp.float32)
def mm(a, b):
    return jnp.dot(a, b, preferred_element_type=jnp.float32)

def fwd_kernel(q_ref, k_ref, v_ref, g_ref, crow_ref, scol_ref, srow_ref, z_ref, o_ref, lse_ref):
    length, width = q_ref.shape
    hp = width // HEAD
    lane = lax.broadcasted_iota(jnp.int32, (1, width), 1) // HEAD
    tri = lax.broadcasted_iota(jnp.int32, (BLK, BLK), 0) >= lax.broadcasted_iota(jnp.int32, (BLK, BLK), 1)
    for i in range(length // BLK):
        rows = pl.ds(i * BLK, BLK)
        reach = (i + 1) * BLK
        q = q_ref[rows, :]
        same = scol_ref[rows, :] == srow_ref[:, :reach]
        if i:
            allowed = jnp.concatenate([same[:, :reach - BLK], same[:, reach - BLK:] & tri], axis=1)
        else:
            allowed = same & tri
        out = jnp.zeros((BLK, width), jnp.float32)
        stats = jnp.zeros((BLK, 128), jnp.float32)
        for h in range(hp):
            s = last(jnp.where(lane == h, q, 0), k_ref[:reach, :])
            s = jnp.where(allowed, s - crow_ref[0, h:h + 1, :reach], -1e30)
            top = jnp.max(s, axis=1, keepdims=True)
            e = jnp.exp2(s - top)
            total = jnp.sum(e, axis=1, keepdims=True)
            part = mm(e.astype(jnp.bfloat16), v_ref[:reach, :])
            out = jnp.where(lane == h, part * (1.0 / total), out)
            stats = jnp.where(lax.broadcasted_iota(jnp.int32, (BLK, 128), 1) == h, top + jnp.log2(total), stats)
        g = g_ref[rows, :].astype(jnp.float32)
        z_ref[rows, :] = (out * jax.nn.sigmoid(g)).astype(jnp.bfloat16)
        o_ref[rows, :] = out.astype(jnp.bfloat16)
        lse_ref[0, :, i * BLK:(i + 1) * BLK] = stats.T[:hp, :]

def attend_forward(q, k, v, g, crow, scol, srow):
    length, n = q.shape
    heads = n // HEAD
    hp = 2 if heads % 2 == 0 else heads
    steps = heads // hp
    width = hp * HEAD
    blk = pl.BlockSpec((length, width), lambda i: (0, i))
    return pl.pallas_call(
        fwd_kernel,
        grid=(steps,),
        in_specs=[blk] * 4 + [pl.BlockSpec((1, hp, length), lambda i: (i, 0, 0)),
                  pl.BlockSpec((length, 1), lambda i: (0, 0)), pl.BlockSpec((1, length), lambda i: (0, 0))],
        out_specs=[blk, blk, pl.BlockSpec((1, hp, length), lambda i: (i, 0, 0))],
        out_shape=[jax.ShapeDtypeStruct((length, n), jnp.bfloat16), jax.ShapeDtypeStruct((length, n), jnp.bfloat16),
                   jax.ShapeDtypeStruct((steps, hp, length), jnp.float32)],
        compiler_params=pltpu.CompilerParams(vmem_limit_bytes=40 << 20),
        cost_estimate=pl.CostEstimate(flops=heads * length * length * 512, bytes_accessed=12 * length * n, transcendentals=heads * length * length // 2),
        name="attend_forward",
    )(q, k, v, g, crow.reshape(steps, hp, length), scol, srow)

def bwd_kernel(q_ref, k_ref, v_ref, g_ref, o_ref, dz_ref, lse_ref, ccol_ref, scol_ref, srow_ref,
               dq_ref, dk_ref, dv_ref, dg_ref, dc_ref, dqacc):
    length, width = q_ref.shape
    hp = width // HEAD
    lane = lax.broadcasted_iota(jnp.int32, (1, width), 1) // HEAD
    tri = lax.broadcasted_iota(jnp.int32, (BLK, BLK), 1) >= lax.broadcasted_iota(jnp.int32, (BLK, BLK), 0)
    blocks = length // BLK
    sig = jax.nn.sigmoid(g_ref[...].astype(jnp.float32))
    dz = dz_ref[...].astype(jnp.float32)
    out = o_ref[...].astype(jnp.float32)
    dout = (dz * sig).astype(jnp.bfloat16)
    dg_ref[...] = (dz * out * sig * (1.0 - sig)).astype(jnp.bfloat16)
    prod = (dout.astype(jnp.float32) * out)
    prod_hi = prod.astype(jnp.bfloat16)
    prod_lo = (prod - prod_hi.astype(jnp.float32)).astype(jnp.bfloat16)
    dqs = [None] * blocks
    for h in range(hp):
        head = lane == h
        ones = jnp.broadcast_to(jnp.where(head, 1.0, 0.0).astype(jnp.bfloat16), (8, width))
        centre = (last(ones, prod_hi) + last(ones, prod_lo))[0:1, :]
        q_one = jnp.where(head, q_ref[...], 1.0)
        q_zero = jnp.where(head, q_ref[...], 0.0)
        k_one = jnp.where(head, k_ref[...], 1.0)
        d_zero = jnp.where(head, dout, 0.0)
        dqacc[...] = jnp.zeros_like(dqacc)
        for j in range(blocks):
            keys = pl.ds(j * BLK, BLK)
            lo = j * BLK
            s = last(k_ref[keys, :], q_zero[lo:, :])
            s = s - ccol_ref[0, keys, h:h + 1] - lse_ref[0, h:h + 1, lo:]
            same = scol_ref[keys, :] == srow_ref[:, lo:]
            if j < blocks - 1:
                allowed = jnp.concatenate([same[:, :BLK] & tri, same[:, BLK:]], axis=1)
            else:
                allowed = same & tri
            p = jnp.where(allowed, jnp.exp2(s), 0.0)
            dp = last(v_ref[keys, :], d_zero[lo:, :])
            ds = (p * (dp - centre[:, lo:])).astype(jnp.bfloat16)
            dv = mm(p.astype(jnp.bfloat16), dout[lo:, :])
            dk = mm(ds, q_one[lo:, :])
            dqacc[lo:, :] += first(ds, k_one[lo:lo + BLK, :])
            if h == 0:
                dk_ref[keys, :] = (dk * LN2).astype(jnp.bfloat16)
                dv_ref[keys, :] = dv.astype(jnp.bfloat16)
                dc_ref[0, keys, :] = -dk
            else:
                dk_ref[keys, :] = jnp.where(head, (dk * LN2).astype(jnp.bfloat16), dk_ref[keys, :])
                dv_ref[keys, :] = jnp.where(head, dv.astype(jnp.bfloat16), dv_ref[keys, :])
                dc_ref[0, keys, :] = jnp.where(lane == 0, -dk, dc_ref[0, keys, :]) if h == 1 else jnp.where(lane == h - 1, -dk, dc_ref[0, keys, :])
        dq = dqacc[...]
        if h == 0:
            dq_ref[...] = (dq * 0.125).astype(jnp.bfloat16)
            dc_ref[0] = dc_ref[0] + dq
        else:
            dq_ref[...] = jnp.where(head, (dq * 0.125).astype(jnp.bfloat16), dq_ref[...])
            dc_ref[0] = jnp.where(lane == h - 1, dc_ref[0] + dq, dc_ref[0])

def attend_backward(q, k, v, g, o, dz, lse, ccol, scol, srow):
    length, n = q.shape
    heads = n // HEAD
    hp = 2 if heads % 2 == 0 else heads
    steps = heads // hp
    width = hp * HEAD
    blk = pl.BlockSpec((length, width), lambda i: (0, i))
    low = jax.ShapeDtypeStruct((length, n), jnp.bfloat16)
    return pl.pallas_call(
        bwd_kernel,
        grid=(steps,),
        in_specs=[blk] * 6 + [pl.BlockSpec((1, hp, length), lambda i: (i, 0, 0)),
                  pl.BlockSpec((1, length, hp), lambda i: (i, 0, 0)),
                  pl.BlockSpec((length, 1), lambda i: (0, 0)), pl.BlockSpec((1, length), lambda i: (0, 0))],
        out_specs=[blk] * 4 + [pl.BlockSpec((1, length, width), lambda i: (i, 0, 0))],
        out_shape=[low] * 4 + [jax.ShapeDtypeStruct((steps, length, width), jnp.float32)],
        scratch_shapes=[pltpu.VMEM((length, width), jnp.float32)],
        compiler_params=pltpu.CompilerParams(vmem_limit_bytes=48 << 20),
        cost_estimate=pl.CostEstimate(flops=heads * length * length * 1280, bytes_accessed=24 * length * n, transcendentals=heads * length * length // 2),
        name="attend_backward",
    )(q, k, v, g, o, dz, lse, ccol.reshape(length, steps, hp).transpose(1, 0, 2), scol, srow)
eps = 1e-06


def normalize(values, scale_gain):
    inverse = lax.rsqrt(jnp.mean(values * values, axis=-1, keepdims=True) + eps)
    return values * inverse * scale_gain, inverse


def norm_back(values, inverse, scale_gain, upstream):
    unit_rows = values * inverse
    scaled = upstream * scale_gain
    return inverse * (scaled - unit_rows * jnp.mean(scaled * unit_rows, axis=-1, keepdims=True))


def log_keep(values):
    return jnp.minimum(values, 0.0) - jnp.log1p(jnp.exp(-jnp.abs(values)))


def low(values):
    return values.astype(jnp.bfloat16)


def bits_of(size):
    return [1 << b for b in range(size.bit_length() - 1)]


class Place:
    def __init__(self, rows):
        self.tensor = lax.axis_size("tensor")
        self.dp = lax.axis_size("dp")
        self.rows = rows
        self.group = self.tensor // rows
        self.at = lax.axis_index("tensor")
        self.dp_at = lax.axis_index("dp")
        self.row = self.at // self.group
        self.member = self.at % self.group

    def slot_owner(self, at, step, turn):
        row, member = at // self.group, at % self.group
        return ((row + turn) % self.rows) * self.group + (member + step) % self.group

    def from_slot(self, value, step, turn):
        pairs = [(self.slot_owner(i, step, turn), i) for i in range(self.tensor)]
        return lax.ppermute(value, "tensor", pairs)

    def to_slot(self, value, step, turn):
        pairs = [(i, self.slot_owner(i, step, turn)) for i in range(self.tensor)]
        return lax.ppermute(value, "tensor", pairs)

    def swap(self, value, bit):
        return lax.ppermute(value, "dp", [(i, i ^ bit) for i in range(self.dp)])

    def has(self, bit):
        return (self.dp_at // bit) % 2

    def piece(self, shard):
        count = shard.shape[0] // self.dp
        return lax.dynamic_slice_in_dim(shard, self.dp_at * count, count, 0)

    def gather(self, piece, flip):
        bits = bits_of(self.dp)
        order = bits[1:] if flip else bits[:0:-1]
        held = piece
        done = []
        for bit in order + bits[:1]:
            other = self.swap(held, bit)
            axis = sum(1 for b in done if b > bit)
            mine_high = self.has(bit) == 1
            first_half = jnp.where(mine_high, other, held)
            second_half = jnp.where(mine_high, held, other)
            held = jnp.stack([first_half, second_half], axis)
            done.append(bit)
        return held.reshape((-1, piece.shape[-1]))

    def scatter(self, partial, flip):
        bits = bits_of(self.dp)
        rows, width = partial.shape
        held = partial.reshape((2,) * len(bits) + (rows // self.dp, width))
        order = bits[:1] + (bits[1:] if flip else bits[:0:-1])
        left = bits[::-1]
        for bit in order:
            axis = left.index(bit)
            mine = self.has(bit)
            keep = lax.dynamic_index_in_dim(held, mine, axis, keepdims=False)
            send = lax.dynamic_index_in_dim(held, 1 - mine, axis, keepdims=False)
            got = self.swap(send, bit)
            held = low(keep.astype(jnp.float32) + got.astype(jnp.float32))
            left = [b for b in left if b != bit]
        return held

    def sum_all(self, value):
        for bit in bits_of(self.dp):
            value = value + self.swap(value, bit)
        for bit in bits_of(self.tensor):
            value = value + lax.ppermute(value, "tensor", [(i, i ^ bit) for i in range(self.tensor)])
        return value

    def shares(self, make):
        total = make(self.member)
        for step in range(1, self.group):
            theirs = low(make((self.member + step) % self.group))
            pairs = [(i, (i // self.group) * self.group + (i % self.group + step) % self.group) for i in range(self.tensor)]
            total = total + lax.ppermute(theirs, "tensor", pairs).astype(jnp.float32)
        return total


def on_device(
    inputs, gain_attn, w_query, w_key, w_value, w_outgate, w_forget, forget_bias, w_out,
    gain_mlp, w_gate, w_up, w_down, segment_ids, cotangent,
):
    rows, length = segment_ids.shape
    here = Place(rows)
    head_local = w_forget.shape[1]
    width = w_query.shape[1]
    hidden = w_gate.shape[1]
    model = inputs.shape[1]
    own_count = length // here.group
    slots = [(s, j) for s in range(here.group) for j in range(rows)]

    def own_row(array):
        return lax.dynamic_slice_in_dim(array, here.row * length, length, 0)

    def share(array, member):
        return lax.dynamic_slice_in_dim(array, member * own_count, own_count, 0)

    attn_own = jnp.concatenate([w_query, w_key, w_value, w_outgate, w_forget], axis=1)
    attn_piece = here.piece(attn_own)
    attn_w = [attn_own] + [here.gather(here.from_slot(attn_piece, 0, j), False) for j in range(1, rows)]
    bias = [forget_bias] + [here.from_slot(forget_bias, 0, j) for j in range(1, rows)]
    out_piece = here.piece(w_out)
    out_rest = here.gather(
        jnp.concatenate([here.from_slot(out_piece, s, j) for s, j in slots[1:]], axis=1), True
    )
    out_w = jnp.concatenate([w_out, out_rest], axis=1)
    gate_piece = here.piece(jnp.concatenate([w_gate, w_up], axis=1))
    down_piece = here.piece(w_down)
    gate_w, up_w, down_w = [w_gate], [w_up], [w_down]
    for j in range(1, rows):
        both = here.gather(here.from_slot(gate_piece, 0, j), False)
        gate_w.append(both[:, :hidden])
        up_w.append(both[:, hidden:])
        down_w.append(here.gather(here.from_slot(down_piece, 0, j), True))

    inputs_row = own_row(inputs).astype(jnp.float32)
    normed, inverse_attn = normalize(inputs_row, gain_attn)
    normed_low = low(normed)
    segment = lax.dynamic_index_in_dim(segment_ids, here.row, 0, keepdims=False)
    scol, srow = segment[:, None], segment[None, :]
    below = (
        lax.broadcasted_iota(jnp.int32, (length, length), 0)
        >= lax.broadcasted_iota(jnp.int32, (length, length), 1)
    ).astype(jnp.float32)
    kept = []
    gated = []
    for j in range(rows):
        mixed = mm(normed_low, attn_w[j])
        queries = low(mixed[:, :width] * (HEAD ** -0.5 * LOG2E))
        key_rows = low(mixed[:, width:2 * width])
        value_rows = low(mixed[:, 2 * width:3 * width])
        outgate = low(mixed[:, 3 * width:4 * width])
        forget = mixed[:, 4 * width:] + bias[j]
        running = jnp.dot(below, log_keep(forget) * LOG2E, precision=lax.Precision.HIGHEST)
        z, attended, log_total = attend_forward(
            queries, key_rows, value_rows, outgate, running.T, scol, srow
        )
        kept.append((queries, key_rows, value_rows, outgate, forget, running, attended, log_total))
        gated.append(z)
    gated_full = list(gated)
    for s in range(1, here.group):
        gated_full += [here.from_slot(z, s, 0) for z in gated]
    gated_full = jnp.concatenate(gated_full, axis=1)
    hidden_row = inputs_row + last(gated_full, out_w)

    mlp_normed, inverse_mlp = normalize(hidden_row, gain_mlp)
    mlp_low = low(mlp_normed)
    cotangent_row = own_row(cotangent)
    middle, grad_gate, grad_up = [], [], []
    for j in range(rows):
        gate_pre = mm(mlp_low, gate_w[j])
        up_pre = mm(mlp_low, up_w[j])
        grad_middle = mm(cotangent_row, down_w[j])
        sig = jax.nn.sigmoid(gate_pre)
        middle.append(low(gate_pre * sig * up_pre))
        grad_gate.append(low(grad_middle * up_pre * sig * (1.0 + gate_pre * (1.0 - sig))))
        grad_up.append(low(grad_middle * gate_pre * sig))

    def mlp_back(member):
        total = 0.0
        for j in range(rows):
            total = total + last(share(grad_gate[j], member), gate_w[j]) + last(share(grad_up[j], member), up_w[j])
        return total

    def mlp_out(member):
        return sum(last(share(middle[j], member), down_w[j]) for j in range(rows))

    hidden_own = share(hidden_row, here.member)
    inverse_own = share(inverse_mlp, here.member)
    mlp_grad = here.shares(mlp_back)
    dh_own = share(cotangent_row, here.member).astype(jnp.float32) + norm_back(
        hidden_own, inverse_own, gain_mlp, mlp_grad
    )
    gain_mlp_part = jnp.sum(mlp_grad * (hidden_own * inverse_own), axis=0)
    dh_low = low(dh_own)
    output = hidden_own + here.shares(mlp_out)

    def settle(parts, flip):
        total = 0.0
        for j, part in enumerate(parts):
            mine = here.scatter(low(part), flip)
            if j:
                mine = here.to_slot(mine, 0, j)
            total = total + mine.astype(jnp.float32)
        return total

    grad_down_w = settle([first(cotangent_row, m) for m in middle], True)
    grad_gate_w = settle([first(mlp_low, g) for g in grad_gate], False)
    grad_up_w = settle([first(mlp_low, g) for g in grad_up], True)

    block = rows * width
    dz_own = low(mm(dh_low, out_w))
    dz = jnp.zeros((length, block), jnp.bfloat16)
    dz = lax.dynamic_update_slice_in_dim(dz, dz_own[:, :block], here.member * own_count, 0)
    for s in range(1, here.group):
        back = here.group - s
        got = here.from_slot(dz_own[:, back * block:(back + 1) * block], s, 0)
        dz = lax.dynamic_update_slice_in_dim(dz, got, (here.member + s) % here.group * own_count, 0)
    out_part = here.scatter(low(first(dh_low, share(gated_full, here.member))), False)
    grad_out_w = 0.0
    for i, (s, j) in enumerate(slots):
        mine = out_part[:, i * width:(i + 1) * width]
        if i:
            mine = here.to_slot(mine, s, j)
        grad_out_w = grad_out_w + mine.astype(jnp.float32)

    mixed_back = [None] * rows
    attn_parts = [None] * rows
    bias_parts = [None] * rows
    for j in reversed(range(rows)):
        queries, key_rows, value_rows, outgate, forget, running, attended, log_total = kept[j]
        dq, dk, dv, dg, dc = attend_backward(
            queries, key_rows, value_rows, outgate, attended,
            dz[:, j * width:(j + 1) * width], log_total, running, scol, srow,
        )
        per_step = dc.shape[2] // HEAD
        columns = [dc[i, :, (HEAD if h == 0 else (h - 1) * HEAD)] for i in range(dc.shape[0]) for h in range(per_step)]
        rate_back = lax.dot_general(
            below, jnp.stack(columns, axis=1), (((0,), (0,)), ((), ())), precision=lax.Precision.HIGHEST
        )
        grad_forget = low(rate_back * jax.nn.sigmoid(-forget))
        bias_parts[j] = jnp.sum(grad_forget.astype(jnp.float32), axis=0)
        mixed_back[j] = jnp.concatenate([dq, dk, dv, dg, grad_forget], axis=1)
        attn_parts[j] = first(normed_low, mixed_back[j])

    def attn_back(member):
        return sum(last(share(mixed_back[j], member), attn_w[j]) for j in range(rows))

    attn_grad = here.shares(attn_back)
    inputs_own = share(inputs_row, here.member)
    inverse_own_attn = share(inverse_attn, here.member)
    grad_inputs = dh_own + norm_back(inputs_own, inverse_own_attn, gain_attn, attn_grad)
    gain_attn_part = jnp.sum(attn_grad * (inputs_own * inverse_own_attn), axis=0)
    grad_attn = settle(attn_parts, False)

    bias_full = jnp.zeros((here.tensor, head_local), jnp.float32)
    for j in range(rows):
        owner = here.slot_owner(here.at, 0, j)
        bias_full = lax.dynamic_update_slice(bias_full, bias_parts[j][None], (owner, 0))
    small = jnp.concatenate([gain_attn_part, gain_mlp_part, bias_full.reshape(-1)])[None]
    small = here.sum_all(small)[0]
    bias_own = lax.dynamic_slice_in_dim(small[2 * model:], here.at * head_local, head_local, 0)

    return (
        output,
        grad_inputs,
        small[:model],
        grad_attn[:, :width],
        grad_attn[:, width:2 * width],
        grad_attn[:, 2 * width:3 * width],
        grad_attn[:, 3 * width:4 * width],
        grad_attn[:, 4 * width:],
        bias_own,
        grad_out_w,
        small[model:2 * model],
        grad_gate_w,
        grad_up_w,
        grad_down_w,
    )


def solution(mesh):
    placed = (
        P("dp", None), P(), P(None, "tensor"), P(None, "tensor"), P(None, "tensor"),
        P(None, "tensor"), P(None, "tensor"), P("tensor"), P(None, "tensor"), P(),
        P(None, "tensor"), P(None, "tensor"), P(None, "tensor"), P("dp", None), P("dp", None),
    )
    weight = P("dp", "tensor")
    tokens = P(("dp", "tensor"), None)
    return jax.shard_map(
        on_device,
        mesh=mesh,
        in_specs=placed,
        out_specs=(
            tokens, tokens, P(), weight, weight, weight, weight, weight, P("tensor"),
            weight, P(), weight, weight, weight,
        ),
        check_vma=False,
    )
```

time: 1740 us -> 820 us (0.47)
  waiting for transfers between devices: 930 us -> 304 us
  matrix products: 418 us -> 190 us
  other arithmetic: 183 us -> 71.7 us
  starting transfers between devices: 1.43 us -> 65.4 us
  Pallas kernels: 0 us -> 58.2 us
  blocking collectives: 39.4 us -> 0 us
  local copies, waits for them, and re-layouts: 141 us -> 119 us
    psum x3 -> x0, waiting for transfers between devices: 836 us -> none  [the longest x1 428 us: on_device(): lax.psum(ffn_part.astype(jnp.bfloat16), 'tensor').astype(jnp.float32)]
    ppermute x0 -> x64, waiting for transfers between devices: none -> 304 us  [the longest x42 136 us: swap(): return lax.ppermute(value, 'dp', [(i, i ^ bit) for i in range(self.dp)])]
    dot_general x41 -> x39, matrix products: 418 us -> 190 us  [the longest x17 73.2 us: last(): lax.dot_general(a, b, (((1,), (1,)), ((), ())), preferred_element_type=jn...]
    reduce_scatter x7 -> x0, waiting for transfers between devices: 93.8 us -> none  [the longest x1 39.3 us: on_device(): lax.psum_scatter(grad_outgate_w.astype(jnp.bfloat16), 'dp', scatter_dimen...]
    reduce_sum x8 -> x1, other arithmetic: 87.8 us -> 0.15 us  [on_device(): bias_parts[j] = jnp.sum(grad_forget.astype(jnp.float32), axis=0)]
    ppermute x0 -> x64, starting transfers between devices: none -> 65.4 us  [the longest x42 34.6 us: swap(): return lax.ppermute(value, 'dp', [(i, i ^ bit) for i in range(self.dp)])]
    dynamic_update_slice x5 -> x3, local copies, waits for them, and re-layouts: 61.2 us -> 1 us  [the longest x2 0.94 us: on_device(): lax.dynamic_update_slice(bias_full, bias_parts[j][None], (owner, 0))]
    pallas_call x0 -> x4, Pallas kernels: none -> 58.2 us  [the longest x2 33.7 us: attend_backward(): pl.pallas_call(bwd_kernel, grid=(steps,), in_specs=[blk] * 6 + [pl.BlockS...]
  transfers between devices with their start and end apart: 12 -> 64, of which waited for: 6 -> 21; matrix products, arithmetic and copies ran while one was open for 24% -> 43% of each run, Pallas kernels for 0% -> 7%
where the time goes in v1:
time: 820 us; the launch traced here: 811 us
  waiting for transfers between devices  304 us (37%)
  matrix products  190 us (23%)
  local copies, waits for them, and re-layouts  119 us (15%)
  other arithmetic  71.7 us (9%)
  starting transfers between devices  65.4 us (8%)
  Pallas kernels  58.2 us (7%)
    ppermute x42, waiting for transfers between devices, swap(): return lax.ppermute(value, 'dp', [(i, i ^ bit) for i in range(self.dp)])  136 us
    dot_general x17, matrix products, last(): lax.dot_general(a, b, (((1,), (1,)), ((), ())), preferred_element_type=jn...  73.2 us
    ppermute x7, waiting for transfers between devices, to_slot(): return lax.ppermute(value, 'tensor', pairs)  63.9 us
    ppermute x10, waiting for transfers between devices, from_slot(): return lax.ppermute(value, 'tensor', pairs)  61 us
    dot_general x9, matrix products, mm(): return jnp.dot(a, b, preferred_element_type=jnp.float32)  54.7 us
    dot_general x9, matrix products, first(): lax.dot_general(a, b, (((0,), (0,)), ((), ())), preferred_element_type=jn...  51.7 us
    unnamed x285, local copies, waits for them, and re-layouts  47.4 us
    ppermute x3, waiting for transfers between devices, shares(): total = total + lax.ppermute(theirs, 'tensor', pairs).astype(jnp.float32)  38.8 us
  transfers between devices with their start and end apart: 64, of which 21 were waited for; matrix products, arithmetic and copies ran while one was open for 43% of the time, Pallas kernels for 7%

profile of v1, /device:TPU:0, one launch (start us, length us, event | category | flops | bytes accessed | tf_op | source)
XLA Modules:
  0.0 811.5 jit_solution(17524574122346794030)
XLA Ops:
  2.4 4.0 collective-permute-start.7
  20.7 10.5 %fusion.149 = (bf16[1024,1542]{1,0:T(8,128)(2,1)}, f32[1024,1542]{1,0:T(8,128)S(1)}) fusion(bf16[1536,1542]{1,0:T(8,128)(2,1)} %constant_dynamic-update-slice_fusion, f32[1536]{0:T(1024)S(1)} %copy-done.95, f32[1024]{0:T(1024)S(1)} %add_rsqrt_fusion.1, bf16[2048,1536]{1,0:T(8,128)(2,1)} %param.15, s32[]{:T(128)S(6)} %select_n.444), kind=kOutput, calls=%fused_computation.347 | convolution fusion | flops 4858583040 | bytes 17741828 | tf_op jit(solution)/shard_map/dot_general | solution.py:18
  45.5 12.3 %attend_forward.2 = (bf16[1024,384]{1,0:T(8,128)(2,1)}, bf16[1024,384]{1,0:T(8,128)(2,1)S(1)}, f32[3,2,1024]{2,1,0:T(2,128)S(1)}) custom-call(bf16[1024,384]{1,0:T(8,128)(2,1)S(1)} %copy-done.12, bf16[1024,384]{1,0:T(8,128)(2,1)S(1)} %copy-done.5, bf16[1024,384]{1,0:T(8,128)(2,1)S(1)} %copy-done.3, bf16[1024,384]{1,0:T(8,128)(2,1)S(1)} %copy-done.2, ...), custom_call_target="tpu_custom_call" | custom-call | flops 3221225472 | bytes 4718592 | tf_op jit(solution)/shard_map/attend_forward/pallas_call | solution.py:57
  77.8 5.5 dynamic-slice_convert_fusion
  83.3 47.0 %collective-permute-done.17 = bf16[192,1024]{1,0:T(8,128)(2,1)} collective-permute-done((bf16[192,1024]{1,0:T(8,128)(2,1)}, bf16[192,1024]{1,0:T(8,128)(2,1)}, u32[]{:S(2)}, u32[]{:S(2)}) %collective-permute-start.17) | collective-permute-done | bytes 393248 | tf_op jit(solution)/shard_map/ppermute | solution.py:191
  140.2 6.1 collective-permute-done.13
  151.9 23.0 %collective-permute-done.14 = bf16[192,2048]{1,0:T(8,128)(2,1)S(1)} collective-permute-done((bf16[192,2048]{1,0:T(8,128)(2,1)S(1)}, bf16[192,2048]{1,0:T(8,128)(2,1)S(1)}, u32[]{:S(2)}, u32[]{:S(2)}) %collective-permute-start.14) | collective-permute-done | bytes 786464 | tf_op jit(solution)/shard_map/ppermute | solution.py:198
  176.7 10.1 %collective-permute-done.19 = bf16[2,192,1024]{2,1,0:T(8,128)(2,1)S(1)} collective-permute-done((bf16[2,192,1024]{2,1,0:T(8,128)(2,1)S(1)}, bf16[2,192,1024]{2,1,0:T(8,128)(2,1)S(1)}, u32[]{:S(2)}, u32[]{:S(2)}) %collective-permute-start.19) | collective-permute-done | bytes 786464 | tf_op jit(solution)/shard_map/ppermute | solution.py:198
  190.7 22.9 %collective-permute-done.15 = bf16[2,192,2048]{2,1,0:T(8,128)(2,1)S(1)} collective-permute-done((bf16[2,192,2048]{2,1,0:T(8,128)(2,1)S(1)}, bf16[2,192,2048]{2,1,0:T(8,128)(2,1)S(1)}, u32[]{:S(2)}, u32[]{:S(2)}) %collective-permute-start.15) | collective-permute-done | bytes 1572896 | tf_op jit(solution)/shard_map/ppermute | solution.py:198
  224.6 7.7 fusion.150
  238.9 12.2 %attend_forward.3 = (bf16[1024,384]{1,0:T(8,128)(2,1)}, bf16[1024,384]{1,0:T(8,128)(2,1)S(1)}, f32[3,2,1024]{2,1,0:T(2,128)S(1)}) custom-call(bf16[1024,384]{1,0:T(8,128)(2,1)S(1)} %fusion.48.q_ref, bf16[1024,384]{1,0:T(8,128)(2,1)S(1)} %get-tuple-element.150.k_ref, bf16[1024,384]{1,0:T(8,128)(2,1)S(1)} %get-tuple-element.149.v_ref, ...), custom_call_target="tpu_custom_call" | custom-call | flops 3221225472 | bytes 4718592 | tf_op jit(solution)/shard_map/attend_forward/pallas_call | solution.py:57
  264.9 7.8 collective-permute-done.6
  274.9 8.1 multiply_reduce_fusion
  290.6 5.2 fusion.152
  296.4 8.2 %multiply_convert_fusion.4 = (bf16[1024,1024]{1,0:T(8,128)(2,1)}, bf16[1024,1024]{1,0:T(8,128)(2,1)}, bf16[1024,1024]{1,0:T(8,128)(2,1)S(1)}) fusion(f32[1024,1024]{1,0:T(8,128)S(1)} %fusion.151, f32[1024,1024]{1,0:T(8,128)} %fusion.152, bf16[1536,1024]{1,0:T(8,128)(2,1)S(1)} %copy-done, bf16[2048,1536]{1,0:T(8,128)(2,1)S(1)} %bitcast.337, s32[]{:T(128)S(6)} %select_n.444), kind=kOutput, calls=%fused_computation.21 | convolution fusion | flops 3238002688 | bytes 20971524 | tf_op jit(solution)/shard_map/dot_general | solution.py:18
  313.5 3.9 convolution_convert_fusion.8
  327.7 4.9 convolution_convert_fusion.4
  332.6 4.9 convolution_convert_fusion.6
  343.6 5.0 fusion.25
  348.7 8.5 %multiply_convert_fusion.2 = (bf16[1024,1024]{1,0:T(8,128)(2,1)}, bf16[1024,1024]{1,0:T(8,128)(2,1)}, bf16[1024,1024]{1,0:T(8,128)(2,1)S(1)}) fusion(f32[1024,1024]{1,0:T(8,128)S(1)} %fusion.31, f32[1024,1024]{1,0:T(8,128)} %fusion.25, bf16[1536,1024]{1,0:T(8,128)(2,1)S(1)} %bitcast.303, bf16[2048,1536]{1,0:T(8,128)(2,1)S(1)} %bitcast.339, s32[]{:T(128)S(6)} %select_n.444), kind=kOutput, calls=%fused_computation.19 | convolution fusion | flops 3238002688 | bytes 20971524 | tf_op jit(solution)/shard_map/dot_general | solution.py:18
  357.1 5.0 convolution_convert_fusion.3
  366.9 3.7 convolution_convert_fusion.7
  373.3 3.9 convolution_convert_fusion.5
  397.2 38.8 %collective-permute-done.22 = bf16[512,1536]{1,0:T(8,128)(2,1)} collective-permute-done((bf16[512,1536]{1,0:T(8,128)(2,1)}, bf16[512,1536]{1,0:T(8,128)(2,1)}, u32[]{:S(2)}, u32[]{:S(2)}) %collective-permute-start.22) | collective-permute-done | bytes 1572896 | tf_op jit(solution)/shard_map/ppermute | solution.py:250
  436.0 4.4 multiply_reduce_fusion.2
  463.0 4.5 convolution_convert_fusion.2
  467.9 6.8 add_add_fusion
  485.4 17.0 %attend_backward.2 = (bf16[1024,384]{1,0:T(8,128)(2,1)S(1)}, bf16[1024,384]{1,0:T(8,128)(2,1)S(1)}, bf16[1024,384]{1,0:T(8,128)(2,1)S(1)}, bf16[1024,384]{1,0:T(8,128)(2,1)S(1)}, f32[3,1024,128]{2,1,0:T(8,128)}) custom-call(bf16[1024,384]{1,0:T(8,128)(2,1)S(1)} %copy-done.13, bf16[1024,384]{1,0:T(8,128)(2,1)S(1)} %copy-done.6, ...), custom_call_target="tpu_custom_call" | custom-call | flops 8053063680 | bytes 9437184 | tf_op jit(solution)/shard_map/attend_backward/pallas_call | solution.py:135
  506.7 16.7 %attend_backward.3 = (bf16[1024,384]{1,0:T(8,128)(2,1)S(1)}, bf16[1024,384]{1,0:T(8,128)(2,1)S(1)}, bf16[1024,384]{1,0:T(8,128)(2,1)S(1)}, bf16[1024,384]{1,0:T(8,128)(2,1)S(1)}, f32[3,1024,128]{2,1,0:T(8,128)}) custom-call(bf16[1024,384]{1,0:T(8,128)(2,1)S(1)} %copy-done.15, bf16[1024,384]{1,0:T(8,128)(2,1)S(1)} %copy-done.11, ...), custom_call_target="tpu_custom_call" | custom-call | flops 8053063680 | bytes 9437184 | tf_op jit(solution)/shard_map/attend_backward/pallas_call | solution.py:135
  532.2 11.1 %convolution_convert_fusion = bf16[1536,1542]{0,1:T(8,128)(2,1)} fusion(bf16[1024,1542]{1,0:T(8,128)(2,1)S(1)} %constant_dynamic-update-slice_fusion.17, f32[1536]{0:T(1024)S(1)} %copy-done.96, f32[1024]{0:T(1024)S(1)} %copy-done.92, bf16[2048,1536]{1,0:T(8,128)(2,1)} %param.15, s32[]{:T(128)S(6)} %select_n.444), kind=kOutput, calls=%fused_computation | convolution fusion | flops 4859372544 | bytes 11051012 | tf_op jit(solution)/shard_map/dot_general | solution.py:16
  546.4 3.7 constant_dynamic-update-slice_fusion.12
  550.2 9.8 %convolution_convert_fusion.1 = bf16[1536,1542]{0,1:T(8,128)(2,1)} fusion(bf16[1024,1542]{1,0:T(8,128)(2,1)} %get-tuple-element.198, f32[1536]{0:T(1024)S(1)} %copy-done.96, f32[1024]{0:T(1024)S(1)} %copy-done.92, bf16[2048,1536]{1,0:T(8,128)(2,1)} %param.15, s32[]{:T(128)S(6)} %select_n.444), kind=kOutput, calls=%fused_computation.1 | convolution fusion | flops 4859372544 | bytes 11300868 | tf_op jit(solution)/shard_map/dot_general | solution.py:16
  560.0 7.4 copy.185
  567.4 7.4 copy.184
  574.8 5.7 fusion.41
  585.3 7.3 fusion.16
  604.7 4.8 fusion.46
  619.8 7.6 collective-permute-done.62
  629.0 7.4 collective-permute-done.49
  639.0 13.2 %collective-permute-done.56 = bf16[192,1024]{1,0:T(8,128)(2,1)S(1)} collective-permute-done((bf16[192,1024]{1,0:T(8,128)(2,1)S(1)}, bf16[192,1024]{1,0:T(8,128)(2,1)S(1)}, u32[]{:S(2)}, u32[]{:S(2)}) %collective-permute-start.56) | collective-permute-done | bytes 393248 | tf_op jit(solution)/shard_map/ppermute | solution.py:195
  656.3 8.8 %multiply_reduce_fusion.3 = (f32[1536]{0:T(1024)S(1)}, f32[512]{0:T(512)S(1)}, f32[512,1536]{1,0:T(8,128)S(1)}) fusion(f32[1024,1536]{1,0:T(8,128)} %dynamic-slice_convert_fusion, s32[]{:T(128)S(6)} %select_n.471, f32[512]{0:T(512)S(1)} %copy-done.97, f32[1536]{0:T(1024)S(1)} %copy-done.96, bf16[512,1536]{1,0:T(8,128)(2,1)} %collective-permute-done.24, ...), kind=kOutput, calls=%fused_computation.63 | convolution fusion | flops 2432432128 | bytes 17843200 | tf_op jit(solution)/shard_map/dot_general | solution.py:14
  665.2 9.8 %collective-permute-done.63 = bf16[192,1024]{1,0:T(8,128)(2,1)S(1)} collective-permute-done((bf16[192,1024]{1,0:T(8,128)(2,1)S(1)}, bf16[192,1024]{1,0:T(8,128)(2,1)S(1)}, u32[]{:S(2)}, u32[]{:S(2)}) %collective-permute-start.63) | collective-permute-done | bytes 393248 | tf_op jit(solution)/shard_map/ppermute | solution.py:195
  693.9 19.2 %collective-permute-done.38 = bf16[2,192,1536]{2,1,0:T(8,128)(2,1)} collective-permute-done((bf16[2,192,1536]{2,1,0:T(8,128)(2,1)S(1)}, bf16[2,192,1536]{2,1,0:T(8,128)(2,1)}, u32[]{:S(2)}, u32[]{:S(2)}) %collective-permute-start.38) | collective-permute-done | bytes 1179680 | tf_op jit(solution)/shard_map/ppermute | solution.py:198
  717.1 7.9 collective-permute-done.39
  725.2 15.1 %collective-permute-done.34 = bf16[2,192,1542]{2,1,0:T(8,128)(2,1)S(1)} collective-permute-done((bf16[2,192,1542]{2,1,0:T(8,128)(2,1)S(1)}, bf16[2,192,1542]{2,1,0:T(8,128)(2,1)S(1)}, u32[]{:S(2)}, u32[]{:S(2)}) %collective-permute-start.34) | collective-permute-done | bytes 1184288 | tf_op jit(solution)/shard_map/ppermute | solution.py:198
  741.9 23.3 %collective-permute-done.31 = bf16[2,192,1542]{2,1,0:T(8,128)(2,1)S(1)} collective-permute-done((bf16[2,192,1542]{2,1,0:T(8,128)(2,1)S(1)}, bf16[2,192,1542]{2,1,0:T(8,128)(2,1)S(1)}, u32[]{:S(2)}, u32[]{:S(2)}) %collective-permute-start.31) | collective-permute-done | bytes 1184288 | tf_op jit(solution)/shard_map/ppermute | solution.py:198
  774.9 14.3 %collective-permute-done.42 = bf16[192,384]{1,0:T(8,128)(2,1)S(1)} collective-permute-done((bf16[192,384]{1,0:T(8,128)(2,1)S(1)}, bf16[192,384]{1,0:T(8,128)(2,1)S(1)}, u32[]{:S(2)}, u32[]{:S(2)}) %collective-permute-start.42) | collective-permute-done | bytes 147488 | tf_op jit(solution)/shard_map/ppermute | solution.py:195
  789.1 19.1 %collective-permute-done.40 = bf16[192,384]{1,0:T(8,128)(2,1)S(1)} collective-permute-done((bf16[192,384]{1,0:T(8,128)(2,1)S(1)}, bf16[192,384]{1,0:T(8,128)(2,1)S(1)}, u32[]{:S(2)}, u32[]{:S(2)}) %collective-permute-start.40) | collective-permute-done | bytes 147488 | tf_op jit(solution)/shard_map/ppermute | solution.py:195
  (562 shorter events, 286.7 us)
Async XLA Ops:
  2.4 63.8 %collective-permute-start.7 = (bf16[192,384]{1,0:T(8,128)(2,1)}, bf16[192,384]{1,0:T(8,128)(2,1)}, u32[]{:S(2)}, u32[]{:S(2)}) collective-permute-start(bf16[192,384]{1,0:T(8,128)(2,1)} %constant_dynamic-slice_fusion.10), channel_id=1, source_target_pairs={{2,0},{3,1},{0,2},{1,3},{6,4},{7,5},{4,6},{5,7},{10,8},{11,9},{8,1... | collective-permute-start | bytes 442376 | tf_op jit(solution)/shard_map/ppermute | solution.py:191
  6.4 61.3 %collective-permute-start.8 = (bf16[192,384]{1,0:T(8,128)(2,1)}, bf16[192,384]{1,0:T(8,128)(2,1)}, u32[]{:S(2)}, u32[]{:S(2)}) collective-permute-start(bf16[192,384]{1,0:T(8,128)(2,1)} %constant_dynamic-slice_fusion.10), channel_id=1, source_target_pairs={{1,0},{0,1},{3,2},{2,3},{5,4},{4,5},{7,6},{6,7},{9,8},{8,9},{11,10... | collective-permute-start | bytes 442376 | tf_op jit(solution)/shard_map/ppermute | solution.py:191
  8.0 64.3 %collective-permute-start.9 = (bf16[192,384]{1,0:T(8,128)(2,1)}, bf16[192,384]{1,0:T(8,128)(2,1)}, u32[]{:S(2)}, u32[]{:S(2)}) collective-permute-start(bf16[192,384]{1,0:T(8,128)(2,1)} %constant_dynamic-slice_fusion.10), channel_id=1, source_target_pairs={{3,0},{2,1},{1,2},{0,3},{7,4},{6,5},{5,6},{4,7},{11,8},{10,9},{9,1... | collective-permute-start | bytes 442376 | tf_op jit(solution)/shard_map/ppermute | solution.py:191
  8.0 224.3 %collective-permute-start.4 = (f32[6]{0:T(128)}, f32[6]{0:T(128)S(1)}, u32[]{:S(2)}, u32[]{:S(2)}) collective-permute-start(f32[6]{0:T(128)} %param.22), channel_id=1, source_target_pairs={{2,0},{3,1},{0,2},{1,3},{6,4},{7,5},{4,6},{5,7},{10,8},{11,9},{8,1... | collective-permute-start | bytes 80 | tf_op jit(solution)/shard_map/ppermute | solution.py:191
  57.8 205.0 %collective-permute-start.5 = (bf16[1024,384]{1,0:T(8,128)(2,1)}, bf16[1024,384]{1,0:T(8,128)(2,1)}, u32[]{:S(2)}, u32[]{:S(2)}) collective-permute-start(bf16[1024,384]{1,0:T(8,128)(2,1)} %get-tuple-element.30), channel_id=1, source_target_pairs={{1,0},{0,1},{3,2},{2,3},{5,4},{4,5},{7,6},{6,7},{9,8},{8,9},{11,10... | collective-permute-start | bytes 2359304 | tf_op jit(solution)/shard_map/ppermute | solution.py:191
  66.2 65.9 %collective-permute-start = (bf16[192,1542]{1,0:T(8,128)(2,1)}, bf16[192,1542]{1,0:T(8,128)(2,1)}, u32[]{:S(2)}, u32[]{:S(2)}) collective-permute-start(bf16[192,1542]{1,0:T(8,128)(2,1)} %constant_dynamic-slice_fusion.11), channel_id=1, source_target_pairs={{2,0},{3,1},{0,2},{1,3},{6,4},{7,5},{4,6},{5,7},{10,8},{11,9},{8,1... | collective-permute-start | bytes 1776392 | tf_op jit(solution)/shard_map/ppermute | solution.py:191
  67.8 62.6 %collective-permute-start.17 = (bf16[192,1024]{1,0:T(8,128)(2,1)}, bf16[192,1024]{1,0:T(8,128)(2,1)}, u32[]{:S(2)}, u32[]{:S(2)}) collective-permute-start(bf16[192,1024]{1,0:T(8,128)(2,1)} %constant_dynamic-slice_fusion.9), channel_id=1, source_target_pairs={{2,0},{3,1},{0,2},{1,3},{6,4},{7,5},{4,6},{5,7},{10,8},{11,9},{8,1... | collective-permute-start | bytes 1179656 | tf_op jit(solution)/shard_map/ppermute | solution.py:191
  73.9 56.5 %collective-permute-start.10 = (bf16[192,1152]{1,0:T(8,128)(2,1)}, bf16[192,1152]{1,0:T(8,128)(2,1)}, u32[]{:S(2)}, u32[]{:S(2)}) collective-permute-start(bf16[192,1152]{1,0:T(8,128)(2,1)} %constant_dynamic-update-slice_fusion.9), channel_id=1, source_target_pairs={{0,8},{4,12},{8,0},{12,4},{16,24},{20,28},{24,16},{28,20},{1,9},{5... | collective-permute-start | bytes 1327112 | tf_op jit(solution)/shard_map/ppermute | solution.py:198
  138.4 49.9 %collective-permute-start.11 = (bf16[2,192,1152]{2,1,0:T(8,128)(2,1)S(1)}, bf16[2,192,1152]{2,1,0:T(8,128)(2,1)S(1)}, u32[]{:S(2)}, u32[]{:S(2)}) collective-permute-start(bf16[2,192,1152]{2,1,0:T(8,128)(2,1)S(1)} %pad_maximum_fusion.15), channel_id=1, source_target_pairs={{0,16},{4,20},{8,24},{12,28},{16,0},{20,4},{24,8},{28,12},{1,17},{... | collective-permute-start | bytes 2654216 | tf_op jit(solution)/shard_map/ppermute | solution.py:198
  146.3 28.5 %collective-permute-start.14 = (bf16[192,2048]{1,0:T(8,128)(2,1)S(1)}, bf16[192,2048]{1,0:T(8,128)(2,1)S(1)}, u32[]{:S(2)}, u32[]{:S(2)}) collective-permute-start(bf16[192,2048]{1,0:T(8,128)(2,1)S(1)} %collective-permute-done.13), channel_id=1, source_target_pairs={{0,16},{4,20},{8,24},{12,28},{16,0},{20,4},{24,8},{28,12},{1,17},{... | collective-permute-start | bytes 2359304 | tf_op jit(solution)/shard_map/ppermute | solution.py:198
  150.3 37.3 %collective-permute-start.2 = (bf16[2,192,1542]{2,1,0:T(8,128)(2,1)S(1)}, bf16[2,192,1542]{2,1,0:T(8,128)(2,1)S(1)}, u32[]{:S(2)}, u32[]{:S(2)}) collective-permute-start(bf16[2,192,1542]{2,1,0:T(8,128)(2,1)S(1)} %pad_maximum_fusion.14), channel_id=1, source_target_pairs={{0,8},{4,12},{8,0},{12,4},{16,24},{20,28},{24,16},{28,20},{1,9},{5... | collective-permute-start | bytes 3552776 | tf_op jit(solution)/shard_map/ppermute | solution.py:198
  186.8 26.8 %collective-permute-start.15 = (bf16[2,192,2048]{2,1,0:T(8,128)(2,1)S(1)}, bf16[2,192,2048]{2,1,0:T(8,128)(2,1)S(1)}, u32[]{:S(2)}, u32[]{:S(2)}) collective-permute-start(bf16[2,192,2048]{2,1,0:T(8,128)(2,1)S(1)} %pad_maximum_fusion.12), channel_id=1, source_target_pairs={{0,8},{4,12},{8,0},{12,4},{16,24},{20,28},{24,16},{28,20},{1,9},{5... | collective-permute-start | bytes 4718600 | tf_op jit(solution)/shard_map/ppermute | solution.py:198
  188.1 31.0 %collective-permute-start.3 = (bf16[2,2,192,1542]{3,2,0,1:T(8,128)(2,1)S(1)}, bf16[2,2,192,1542]{3,2,0,1:T(8,128)(2,1)S(1)}, u32[]{:S(2)}, u32[]{:S(2)}) collective-permute-start(bf16[2,2,192,1542]{3,2,0,1:T(8,128)(2,1)S(1)} %pad_maximum_fusion.10), channel_id=1, source_target_pairs={{0,4},{4,0},{8,12},{12,8},{16,20},{20,16},{24,28},{28,24},{1,5},{5... | collective-permute-start | bytes 7105544 | tf_op jit(solution)/shard_map/ppermute | solution.py:198
  188.3 28.1 %collective-permute-start.20 = (bf16[2,2,192,1024]{3,2,1,0:T(8,128)(2,1)S(1)}, bf16[2,2,192,1024]{3,2,1,0:T(8,128)(2,1)S(1)}, u32[]{:S(2)}, u32[]{:S(2)}) collective-permute-start(bf16[2,2,192,1024]{3,2,1,0:T(8,128)(2,1)S(1)} %pad_maximum_fusion.13), channel_id=1, source_target_pairs={{0,4},{4,0},{8,12},{12,8},{16,20},{20,16},{24,28},{28,24},{1,5},{5... | collective-permute-start | bytes 4718600 | tf_op jit(solution)/shard_map/ppermute | solution.py:198
  213.6 41.1 %collective-permute-start.12 = (bf16[2,2,192,1152]{3,2,1,0:T(8,128)(2,1)}, bf16[2,2,192,1152]{3,2,1,0:T(8,128)(2,1)}, u32[]{:S(2)}, u32[]{:S(2)}) collective-permute-start(bf16[2,2,192,1152]{3,2,1,0:T(8,128)(2,1)} %pad_maximum_fusion.11), channel_id=1, source_target_pairs={{0,4},{4,0},{8,12},{12,8},{16,20},{20,16},{24,28},{28,24},{1,5},{5... | collective-permute-start | bytes 5308424 | tf_op jit(solution)/shard_map/ppermute | solution.py:198
  216.4 121.0 %collective-permute-start.16 = (bf16[2,2,192,2048]{3,2,1,0:T(8,128)(2,1)}, bf16[2,2,192,2048]{3,2,1,0:T(8,128)(2,1)}, u32[]{:S(2)}, u32[]{:S(2)}) collective-permute-start(bf16[2,2,192,2048]{3,2,1,0:T(8,128)(2,1)} %pad_maximum_fusion.4), channel_id=1, source_target_pairs={{0,4},{4,0},{8,12},{12,8},{16,20},{20,16},{24,28},{28,24},{1,5},{5... | collective-permute-start | bytes 9437192 | tf_op jit(solution)/shard_map/ppermute | solution.py:198
  251.1 21.7 %collective-permute-start.6 = (bf16[1024,384]{1,0:T(8,128)(2,1)}, bf16[1024,384]{1,0:T(8,128)(2,1)}, u32[]{:S(2)}, u32[]{:S(2)}) collective-permute-start(bf16[1024,384]{1,0:T(8,128)(2,1)} %get-tuple-element.31), channel_id=1, source_target_pairs={{1,0},{0,1},{3,2},{2,3},{5,4},{4,5},{7,6},{6,7},{9,8},{8,9},{11,10... | collective-permute-start | bytes 2359304 | tf_op jit(solution)/shard_map/ppermute | solution.py:191
  318.9 75.0 %collective-permute-start.43 = (bf16[2,2,192,1024]{3,2,1,0:T(8,128)(2,1)}, bf16[2,2,192,1024]{3,2,1,0:T(8,128)(2,1)}, u32[]{:S(2)}, u32[]{:S(2)}) collective-permute-start(bf16[2,2,192,1024]{3,2,1,0:T(8,128)(2,1)} %dynamic-slice_bitcast_fusion.4), channel_id=1, source_target_pairs={{0,4},{4,0},{8,12},{12,8},{16,20},{20,16},{24,28},{28,24},{1,5},{5... | collective-permute-start | bytes 4718600 | tf_op jit(solution)/shard_map/ppermute | solution.py:198
  365.1 102.4 %collective-permute-start.21 = (bf16[512,1536]{1,0:T(8,128)(2,1)}, bf16[512,1536]{1,0:T(8,128)(2,1)}, u32[]{:S(2)}, u32[]{:S(2)}) collective-permute-start(bf16[512,1536]{1,0:T(8,128)(2,1)} %fusion.14), channel_id=1, source_target_pairs={{0,1},{1,0},{2,3},{3,2},{4,5},{5,4},{6,7},{7,6},{8,9},{9,8},{10,11... | collective-permute-start | bytes 4718600 | tf_op jit(solution)/shard_map/ppermute | solution.py:250
  380.3 55.6 %collective-permute-start.22 = (bf16[512,1536]{1,0:T(8,128)(2,1)}, bf16[512,1536]{1,0:T(8,128)(2,1)}, u32[]{:S(2)}, u32[]{:S(2)}) collective-permute-start(bf16[512,1536]{1,0:T(8,128)(2,1)} %fusion.15), channel_id=1, source_target_pairs={{0,1},{1,0},{2,3},{3,2},{4,5},{5,4},{6,7},{7,6},{8,9},{9,8},{10,11... | collective-permute-start | bytes 4718600 | tf_op jit(solution)/shard_map/ppermute | solution.py:250
  381.9 65.3 %collective-permute-start.46 = (bf16[2,2,192,1024]{3,2,1,0:T(8,128)(2,1)}, bf16[2,2,192,1024]{3,2,1,0:T(8,128)(2,1)S(1)}, u32[]{:S(2)}, u32[]{:S(2)}) collective-permute-start(bf16[2,2,192,1024]{3,2,1,0:T(8,128)(2,1)} %dynamic-slice_bitcast_fusion.3), channel_id=1, source_target_pairs={{0,4},{4,0},{8,12},{12,8},{16,20},{20,16},{24,28},{28,24},{1,5},{5... | collective-permute-start | bytes 4718600 | tf_op jit(solution)/shard_map/ppermute | solution.py:198
  384.8 64.5 %collective-permute-start.53 = (bf16[2,2,192,1024]{3,2,0,1:T(8,128)(2,1)}, bf16[2,2,192,1024]{3,2,0,1:T(8,128)(2,1)}, u32[]{:S(2)}, u32[]{:S(2)}) collective-permute-start(bf16[2,2,192,1024]{3,2,0,1:T(8,128)(2,1)} %bitcast.285), channel_id=1, source_target_pairs={{0,4},{4,0},{8,12},{12,8},{16,20},{20,16},{24,28},{28,24},{1,5},{5... | collective-permute-start | bytes 4718600 | tf_op jit(solution)/shard_map/ppermute | solution.py:198
  393.9 60.7 %collective-permute-start.50 = (bf16[2,2,192,1024]{3,2,0,1:T(8,128)(2,1)}, bf16[2,2,192,1024]{3,2,0,1:T(8,128)(2,1)}, u32[]{:S(2)}, u32[]{:S(2)}) collective-permute-start(bf16[2,2,192,1024]{3,2,0,1:T(8,128)(2,1)} %bitcast.286), channel_id=1, source_target_pairs={{0,4},{4,0},{8,12},{12,8},{16,20},{20,16},{24,28},{28,24},{1,5},{5... | collective-permute-start | bytes 4718600 | tf_op jit(solution)/shard_map/ppermute | solution.py:198
  436.0 22.4 %collective-permute-start.60 = (bf16[2,2,192,1024]{3,2,0,1:T(8,128)(2,1)}, bf16[2,2,192,1024]{3,2,0,1:T(8,128)(2,1)}, u32[]{:S(2)}, u32[]{:S(2)}) collective-permute-start(bf16[2,2,192,1024]{3,2,0,1:T(8,128)(2,1)} %bitcast.283), channel_id=1, source_target_pairs={{0,4},{4,0},{8,12},{12,8},{16,20},{20,16},{24,28},{28,24},{1,5},{5... | collective-permute-start | bytes 4718600 | tf_op jit(solution)/shard_map/ppermute | solution.py:198
  447.7 27.9 %collective-permute-start.57 = (bf16[2,2,192,1024]{3,2,0,1:T(8,128)(2,1)S(1)}, bf16[2,2,192,1024]{3,2,0,1:T(8,128)(2,1)}, u32[]{:S(2)}, u32[]{:S(2)}) collective-permute-start(bf16[2,2,192,1024]{3,2,0,1:T(8,128)(2,1)S(1)} %bitcast.333), channel_id=1, source_target_pairs={{0,4},{4,0},{8,12},{12,8},{16,20},{20,16},{24,28},{28,24},{1,5},{5... | collective-permute-start | bytes 4718600 | tf_op jit(solution)/shard_map/ppermute | solution.py:198
  449.4 31.4 %collective-permute-start.44 = (bf16[2,192,1024]{2,1,0:T(8,128)(2,1)}, bf16[2,192,1024]{2,1,0:T(8,128)(2,1)S(1)}, u32[]{:S(2)}, u32[]{:S(2)}) collective-permute-start(bf16[2,192,1024]{2,1,0:T(8,128)(2,1)} %dynamic-slice_bitcast_fusion.13), channel_id=1, source_target_pairs={{0,16},{4,20},{8,24},{12,28},{16,0},{20,4},{24,8},{28,12},{1,17},{... | collective-permute-start | bytes 2359304 | tf_op jit(solution)/shard_map/ppermute | solution.py:198
  454.5 29.0 %collective-permute-start.23 = (bf16[512,768]{1,0:T(8,128)(2,1)}, bf16[512,768]{1,0:T(8,128)(2,1)S(1)}, u32[]{:S(2)}, u32[]{:S(2)}) collective-permute-start(bf16[512,768]{1,0:T(8,128)(2,1)} %get-tuple-element.172), channel_id=1, source_target_pairs={{1,0},{0,1},{3,2},{2,3},{5,4},{4,5},{7,6},{6,7},{9,8},{8,9},{11,10... | collective-permute-start | bytes 2359304 | tf_op jit(solution)/shard_map/ppermute | solution.py:191
  458.4 122.1 %collective-permute-start.47 = (bf16[2,192,1024]{2,1,0:T(8,128)(2,1)}, bf16[2,192,1024]{2,1,0:T(8,128)(2,1)}, u32[]{:S(2)}, u32[]{:S(2)}) collective-permute-start(bf16[2,192,1024]{2,1,0:T(8,128)(2,1)} %dynamic-slice_bitcast_fusion.12), channel_id=1, source_target_pairs={{0,16},{4,20},{8,24},{12,28},{16,0},{20,4},{24,8},{28,12},{1,17},{... | collective-permute-start | bytes 2359304 | tf_op jit(solution)/shard_map/ppermute | solution.py:198
  467.5 127.0 %collective-permute-start.54 = (bf16[2,192,1024]{2,1,0:T(8,128)(2,1)}, bf16[2,192,1024]{2,1,0:T(8,128)(2,1)}, u32[]{:S(2)}, u32[]{:S(2)}) collective-permute-start(bf16[2,192,1024]{2,1,0:T(8,128)(2,1)} %dynamic-slice_bitcast_fusion.10), channel_id=1, source_target_pairs={{0,8},{4,12},{8,0},{12,4},{16,24},{20,28},{24,16},{28,20},{1,9},{5... | collective-permute-start | bytes 2359304 | tf_op jit(solution)/shard_map/ppermute | solution.py:198
  475.6 117.0 %collective-permute-start.51 = (bf16[2,192,1024]{2,1,0:T(8,128)(2,1)}, bf16[2,192,1024]{2,1,0:T(8,128)(2,1)}, u32[]{:S(2)}, u32[]{:S(2)}) collective-permute-start(bf16[2,192,1024]{2,1,0:T(8,128)(2,1)} %dynamic-slice_bitcast_fusion.11), channel_id=1, source_target_pairs={{0,8},{4,12},{8,0},{12,4},{16,24},{20,28},{24,16},{28,20},{1,9},{5... | collective-permute-start | bytes 2359304 | tf_op jit(solution)/shard_map/ppermute | solution.py:198
  480.8 120.0 %collective-permute-start.61 = (bf16[2,192,1024]{2,1,0:T(8,128)(2,1)}, bf16[2,192,1024]{2,1,0:T(8,128)(2,1)}, u32[]{:S(2)}, u32[]{:S(2)}) collective-permute-start(bf16[2,192,1024]{2,1,0:T(8,128)(2,1)} %dynamic-slice_bitcast_fusion.8), channel_id=1, source_target_pairs={{0,8},{4,12},{8,0},{12,4},{16,24},{20,28},{24,16},{28,20},{1,9},{5... | collective-permute-start | bytes 2359304 | tf_op jit(solution)/shard_map/ppermute | solution.py:198
  483.5 125.9 %collective-permute-start.58 = (bf16[2,192,1024]{2,1,0:T(8,128)(2,1)}, bf16[2,192,1024]{2,1,0:T(8,128)(2,1)}, u32[]{:S(2)}, u32[]{:S(2)}) collective-permute-start(bf16[2,192,1024]{2,1,0:T(8,128)(2,1)} %dynamic-slice_bitcast_fusion.9), channel_id=1, source_target_pairs={{0,8},{4,12},{8,0},{12,4},{16,24},{20,28},{24,16},{28,20},{1,9},{5... | collective-permute-start | bytes 2359304 | tf_op jit(solution)/shard_map/ppermute | solution.py:198
  580.5 48.4 %collective-permute-start.45 = (bf16[192,1024]{1,0:T(8,128)(2,1)S(1)}, bf16[192,1024]{1,0:T(8,128)(2,1)}, u32[]{:S(2)}, u32[]{:S(2)}) collective-permute-start(bf16[192,1024]{1,0:T(8,128)(2,1)S(1)} %copy-done.76), channel_id=1, source_target_pairs={{0,8},{4,12},{8,0},{12,4},{16,24},{20,28},{24,16},{28,20},{1,9},{5... | collective-permute-start | bytes 1179656 | tf_op jit(solution)/shard_map/ppermute | solution.py:198
  592.6 63.6 %collective-permute-start.24 = (bf16[512,1536]{1,0:T(8,128)(2,1)}, bf16[512,1536]{1,0:T(8,128)(2,1)}, u32[]{:S(2)}, u32[]{:S(2)}) collective-permute-start(bf16[512,1536]{1,0:T(8,128)(2,1)} %fusion.16), channel_id=1, source_target_pairs={{0,1},{1,0},{2,3},{3,2},{4,5},{5,4},{6,7},{7,6},{8,9},{9,8},{10,11... | collective-permute-start | bytes 4718600 | tf_op jit(solution)/shard_map/ppermute | solution.py:250
  609.5 29.0 %collective-permute-start.52 = (bf16[192,1024]{1,0:T(8,128)(2,1)}, bf16[192,1024]{1,0:T(8,128)(2,1)}, u32[]{:S(2)}, u32[]{:S(2)}) collective-permute-start(bf16[192,1024]{1,0:T(8,128)(2,1)} %dynamic-slice_bitcast_fusion.20), channel_id=1, source_target_pairs={{0,16},{4,20},{8,24},{12,28},{16,0},{20,4},{24,8},{28,12},{1,17},{... | collective-permute-start | bytes 1179656 | tf_op jit(solution)/shard_map/ppermute | solution.py:198
  616.7 19.7 %collective-permute-start.49 = (bf16[192,1024]{1,0:T(8,128)(2,1)S(1)}, bf16[192,1024]{1,0:T(8,128)(2,1)S(1)}, u32[]{:S(2)}, u32[]{:S(2)}) collective-permute-start(bf16[192,1024]{1,0:T(8,128)(2,1)S(1)} %fusion.89), channel_id=1, source_target_pairs={{0,2},{1,3},{2,0},{3,1},{4,6},{5,7},{6,4},{7,5},{8,10},{9,11},{10,... | collective-permute-start | bytes 1179656 | tf_op jit(solution)/shard_map/ppermute | solution.py:195
  627.4 24.9 %collective-permute-start.56 = (bf16[192,1024]{1,0:T(8,128)(2,1)S(1)}, bf16[192,1024]{1,0:T(8,128)(2,1)S(1)}, u32[]{:S(2)}, u32[]{:S(2)}) collective-permute-start(bf16[192,1024]{1,0:T(8,128)(2,1)S(1)} %fusion.87), channel_id=1, source_target_pairs={{0,2},{1,3},{2,0},{3,1},{4,6},{5,7},{6,4},{7,5},{8,10},{9,11},{10,... | collective-permute-start | bytes 1179656 | tf_op jit(solution)/shard_map/ppermute | solution.py:195
  628.9 48.0 %collective-permute-start.37 = (bf16[2,2,192,1536]{3,2,1,0:T(8,128)(2,1)}, bf16[2,2,192,1536]{3,2,1,0:T(8,128)(2,1)}, u32[]{:S(2)}, u32[]{:S(2)}) collective-permute-start(bf16[2,2,192,1536]{3,2,1,0:T(8,128)(2,1)} %dynamic-slice_bitcast_fusion.2), channel_id=1, source_target_pairs={{0,4},{4,0},{8,12},{12,8},{16,20},{20,16},{24,28},{28,24},{1,5},{5... | collective-permute-start | bytes 7077896 | tf_op jit(solution)/shard_map/ppermute | solution.py:198
  636.4 56.0 %collective-permute-start.33 = (bf16[2,2,192,1542]{3,2,1,0:T(8,128)(2,1)}, bf16[2,2,192,1542]{3,2,1,0:T(8,128)(2,1)S(1)}, u32[]{:S(2)}, u32[]{:S(2)}) collective-permute-start(bf16[2,2,192,1542]{3,2,1,0:T(8,128)(2,1)} %dynamic-slice_bitcast_fusion), channel_id=1, source_target_pairs={{0,4},{4,0},{8,12},{12,8},{16,20},{20,16},{24,28},{28,24},{1,5},{5... | collective-permute-start | bytes 7105544 | tf_op jit(solution)/shard_map/ppermute | solution.py:198
  638.5 77.3 %collective-permute-start.30 = (bf16[2,2,192,1542]{3,2,1,0:T(8,128)(2,1)S(1)}, bf16[2,2,192,1542]{3,2,1,0:T(8,128)(2,1)S(1)}, u32[]{:S(2)}, u32[]{:S(2)}) collective-permute-start(bf16[2,2,192,1542]{3,2,1,0:T(8,128)(2,1)S(1)} %copy-done.69), channel_id=1, source_target_pairs={{0,4},{4,0},{8,12},{12,8},{16,20},{20,16},{24,28},{28,24},{1,5},{5... | collective-permute-start | bytes 7105544 | tf_op jit(solution)/shard_map/ppermute | solution.py:198
  684.0 29.1 %collective-permute-start.38 = (bf16[2,192,1536]{2,1,0:T(8,128)(2,1)S(1)}, bf16[2,192,1536]{2,1,0:T(8,128)(2,1)}, u32[]{:S(2)}, u32[]{:S(2)}) collective-permute-start(bf16[2,192,1536]{2,1,0:T(8,128)(2,1)S(1)} %dynamic-slice_bitcast_fusion.7), channel_id=1, source_target_pairs={{0,16},{4,20},{8,24},{12,28},{16,0},{20,4},{24,8},{28,12},{1,17},{... | collective-permute-start | bytes 3538952 | tf_op jit(solution)/shard_map/ppermute | solution.py:198
  693.2 47.1 %collective-permute-start.34 = (bf16[2,192,1542]{2,1,0:T(8,128)(2,1)S(1)}, bf16[2,192,1542]{2,1,0:T(8,128)(2,1)S(1)}, u32[]{:S(2)}, u32[]{:S(2)}) collective-permute-start(bf16[2,192,1542]{2,1,0:T(8,128)(2,1)S(1)} %dynamic-slice_bitcast_fusion.5), channel_id=1, source_target_pairs={{0,16},{4,20},{8,24},{12,28},{16,0},{20,4},{24,8},{28,12},{1,17},{... | collective-permute-start | bytes 3552776 | tf_op jit(solution)/shard_map/ppermute | solution.py:198
  716.6 48.6 %collective-permute-start.31 = (bf16[2,192,1542]{2,1,0:T(8,128)(2,1)S(1)}, bf16[2,192,1542]{2,1,0:T(8,128)(2,1)S(1)}, u32[]{:S(2)}, u32[]{:S(2)}) collective-permute-start(bf16[2,192,1542]{2,1,0:T(8,128)(2,1)S(1)} %dynamic-slice_bitcast_fusion.6), channel_id=1, source_target_pairs={{0,16},{4,20},{8,24},{12,28},{16,0},{20,4},{24,8},{28,12},{1,17},{... | collective-permute-start | bytes 3552776 | tf_op jit(solution)/shard_map/ppermute | solution.py:198
  740.7 26.2 %collective-permute-start.35 = (bf16[192,1542]{1,0:T(8,128)(2,1)S(1)}, bf16[192,1542]{1,0:T(8,128)(2,1)S(1)}, u32[]{:S(2)}, u32[]{:S(2)}) collective-permute-start(bf16[192,1542]{1,0:T(8,128)(2,1)S(1)} %dynamic-slice_bitcast_fusion.14), channel_id=1, source_target_pairs={{0,8},{4,12},{8,0},{12,4},{16,24},{20,28},{24,16},{28,20},{1,9},{5... | collective-permute-start | bytes 1776392 | tf_op jit(solution)/shard_map/ppermute | solution.py:198
  765.6 43.5 %collective-permute-start.32 = (bf16[192,1542]{1,0:T(8,128)(2,1)S(1)}, bf16[192,1542]{1,0:T(8,128)(2,1)S(1)}, u32[]{:S(2)}, u32[]{:S(2)}) collective-permute-start(bf16[192,1542]{1,0:T(8,128)(2,1)S(1)} %dynamic-slice_bitcast_fusion.15), channel_id=1, source_target_pairs={{0,8},{4,12},{8,0},{12,4},{16,24},{20,28},{24,16},{28,20},{1,9},{5... | collective-permute-start | bytes 1776392 | tf_op jit(solution)/shard_map/ppermute | solution.py:198
  767.1 41.9 %collective-permute-start.36 = (bf16[192,1542]{1,0:T(8,128)(2,1)S(1)}, bf16[192,1542]{1,0:T(8,128)(2,1)S(1)}, u32[]{:S(2)}, u32[]{:S(2)}) collective-permute-start(bf16[192,1542]{1,0:T(8,128)(2,1)S(1)} %fusion.57), channel_id=1, source_target_pairs={{0,2},{1,3},{2,0},{3,1},{4,6},{5,7},{6,4},{7,5},{8,10},{9,11},{10,... | collective-permute-start | bytes 1776392 | tf_op jit(solution)/shard_map/ppermute | solution.py:195
  769.2 19.9 %collective-permute-start.42 = (bf16[192,384]{1,0:T(8,128)(2,1)S(1)}, bf16[192,384]{1,0:T(8,128)(2,1)S(1)}, u32[]{:S(2)}, u32[]{:S(2)}) collective-permute-start(bf16[192,384]{1,0:T(8,128)(2,1)S(1)} %get-tuple-element.189), channel_id=1, source_target_pairs={{0,3},{1,2},{2,1},{3,0},{4,7},{5,6},{6,5},{7,4},{8,11},{9,10},{10,... | collective-permute-start | bytes 442376 | tf_op jit(solution)/shard_map/ppermute | solution.py:195
  771.4 36.9 %collective-permute-start.40 = (bf16[192,384]{1,0:T(8,128)(2,1)S(1)}, bf16[192,384]{1,0:T(8,128)(2,1)S(1)}, u32[]{:S(2)}, u32[]{:S(2)}) collective-permute-start(bf16[192,384]{1,0:T(8,128)(2,1)S(1)} %get-tuple-element.188), channel_id=1, source_target_pairs={{0,2},{1,3},{2,0},{3,1},{4,6},{5,7},{6,4},{7,5},{8,10},{9,11},{10,... | collective-permute-start | bytes 442376 | tf_op jit(solution)/shard_map/ppermute | solution.py:195
  (150 other events, 1755.3 us)

commit v2 on v0

v2 whole, which is shorter than its diff:
```python
import jax
import jax.numpy as jnp
from jax import lax
from jax.sharding import PartitionSpec as P
from jax.experimental import pallas as pl
from jax.experimental.pallas import tpu as pltpu

LOG2E = 1.4426950408889634
LN2 = 0.6931471805599453
HEAD = 64
BLK = 256
EPS = 1e-06
ROW, MEMBER, CORE, CHIP, PIECE = 0, 1, 2, 3, 4
f32 = jnp.float32
bf16 = jnp.bfloat16


def last(a, b):
    return lax.dot_general(a, b, (((1,), (1,)), ((), ())), preferred_element_type=f32)


def first(a, b):
    return lax.dot_general(a, b, (((0,), (0,)), ((), ())), preferred_element_type=f32)


def mm(a, b):
    return jnp.dot(a, b, preferred_element_type=f32)


def low(values):
    return values.astype(bf16)


def shape(dims, dtype):
    return jax.ShapeDtypeStruct(dims, dtype)


def run(name, body, where, grid, ins, outs, scratch=(), after=(), flops=0, vmem=56):
    count, extra, made = len(ins), len(after), len(outs)

    def kernel(where_ref, *refs):
        body(where_ref, refs[:count], refs[count + extra:count + extra + made], refs[count + extra + made:])

    return pl.pallas_call(
        kernel,
        grid_spec=pltpu.PrefetchScalarGridSpec(
            num_scalar_prefetch=1,
            grid=grid,
            in_specs=[pl.BlockSpec(b, m) for _, b, m in ins]
            + [pl.BlockSpec(memory_space=pl.ANY)] * extra,
            out_specs=[pl.BlockSpec(b, m) for _, b, m in outs],
            scratch_shapes=list(scratch),
        ),
        out_shape=[s for s, _, _ in outs],
        compiler_params=pltpu.CompilerParams(vmem_limit_bytes=vmem << 20),
        cost_estimate=pl.CostEstimate(flops=int(flops) + 10 ** 9, bytes_accessed=1, transcendentals=0),
        name=name,
    )(where, *[a for a, _, _ in ins], *after)


def fixed(array):
    return (array, array.shape, lambda i, w: (0,) * array.ndim)


def fixed_out(dims, dtype):
    return (shape(dims, dtype), dims, lambda i, w: (0,) * len(dims))


def halves(values, pieces, core):
    count = values.shape[1] // pieces
    even = jnp.concatenate([values[:, p * count:(p + 1) * count] for p in range(0, pieces, 2)], axis=1)
    odd = jnp.concatenate([values[:, p * count:(p + 1) * count] for p in range(1, pieces, 2)], axis=1)
    return jnp.where(core == 0, odd, even), jnp.where(core == 0, even, odd)


def three(values):
    top = low(values)
    rest = values - top.astype(f32)
    middle = low(rest)
    return top, middle, low(rest - middle.astype(f32))


def log_keep(values):
    return jnp.minimum(values, 0.0) - jnp.log1p(jnp.exp(-jnp.abs(values)))


def lower(flip=False):
    r = lax.broadcasted_iota(jnp.int32, (BLK, BLK), 0)
    c = lax.broadcasted_iota(jnp.int32, (BLK, BLK), 1)
    return jnp.where(r <= c if flip else r >= c, 1.0, 0.0).astype(bf16)


TOK = 512


def project_tail(i, mixed, width, bias, outs, carry):
    q_ref, k_ref, v_ref, g_ref, f_ref, ccol_ref, crow_ref = outs
    q_ref[...] = low(mixed[:, :width] * (HEAD ** -0.5 * LOG2E))
    for p, ref in ((1, k_ref), (2, v_ref), (3, g_ref)):
        ref[...] = low(mixed[:, p * width:(p + 1) * width])
    heads = f_ref.shape[1]
    forget = mixed[:, 4 * width:4 * width + heads] + bias
    f_ref[...] = forget

    @pl.when(i == 0)
    def _():
        carry[...] = jnp.zeros_like(carry)

    mask = lower()
    hp = crow_ref.shape[1]
    tokens = forget.shape[0]
    for t in range(tokens // BLK):
        rows = slice(t * BLK, (t + 1) * BLK)
        wide = jnp.concatenate([log_keep(forget[rows]) * LOG2E, jnp.zeros((BLK, 128 - heads), f32)], axis=1)
        sums = sum(mm(mask, part) for part in three(wide)) + carry[0:1, :]
        carry[0:1, :] = sums[BLK - 1:BLK, :]
        ccol_ref[rows, :] = sums[:, :heads]
        flat = sums.T
        for s in range(crow_ref.shape[0]):
            crow_ref[s, :, rows] = flat[s * hp:(s + 1) * hp, :]


def together(heads):
    return 2 if heads % 2 == 0 else heads


def project_outs(length, width, heads):
    tokens = lambda i, w: (i, 0)
    return [(shape((length, width), bf16), (TOK, width), tokens) for _ in range(4)] + [
        (shape((length, heads), f32), (TOK, heads), tokens),
        (shape((length, heads), f32), (TOK, heads), tokens),
        (shape((heads // together(heads), together(heads), length), f32),
         (heads // together(heads), together(heads), TOK), lambda i, w: (0, 0, i)),
    ]


def project_own(where, length, pieces, inputs, gain, weights, bias, after=()):
    model = inputs.shape[1]
    width, heads = weights[0].shape[1], weights[4].shape[1]
    half = model // 2

    def body(w, ins, outs, scratch):
        x_ref, gain_ref, wq, wk, wv, wg, wf, b_ref = ins
        a_ref, send_ref, keep_ref, inv_ref = outs[:4]
        x = x_ref[...].astype(f32)
        inverse = lax.rsqrt(jnp.mean(x * x, axis=1, keepdims=True) + EPS)
        a = low(x * inverse * gain_ref[...])
        a_ref[...] = a
        inv_ref[...] = inverse
        send_ref[...], keep_ref[...] = halves(a, pieces, w[CORE])
        mixed = mm(a, jnp.concatenate([r[...] for r in (wq, wk, wv, wg, wf)], axis=1))
        project_tail(pl.program_id(0), mixed, width, b_ref[...], outs[4:], scratch[0])

    blocks = length // TOK
    tokens = lambda i, w: (i, 0)
    return run(
        "project_own", body, where, (blocks,),
        [(inputs, (TOK, model), lambda i, w: (w[ROW] * blocks + i, 0)), fixed(gain)]
        + [fixed(a) for a in weights] + [fixed(bias)],
        [(shape((length, model), bf16), (TOK, model), tokens),
         (shape((length, half), bf16), (TOK, half), tokens), (shape((length, half), bf16), (TOK, half), tokens),
         (shape((length, 1), f32), (TOK, 1), tokens)]
        + project_outs(length, width, heads),
        [pltpu.VMEM((8, 128), f32)], after, 2 * length * model * (4 * width + heads),
    )


def core_halves(ref, w, half):
    return (ref[:, pl.ds(pl.multiple_of(w[CORE] * half, 128), half)],
            ref[:, pl.ds(pl.multiple_of((1 - w[CORE]) * half, 128), half)])


def project_other(where, normed, mine, theirs, width, heads, bias, after=()):
    length, model = normed.shape
    half = model // 2

    def body(w, ins, outs, scratch):
        a_ref, m_ref, t_ref, b_ref = ins
        am, at = core_halves(a_ref, w, half)
        mixed = mm(am, m_ref[...]) + mm(at, t_ref[...])
        project_tail(pl.program_id(0), mixed, width, b_ref[...], outs, scratch[0])

    return run(
        "project_other", body, where, (length // TOK,),
        [(normed, (TOK, model), lambda i, w: (i, 0)), fixed(mine), fixed(theirs), fixed(bias)],
        project_outs(length, width, heads),
        [pltpu.VMEM((8, 128), f32)], after, 2 * length * model * (4 * width + heads),
    )


def attend_forward(where, q, k, v, g, crow, scol, srow, after=()):
    length, n = q.shape
    heads = n // HEAD
    hp = together(heads)
    width = hp * HEAD

    def body(w, ins, outs, scratch):
        q_ref, k_ref, v_ref, g_ref, crow_ref, scol_ref, srow_ref = ins
        z_ref, lse_ref = outs
        lane = lax.broadcasted_iota(jnp.int32, (1, width), 1) // HEAD
        lane1 = lax.broadcasted_iota(jnp.int32, (BLK, 128), 1)
        tri = lax.broadcasted_iota(jnp.int32, (BLK, BLK), 0) >= lax.broadcasted_iota(jnp.int32, (BLK, BLK), 1)
        crows = crow_ref[0]
        for i in range(length // BLK):
            rows = pl.ds(i * BLK, BLK)
            reach = (i + 1) * BLK
            q = q_ref[rows, :]
            same = scol_ref[rows, :] == srow_ref[:, :reach]
            if i:
                allowed = jnp.concatenate([same[:, :reach - BLK], same[:, reach - BLK:] & tri], axis=1)
            else:
                allowed = same & tri
            out = jnp.zeros((BLK, width), f32)
            stats = jnp.zeros((BLK, 128), f32)
            for h in range(hp):
                s = last(jnp.where(lane == h, q, 0), k_ref[:reach, :])
                s = jnp.where(allowed, s - crows[h:h + 1, :reach], -1e30)
                top = jnp.max(s, axis=1, keepdims=True)
                e = jnp.exp2(s - top)
                total = jnp.sum(e, axis=1, keepdims=True)
                part = mm(low(e), v_ref[:reach, :])
                out = jnp.where(lane == h, part * (1.0 / total), out)
                stats = jnp.where(lane1 == h, top + jnp.log2(total), stats)
            z_ref[rows, :] = low(out * jax.nn.sigmoid(g_ref[rows, :].astype(f32)))
            lse_ref[0, :, i * BLK:(i + 1) * BLK] = stats.T[:hp, :]

    tokens = lambda i, w: (0, i)
    return run(
        "attend_forward", body, where, (heads // hp,),
        [(a, (length, width), tokens) for a in (q, k, v, g)]
        + [(crow, (1, hp, length), lambda i, w: (i, 0, 0)), fixed(scol), fixed(srow)],
        [(shape((length, n), bf16), (length, width), tokens),
         (shape((heads // hp, hp, length), f32), (1, hp, length), lambda i, w: (i, 0, 0))],
        (), after, heads * length * length * 1100,
    )


def attend_backward(where, q, k, v, g, z, dz_parts, lse, ccol, forget, scol, srow, after=()):
    length, n = q.shape
    heads = n // HEAD
    hp = together(heads)
    width = hp * HEAD
    steps = heads // hp
    group = len(dz_parts)
    share = length // group

    def body(w, ins, outs, scratch):
        q_ref, k_ref, v_ref, g_ref, z_ref = ins[:5]
        dz_refs = ins[5:5 + group]
        lse_ref, ccol_ref, f_ref, scol_ref, srow_ref = ins[5 + group:]
        dq_ref, dk_ref, dv_ref, dg_ref, df_ref, db_ref = outs
        dqacc, dkacc, rates, dzfull = scratch
        step = pl.program_id(0)
        lane = lax.broadcasted_iota(jnp.int32, (1, width), 1) // HEAD
        lane1 = lax.broadcasted_iota(jnp.int32, (1, 128), 1)
        tri = lax.broadcasted_iota(jnp.int32, (BLK, BLK), 1) >= lax.broadcasted_iota(jnp.int32, (BLK, BLK), 0)
        blocks = length // BLK

        @pl.when(step == 0)
        def _():
            rates[...] = jnp.zeros_like(rates)

        for s in range(group):
            at = lax.rem(w[MEMBER] + s, group) * share
            dzfull[pl.ds(pl.multiple_of(at, share), share), :] = dz_refs[s][...]
        sig = jax.nn.sigmoid(g_ref[...].astype(f32))
        dz = dzfull[...].astype(f32)
        prod = dz * z_ref[...].astype(f32)
        dout = low(dz * sig)
        dg_ref[...] = low(prod * (1.0 - sig))
        prod_hi = low(prod)
        prod_lo = low(prod - prod_hi.astype(f32))
        lses = lse_ref[0]
        for h in range(hp):
            head = lane == h
            index = step * hp + h
            decay = jnp.sum(jnp.where(lane1[:, :heads] == index, ccol_ref[...], 0.0), axis=1, keepdims=True)
            ones = jnp.broadcast_to(jnp.where(head, 1.0, 0.0).astype(bf16), (8, width))
            centre = (last(ones, prod_hi) + last(ones, prod_lo))[0:1, :]
            q_one = jnp.where(head, q_ref[...], 1.0)
            q_zero = jnp.where(head, q_ref[...], 0.0)
            k_one = jnp.where(head, k_ref[...], 1.0)
            d_zero = jnp.where(head, dout, 0.0)
            dqacc[...] = jnp.zeros_like(dqacc)
            for j in range(blocks):
                keys = pl.ds(j * BLK, BLK)
                lo = j * BLK
                s = last(k_ref[keys, :], q_zero[lo:, :])
                s = s - decay[lo:lo + BLK, :] - lses[h:h + 1, lo:]
                same = scol_ref[keys, :] == srow_ref[:, lo:]
                if j < blocks - 1:
                    allowed = jnp.concatenate([same[:, :BLK] & tri, same[:, BLK:]], axis=1)
                else:
                    allowed = same & tri
                p = jnp.exp2(jnp.where(allowed, s, -1e30))
                dp = last(v_ref[keys, :], d_zero[lo:, :])
                ds = low(p * (dp - centre[:, lo:]))
                dv = mm(low(p), dout[lo:, :])
                dk = mm(ds, q_one[lo:, :])
                dqacc[lo:, :] += first(ds, k_one[lo:lo + BLK, :])
                dkacc[keys, :] = dk
                if h == 0:
                    dk_ref[keys, :] = low(dk * LN2)
                    dv_ref[keys, :] = low(dv)
                else:
                    dk_ref[keys, :] = jnp.where(head, low(dk * LN2), dk_ref[keys, :])
                    dv_ref[keys, :] = jnp.where(head, low(dv), dv_ref[keys, :])
            dq = dqacc[...]
            if h == 0:
                dq_ref[...] = low(dq * HEAD ** -0.5)
            else:
                dq_ref[...] = jnp.where(head, low(dq * HEAD ** -0.5), dq_ref[...])
            spare = HEAD if h == 0 else 0
            rate = (dq - dkacc[...])[:, spare:spare + 1]
            rates[...] = jnp.where(lane1 == index, rate, rates[...])

        @pl.when(step == steps - 1)
        def _():
            mask = lower(True)
            carry = jnp.zeros((1, 128), f32)
            bias = jnp.zeros((1, heads), f32)
            for b in reversed(range(blocks)):
                rows = pl.ds(b * BLK, BLK)
                sums = sum(mm(mask, part) for part in three(rates[rows, :])) + carry
                carry = sums[0:1, :]
                df = low(sums[:, :heads] * jax.nn.sigmoid(-f_ref[rows, :]))
                df_ref[rows, :] = df
                bias = bias + jnp.sum(df.astype(f32), axis=0, keepdims=True)
            db_ref[...] = bias

    tokens = lambda i, w: (0, i)
    wide = (shape((length, n), bf16), (length, width), tokens)
    return run(
        "attend_backward", body, where, (steps,),
        [(a, (length, width), tokens) for a in (q, k, v, g, z)]
        + [(a, (share, width), lambda i, w, off=off: (0, off + i)) for a, off in dz_parts]
        + [(lse, (1, hp, length), lambda i, w: (i, 0, 0))] + [fixed(a) for a in (ccol, forget, scol, srow)],
        [wide] * 4 + [fixed_out((length, heads), bf16), fixed_out((1, heads), f32)],
        [pltpu.VMEM((length, width), f32), pltpu.VMEM((length, width), f32), pltpu.VMEM((length, 128), f32),
         pltpu.VMEM((length, width), bf16)],
        after, heads * length * length * 1500,
    )


def close_attention(where, length, pieces, inputs, gated, out_own, out_mine, out_theirs, gain, after=()):
    model = inputs.shape[1]
    half = model // 2
    width = out_own.shape[1]

    def body(w, ins, outs, scratch):
        x_ref, own_ref, m_ref, t_ref, gain_ref = ins[:5]
        z = jnp.concatenate([r[...] for r in ins[5:]], axis=1)
        h_ref, a_ref, send_ref, keep_ref, inv_ref = outs
        for ref, core in ((m_ref, w[CORE]), (t_ref, 1 - w[CORE])):
            at = pl.ds(pl.multiple_of(core * half, 128), half)
            own = own_ref[pl.ds(pl.multiple_of(core * half, 128), half), :]
            rest = ref[:, :(len(gated) - 1) * width]
            h_ref[:, at] = x_ref[:, at].astype(f32) + last(z, jnp.concatenate([own, rest], axis=1))
        h = h_ref[...]
        inverse = lax.rsqrt(jnp.mean(h * h, axis=1, keepdims=True) + EPS)
        a = low(h * inverse * gain_ref[...])
        a_ref[...] = a
        inv_ref[...] = inverse
        send_ref[...], keep_ref[...] = halves(a, pieces, w[CORE])

    blocks = length // TOK
    tokens = lambda i, w: (i, 0)
    side = (shape((length, half), bf16), (TOK, half), tokens)
    return run(
        "close_attention", body, where, (blocks,),
        [(inputs, (TOK, model), lambda i, w: (w[ROW] * blocks + i, 0))]
        + [fixed(a) for a in (out_own, out_mine, out_theirs, gain)]
        + [(z, (TOK, width), tokens) for z in gated],
        [(shape((length, model), f32), (TOK, model), tokens), (shape((length, model), bf16), (TOK, model), tokens),
         side, side, (shape((length, 1), f32), (TOK, 1), tokens)],
        (), after, 2 * length * model * width * len(gated),
    )


def split_rows(where, length, pieces, array, after=()):
    model = array.shape[1]
    half = model // 2
    blocks = length // BLK

    def body(w, ins, outs, scratch):
        outs[0][...], outs[1][...] = halves(ins[0][...], pieces, w[CORE])

    side = (shape((length, half), bf16), (BLK, half), lambda i, w: (i, 0))
    return run(
        "split_rows", body, where, (blocks,),
        [(array, (BLK, model), lambda i, w: (w[ROW] * blocks + i, 0))], [side, side], (), after,
    )


def feed_forward(where, normed, cotangent, weights, hidden, after=()):
    length, model = normed.shape
    half = model // 2
    wide = BLK if hidden % BLK == 0 else hidden
    steps = hidden // wide
    own = len(weights) == 3

    def body(w, ins, outs, scratch):
        a_ref, e_ref = ins[:2]
        m_ref, du_ref, dw_ref = outs
        if not own:
            core = pl.ds(pl.multiple_of(w[CORE] * half, 128), half)
            other = pl.ds(pl.multiple_of((1 - w[CORE]) * half, 128), half)
        for t in range(length // TOK):
            rows = pl.ds(t * TOK, TOK)
            if own:
                gate, up = mm(a_ref[rows, :], ins[2][...]), mm(a_ref[rows, :], ins[3][...])
                dm = mm(e_ref[rows, :], ins[4][...])
            else:
                both = lambda ref, p: mm(ref[rows, core], ins[2 + p][...]) + mm(ref[rows, other], ins[5 + p][...])
                gate, up, dm = both(a_ref, 0), both(a_ref, 1), both(e_ref, 2)
            sig = jax.nn.sigmoid(gate)
            act = gate * sig
            m_ref[rows, :] = low(act * up)
            dw_ref[rows, :] = low(dm * act)
            du_ref[rows, :] = low(dm * up * (sig * (1.0 + gate * (1.0 - sig))))

    if own:
        parts = [(a, (model, wide), lambda i, w: (0, i)) for a in weights]
    else:
        gm, gt, dm, dt = weights
        parts = [
            (a, (half, wide), lambda i, w, p=p: (0, p * steps + i))
            for a, p in ((gm, 0), (gm, 1), (dm, 0), (gt, 0), (gt, 1), (dt, 0))
        ]
    result = (shape((length, hidden), bf16), (length, wide), lambda i, w: (0, i))
    return run(
        "feed_forward", body, where, (steps,),
        [fixed(normed), (cotangent, (length, model), lambda i, w: (w[ROW], 0))] + parts,
        [result] * 3, (), after, 6 * length * model * hidden,
    )


def weight_grads(name, where, sides, groups, rows_of=False, after=()):
    length, half = sides[0][0].shape
    widths = [sum(r.shape[1] for r in rights) for _, rights in groups]
    padded = [-(-n // 256) * 256 for n in widths]
    several = len(groups) > 1
    tall = half if several else half // 2
    count = 2 * len(sides)

    def body(w, ins, outs, scratch):
        at = count
        for k, (s, rights) in enumerate(groups):
            for which in (0, 1):
                @pl.when((pl.program_id(0) == (k if several else which)) & (pl.program_id(1) == which)
                         if several else pl.program_id(0) == which)
                def _(k=k, s=s, at=at, n=len(rights), which=which):
                    right = [ins[at + c][...] for c in range(n)]
                    value = first(ins[2 * s + which][...], right[0] if n == 1 else jnp.concatenate(right, axis=1))
                    outs[which][:, :widths[k]] = low(value)
                    if widths[k] < padded[k]:
                        outs[which][:, widths[k]:] = jnp.zeros((tall, padded[k] - widths[k]), bf16)
            at += len(rights)

    pick = (lambda i, c, w: (w[MEMBER], 0)) if rows_of else (lambda i, c, w: (0, 0))
    if several:
        grid = (len(groups), 2)
        left_at = [lambda i, c, w: (0, 0)] * 2
        out_at = [lambda i, c, w: (0, i)] * 2
    else:
        grid = (2, 2)
        left_at = [lambda i, c, w: (0, jnp.where(i == 0, c, 1)), lambda i, c, w: (0, jnp.where(i == 0, 0, c))]
        out_at = [lambda i, c, w: (jnp.where(i == 0, c, 1), 0), lambda i, c, w: (jnp.where(i == 0, 0, c), 0)]
    return run(
        name, body, where, grid,
        [(a, (length, tall), left_at[which]) for pair in sides for which, a in enumerate(pair)]
        + [(r, (length, r.shape[1]), pick) for _, rights in groups for r in rights],
        [(shape((half, sum(padded)), bf16), (tall, padded[0]), out_at[which]) for which in (0, 1)],
        (), after, 4 * half * length * sum(padded),
    )


def fold(where, entries, after=()):
    keep, _, bits, _, _, width = entries[0]
    rows = keep.shape[0]
    count = len(bits)
    pieces = 1 << count
    piece = rows // pieces
    wide = next(n for n in (768, 512, 384, width) if width % n == 0)
    across = width // wide
    block = (piece, wide)
    ins, outs = [], []
    for keep, got, bits, bit_at, col, _ in entries:
        place = count - 1 - bits.index(bit_at)

        def index(mine, place=place, bit_at=bit_at, col=col):
            def at(i, c, w):
                own = lax.rem(w[CHIP] // (bit_at >> 1), 2)
                bit = own if mine else 1 - own
                low_part = lax.rem(i, 1 << place)
                high = i // (1 << place)
                return ((high * 2 + bit) * (1 << place) + low_part, col * across + c)
            return at

        for mine in (False, True):
            ins += [(keep, block, index(mine)), (got, block, index(mine))]
            outs.append((shape((rows // 2, width), bf16), block, lambda i, c, w: (i, c)))

    def body(w, ins_, outs_, scratch):
        for k, out in enumerate(outs_):
            out[...] = low(ins_[2 * k][...].astype(f32) + ins_[2 * k + 1][...].astype(f32))

    return run("fold", body, where, (pieces // 2, across), ins, outs, (), after, 10 ** 9)


def assemble(where, pieces, masks, after=()):
    count, extra = len(pieces), len(after)
    rows, width = pieces[0].shape

    def kernel(w, *refs):
        out, sems = refs[count + extra], refs[count + extra + 1]
        copies = []
        for k in range(count):
            at = pl.multiple_of(jnp.bitwise_xor(w[CHIP], masks[k]) * rows, rows)
            copies.append(pltpu.make_async_copy(refs[k], out.at[pl.ds(at, rows), :], sems.at[k]))
        for c in copies:
            c.start()
        for c in copies:
            c.wait()

    return pl.pallas_call(
        kernel,
        grid_spec=pltpu.PrefetchScalarGridSpec(
            num_scalar_prefetch=1, grid=(),
            in_specs=[pl.BlockSpec(memory_space=pl.ANY)] * (count + extra),
            out_specs=pl.BlockSpec(memory_space=pl.ANY),
            scratch_shapes=[pltpu.SemaphoreType.DMA((count,))],
        ),
        out_shape=shape((count * rows, width), bf16),
        compiler_params=pltpu.CompilerParams(vmem_limit_bytes=4 << 20),
        cost_estimate=pl.CostEstimate(flops=10 ** 9, bytes_accessed=1, transcendentals=0),
        name="assemble",
    )(where, *pieces, *after)


def back_rows(name, where, steps, group, share, own_terms, pair_terms, model, dtypes, adds=(), unit=None, after=()):
    half = model // 2
    count = len(steps)
    turn = lambda m: sum(jnp.where(m == k, s, 0) for k, s in enumerate(steps))
    member = lambda m, w: lax.rem(w[MEMBER] + turn(m), group)
    side = lambda i, w: lax.rem(w[CORE] + i, 2)
    ins = []

    def put(array, block, at):
        ins.append((array, block, at))
        return len(ins) - 1

    rows_at = lambda i, m, w: (member(m, w), 0)
    own_plan = [
        ([put(x, (share, x.shape[1]), rows_at) for x in xs],
         [put(a, (half, a.shape[1]), lambda i, m, w: (side(i, w), 0)) for a in weights])
        for xs, weights in own_terms
    ]
    known = {}
    pair_plan = []
    for xs, mine, theirs, lo in pair_terms:
        for a in (mine, theirs):
            if id(a) not in known:
                known[id(a)] = put(a, a.shape, lambda i, m, w: (0, 0))
        pair_plan.append(([put(x, (share, x.shape[1]), rows_at) for x in xs],
                          known[id(mine)], known[id(theirs)], lo, sum(x.shape[1] for x in xs)))
    first_add = len(ins)
    for a, kind in adds:
        ins.append((a, (share, half), (lambda i, m, w: (w[MEMBER], side(i, w))) if kind == "row"
                    else (lambda i, m, w: (0, side(i, w)))))
    if unit is not None:
        values, base, inverse = unit
        ins.append((values, (share, half), lambda i, m, w: (w[ROW] * base + member(m, w), side(i, w))))
        ins.append((inverse, (share, 1), rows_at))

    def body(w, ins_, outs, scratch):
        wide = lambda refs: ins_[refs[0]][...] if len(refs) == 1 else jnp.concatenate([ins_[r][...] for r in refs], axis=1)
        at = pl.program_id(1)
        total = 0.0
        for xs, weights in own_plan:
            total = total + last(wide(xs), wide(weights))
        scratch[0][...] = total
        for which in (0, 1):
            @pl.when(pl.program_id(0) == which)
            def _():
                part = 0.0
                for xs, mine, theirs, lo, n in pair_plan:
                    part = part + last(wide(xs), ins_[(mine, theirs)[which]][:, lo:lo + n])
                scratch[0][...] += part
        if unit is not None:
            u = ins_[-2][...].astype(f32) * ins_[-1][...]
            gained = jnp.sum(scratch[0][...] * u, axis=0, keepdims=True)
            outs[count][...] = jnp.where(at == 0, 0.0, outs[count][...]) + gained
        for k in range(count):
            @pl.when(at == k)
            def _():
                total = scratch[0][...]
                if k == count - 1:
                    for a in range(len(adds)):
                        total = total + ins_[first_add + a][...].astype(f32)
                outs[k][...] = total.astype(dtypes[k])

    outs = [(shape((share, model), d), (share, half), lambda i, m, w: (0, side(i, w))) for d in dtypes]
    if unit is not None:
        outs.append((shape((1, model), f32), (1, half), lambda i, m, w: (0, side(i, w))))
    flops = 2 * share * model * count * sum(x.shape[1] for t in tuple(own_terms) + tuple(pair_terms) for x in t[0])
    return run(name, body, where, (2, count), ins, outs, [pltpu.VMEM((share, half), f32)], after, flops)


def close_feed_forward(where, share, group, pieces, part, got, hidden_row, inverse, gain, cotangent,
                       out_own, out_mine, out_theirs, after=()):
    model = part.shape[1]
    half = model // 2
    width = out_own.shape[1]
    filled = width + out_mine.shape[1]
    own_slots = filled // group

    def body(w, ins, outs, scratch):
        p_ref, h_ref, i_ref, gain_ref, e_ref, own_ref, m_ref, t_ref = ins[:8]
        dh_ref, send_ref, keep_ref, mine_out, peer_out = outs
        total = p_ref[...]
        for r in ins[8:]:
            total = total + r[...].astype(f32)
        unit = h_ref[...] * i_ref[...]
        scaled = total * gain_ref[...]
        dh = e_ref[...].astype(f32) + i_ref[...] * (scaled - unit * jnp.mean(scaled * unit, axis=1, keepdims=True))
        dh_ref[...] = dh
        d = low(dh)
        send_ref[...], keep_ref[...] = halves(d, pieces, w[CORE])
        scratch[0][...] = d
        dz = 0.0
        for d_half, ref, core in zip(core_halves(scratch[0], w, half), (m_ref, t_ref), (w[CORE], 1 - w[CORE])):
            own = own_ref[pl.ds(pl.multiple_of(core * half, 128), half), :]
            dz = dz + mm(d_half, jnp.concatenate([own, ref[...]], axis=1))
        mine_out[...] = low(dz[:, :own_slots])
        peer_out[...] = low(dz[:, own_slots:])

    whole = lambda i, w: (0, 0)
    mine = lambda i, w: (w[MEMBER], 0)
    side = (shape((share, half), bf16), (share, half), whole)
    return run(
        "close_feed_forward", body, where, (1,),
        [fixed(part), (hidden_row, (share, model), mine), (inverse, (share, 1), mine), fixed(gain),
         (cotangent, (share, model), lambda i, w: (w[ROW] * group + w[MEMBER], 0)),
         fixed(out_own), fixed(out_mine), fixed(out_theirs)] + [fixed(a) for a in got],
        [(shape((share, model), f32), (share, model), whole), side, side,
         (shape((share, own_slots), bf16), (share, own_slots), whole),
         (shape((share, filled - own_slots), bf16), (share, filled - own_slots), whole)],
        [pltpu.VMEM((share, model), bf16)], after, 2 * share * model * filled,
    )


def close_block(where, share, group, part, got, inputs, inverse, gain, dh, after=()):
    model = part.shape[1]
    step_rows = min(BLK, share)
    blocks = share // step_rows
    row_blocks = group * blocks

    def body(w, ins, outs, scratch):
        p_ref, x_ref, i_ref, gain_ref, dh_ref = ins[:5]
        total = p_ref[...]
        for r in ins[5:]:
            total = total + r[...].astype(f32)
        unit = x_ref[...].astype(f32) * i_ref[...]
        scaled = total * gain_ref[...]
        outs[0][...] = dh_ref[...] + i_ref[...] * (scaled - unit * jnp.mean(scaled * unit, axis=1, keepdims=True))

    tokens = lambda i, w: (i, 0)
    return run(
        "close_block", body, where, (blocks,),
        [(part, (step_rows, model), tokens),
         (inputs, (step_rows, model), lambda i, w: (w[ROW] * row_blocks + w[MEMBER] * blocks + i, 0)),
         (inverse, (step_rows, 1), lambda i, w: (w[MEMBER] * blocks + i, 0)), fixed(gain),
         (dh, (step_rows, model), tokens)] + [(a, (step_rows, model), tokens) for a in got],
        [(shape((share, model), f32), (step_rows, model), tokens)], (), after,
    )[0]


def collect(where, arrays, pieces, unit=1, after=()):
    count = arrays[0].shape[0] // pieces
    filled = sum(a.shape[1] for a in arrays)
    total = -(-filled // unit) * unit

    def body(w, ins, outs, scratch):
        at = 0
        for r in ins:
            n = r.shape[1]
            outs[0][:, at:at + n] = r[...]
            at += n
        if at < total:
            outs[0][:, at:] = jnp.zeros((count, total - at), bf16)

    return run(
        "collect", body, where, (1,),
        [(a, (count, a.shape[1]), lambda i, w: (w[PIECE], 0)) for a in arrays],
        [(shape((count, total), bf16), (count, total), lambda i, w: (0, 0))], (), after,
    )[0]


class Place:
    def __init__(self, rows):
        self.tensor = lax.axis_size("tensor")
        self.dp = lax.axis_size("dp")
        self.rows = rows
        self.group = self.tensor // rows
        self.at = lax.axis_index("tensor")
        self.dp_at = lax.axis_index("dp")
        self.bits = [1 << b for b in reversed(range(1, self.dp.bit_length() - 1))]

    def owner(self, at, step, turn):
        row, member = at // self.group, at % self.group
        return ((row + turn) % self.rows) * self.group + (member + step) % self.group

    def fetch(self, value, step, turn):
        pairs = [(self.owner(i, step, turn), i) for i in range(self.tensor)]
        return lax.ppermute(value, "tensor", pairs)

    def deliver(self, value, step, turn):
        pairs = [(i, self.owner(i, step, turn)) for i in range(self.tensor)]
        return lax.ppermute(value, "tensor", pairs)

    def swap(self, value, bit):
        return lax.ppermute(value, "dp", [(i, i ^ bit) for i in range(self.dp)])

    def sum_rest(self, value):
        for bit in self.bits[1:]:
            value = value + self.swap(value, bit)
        for bit in [1 << b for b in range(self.tensor.bit_length() - 1)]:
            value = value + lax.ppermute(value, "tensor", [(i, i ^ bit) for i in range(self.tensor)])
        return value


class Chain:
    def __init__(self, where):
        self.where = where
        self.behind = ()

    def __call__(self, make, *args, extra=(), **keys):
        made = make(self.where, *args, after=self.behind + tuple(extra), **keys)
        outs = made if isinstance(made, (list, tuple)) else [made]
        self.behind = (min(outs, key=lambda a: a.size),)
        return made

    def sync(self, *values):
        out = lax.optimization_barrier((*values, *self.behind))
        self.behind = tuple(out[len(values):])
        return out[:len(values)]


def on_device(
    inputs, gain_attn, w_query, w_key, w_value, w_outgate, w_forget, forget_bias, w_out,
    gain_mlp, w_gate, w_up, w_down, segment_ids, cotangent,
):
    rows, length = segment_ids.shape
    here = Place(rows)
    group, pieces = here.group, here.dp
    heads, width, hidden = w_forget.shape[1], w_query.shape[1], w_gate.shape[1]
    model = inputs.shape[1]
    share = length // group
    row, member = here.at // group, here.at % group
    core, chip = here.dp_at % 2, here.dp_at // 2
    where = jnp.stack([row, member, core, chip, core * (pieces // 2) + chip]).astype(jnp.int32)
    go = Chain(where)
    gain_attn, gain_mlp = gain_attn[None], gain_mlp[None]
    segment = lax.dynamic_index_in_dim(segment_ids, row, 0, keepdims=False)
    scol, srow = segment[:, None], segment[None, :]
    turns = range(1, rows)
    slots = [(s, j) for s in range(group) for j in range(rows)]

    def to_member(value, step):
        return lax.ppermute(value, "tensor", [
            (i, (i // group) * group + (i % group + step) % group) for i in range(here.tensor)])

    class Gather:
        def __init__(self, piece, flip):
            self.held, self.masks = [piece], [0]
            self.left = here.bits[::-1] if flip else list(here.bits)
            self.sent = {}
            self.send()

        def send(self):
            for bit in self.left:
                for i, p in enumerate(self.held):
                    if (bit, i) not in self.sent:
                        self.sent[bit, i] = here.swap(p, bit)

        def hop(self):
            bit = self.left.pop(0)
            got = go.sync(*[self.sent[bit, i] for i in range(len(self.held))])
            self.masks = self.masks + [k ^ (bit >> 1) for k in self.masks]
            self.held = self.held + list(got)
            self.send()

        def close(self):
            while self.left:
                self.hop()
            self.mine = go(assemble, self.held, self.masks)
            self.theirs = here.swap(self.mine, 1)
            return self.mine, self.theirs

    class Reduce:
        def __init__(self, send, keep, orders):
            self.parts = None
            self.keep, self.got, self.orders = keep, here.swap(send, 1), orders

        def hop(self):
            if self.parts is None:
                n = self.keep.shape[1]
                split = len(self.orders) if n % (128 * len(self.orders)) == 0 else 1
                entries = [(self.keep, self.got, list(here.bits), self.orders[c][0], c, n // split) for c in range(split)]
                orders = [order[1:] for order in self.orders[:split]]
            else:
                entries = [(kept, got, left, order[0], 0, kept.shape[1]) for kept, got, left, order in self.parts]
                orders = [order[1:] for _, _, _, order in self.parts]
            outs = go(fold, entries)
            self.parts = [
                [outs[2 * c + 1], here.swap(outs[2 * c], e[3]), [b for b in e[2] if b != e[3]], orders[c]]
                for c, e in enumerate(entries)
            ]

        def close(self):
            while self.parts is None or self.parts[0][3]:
                self.hop()
            sums = [kept.astype(f32) + got.astype(f32) for kept, got, _, _ in self.parts]
            return sums[0] if len(sums) == 1 else jnp.concatenate(sums, axis=1)

        def wait(self):
            got = go.sync(*([self.got] if self.parts is None else [p[1] for p in self.parts]))
            if self.parts is None:
                self.got = got[0]
            else:
                for p, g in zip(self.parts, got):
                    p[1] = g

    both_ways = [here.bits, here.bits[::-1]]

    attn_piece = go(collect, [w_query, w_key, w_value, w_outgate, w_forget], pieces, 256)
    attn_got = [here.fetch(attn_piece, 0, j) for j in turns]
    bias_got = [here.fetch(forget_bias, 0, j) for j in turns]
    own = go(project_own, length, pieces, inputs, gain_attn,
             [w_query, w_key, w_value, w_outgate, w_forget], forget_bias[None])
    normed, norm_send, norm_keep, inverse_attn = own[:4]
    mixed = {0: own[4:]}
    gated = {}
    logs = {}

    def attend(j):
        q, k, v, g, _, _, crow = mixed[j]
        z, logs[j] = go(attend_forward, q, k, v, g, crow, scol, srow)
        gated[0, j] = z
        for s in range(1, group):
            gated[s, j] = here.fetch(z, s, 0)

    attend(0)
    arrived = go.sync(*attn_got, *bias_got)
    attn_got, bias_got = arrived[:rows - 1], arrived[rows - 1:]
    attn_gather = [Gather(p, False) for p in attn_got]
    out_piece = go(collect, [w_out], pieces)
    out_got = [here.fetch(out_piece, 0, j) for j in turns]
    gate_piece = go(collect, [w_gate, w_up], pieces)
    gate_got = [here.fetch(gate_piece, 0, j) for j in turns]
    cot_sides = go(split_rows, length, pieces, cotangent)
    for gather in attn_gather:
        gather.hop()
    out_got = go.sync(*out_got)
    out_own = jnp.concatenate([out_piece, *out_got], axis=1)
    out_peers = [here.fetch(out_own, s, 0) for s in range(1, group)]
    attn_w = [gather.close() for gather in attn_gather]
    out_peers = go.sync(*out_peers)
    out_gather = Gather(jnp.concatenate([*out_got, *out_peers], axis=1), True)
    for j in turns:
        mixed[j] = go(project_other, normed, *attn_w[j - 1], width, heads, bias_got[j - 1][None])
    down_piece = go(collect, [w_down], pieces)
    gate_got = go.sync(*gate_got)
    gate_gather = [Gather(p, False) for p in gate_got]
    for j in turns:
        attend(j)
    down_got = [here.fetch(down_piece, 0, j) for j in turns]
    out_gather.hop()
    for gather in gate_gather:
        gather.hop()
    out_mine, out_theirs = out_gather.close()
    gate_w = [gather.close() for gather in gate_gather]
    hidden_row, mlp_normed, mlp_send, mlp_keep, inverse_mlp = go(
        close_attention, length, pieces, inputs, [gated[slot] for slot in slots], w_out, out_mine, out_theirs, gain_mlp
    )
    down_got = go.sync(*down_got)
    down_gather = [Gather(p, True) for p in down_got]

    ffn = {0: go(feed_forward, mlp_normed, cotangent, [w_gate, w_up, w_down], hidden)}
    for gather in down_gather:
        gather.hop()

    def mlp_grads(j):
        m, du, dw = ffn[j]
        sides = [(mlp_send, mlp_keep), cot_sides]
        send, keep = go(lambda w, after: weight_grads(
            "mlp_grads", w, sides, [(0, [du]), (0, [dw]), (1, [m])], after=after))
        return Reduce(send, keep, both_ways)

    mlp_sums = {0: mlp_grads(0)}
    mlp_w = {}
    for j in turns:
        mlp_w[j] = gate_w[j - 1] + down_gather[j - 1].close()
        gm, gt, dm, dt = mlp_w[j]
        ffn[j] = go(feed_forward, mlp_normed, cotangent, [gm, gt, dm, dt], hidden)
    peers = list(range(1, group))
    own_terms = [([ffn[0][1]], [w_gate]), ([ffn[0][2]], [w_up])]
    pair_terms = [([ffn[j][1], ffn[j][2]], *mlp_w[j][:2], 0) for j in turns]
    made = go(lambda w, after: back_rows(
        "mlp_back", w, peers + [0], group, share, own_terms, pair_terms, model, [bf16] * len(peers) + [f32],
        (), (hidden_row, 0, inverse_mlp), after))
    part, gain_mlp_part = made[-2:]
    got = [to_member(v, s) for v, s in zip(made, peers)]
    mlp_sums[0].hop()
    for j in turns:
        mlp_sums[j] = mlp_grads(j)
    mlp_sums[0].hop()
    for j in turns:
        mlp_sums[j].hop()
    dh, dh_send, dh_keep, dz_mine, dz_peers = go(
        close_feed_forward, share, group, pieces, part, got, hidden_row, inverse_mlp, gain_mlp, cotangent,
        w_out, out_mine, out_theirs,
    )
    dz_parts = [dz_mine]
    own_slots = rows * width
    for s in peers:
        lo = (group - s - 1) * own_slots
        dz_parts.append(here.fetch(dz_peers if group == 2 else dz_peers[:, lo:lo + own_slots], s, 0))

    def mlp_out(steps, dtypes, adds):
        own_terms = [([ffn[0][0]], [w_down])]
        pair_terms = [([ffn[j][0]], *mlp_w[j][2:], 0) for j in turns]
        return go(lambda w, after: back_rows(
            "mlp_out", w, steps, group, share, own_terms, pair_terms, model, dtypes, adds, None, after))

    out_send = mlp_out(peers, [bf16] * len(peers), ())
    out_sum = Reduce(*go(lambda w, after: weight_grads(
        "out_grads", w, [(dh_send, dh_keep)], [(0, [gated[slot] for slot in slots])], True, after)), both_ways)
    for j in turns:
        mlp_sums[j].hop()
    mlp_own = mlp_sums[0].close()

    back = {}
    attn_sums = {}
    per_step = together(heads) * HEAD

    def attend_back(j):
        q, k, v, g, forget, ccol, _ = mixed[j]
        parts = [(d, j * width // per_step) for d in dz_parts]
        if width % 128:
            parts = [(a[:, o * per_step:(o + 1) * per_step], 0) for a, o in parts]
        back[j] = go(attend_backward, q, k, v, g, gated[0, j], parts, logs[j], ccol, forget, scol, srow)

    def attn_grads(j):
        attn_sums[j] = Reduce(*go(lambda w, after: weight_grads(
            "attn_grads", w, [(norm_send, norm_keep)], [(0, back[j][:5])], False, after)), both_ways)

    dz_parts[1:] = go.sync(*dz_parts[1:])
    out_got = [to_member(v, s) for v, s in zip(out_send, peers)]
    for j in turns:
        attend_back(j)
    out_sum.hop()
    for j in turns:
        mlp_sums[j].wait()
    mlp_other = [here.deliver(low(mlp_sums[j].close()), 0, j) for j in turns]
    for j in turns:
        attn_grads(j)
    out_got = go.sync(*out_got)
    attend_back(0)
    out_sum.hop()
    for j in turns:
        attn_sums[j].hop()
    attn_grads(0)
    mlp_other = go.sync(*mlp_other)
    own_terms = [(back[0][:5], [w_query, w_key, w_value, w_outgate, w_forget])]
    pair_terms = [(back[j][:5], *attn_w[j - 1], 0) for j in turns]
    made = go(lambda w, after: back_rows(
        "attn_back", w, peers + [0], group, share, own_terms, pair_terms, model, [bf16] * len(peers) + [f32],
        (), (inputs, group, inverse_attn), after))
    part, gain_attn_part = made[-2:]
    got = [to_member(v, s) for v, s in zip(made, peers)]
    bias_full = jnp.zeros((here.tensor, heads), f32)
    for j in range(rows):
        bias_full = lax.dynamic_update_slice(bias_full, back[j][5], (here.owner(here.at, 0, j), 0))
    small = jnp.concatenate([gain_attn_part, gain_mlp_part, bias_full.reshape(1, -1)], axis=1)
    small = go.sync(small + here.swap(small, 1))[0]
    attn_sums[0].hop()
    small = small + here.swap(small, here.bits[0])
    for j in turns:
        attn_sums[j].hop()
    small = go.sync(small)[0]
    small = here.sum_rest(small)
    out_sum.wait()
    out_part = out_sum.close()
    grad_out = out_part[:, :width]
    out_rest = [here.deliver(low(out_part[:, (i + 1) * width:(i + 2) * width]), s, j) for i, (s, j) in enumerate(slots[1:])]
    attn_other = [here.deliver(low(attn_sums[j].close()), 0, j) for j in turns]
    output = mlp_out([0], [f32], [(hidden_row, "row")] + [(v, "own") for v in out_got])[0]
    attn_sums[0].hop()
    grad_inputs = go(close_block, share, group, part, got, inputs, inverse_attn, gain_attn, dh)
    mlp = mlp_own
    for v in mlp_other:
        mlp = mlp + v.astype(f32)
    for v in out_rest:
        grad_out = grad_out + v.astype(f32)
    attn = attn_sums[0].close()
    for v in attn_other:
        attn = attn + v.astype(f32)
    bias_own = lax.dynamic_slice_in_dim(small[0, 2 * model:], here.at * heads, heads, 0)
    return (
        output,
        grad_inputs,
        small[0, :model],
        attn[:, :width],
        attn[:, width:2 * width],
        attn[:, 2 * width:3 * width],
        attn[:, 3 * width:4 * width],
        attn[:, 4 * width:4 * width + heads],
        bias_own,
        grad_out,
        small[0, model:2 * model],
        mlp[:, :hidden],
        mlp[:, hidden:2 * hidden],
        mlp[:, 2 * hidden:],
    )


def solution(mesh):
    placed = (
        P("dp", None), P(), P(None, "tensor"), P(None, "tensor"), P(None, "tensor"),
        P(None, "tensor"), P(None, "tensor"), P("tensor"), P(None, "tensor"), P(),
        P(None, "tensor"), P(None, "tensor"), P(None, "tensor"), P("dp", None), P("dp", None),
    )
    weight = P("dp", "tensor")
    tokens = P(("dp", "tensor"), None)
    return jax.shard_map(
        on_device,
        mesh=mesh,
        in_specs=placed,
        out_specs=(
            tokens, tokens, P(), weight, weight, weight, weight, weight, P("tensor"),
            weight, P(), weight, weight, weight,
        ),
        check_vma=False,
    )
```

time: 1740 us -> 682 us (0.39)
  waiting for transfers between devices: 930 us -> 208 us
  matrix products: 418 us -> 0 us
  Pallas kernels: 0 us -> 358 us
  other arithmetic: 183 us -> 8.15 us
  local copies, waits for them, and re-layouts: 141 us -> 31.6 us
  starting transfers between devices: 1.43 us -> 65 us
  blocking collectives: 39.4 us -> 0 us
    psum x3 -> x0, waiting for transfers between devices: 836 us -> none  [the longest x1 428 us: on_device(): lax.psum(ffn_part.astype(jnp.bfloat16), 'tensor').astype(jnp.float32)]
    dot_general x41 -> x0, matrix products: 418 us -> none  [the longest x9 94.5 us: contract_last(): lax.dot_general(left, right, (((1,), (1,)), ((), ())), preferred_element_...]
    pallas_call x0 -> x39, Pallas kernels: none -> 358 us  [the longest x35 351 us: run(): pl.pallas_call(kernel, grid_spec=pltpu.PrefetchScalarGridSpec(num_scalar_...]
    ppermute x0 -> x63, waiting for transfers between devices: none -> 208 us  [the longest x44 149 us: swap(): return lax.ppermute(value, 'dp', [(i, i ^ bit) for i in range(self.dp)])]
    reduce_sum x10 -> x0, other arithmetic: 98.9 us -> none  [the longest x2 45.1 us: attend_backward(): grad_running = (jnp.sum(score_full, axis=2) - jnp.sum(score_full, axis=1)).T]
    reduce_scatter x7 -> x0, waiting for transfers between devices: 93.8 us -> none  [the longest x1 39.3 us: on_device(): lax.psum_scatter(grad_outgate_w.astype(jnp.bfloat16), 'dp', scatter_dimen...]
    ppermute x0 -> x63, starting transfers between devices: none -> 65 us  [the longest x44 39.2 us: swap(): return lax.ppermute(value, 'dp', [(i, i ^ bit) for i in range(self.dp)])]
    dynamic_update_slice x5 -> x2, local copies, waits for them, and re-layouts: 61.2 us -> 0.07 us  [on_device(): lax.dynamic_update_slice(bias_full, back[j][5], (here.owner(here.at, 0, j...]
  transfers between devices with their start and end apart: 12 -> 63, of which waited for: 6 -> 27; matrix products, arithmetic and copies ran while one was open for 24% -> 2% of each run, Pallas kernels for 0% -> 44%
where the time goes in v2:
time: 682 us; the launch traced here: 673 us
  Pallas kernels  358 us (52%)
  waiting for transfers between devices  208 us (30%)
  starting transfers between devices  65 us (10%)
  local copies, waits for them, and re-layouts  31.6 us (5%)
  other arithmetic  8.15 us (1%)
    pallas_call x35, Pallas kernels, run(): pl.pallas_call(kernel, grid_spec=pltpu.PrefetchScalarGridSpec(num_scalar_...  351 us
    ppermute x44, waiting for transfers between devices, swap(): return lax.ppermute(value, 'dp', [(i, i ^ bit) for i in range(self.dp)])  149 us
    ppermute x44, starting transfers between devices, swap(): return lax.ppermute(value, 'dp', [(i, i ^ bit) for i in range(self.dp)])  39.2 us
    ppermute x9, waiting for transfers between devices, fetch(): return lax.ppermute(value, 'tensor', pairs)  30.8 us
    unnamed x139, local copies, waits for them, and re-layouts  24.2 us
    ppermute x5, waiting for transfers between devices, deliver(): return lax.ppermute(value, 'tensor', pairs)  21.7 us
    ppermute x9, starting transfers between devices, fetch(): return lax.ppermute(value, 'tensor', pairs)  15.9 us
  transfers between devices with their start and end apart: 63, of which 27 were waited for; matrix products, arithmetic and copies ran while one was open for 2% of the time, Pallas kernels for 44%

profile of v2, /device:TPU:0, one launch (start us, length us, event | category | flops | bytes accessed | tf_op | source)
XLA Modules:
  0.0 672.8 jit_solution(6361279664799675549)
XLA Ops:
  5.9 4.0 collective-permute-start
  12.2 13.7 %project_own.1 = (bf16[1024,1536]{1,0:T(8,128)(2,1)}, bf16[1024,768]{1,0:T(8,128)(2,1)}, bf16[1024,768]{1,0:T(8,128)(2,1)}, f32[1024,1]{1,0:T(8,128)}, bf16[1024...) custom-call(s32[5]{0:T(128)} %stack.23.where_ref.w, ...), custom_call_target="tpu_custom_call" | custom-call | flops 5850712576 | bytes 1 | tf_op jit(solution)/shard_map/project_own/pallas_call | solution.py:44
  25.9 13.7 %attend_forward.2 = (bf16[1024,384]{1,0:T(8,128)(2,1)}, f32[3,2,1024]{2,1,0:T(2,128)}) custom-call(s32[5]{0:T(128)} %stack.23.where_ref.w, bf16[1024,384]{1,0:T(8,128)(2,1)} %get-tuple-element.169.refs_0_, bf16[1024,384]{1,0:T(8,128)(2,1)} %get-tuple-element.170.refs_1_, bf16[1024,384]{1,0:T(8,128)(2,1)} %get-tuple-element.171.refs_2_, ...), custom_call_target="tpu_custom_call" | custom-call | flops 7920601600 | bytes 1 | tf_op jit(solution)/shard_map/attend_forward/pallas_call | solution.py:44
  48.5 5.4 split_rows.1
  60.7 6.4 collective-permute-done.2
  67.1 5.6 collective-permute-done.6.refs_3_
  81.5 10.1 %collective-permute-done.4 = bf16[192,768]{1,0:T(8,128)(2,1)S(1)} collective-permute-done((bf16[192,768]{1,0:T(8,128)(2,1)S(1)}, bf16[192,768]{1,0:T(8,128)(2,1)S(1)}, u32[]{:S(2)}, u32[]{:S(2)}) %collective-permute-start.4) | collective-permute-done | bytes 294944 | tf_op jit(solution)/shard_map/ppermute | solution.py:716
  96.2 11.7 %project_other.1 = (bf16[1024,384]{1,0:T(8,128)(2,1)}, bf16[1024,384]{1,0:T(8,128)(2,1)}, bf16[1024,384]{1,0:T(8,128)(2,1)}, bf16[1024,384]{1,0:T(8,128)(2,1)}, ...) custom-call(s32[5]{0:T(128)} %stack.23.where_ref.w, bf16[1024,1536]{1,0:T(8,128)(2,1)} %get-tuple-element.187.refs_0_, ...), custom_call_target="tpu_custom_call" | custom-call | flops 5850712576 | bytes 1 | tf_op jit(solution)/shard_map/project_other/pallas_call | solution.py:44
  110.3 6.0 collective-permute-done.9.refs_0_
  117.8 14.0 %attend_forward.3 = (bf16[1024,384]{1,0:T(8,128)(2,1)}, f32[3,2,1024]{2,1,0:T(2,128)}) custom-call(s32[5]{0:T(128)} %stack.23.where_ref.w, bf16[1024,384]{1,0:T(8,128)(2,1)} %get-tuple-element.190.refs_0_, bf16[1024,384]{1,0:T(8,128)(2,1)} %get-tuple-element.191.refs_1_, bf16[1024,384]{1,0:T(8,128)(2,1)} %get-tuple-element.192.refs_2_, ...), custom_call_target="tpu_custom_call" | custom-call | flops 7920601600 | bytes 1 | tf_op jit(solution)/shard_map/attend_forward/pallas_call | solution.py:44
  132.4 4.3 collective-permute-done.12.refs_1_
  136.7 8.2 %collective-permute-done.11.refs_3_ = bf16[192,1152]{1,0:T(8,128)(2,1)S(1)} collective-permute-done((bf16[192,1152]{1,0:T(8,128)(2,1)S(1)}, bf16[192,1152]{1,0:T(8,128)(2,1)S(1)}, u32[]{:S(2)}, u32[]{:S(2)}) %collective-permute-start.11) | collective-permute-done | bytes 442400 | tf_op jit(solution)/shard_map/ppermute | solution.py:723
  152.0 15.7 %collective-permute-done.16.refs_2_ = bf16[192,2048]{1,0:T(8,128)(2,1)S(1)} collective-permute-done((bf16[192,2048]{1,0:T(8,128)(2,1)S(1)}, bf16[192,2048]{1,0:T(8,128)(2,1)S(1)}, u32[]{:S(2)}, u32[]{:S(2)}) %collective-permute-start.16) | collective-permute-done | bytes 786464 | tf_op jit(solution)/shard_map/ppermute | solution.py:723
  167.7 16.4 %collective-permute-done.17.refs_3_ = bf16[192,2048]{1,0:T(8,128)(2,1)S(1)} collective-permute-done((bf16[192,2048]{1,0:T(8,128)(2,1)S(1)}, bf16[192,2048]{1,0:T(8,128)(2,1)S(1)}, u32[]{:S(2)}, u32[]{:S(2)}) %collective-permute-start.17) | collective-permute-done | bytes 786464 | tf_op jit(solution)/shard_map/ppermute | solution.py:723
  186.5 7.5 %collective-permute-done.15.refs_8_.refs_5_ = bf16[1024,384]{1,0:T(8,128)(2,1)S(1)} collective-permute-done((bf16[1024,384]{1,0:T(8,128)(2,1)S(1)}, bf16[1024,384]{1,0:T(8,128)(2,1)S(1)}, u32[]{:S(2)}, u32[]{:S(2)}) %collective-permute-start.15) | collective-permute-done | bytes 786464 | tf_op jit(solution)/shard_map/ppermute | solution.py:716
  196.2 13.2 %close_attention.1 = (f32[1024,1536]{1,0:T(8,128)}, bf16[1024,1536]{1,0:T(8,128)(2,1)}, bf16[1024,768]{1,0:T(8,128)(2,1)}, bf16[1024,768]{1,0:T(8,128)(2,1)}, f32[1024,1]{1,0:T(8,128)}) custom-call(s32[5]{0:T(128)} %stack.23.where_ref.w, bf16[2048,1536]{1,0:T(8,128)(2,1)} %refs_1_.17, bf16[1536,384]{1,0:T(8,128)(2,1)} %refs_5_.4, ...), custom_call_target="tpu_custom_call" | custom-call | flops 5831838208 | bytes 1 | tf_op jit(solution)/shard_map/close_attention/pallas_call | solution.py:44
  211.0 16.4 %feed_forward.2 = (bf16[1024,1024]{1,0:T(8,128)(2,1)}, bf16[1024,1024]{1,0:T(8,128)(2,1)}, bf16[1024,1024]{1,0:T(8,128)(2,1)}) custom-call(s32[5]{0:T(128)} %stack.23.where_ref.w, bf16[1024,1536]{1,0:T(8,128)(2,1)} %get-tuple-element.211.refs_0_, bf16[2048,1536]{1,0:T(8,128)(2,1)} %refs_4_.6, bf16[1536,1024]{1,0:T(8,128)(2,1)} %refs_1_.14, ...), custom_call_target="tpu_custom_call" | custom-call | flops 10663675904 | bytes 1 | tf_op jit(solution)/shard_map/feed_forward/pallas_call | solution.py:44
  227.4 18.8 %mlp_grads.2 = (bf16[768,3072]{1,0:T(8,128)(2,1)}, bf16[768,3072]{1,0:T(8,128)(2,1)}) custom-call(s32[5]{0:T(128)} %stack.23.where_ref.w, bf16[1024,768]{1,0:T(8,128)(2,1)} %get-tuple-element.217.refs_0_, bf16[1024,768]{1,0:T(8,128)(2,1)} %get-tuple-element.218.refs_1_, bf16[1024,768]{1,0:T(8,128)(2,1)} %get-tuple-element.185.refs_4_.refs_2_, ...), custom_call_target="tpu_custom_call" | custom-call | flops 10663675904 | bytes 1 | tf_op jit(solution)/shard_map/mlp_grads/pallas_call | solution.py:44
  248.3 9.9 %collective-permute-done.20.refs_2_ = bf16[192,1024]{1,0:T(8,128)(2,1)S(1)} collective-permute-done((bf16[192,1024]{1,0:T(8,128)(2,1)S(1)}, bf16[192,1024]{1,0:T(8,128)(2,1)S(1)}, u32[]{:S(2)}, u32[]{:S(2)}) %collective-permute-start.20) | collective-permute-done | bytes 393248 | tf_op jit(solution)/shard_map/ppermute | solution.py:723
  258.2 8.0 %collective-permute-done.21.refs_3_ = bf16[192,1024]{1,0:T(8,128)(2,1)S(1)} collective-permute-done((bf16[192,1024]{1,0:T(8,128)(2,1)S(1)}, bf16[192,1024]{1,0:T(8,128)(2,1)S(1)}, u32[]{:S(2)}, u32[]{:S(2)}) %collective-permute-start.21) | collective-permute-done | bytes 393248 | tf_op jit(solution)/shard_map/ppermute | solution.py:723
  274.6 16.6 %feed_forward.3 = (bf16[1024,1024]{1,0:T(8,128)(2,1)}, bf16[1024,1024]{1,0:T(8,128)(2,1)}, bf16[1024,1024]{1,0:T(8,128)(2,1)}) custom-call(s32[5]{0:T(128)} %stack.23.where_ref.w, bf16[1024,1536]{1,0:T(8,128)(2,1)} %get-tuple-element.211.refs_0_, bf16[2048,1536]{1,0:T(8,128)(2,1)} %refs_4_.6, bf16[768,2048]{1,0:T(8,128)(2,1)} %assemble.6.refs_9_.refs_2_.refs_3_.refs_4_, ...), custom_call_target="tpu_custom_call" | custom-call | flops 10663675904 | bytes 1 | tf_op jit(solution)/shard_map/feed_forward/pallas_call | solution.py:44
  291.2 24.3 %mlp_back.1 = (bf16[512,1536]{1,0:T(8,128)(2,1)}, f32[512,1536]{1,0:T(8,128)}, f32[1,1536]{1,0:T(1,128)}) custom-call(s32[5]{0:T(128)} %stack.23.where_ref.w, bf16[1024,1024]{1,0:T(8,128)(2,1)} %get-tuple-element.220.refs_4_.refs_0_, bf16[1536,1024]{1,0:T(8,128)(2,1)} %refs_1_.14, bf16[1024,1024]{1,0:T(8,128)(2,1)} %get-tuple-element.221.refs_5_.refs_2_, ...), custom_call_target="tpu_custom_call" | custom-call | flops 13884901376 | bytes 1 | tf_op jit(solution)/shard_map/mlp_back/pallas_call | solution.py:44
  315.5 7.1 %fold.10 = (bf16[384,1536]{1,0:T(8,128)(2,1)}, bf16[384,1536]{1,0:T(8,128)(2,1)}, bf16[384,1536]{1,0:T(8,128)(2,1)}, bf16[384,1536]{1,0:T(8,128)(2,1)}) custom-call(s32[5]{0:T(128)} %stack.23.where_ref.w, bf16[768,3072]{1,0:T(8,128)(2,1)} %get-tuple-element.233.refs_0_.refs_2_.refs_4_.refs_6_, ...), custom_call_target="tpu_custom_call" | custom-call | flops 2000000000 | bytes 1 | tf_op jit(solution)/shard_map/fold/pallas_call | solution.py:44
  322.6 18.7 %mlp_grads.3 = (bf16[768,3072]{1,0:T(8,128)(2,1)}, bf16[768,3072]{1,0:T(8,128)(2,1)}) custom-call(s32[5]{0:T(128)} %stack.23.where_ref.w, bf16[1024,768]{1,0:T(8,128)(2,1)} %get-tuple-element.217.refs_0_, bf16[1024,768]{1,0:T(8,128)(2,1)} %get-tuple-element.218.refs_1_, bf16[1024,768]{1,0:T(8,128)(2,1)} %get-tuple-element.185.refs_4_.refs_2_, ...), custom_call_target="tpu_custom_call" | custom-call | flops 10663675904 | bytes 1 | tf_op jit(solution)/shard_map/mlp_grads/pallas_call | solution.py:44
  343.4 26.5 %collective-permute-done.27.refs_1_.refs_3_ = bf16[384,1536]{1,0:T(8,128)(2,1)S(1)} collective-permute-done((bf16[384,1536]{1,0:T(8,128)(2,1)}, bf16[384,1536]{1,0:T(8,128)(2,1)S(1)}, u32[]{:S(2)}, u32[]{:S(2)}) %collective-permute-start.27) | collective-permute-done | bytes 1179680 | tf_op jit(solution)/shard_map/ppermute | solution.py:723
  371.9 4.3 fold.11
  378.3 7.1 %fold.12 = (bf16[384,1536]{1,0:T(8,128)(2,1)}, bf16[384,1536]{1,0:T(8,128)(2,1)}, bf16[384,1536]{1,0:T(8,128)(2,1)}, bf16[384,1536]{1,0:T(8,128)(2,1)}) custom-call(s32[5]{0:T(128)} %stack.23.where_ref.w, bf16[768,3072]{1,0:T(8,128)(2,1)} %get-tuple-element.236.refs_0_.refs_2_.refs_4_.refs_6_, bf16[768,3072]{1,0:T(8,128)(2,1)} %copy-done.11, ...), custom_call_target="tpu_custom_call" | custom-call | flops 2000000000 | bytes 1 | tf_op jit(solution)/shard_map/fold/pallas_call | solution.py:44
  385.4 11.3 %close_feed_forward.1 = (f32[512,1536]{1,0:T(8,128)}, bf16[512,768]{1,0:T(8,128)(2,1)}, bf16[512,768]{1,0:T(8,128)(2,1)}, bf16[512,768]{1,0:T(8,128)(2,1)}, bf16[512,768]{1,0:T(8,128)(2,1)}) custom-call(s32[5]{0:T(128)} %stack.23.where_ref.w, f32[512,1536]{1,0:T(8,128)} %get-tuple-element.231.refs_0_, ...), custom_call_target="tpu_custom_call" | custom-call | flops 3415919104 | bytes 1 | tf_op jit(solution)/shard_map/close_feed_forward/pallas_call | solution.py:44
  396.7 9.1 %mlp_out.2.refs_6_ = bf16[512,1536]{1,0:T(8,128)(2,1)} custom-call(s32[5]{0:T(128)} %stack.23.where_ref.w, bf16[1024,1024]{1,0:T(8,128)(2,1)} %get-tuple-element.222.refs_6_.refs_7_.refs_0_, bf16[1536,1024]{1,0:T(8,128)(2,1)} %refs_1_.16, bf16[768,1024]{1,0:T(8,128)(2,1)} %copy-done.3, bf16[768,1024]{1,0:T(8,128)(2,1)} %copy-done.25, ...), custom_call_target="tpu_custom_call" | custom-call | flops 4221225472 | bytes 1 | tf_op jit(solution)/shard_map/mlp_out/pallas_call | solution.py:44
  405.8 7.4 %out_grads.1 = (bf16[768,1536]{1,0:T(8,128)(2,1)}, bf16[768,1536]{1,0:T(8,128)(2,1)}) custom-call(s32[5]{0:T(128)} %stack.23.where_ref.w, bf16[512,768]{1,0:T(8,128)(2,1)} %get-tuple-element.243.refs_5_.refs_0_, bf16[512,768]{1,0:T(8,128)(2,1)} %get-tuple-element.251.refs_1_, bf16[1024,384]{1,0:T(8,128)(2,1)} %get-tuple-element.205.refs_5_.refs_2_.refs_4_, ...), custom_call_target="tpu_custom_call" | custom-call | flops 3415919104 | bytes 1 | tf_op jit(solution)/shard_map/out_grads/pallas_call | solution.py:44
  418.0 23.7 %collective-permute-done.31.refs_1_.refs_3_ = bf16[384,1536]{1,0:T(8,128)(2,1)S(1)} collective-permute-done((bf16[384,1536]{1,0:T(8,128)(2,1)S(1)}, bf16[384,1536]{1,0:T(8,128)(2,1)S(1)}, u32[]{:S(2)}, u32[]{:S(2)}) %collective-permute-start.31) | collective-permute-done | bytes 1179680 | tf_op jit(solution)/shard_map/ppermute | solution.py:723
  444.4 4.5 fold.13
  450.4 18.4 %attend_backward.2 = (bf16[1024,384]{1,0:T(8,128)(2,1)}, bf16[1024,384]{1,0:T(8,128)(2,1)}, bf16[1024,384]{1,0:T(8,128)(2,1)}, bf16[1024,384]{1,0:T(8,128)(2,1)}...) custom-call(s32[5]{0:T(128)} %stack.23.where_ref.w, bf16[1024,384]{1,0:T(8,128)(2,1)} %get-tuple-element.190.refs_0_, ...), custom_call_target="tpu_custom_call" | custom-call | flops 10437183488 | bytes 1 | tf_op jit(solution)/shard_map/attend_backward/pallas_call | solution.py:44
  470.2 4.3 fold.14
  474.5 11.8 %attn_grads.2 = (bf16[768,1792]{1,0:T(8,128)(2,1)}, bf16[768,1792]{1,0:T(8,128)(2,1)}) custom-call(s32[5]{0:T(128)} %stack.23.where_ref.w, bf16[1024,768]{1,0:T(8,128)(2,1)} %get-tuple-element.244.refs_0_, bf16[1024,768]{1,0:T(8,128)(2,1)} %get-tuple-element.245.refs_1_, bf16[1024,384]{1,0:T(8,128)(2,1)} %get-tuple-element.257.refs_2_.refs_12_, ...), custom_call_target="tpu_custom_call" | custom-call | flops 6637144576 | bytes 1 | tf_op jit(solution)/shard_map/attn_grads/pallas_call | solution.py:44
  496.6 18.5 %attend_backward.3 = (bf16[1024,384]{1,0:T(8,128)(2,1)}, bf16[1024,384]{1,0:T(8,128)(2,1)}, bf16[1024,384]{1,0:T(8,128)(2,1)}, bf16[1024,384]{1,0:T(8,128)(2,1)}...) custom-call(s32[5]{0:T(128)} %stack.23.where_ref.w, bf16[1024,384]{1,0:T(8,128)(2,1)} %get-tuple-element.169.refs_0_, ...), custom_call_target="tpu_custom_call" | custom-call | flops 10437183488 | bytes 1 | tf_op jit(solution)/shard_map/attend_backward/pallas_call | solution.py:44
  521.0 4.5 fold.16
  525.4 11.5 %attn_grads.3 = (bf16[768,1792]{1,0:T(8,128)(2,1)}, bf16[768,1792]{1,0:T(8,128)(2,1)}) custom-call(s32[5]{0:T(128)} %stack.23.where_ref.w, bf16[1024,768]{1,0:T(8,128)(2,1)} %get-tuple-element.244.refs_0_, bf16[1024,768]{1,0:T(8,128)(2,1)} %get-tuple-element.245.refs_1_, bf16[1024,384]{1,0:T(8,128)(2,1)} %get-tuple-element.278.refs_2_.refs_0_, ...), custom_call_target="tpu_custom_call" | custom-call | flops 6637144576 | bytes 1 | tf_op jit(solution)/shard_map/attn_grads/pallas_call | solution.py:44
  541.1 6.7 %collective-permute-done.40 = bf16[192,3072]{1,0:T(8,128)(2,1)} collective-permute-done((bf16[192,3072]{1,0:T(8,128)(2,1)}, bf16[192,3072]{1,0:T(8,128)(2,1)}, u32[]{:S(2)}, u32[]{:S(2)}) %collective-permute-start.40) | collective-permute-done | bytes 1179680 | tf_op jit(solution)/shard_map/ppermute | solution.py:720
  547.9 22.7 %attn_back.1 = (bf16[512,1536]{1,0:T(8,128)(2,1)}, f32[512,1536]{1,0:T(8,128)}, f32[1,1536]{1,0:T(1,128)}) custom-call(s32[5]{0:T(128)} %stack.23.where_ref.w, bf16[1024,384]{1,0:T(8,128)(2,1)} %get-tuple-element.278.refs_2_.refs_0_, bf16[1024,384]{1,0:T(8,128)(2,1)} %get-tuple-element.279.refs_3_.refs_1_, ...), custom_call_target="tpu_custom_call" | custom-call | flops 10701424640 | bytes 1 | tf_op jit(solution)/shard_map/attn_back/pallas_call | solution.py:44
  580.1 4.5 fold.17
  585.5 3.8 collective-permute-done.45.refs_5_.refs_7_
  595.2 7.9 %collective-permute-done.50 = f32[1,3096]{1,0:T(1,128)S(1)} collective-permute-done((f32[1,3096]{1,0:T(1,128)S(1)}, f32[1,3096]{1,0:T(1,128)S(1)}, u32[]{:S(2)}, u32[]{:S(2)}) %collective-permute-start.50) | collective-permute-done | bytes 12416 | tf_op jit(solution)/shard_map/ppermute | solution.py:723
  603.2 10.6 %mlp_out.3.refs_8_ = f32[512,1536]{1,0:T(8,128)} custom-call(s32[5]{0:T(128)} %stack.23.where_ref.w, bf16[1024,1024]{1,0:T(8,128)(2,1)} %get-tuple-element.222.refs_6_.refs_7_.refs_0_, bf16[1536,1024]{1,0:T(8,128)(2,1)} %refs_1_.16, bf16[768,1024]{1,0:T(8,128)(2,1)} %copy-done.3, bf16[768,1024]{1,0:T(8,128)(2,1)} %copy-done.25, ...), custom_call_target="tpu_custom_call" | custom-call | flops 4221225472 | bytes 1 | tf_op jit(solution)/shard_map/mlp_out/pallas_call | solution.py:44
  613.8 3.9 collective-permute-done.51
  632.3 6.4 collective-permute-done.49.refs_5_.refs_7_
  645.3 12.3 %collective-permute-done.58 = bf16[192,384]{1,0:T(8,128)(2,1)S(1)} collective-permute-done((bf16[192,384]{1,0:T(8,128)(2,1)S(1)}, bf16[192,384]{1,0:T(8,128)(2,1)S(1)}, u32[]{:S(2)}, u32[]{:S(2)}) %collective-permute-start.58) | collective-permute-done | bytes 147488 | tf_op jit(solution)/shard_map/ppermute | solution.py:720
  660.4 6.6 close_block.1
  (296 shorter events, 147.2 us)
Async XLA Ops:
  5.9 34.5 %collective-permute-start = (bf16[192,1792]{1,0:T(8,128)(2,1)}, bf16[192,1792]{1,0:T(8,128)(2,1)S(1)}, u32[]{:S(2)}, u32[]{:S(2)}) collective-permute-start(bf16[192,1792]{1,0:T(8,128)(2,1)} %collect.4.refs_8_), channel_id=1, source_target_pairs={{2,0},{3,1},{0,2},{1,3},{6,4},{7,5},{4,6},{5,7},{10,8},{11,9},{8,1... | collective-permute-start | bytes 2064392 | tf_op jit(solution)/shard_map/ppermute | solution.py:716
  9.9 30.5 %collective-permute-start.1 = (f32[6]{0:T(128)S(1)}, f32[6]{0:T(128)S(1)}, u32[]{:S(2)}, u32[]{:S(2)}) collective-permute-start(f32[6]{0:T(128)S(1)} %copy-done.65), channel_id=1, source_target_pairs={{2,0},{3,1},{0,2},{1,3},{6,4},{7,5},{4,6},{5,7},{10,8},{11,9},{8,1... | collective-permute-start | bytes 80 | tf_op jit(solution)/shard_map/ppermute | solution.py:716
  40.4 16.6 %collective-permute-start.3 = (bf16[192,1792]{1,0:T(8,128)(2,1)S(1)}, bf16[192,1792]{1,0:T(8,128)(2,1)S(1)}, u32[]{:S(2)}, u32[]{:S(2)}) collective-permute-start(bf16[192,1792]{1,0:T(8,128)(2,1)S(1)} %collective-permute-done.refs_0_), channel_id=1, source_target_pairs={{0,16},{4,20},{8,24},{12,28},{16,0},{20,4},{24,8},{28,12},{1,17},{... | collective-permute-start | bytes 2064392 | tf_op jit(solution)/shard_map/ppermute | solution.py:723
  42.0 25.2 %collective-permute-start.5 = (bf16[192,1792]{1,0:T(8,128)(2,1)S(1)}, bf16[192,1792]{1,0:T(8,128)(2,1)S(1)}, u32[]{:S(2)}, u32[]{:S(2)}) collective-permute-start(bf16[192,1792]{1,0:T(8,128)(2,1)S(1)} %collective-permute-done.refs_0_), channel_id=1, source_target_pairs={{0,8},{4,12},{8,0},{12,4},{16,24},{20,28},{24,16},{28,20},{1,9},{5... | collective-permute-start | bytes 2064392 | tf_op jit(solution)/shard_map/ppermute | solution.py:723
  75.7 18.9 %collective-permute-start.8 = (bf16[768,1792]{1,0:T(8,128)(2,1)S(1)}, bf16[768,1792]{1,0:T(8,128)(2,1)S(1)}, u32[]{:S(2)}, u32[]{:S(2)}) collective-permute-start(bf16[768,1792]{1,0:T(8,128)(2,1)S(1)} %assemble.4.refs_1_.refs_4_.refs_10_), channel_id=1, source_target_pairs={{0,4},{4,0},{8,12},{12,8},{16,20},{20,16},{24,28},{28,24},{1,5},{5... | collective-permute-start | bytes 8257544 | tf_op jit(solution)/shard_map/ppermute | solution.py:723
  77.8 38.5 %collective-permute-start.9 = (bf16[192,2048]{1,0:T(8,128)(2,1)S(1)}, bf16[192,2048]{1,0:T(8,128)(2,1)S(1)}, u32[]{:S(2)}, u32[]{:S(2)}) collective-permute-start(bf16[192,2048]{1,0:T(8,128)(2,1)S(1)} %copy-done.21), channel_id=1, source_target_pairs={{2,0},{3,1},{0,2},{1,3},{6,4},{7,5},{4,6},{5,7},{10,8},{11,9},{8,1... | collective-permute-start | bytes 2359304 | tf_op jit(solution)/shard_map/ppermute | solution.py:716
  91.5 40.2 %collective-permute-start.7 = (bf16[192,1152]{1,0:T(8,128)(2,1)S(1)}, bf16[192,1152]{1,0:T(8,128)(2,1)S(1)}, u32[]{:S(2)}, u32[]{:S(2)}) collective-permute-start(bf16[192,1152]{1,0:T(8,128)(2,1)S(1)} %constant_dynamic-update-slice_fusion.refs_0_), channel_id=1, source_target_pairs={{0,8},{4,12},{8,0},{12,4},{16,24},{20,28},{24,16},{28,20},{1,9},{5... | collective-permute-start | bytes 1327112 | tf_op jit(solution)/shard_map/ppermute | solution.py:723
  93.1 43.6 %collective-permute-start.10 = (bf16[192,1152]{1,0:T(8,128)(2,1)S(1)}, bf16[192,1152]{1,0:T(8,128)(2,1)S(1)}, u32[]{:S(2)}, u32[]{:S(2)}) collective-permute-start(bf16[192,1152]{1,0:T(8,128)(2,1)S(1)} %constant_dynamic-update-slice_fusion.refs_0_), channel_id=1, source_target_pairs={{0,16},{4,20},{8,24},{12,28},{16,0},{20,4},{24,8},{28,12},{1,17},{... | collective-permute-start | bytes 1327112 | tf_op jit(solution)/shard_map/ppermute | solution.py:723
  116.2 20.4 %collective-permute-start.12 = (bf16[192,2048]{1,0:T(8,128)(2,1)S(1)}, bf16[192,2048]{1,0:T(8,128)(2,1)S(1)}, u32[]{:S(2)}, u32[]{:S(2)}) collective-permute-start(bf16[192,2048]{1,0:T(8,128)(2,1)S(1)} %collective-permute-done.9.refs_0_), channel_id=1, source_target_pairs={{0,16},{4,20},{8,24},{12,28},{16,0},{20,4},{24,8},{28,12},{1,17},{... | collective-permute-start | bytes 2359304 | tf_op jit(solution)/shard_map/ppermute | solution.py:723
  147.2 47.7 %collective-permute-start.13 = (bf16[768,1152]{1,0:T(8,128)(2,1)S(1)}, bf16[768,1152]{1,0:T(8,128)(2,1)S(1)}, u32[]{:S(2)}, u32[]{:S(2)}) collective-permute-start(bf16[768,1152]{1,0:T(8,128)(2,1)S(1)} %assemble.5.refs_4_.refs_2_.refs_6_), channel_id=1, source_target_pairs={{0,4},{4,0},{8,12},{12,8},{16,20},{20,16},{24,28},{28,24},{1,5},{5... | collective-permute-start | bytes 5308424 | tf_op jit(solution)/shard_map/ppermute | solution.py:723
  147.3 20.4 %collective-permute-start.16 = (bf16[192,2048]{1,0:T(8,128)(2,1)S(1)}, bf16[192,2048]{1,0:T(8,128)(2,1)S(1)}, u32[]{:S(2)}, u32[]{:S(2)}) collective-permute-start(bf16[192,2048]{1,0:T(8,128)(2,1)S(1)} %collective-permute-done.9.refs_0_), channel_id=1, source_target_pairs={{0,8},{4,12},{8,0},{12,4},{16,24},{20,28},{24,16},{28,20},{1,9},{5... | collective-permute-start | bytes 2359304 | tf_op jit(solution)/shard_map/ppermute | solution.py:723
  148.9 35.3 %collective-permute-start.17 = (bf16[192,2048]{1,0:T(8,128)(2,1)S(1)}, bf16[192,2048]{1,0:T(8,128)(2,1)S(1)}, u32[]{:S(2)}, u32[]{:S(2)}) collective-permute-start(bf16[192,2048]{1,0:T(8,128)(2,1)S(1)} %collective-permute-done.12.refs_1_), channel_id=1, source_target_pairs={{0,8},{4,12},{8,0},{12,4},{16,24},{20,28},{24,16},{28,20},{1,9},{5... | collective-permute-start | bytes 2359304 | tf_op jit(solution)/shard_map/ppermute | solution.py:723
  149.4 37.0 %collective-permute-start.14 = (bf16[1024,384]{1,0:T(8,128)(2,1)S(1)}, bf16[1024,384]{1,0:T(8,128)(2,1)S(1)}, u32[]{:S(2)}, u32[]{:S(2)}) collective-permute-start(bf16[1024,384]{1,0:T(8,128)(2,1)S(1)} %copy-done.53), channel_id=1, source_target_pairs={{1,0},{0,1},{3,2},{2,3},{5,4},{4,5},{7,6},{6,7},{9,8},{8,9},{11,10... | collective-permute-start | bytes 2359304 | tf_op jit(solution)/shard_map/ppermute | solution.py:716
  149.4 44.6 %collective-permute-start.15 = (bf16[1024,384]{1,0:T(8,128)(2,1)S(1)}, bf16[1024,384]{1,0:T(8,128)(2,1)S(1)}, u32[]{:S(2)}, u32[]{:S(2)}) collective-permute-start(bf16[1024,384]{1,0:T(8,128)(2,1)S(1)} %copy-done.54), channel_id=1, source_target_pairs={{1,0},{0,1},{3,2},{2,3},{5,4},{4,5},{7,6},{6,7},{9,8},{8,9},{11,10... | collective-permute-start | bytes 2359304 | tf_op jit(solution)/shard_map/ppermute | solution.py:716
  167.7 41.7 %collective-permute-start.18 = (bf16[192,1024]{1,0:T(8,128)(2,1)S(1)}, bf16[192,1024]{1,0:T(8,128)(2,1)S(1)}, u32[]{:S(2)}, u32[]{:S(2)}) collective-permute-start(bf16[192,1024]{1,0:T(8,128)(2,1)S(1)} %copy-done.36), channel_id=1, source_target_pairs={{2,0},{3,1},{0,2},{1,3},{6,4},{7,5},{4,6},{5,7},{10,8},{11,9},{8,1... | collective-permute-start | bytes 1179656 | tf_op jit(solution)/shard_map/ppermute | solution.py:716
  186.4 83.6 %collective-permute-start.23 = (bf16[768,2048]{1,0:T(8,128)(2,1)}, bf16[768,2048]{1,0:T(8,128)(2,1)S(1)}, u32[]{:S(2)}, u32[]{:S(2)}) collective-permute-start(bf16[768,2048]{1,0:T(8,128)(2,1)} %assemble.6.refs_9_.refs_2_.refs_3_.refs_4_), channel_id=1, source_target_pairs={{0,4},{4,0},{8,12},{12,8},{16,20},{20,16},{24,28},{28,24},{1,5},{5... | collective-permute-start | bytes 9437192 | tf_op jit(solution)/shard_map/ppermute | solution.py:723
  209.4 18.0 %collective-permute-start.19 = (bf16[192,1024]{1,0:T(8,128)(2,1)S(1)}, bf16[192,1024]{1,0:T(8,128)(2,1)S(1)}, u32[]{:S(2)}, u32[]{:S(2)}) collective-permute-start(bf16[192,1024]{1,0:T(8,128)(2,1)S(1)} %collective-permute-done.18.refs_0_), channel_id=1, source_target_pairs={{0,8},{4,12},{8,0},{12,4},{16,24},{20,28},{24,16},{28,20},{1,9},{5... | collective-permute-start | bytes 1179656 | tf_op jit(solution)/shard_map/ppermute | solution.py:723
  246.2 69.2 %collective-permute-start.25 = (bf16[768,3072]{1,0:T(8,128)(2,1)}, bf16[768,3072]{1,0:T(8,128)(2,1)}, u32[]{:S(2)}, u32[]{:S(2)}) collective-permute-start(bf16[768,3072]{1,0:T(8,128)(2,1)} %get-tuple-element.226.refs_4_), channel_id=1, source_target_pairs={{0,4},{4,0},{8,12},{12,8},{16,20},{20,16},{24,28},{28,24},{1,5},{5... | collective-permute-start | bytes 14155784 | tf_op jit(solution)/shard_map/ppermute | solution.py:723
  247.8 18.4 %collective-permute-start.21 = (bf16[192,1024]{1,0:T(8,128)(2,1)S(1)}, bf16[192,1024]{1,0:T(8,128)(2,1)S(1)}, u32[]{:S(2)}, u32[]{:S(2)}) collective-permute-start(bf16[192,1024]{1,0:T(8,128)(2,1)S(1)} %collective-permute-done.19.refs_1_), channel_id=1, source_target_pairs={{0,16},{4,20},{8,24},{12,28},{16,0},{20,4},{24,8},{28,12},{1,17},{... | collective-permute-start | bytes 1179656 | tf_op jit(solution)/shard_map/ppermute | solution.py:723
  341.3 34.9 %collective-permute-start.26 = (bf16[768,3072]{1,0:T(8,128)(2,1)}, bf16[768,3072]{1,0:T(8,128)(2,1)S(1)}, u32[]{:S(2)}, u32[]{:S(2)}) collective-permute-start(bf16[768,3072]{1,0:T(8,128)(2,1)} %get-tuple-element.237.refs_8_), channel_id=1, source_target_pairs={{0,4},{4,0},{8,12},{12,8},{16,20},{20,16},{24,28},{28,24},{1,5},{5... | collective-permute-start | bytes 14155784 | tf_op jit(solution)/shard_map/ppermute | solution.py:723
  341.3 44.1 %collective-permute-start.24 = (bf16[512,1536]{1,0:T(8,128)(2,1)}, bf16[512,1536]{1,0:T(8,128)(2,1)}, u32[]{:S(2)}, u32[]{:S(2)}) collective-permute-start(bf16[512,1536]{1,0:T(8,128)(2,1)} %get-tuple-element.232), channel_id=1, source_target_pairs={{0,1},{1,0},{2,3},{3,2},{4,5},{5,4},{6,7},{7,6},{8,9},{9,8},{10,11... | collective-permute-start | bytes 4718600 | tf_op jit(solution)/shard_map/ppermute | solution.py:771
  341.3 28.6 %collective-permute-start.27 = (bf16[384,1536]{1,0:T(8,128)(2,1)}, bf16[384,1536]{1,0:T(8,128)(2,1)S(1)}, u32[]{:S(2)}, u32[]{:S(2)}) collective-permute-start(bf16[384,1536]{1,0:T(8,128)(2,1)} %get-tuple-element.235.refs_7_), channel_id=1, source_target_pairs={{0,16},{4,20},{8,24},{12,28},{16,0},{20,4},{24,8},{28,12},{1,17},{... | collective-permute-start | bytes 3538952 | tf_op jit(solution)/shard_map/ppermute | solution.py:723
  342.9 28.0 %collective-permute-start.28 = (bf16[384,1536]{1,0:T(8,128)(2,1)S(1)}, bf16[384,1536]{1,0:T(8,128)(2,1)S(1)}, u32[]{:S(2)}, u32[]{:S(2)}) collective-permute-start(bf16[384,1536]{1,0:T(8,128)(2,1)S(1)} %copy-done.52), channel_id=1, source_target_pairs={{0,8},{4,12},{8,0},{12,4},{16,24},{20,28},{24,16},{28,20},{1,9},{5... | collective-permute-start | bytes 3538952 | tf_op jit(solution)/shard_map/ppermute | solution.py:723
  413.2 55.6 %collective-permute-start.35 = (bf16[768,1536]{1,0:T(8,128)(2,1)}, bf16[768,1536]{1,0:T(8,128)(2,1)S(1)}, u32[]{:S(2)}, u32[]{:S(2)}) collective-permute-start(bf16[768,1536]{1,0:T(8,128)(2,1)} %get-tuple-element.252.refs_8_), channel_id=1, source_target_pairs={{0,4},{4,0},{8,12},{12,8},{16,20},{20,16},{24,28},{28,24},{1,5},{5... | collective-permute-start | bytes 7077896 | tf_op jit(solution)/shard_map/ppermute | solution.py:723
  413.3 28.4 %collective-permute-start.31 = (bf16[384,1536]{1,0:T(8,128)(2,1)S(1)}, bf16[384,1536]{1,0:T(8,128)(2,1)S(1)}, u32[]{:S(2)}, u32[]{:S(2)}) collective-permute-start(bf16[384,1536]{1,0:T(8,128)(2,1)S(1)} %copy-done.27), channel_id=1, source_target_pairs={{0,16},{4,20},{8,24},{12,28},{16,0},{20,4},{24,8},{28,12},{1,17},{... | collective-permute-start | bytes 3538952 | tf_op jit(solution)/shard_map/ppermute | solution.py:723
  414.2 29.2 %collective-permute-start.32 = (bf16[384,1536]{1,0:T(8,128)(2,1)S(1)}, bf16[384,1536]{1,0:T(8,128)(2,1)S(1)}, u32[]{:S(2)}, u32[]{:S(2)}) collective-permute-start(bf16[384,1536]{1,0:T(8,128)(2,1)S(1)} %copy-done.51), channel_id=1, source_target_pairs={{0,8},{4,12},{8,0},{12,4},{16,24},{20,28},{24,16},{28,20},{1,9},{5... | collective-permute-start | bytes 3538952 | tf_op jit(solution)/shard_map/ppermute | solution.py:723
  414.8 34.7 %collective-permute-start.30 = (bf16[512,768]{1,0:T(8,128)(2,1)}, bf16[512,768]{1,0:T(8,128)(2,1)S(1)}, u32[]{:S(2)}, u32[]{:S(2)}) collective-permute-start(bf16[512,768]{1,0:T(8,128)(2,1)} %get-tuple-element.247), channel_id=1, source_target_pairs={{1,0},{0,1},{3,2},{2,3},{5,4},{4,5},{7,6},{6,7},{9,8},{8,9},{11,10... | collective-permute-start | bytes 2359304 | tf_op jit(solution)/shard_map/ppermute | solution.py:716
  416.5 71.2 %collective-permute-start.61 = (bf16[192,1536]{1,0:T(8,128)(2,1)}, bf16[192,1536]{1,0:T(8,128)(2,1)}, u32[]{:S(2)}, u32[]{:S(2)}) collective-permute-start(bf16[192,1536]{1,0:T(8,128)(2,1)} %get-tuple-element.241.refs_8_), channel_id=1, source_target_pairs={{0,8},{4,12},{8,0},{12,4},{16,24},{20,28},{24,16},{28,20},{1,9},{5... | collective-permute-start | bytes 1769480 | tf_op jit(solution)/shard_map/ppermute | solution.py:723
  441.7 49.4 %collective-permute-start.29 = (bf16[512,1536]{1,0:T(8,128)(2,1)}, bf16[512,1536]{1,0:T(8,128)(2,1)}, u32[]{:S(2)}, u32[]{:S(2)}) collective-permute-start(bf16[512,1536]{1,0:T(8,128)(2,1)} %mlp_out.2.refs_6_), channel_id=1, source_target_pairs={{0,1},{1,0},{2,3},{3,2},{4,5},{5,4},{6,7},{7,6},{8,9},{9,8},{10,11... | collective-permute-start | bytes 4718600 | tf_op jit(solution)/shard_map/ppermute | solution.py:771
  448.9 25.6 %collective-permute-start.33 = (bf16[192,1536]{1,0:T(8,128)(2,1)}, bf16[192,1536]{1,0:T(8,128)(2,1)S(1)}, u32[]{:S(2)}, u32[]{:S(2)}) collective-permute-start(bf16[192,1536]{1,0:T(8,128)(2,1)} %get-tuple-element.256.refs_12_), channel_id=1, source_target_pairs={{0,8},{4,12},{8,0},{12,4},{16,24},{20,28},{24,16},{28,20},{1,9},{5... | collective-permute-start | bytes 1769480 | tf_op jit(solution)/shard_map/ppermute | solution.py:723
  449.5 25.0 %collective-permute-start.34 = (bf16[192,1536]{1,0:T(8,128)(2,1)}, bf16[192,1536]{1,0:T(8,128)(2,1)S(1)}, u32[]{:S(2)}, u32[]{:S(2)}) collective-permute-start(bf16[192,1536]{1,0:T(8,128)(2,1)} %get-tuple-element.262), channel_id=1, source_target_pairs={{0,16},{4,20},{8,24},{12,28},{16,0},{20,4},{24,8},{28,12},{1,17},{... | collective-permute-start | bytes 1769480 | tf_op jit(solution)/shard_map/ppermute | solution.py:723
  486.4 33.1 %collective-permute-start.41 = (bf16[768,1792]{1,0:T(8,128)(2,1)}, bf16[768,1792]{1,0:T(8,128)(2,1)S(1)}, u32[]{:S(2)}, u32[]{:S(2)}) collective-permute-start(bf16[768,1792]{1,0:T(8,128)(2,1)} %get-tuple-element.274.refs_12_), channel_id=1, source_target_pairs={{0,4},{4,0},{8,12},{12,8},{16,20},{20,16},{24,28},{28,24},{1,5},{5... | collective-permute-start | bytes 8257544 | tf_op jit(solution)/shard_map/ppermute | solution.py:723
  486.5 50.5 %collective-permute-start.62 = (bf16[192,1536]{1,0:T(8,128)(2,1)}, bf16[192,1536]{1,0:T(8,128)(2,1)S(1)}, u32[]{:S(2)}, u32[]{:S(2)}) collective-permute-start(bf16[192,1536]{1,0:T(8,128)(2,1)} %get-tuple-element.322), channel_id=1, source_target_pairs={{0,16},{4,20},{8,24},{12,28},{16,0},{20,4},{24,8},{28,12},{1,17},{... | collective-permute-start | bytes 1769480 | tf_op jit(solution)/shard_map/ppermute | solution.py:723
  490.2 24.9 %collective-permute-start.36 = (bf16[384,768]{1,0:T(8,128)(2,1)}, bf16[384,768]{1,0:T(8,128)(2,1)S(1)}, u32[]{:S(2)}, u32[]{:S(2)}) collective-permute-start(bf16[384,768]{1,0:T(8,128)(2,1)} %get-tuple-element.266.refs_7_), channel_id=1, source_target_pairs={{0,16},{4,20},{8,24},{12,28},{16,0},{20,4},{24,8},{28,12},{1,17},{... | collective-permute-start | bytes 1769480 | tf_op jit(solution)/shard_map/ppermute | solution.py:723
  491.0 24.0 %collective-permute-start.37 = (bf16[384,768]{1,0:T(8,128)(2,1)}, bf16[384,768]{1,0:T(8,128)(2,1)S(1)}, u32[]{:S(2)}, u32[]{:S(2)}) collective-permute-start(bf16[384,768]{1,0:T(8,128)(2,1)} %get-tuple-element.271), channel_id=1, source_target_pairs={{0,8},{4,12},{8,0},{12,4},{16,24},{20,28},{24,16},{28,20},{1,9},{5... | collective-permute-start | bytes 1769480 | tf_op jit(solution)/shard_map/ppermute | solution.py:723
  494.0 53.9 %collective-permute-start.40 = (bf16[192,3072]{1,0:T(8,128)(2,1)}, bf16[192,3072]{1,0:T(8,128)(2,1)}, u32[]{:S(2)}, u32[]{:S(2)}) collective-permute-start(bf16[192,3072]{1,0:T(8,128)(2,1)} %pad_maximum_fusion), channel_id=1, source_target_pairs={{0,2},{1,3},{2,0},{3,1},{4,6},{5,7},{6,4},{7,5},{8,10},{9,11},{10,... | collective-permute-start | bytes 3538952 | tf_op jit(solution)/shard_map/ppermute | solution.py:720
  537.0 41.5 %collective-permute-start.46 = (bf16[768,1792]{1,0:T(8,128)(2,1)}, bf16[768,1792]{1,0:T(8,128)(2,1)S(1)}, u32[]{:S(2)}, u32[]{:S(2)}) collective-permute-start(bf16[768,1792]{1,0:T(8,128)(2,1)} %get-tuple-element.290.refs_19_), channel_id=1, source_target_pairs={{0,4},{4,0},{8,12},{12,8},{16,20},{20,16},{24,28},{28,24},{1,5},{5... | collective-permute-start | bytes 8257544 | tf_op jit(solution)/shard_map/ppermute | solution.py:723
  538.5 55.0 %collective-permute-start.38 = (bf16[192,768]{1,0:T(8,128)(2,1)S(1)}, bf16[192,768]{1,0:T(8,128)(2,1)S(1)}, u32[]{:S(2)}, u32[]{:S(2)}) collective-permute-start(bf16[192,768]{1,0:T(8,128)(2,1)S(1)} %copy-done.43), channel_id=1, source_target_pairs={{0,8},{4,12},{8,0},{12,4},{16,24},{20,28},{24,16},{28,20},{1,9},{5... | collective-permute-start | bytes 884744 | tf_op jit(solution)/shard_map/ppermute | solution.py:723
  540.0 44.6 %collective-permute-start.44 = (bf16[384,896]{1,0:T(8,128)(2,1)}, bf16[384,896]{1,0:T(8,128)(2,1)S(1)}, u32[]{:S(2)}, u32[]{:S(2)}) collective-permute-start(bf16[384,896]{1,0:T(8,128)(2,1)} %get-tuple-element.288.refs_7_), channel_id=1, source_target_pairs={{0,16},{4,20},{8,24},{12,28},{16,0},{20,4},{24,8},{28,12},{1,17},{... | collective-permute-start | bytes 2064392 | tf_op jit(solution)/shard_map/ppermute | solution.py:723
  571.4 17.9 %collective-permute-start.45 = (bf16[384,896]{1,0:T(8,128)(2,1)S(1)}, bf16[384,896]{1,0:T(8,128)(2,1)}, u32[]{:S(2)}, u32[]{:S(2)}) collective-permute-start(bf16[384,896]{1,0:T(8,128)(2,1)S(1)} %copy-done.59), channel_id=1, source_target_pairs={{0,8},{4,12},{8,0},{12,4},{16,24},{20,28},{24,16},{28,20},{1,9},{5... | collective-permute-start | bytes 2064392 | tf_op jit(solution)/shard_map/ppermute | solution.py:723
  577.3 16.2 %collective-permute-start.39 = (bf16[192,768]{1,0:T(8,128)(2,1)S(1)}, bf16[192,768]{1,0:T(8,128)(2,1)S(1)}, u32[]{:S(2)}, u32[]{:S(2)}) collective-permute-start(bf16[192,768]{1,0:T(8,128)(2,1)S(1)} %copy-done.64), channel_id=1, source_target_pairs={{0,16},{4,20},{8,24},{12,28},{16,0},{20,4},{24,8},{28,12},{1,17},{... | collective-permute-start | bytes 884744 | tf_op jit(solution)/shard_map/ppermute | solution.py:723
  578.5 80.7 %collective-permute-start.47 = (bf16[512,1536]{1,0:T(8,128)(2,1)}, bf16[512,1536]{1,0:T(8,128)(2,1)S(1)}, u32[]{:S(2)}, u32[]{:S(2)}) collective-permute-start(bf16[512,1536]{1,0:T(8,128)(2,1)} %get-tuple-element.304), channel_id=1, source_target_pairs={{0,1},{1,0},{2,3},{3,2},{4,5},{5,4},{6,7},{7,6},{8,9},{9,8},{10,11... | collective-permute-start | bytes 4718600 | tf_op jit(solution)/shard_map/ppermute | solution.py:771
  584.6 47.6 %collective-permute-start.48 = (bf16[384,896]{1,0:T(8,128)(2,1)}, bf16[384,896]{1,0:T(8,128)(2,1)S(1)}, u32[]{:S(2)}, u32[]{:S(2)}) collective-permute-start(bf16[384,896]{1,0:T(8,128)(2,1)} %get-tuple-element.298.refs_8_), channel_id=1, source_target_pairs={{0,16},{4,20},{8,24},{12,28},{16,0},{20,4},{24,8},{28,12},{1,17},{... | collective-permute-start | bytes 2064392 | tf_op jit(solution)/shard_map/ppermute | solution.py:723
  593.0 31.5 %collective-permute-start.55 = (bf16[192,896]{1,0:T(8,128)(2,1)}, bf16[192,896]{1,0:T(8,128)(2,1)S(1)}, u32[]{:S(2)}, u32[]{:S(2)}) collective-permute-start(bf16[192,896]{1,0:T(8,128)(2,1)} %get-tuple-element.301.refs_7_), channel_id=1, source_target_pairs={{0,8},{4,12},{8,0},{12,4},{16,24},{20,28},{24,16},{28,20},{1,9},{5... | collective-permute-start | bytes 1032200 | tf_op jit(solution)/shard_map/ppermute | solution.py:723
  595.1 48.7 %collective-permute-start.59 = (bf16[192,384]{1,0:T(8,128)(2,1)S(1)}, bf16[192,384]{1,0:T(8,128)(2,1)S(1)}, u32[]{:S(2)}, u32[]{:S(2)}) collective-permute-start(bf16[192,384]{1,0:T(8,128)(2,1)S(1)} %get-tuple-element.361), channel_id=1, source_target_pairs={{0,1},{1,0},{2,3},{3,2},{4,5},{5,4},{6,7},{7,6},{8,9},{9,8},{10,11... | collective-permute-start | bytes 442376 | tf_op jit(solution)/shard_map/ppermute | solution.py:720
  632.2 25.4 %collective-permute-start.58 = (bf16[192,384]{1,0:T(8,128)(2,1)S(1)}, bf16[192,384]{1,0:T(8,128)(2,1)S(1)}, u32[]{:S(2)}, u32[]{:S(2)}) collective-permute-start(bf16[192,384]{1,0:T(8,128)(2,1)S(1)} %slice.86), channel_id=1, source_target_pairs={{0,2},{1,3},{2,0},{3,1},{4,6},{5,7},{6,4},{7,5},{8,10},{9,11},{10,... | collective-permute-start | bytes 442376 | tf_op jit(solution)/shard_map/ppermute | solution.py:720
  638.7 32.0 %collective-permute-start.57 = (bf16[192,1792]{1,0:T(8,128)(2,1)S(1)}, bf16[192,1792]{1,0:T(8,128)(2,1)S(1)}, u32[]{:S(2)}, u32[]{:S(2)}) collective-permute-start(bf16[192,1792]{1,0:T(8,128)(2,1)S(1)} %pad_maximum_fusion.1), channel_id=1, source_target_pairs={{0,2},{1,3},{2,0},{3,1},{4,6},{5,7},{6,4},{7,5},{8,10},{9,11},{10,... | collective-permute-start | bytes 2064392 | tf_op jit(solution)/shard_map/ppermute | solution.py:720
  643.8 23.2 %collective-permute-start.53 = (bf16[192,896]{1,0:T(8,128)(2,1)}, bf16[192,896]{1,0:T(8,128)(2,1)S(1)}, u32[]{:S(2)}, u32[]{:S(2)}) collective-permute-start(bf16[192,896]{1,0:T(8,128)(2,1)} %get-tuple-element.308.refs_6_), channel_id=1, source_target_pairs={{0,8},{4,12},{8,0},{12,4},{16,24},{20,28},{24,16},{28,20},{1,9},{5... | collective-permute-start | bytes 1032200 | tf_op jit(solution)/shard_map/ppermute | solution.py:723
  (82 other events, 868.6 us)

commit v3 on v2

--- a/solution.py
+++ b/solution.py
@@ -10,6 +10,7 @@
 HEAD = 64
 BLK = 256
 EPS = 1e-06
+STEP = 115 * 10 ** 9
 ROW, MEMBER, CORE, CHIP, PIECE = 0, 1, 2, 3, 4
 f32 = jnp.float32
 bf16 = jnp.bfloat16
@@ -33,6 +34,12 @@
 
 def shape(dims, dtype):
     return jax.ShapeDtypeStruct(dims, dtype)
+
+
+def spec(block, at, mode=None):
+    if block is None:
+        return pl.BlockSpec(memory_space=pl.ANY)
+    return pl.BlockSpec(block, at) if mode is None else pl.BlockSpec(block, at, pipeline_mode=mode)
 
 
 def run(name, body, where, grid, ins, outs, scratch=(), after=(), flops=0, vmem=56):
@@ -46,16 +53,84 @@
         grid_spec=pltpu.PrefetchScalarGridSpec(
             num_scalar_prefetch=1,
             grid=grid,
-            in_specs=[pl.BlockSpec(b, m) for _, b, m in ins]
-            + [pl.BlockSpec(memory_space=pl.ANY)] * extra,
-            out_specs=[pl.BlockSpec(b, m) for _, b, m in outs],
+            in_specs=[spec(*entry[1:]) for entry in ins] + [pl.BlockSpec(memory_space=pl.ANY)] * extra,
+            out_specs=[spec(*entry[1:]) for entry in outs],
             scratch_shapes=list(scratch),
         ),
-        out_shape=[s for s, _, _ in outs],
+        out_shape=[entry[0] for entry in outs],
         compiler_params=pltpu.CompilerParams(vmem_limit_bytes=vmem << 20),
-        cost_estimate=pl.CostEstimate(flops=int(flops) + 10 ** 9, bytes_accessed=1, transcendentals=0),
+        cost_estimate=pl.CostEstimate(flops=STEP, bytes_accessed=1, transcendentals=0),
         name=name,
-    )(where, *[a for a, _, _ in ins], *after)
+    )(where, *[entry[0] for entry in ins], *after)
+
+
+class Part:
+    def __init__(self, array, rows=None, row_at=None, cols=None, col_at=None):
+        self.array = array
+        self.rows = array.shape[0] if rows is None else rows
+        self.cols = array.shape[1] if cols is None else cols
+        self.row_at, self.col_at = row_at, col_at
+
+    def view(self, ref, w):
+        if self.row_at is None and self.col_at is None:
+            return ref
+        row = 0 if self.row_at is None else pl.multiple_of(self.row_at(w), self.rows)
+        col = 0 if self.col_at is None else pl.multiple_of(self.col_at(w), self.cols)
+        return ref.at[pl.ds(row, self.rows), pl.ds(col, self.cols)]
+
+
+def stream(name, body, where, parts, outs, scratch=(), after=()):
+    count, extra, made = len(parts), len(after), len(outs)
+    chunks = 16
+
+    def kernel(w, *refs):
+        sources = refs[:count]
+        targets = refs[count + extra:count + extra + made]
+        at = count + extra + made
+        held = refs[at:at + count]
+        ready = refs[at + count:at + count + made]
+        in_sems, out_sems = refs[at + count + made:at + count + made + 2]
+        rest = refs[at + count + made + 2:]
+        loads = []
+        for k, part in enumerate(parts):
+            copy = pltpu.make_async_copy(part.view(sources[k], w), held[k], in_sems.at[k])
+            copy.start()
+            loads.append(copy)
+        waited = set()
+        sent = []
+
+        def get(k):
+            if k not in waited:
+                loads[k].wait()
+                waited.add(k)
+            return held[k]
+
+        def put(k, row=None, rows=None, col=None, cols=None):
+            spot = (pl.ds(0, outs[k].shape[0]) if row is None else pl.ds(row, rows),
+                    pl.ds(0, outs[k].shape[1]) if col is None else pl.ds(col, cols))
+            copy = pltpu.make_async_copy(ready[k].at[spot], targets[k].at[spot], out_sems.at[k, len([1 for i, _ in sent if i == k])])
+            copy.start()
+            sent.append((k, copy))
+
+        body(w, get, ready, put, rest)
+        for _, copy in sent:
+            copy.wait()
+
+    return pl.pallas_call(
+        kernel,
+        grid_spec=pltpu.PrefetchScalarGridSpec(
+            num_scalar_prefetch=1, grid=(),
+            in_specs=[pl.BlockSpec(memory_space=pl.ANY)] * (count + extra),
+            out_specs=[pl.BlockSpec(memory_space=pl.ANY)] * made,
+            scratch_shapes=[pltpu.VMEM((p.rows, p.cols), p.array.dtype) for p in parts]
+            + [pltpu.VMEM(o.shape, o.dtype) for o in outs]
+            + [pltpu.SemaphoreType.DMA((count,)), pltpu.SemaphoreType.DMA((made, chunks))] + list(scratch),
+        ),
+        out_shape=list(outs),
+        compiler_params=pltpu.CompilerParams(vmem_limit_bytes=58 << 20),
+        cost_estimate=pl.CostEstimate(flops=STEP, bytes_accessed=1, transcendentals=0),
+        name=name,
+    )(where, *[p.array for p in parts], *after)
 
 
 def fixed(array):
@@ -67,9 +142,9 @@
 
 
 def halves(values, pieces, core):
-    count = values.shape[1] // pieces
-    even = jnp.concatenate([values[:, p * count:(p + 1) * count] for p in range(0, pieces, 2)], axis=1)
-    odd = jnp.concatenate([values[:, p * count:(p + 1) * count] for p in range(1, pieces, 2)], axis=1)
+    count = values.shape[0] // pieces
+    even = jnp.concatenate([values[p * count:(p + 1) * count] for p in range(0, pieces, 2)], axis=0)
+    odd = jnp.concatenate([values[p * count:(p + 1) * count] for p in range(1, pieces, 2)], axis=0)
     return jnp.where(core == 0, odd, even), jnp.where(core == 0, even, odd)
 
 
@@ -134,22 +209,20 @@
     ]
 
 
-def project_own(where, length, pieces, inputs, gain, weights, bias, after=()):
+def project_own(where, length, inputs, gain, weights, bias, after=()):
     model = inputs.shape[1]
     width, heads = weights[0].shape[1], weights[4].shape[1]
-    half = model // 2
 
     def body(w, ins, outs, scratch):
         x_ref, gain_ref, wq, wk, wv, wg, wf, b_ref = ins
-        a_ref, send_ref, keep_ref, inv_ref = outs[:4]
+        a_ref, inv_ref = outs[:2]
         x = x_ref[...].astype(f32)
         inverse = lax.rsqrt(jnp.mean(x * x, axis=1, keepdims=True) + EPS)
         a = low(x * inverse * gain_ref[...])
         a_ref[...] = a
         inv_ref[...] = inverse
-        send_ref[...], keep_ref[...] = halves(a, pieces, w[CORE])
         mixed = mm(a, jnp.concatenate([r[...] for r in (wq, wk, wv, wg, wf)], axis=1))
-        project_tail(pl.program_id(0), mixed, width, b_ref[...], outs[4:], scratch[0])
+        project_tail(pl.program_id(0), mixed, width, b_ref[...], outs[2:], scratch[0])
 
     blocks = length // TOK
     tokens = lambda i, w: (i, 0)
@@ -157,9 +230,7 @@
         "project_own", body, where, (blocks,),
         [(inputs, (TOK, model), lambda i, w: (w[ROW] * blocks + i, 0)), fixed(gain)]
         + [fixed(a) for a in weights] + [fixed(bias)],
-        [(shape((length, model), bf16), (TOK, model), tokens),
-         (shape((length, half), bf16), (TOK, half), tokens), (shape((length, half), bf16), (TOK, half), tokens),
-         (shape((length, 1), f32), (TOK, 1), tokens)]
+        [(shape((length, model), bf16), (TOK, model), tokens), (shape((length, 1), f32), (TOK, 1), tokens)]
         + project_outs(length, width, heads),
         [pltpu.VMEM((8, 128), f32)], after, 2 * length * model * (4 * width + heads),
     )
@@ -342,7 +413,7 @@
     )
 
 
-def close_attention(where, length, pieces, inputs, gated, out_own, out_mine, out_theirs, gain, after=()):
+def close_attention(where, length, inputs, gated, out_own, out_mine, out_theirs, gain, after=()):
     model = inputs.shape[1]
     half = model // 2
     width = out_own.shape[1]
@@ -350,7 +421,7 @@
     def body(w, ins, outs, scratch):
         x_ref, own_ref, m_ref, t_ref, gain_ref = ins[:5]
         z = jnp.concatenate([r[...] for r in ins[5:]], axis=1)
-        h_ref, a_ref, send_ref, keep_ref, inv_ref = outs
+        h_ref, a_ref, inv_ref = outs
         for ref, core in ((m_ref, w[CORE]), (t_ref, 1 - w[CORE])):
             at = pl.ds(pl.multiple_of(core * half, 128), half)
             own = own_ref[pl.ds(pl.multiple_of(core * half, 128), half), :]
@@ -361,118 +432,161 @@
         a = low(h * inverse * gain_ref[...])
         a_ref[...] = a
         inv_ref[...] = inverse
-        send_ref[...], keep_ref[...] = halves(a, pieces, w[CORE])
 
     blocks = length // TOK
     tokens = lambda i, w: (i, 0)
-    side = (shape((length, half), bf16), (TOK, half), tokens)
     return run(
         "close_attention", body, where, (blocks,),
         [(inputs, (TOK, model), lambda i, w: (w[ROW] * blocks + i, 0))]
         + [fixed(a) for a in (out_own, out_mine, out_theirs, gain)]
         + [(z, (TOK, width), tokens) for z in gated],
         [(shape((length, model), f32), (TOK, model), tokens), (shape((length, model), bf16), (TOK, model), tokens),
-         side, side, (shape((length, 1), f32), (TOK, 1), tokens)],
+         (shape((length, 1), f32), (TOK, 1), tokens)],
         (), after, 2 * length * model * width * len(gated),
     )
 
 
-def split_rows(where, length, pieces, array, after=()):
-    model = array.shape[1]
-    half = model // 2
-    blocks = length // BLK
-
-    def body(w, ins, outs, scratch):
-        outs[0][...], outs[1][...] = halves(ins[0][...], pieces, w[CORE])
-
-    side = (shape((length, half), bf16), (BLK, half), lambda i, w: (i, 0))
-    return run(
-        "split_rows", body, where, (blocks,),
-        [(array, (BLK, model), lambda i, w: (w[ROW] * blocks + i, 0))], [side, side], (), after,
-    )
-
-
-def feed_forward(where, normed, cotangent, weights, hidden, after=()):
+def once(array_or_shape, block, at):
+    return (array_or_shape, block, at, pl.Buffered(1))
+
+
+def feed_forward(where, normed, cotangent, weights, hidden, gain, group, pieces, before, final, after=()):
     length, model = normed.shape
     half = model // 2
+    share = length // group
     wide = BLK if hidden % BLK == 0 else hidden
     steps = hidden // wide
     own = len(weights) == 3
+    tokens = length // TOK
 
     def body(w, ins, outs, scratch):
-        a_ref, e_ref = ins[:2]
-        m_ref, du_ref, dw_ref = outs
-        if not own:
-            core = pl.ds(pl.multiple_of(w[CORE] * half, 128), half)
-            other = pl.ds(pl.multiple_of((1 - w[CORE]) * half, 128), half)
-        for t in range(length // TOK):
+        a_ref, e_ref, gain_ref = ins[:3]
+        blocks = ins[3:3 + (3 if own else 6)]
+        rest = ins[3 + len(blocks):]
+        back, out = scratch[:2]
+        kept = scratch[2:5]
+        step = pl.program_id(0)
+        core = pl.ds(pl.multiple_of(w[CORE] * half, 128), half)
+        other = pl.ds(pl.multiple_of((1 - w[CORE]) * half, 128), half)
+        copies = [pltpu.make_async_copy(r, scratch[5 + k], scratch[5 + len(rest)].at[k]) for k, r in enumerate(rest)]
+
+        @pl.when(step == 0)
+        def _():
+            for c in copies:
+                c.start()
+            back[...] = jnp.zeros_like(back)
+            out[...] = jnp.zeros_like(out)
+
+        for t in range(tokens):
             rows = pl.ds(t * TOK, TOK)
             if own:
-                gate, up = mm(a_ref[rows, :], ins[2][...]), mm(a_ref[rows, :], ins[3][...])
-                dm = mm(e_ref[rows, :], ins[4][...])
+                gate, up = mm(a_ref[rows, :], blocks[0][...]), mm(a_ref[rows, :], blocks[1][...])
+                dm = mm(e_ref[rows, :], blocks[2][...])
             else:
-                both = lambda ref, p: mm(ref[rows, core], ins[2 + p][...]) + mm(ref[rows, other], ins[5 + p][...])
+                both = lambda ref, p: mm(ref[rows, core], blocks[p][...]) + mm(ref[rows, other], blocks[3 + p][...])
                 gate, up, dm = both(a_ref, 0), both(a_ref, 1), both(e_ref, 2)
             sig = jax.nn.sigmoid(gate)
             act = gate * sig
-            m_ref[rows, :] = low(act * up)
-            dw_ref[rows, :] = low(dm * act)
-            du_ref[rows, :] = low(dm * up * (sig * (1.0 + gate * (1.0 - sig))))
-
+            values = (low(dm * up * (sig * (1.0 + gate * (1.0 - sig)))), low(dm * act), low(act * up))
+            for k, value in enumerate(values):
+                kept[k][rows, :] = value
+                if final:
+                    outs[k][rows, :] = value
+        du, dw, m = kept
+        if own:
+            back[...] += last(du[...], blocks[0][...]) + last(dw[...], blocks[1][...])
+            out[...] += last(m[...], blocks[2][...])
+        else:
+            for where_to, p in ((core, 0), (other, 3)):
+                back[:, where_to] += last(du[...], blocks[p][...]) + last(dw[...], blocks[p + 1][...])
+                out[:, where_to] += last(m[...], blocks[p + 2][...])
+        if not final:
+            for k, left in enumerate((a_ref, a_ref, e_ref)):
+                send, keep = halves(low(first(left[...], kept[k][...])), pieces, w[CORE])
+                outs[0][:, k * wide:(k + 1) * wide] = send
+                outs[1][:, k * wide:(k + 1) * wide] = keep
+
+        @pl.when(step == steps - 1)
+        def _():
+            for c in copies:
+                c.wait()
+            if rest:
+                back[...] += scratch[5][...].astype(f32)
+                out[...] += scratch[6][...].astype(f32)
+            if final:
+                for k in range(group):
+                    member = lax.rem(w[MEMBER] + (k + 1) % group, group)
+                    rows = pl.ds(pl.multiple_of(member * share, share), share)
+                    outs[3 + k][...] = low(back[rows, :])
+                    outs[3 + group + k][...] = low(out[rows, :])
+                outs[3 + 2 * group][...] = jnp.sum(back[...] * a_ref[...].astype(f32), axis=0, keepdims=True) / gain_ref[...]
+            else:
+                outs[2][...] = low(back[...])
+                outs[3][...] = low(out[...])
+
+    whole = lambda i, w: (0, 0)
+    column = lambda i, w: (0, i)
     if own:
-        parts = [(a, (model, wide), lambda i, w: (0, i)) for a in weights]
+        parts = [(a, (model, wide), column) for a in weights]
     else:
         gm, gt, dm, dt = weights
-        parts = [
-            (a, (half, wide), lambda i, w, p=p: (0, p * steps + i))
-            for a, p in ((gm, 0), (gm, 1), (dm, 0), (gt, 0), (gt, 1), (dt, 0))
-        ]
-    result = (shape((length, hidden), bf16), (length, wide), lambda i, w: (0, i))
+        parts = [(a, (half, wide), lambda i, w, p=p: (0, p * steps + i))
+                 for a, p in ((gm, 0), (gm, 1), (dm, 0), (gt, 0), (gt, 1), (dt, 0))]
+    row_sum = once(shape((length, model), bf16), (length, model), whole)
+    if final:
+        outs = [(shape((length, hidden), bf16), (length, wide), column)] * 3
+        outs += [once(shape((share, model), bf16), (share, model), whole)] * (2 * group)
+        outs += [fixed_out((1, model), f32)]
+    else:
+        side = (shape((half, 3 * hidden), bf16), (half, 3 * wide), column)
+        outs = [side, side, row_sum, row_sum]
     return run(
         "feed_forward", body, where, (steps,),
-        [fixed(normed), (cotangent, (length, model), lambda i, w: (w[ROW], 0))] + parts,
-        [result] * 3, (), after, 6 * length * model * hidden,
+        [once(normed, (length, model), whole), once(cotangent, (length, model), lambda i, w: (w[ROW], 0)), fixed(gain)] + parts
+        + [(a, None, None) for a in before],
+        outs,
+        [pltpu.VMEM((length, model), f32)] * 2 + [pltpu.VMEM((length, wide), bf16)] * 3
+        + [pltpu.VMEM((length, model), bf16) for _ in before]
+        + ([pltpu.SemaphoreType.DMA((len(before),))] if before else []),
+        after,
     )
 
 
-def weight_grads(name, where, sides, groups, rows_of=False, after=()):
-    length, half = sides[0][0].shape
+def weight_grads(name, where, lefts, groups, pieces, rows_of=False, row_of=(), mixed=0, after=()):
+    length = groups[0][1][0].shape[0] if not rows_of else lefts[0].shape[0]
+    half = lefts[0].shape[1] // 2
     widths = [sum(r.shape[1] for r in rights) for _, rights in groups]
     padded = [-(-n // 256) * 256 for n in widths]
-    several = len(groups) > 1
-    tall = half if several else half // 2
-    count = 2 * len(sides)
-
-    def body(w, ins, outs, scratch):
-        at = count
-        for k, (s, rights) in enumerate(groups):
-            for which in (0, 1):
-                @pl.when((pl.program_id(0) == (k if several else which)) & (pl.program_id(1) == which)
-                         if several else pl.program_id(0) == which)
-                def _(k=k, s=s, at=at, n=len(rights), which=which):
-                    right = [ins[at + c][...] for c in range(n)]
-                    value = first(ins[2 * s + which][...], right[0] if n == 1 else jnp.concatenate(right, axis=1))
-                    outs[which][:, :widths[k]] = low(value)
-                    if widths[k] < padded[k]:
-                        outs[which][:, widths[k]:] = jnp.zeros((tall, padded[k] - widths[k]), bf16)
-            at += len(rights)
-
-    pick = (lambda i, c, w: (w[MEMBER], 0)) if rows_of else (lambda i, c, w: (0, 0))
-    if several:
-        grid = (len(groups), 2)
-        left_at = [lambda i, c, w: (0, 0)] * 2
-        out_at = [lambda i, c, w: (0, i)] * 2
-    else:
-        grid = (2, 2)
-        left_at = [lambda i, c, w: (0, jnp.where(i == 0, c, 1)), lambda i, c, w: (0, jnp.where(i == 0, 0, c))]
-        out_at = [lambda i, c, w: (jnp.where(i == 0, c, 1), 0), lambda i, c, w: (jnp.where(i == 0, 0, c), 0)]
-    return run(
-        name, body, where, grid,
-        [(a, (length, tall), left_at[which]) for pair in sides for which, a in enumerate(pair)]
-        + [(r, (length, r.shape[1]), pick) for _, rights in groups for r in rights],
-        [(shape((half, sum(padded)), bf16), (tall, padded[0]), out_at[which]) for which in (0, 1)],
-        (), after, 4 * half * length * sum(padded),
-    )
+    parts, plan, loaded = [], [], {}
+    row_at = (lambda w: w[MEMBER] * length) if rows_of else None
+    for k, (s, rights) in enumerate(groups):
+        if s not in loaded:
+            loaded[s] = len(parts)
+            parts.append(Part(lefts[s], length, (lambda w: w[ROW] * length) if s in row_of else None))
+        at = []
+        for r in rights:
+            at.append(len(parts))
+            parts.append(Part(r, length, row_at, r.shape[1]))
+        plan.append((loaded[s], at, sum(padded[:k]), widths[k], padded[k]))
+
+    def body(w, get, ready, put, rest):
+        for k, (left, at, col, n, full) in enumerate(plan):
+            left = get(left)[...]
+            right = [get(k)[...] for k in at]
+            value = low(first(left, right[0] if len(right) == 1 else jnp.concatenate(right, axis=1)))
+            for which, part in enumerate(halves(value, pieces, w[CORE])):
+                if mixed:
+                    for b in range(n // mixed):
+                        spot = (b * len(plan) + k) * mixed
+                        ready[which][:, spot:spot + mixed] = part[:, b * mixed:(b + 1) * mixed]
+                        put(which, col=spot, cols=mixed)
+                    continue
+                ready[which][:, col:col + n] = part
+                if n < full:
+                    ready[which][:, col + n:col + full] = jnp.zeros((half, full - n), bf16)
+                put(which, col=col, cols=full)
+
+    return stream(name, body, where, parts, [shape((half, sum(padded)), bf16)] * 2, (), after)
 
 
 def fold(where, entries, after=()):
@@ -503,7 +617,7 @@
 
     def body(w, ins_, outs_, scratch):
         for k, out in enumerate(outs_):
-            out[...] = low(ins_[2 * k][...].astype(f32) + ins_[2 * k + 1][...].astype(f32))
+            out[...] = ins_[2 * k][...] + ins_[2 * k + 1][...]
 
     return run("fold", body, where, (pieces // 2, across), ins, outs, (), after, 10 ** 9)
 
@@ -526,14 +640,14 @@
     return pl.pallas_call(
         kernel,
         grid_spec=pltpu.PrefetchScalarGridSpec(
-            num_scalar_prefetch=1, grid=(),
+            num_scalar_prefetch=1, grid=(1,),
             in_specs=[pl.BlockSpec(memory_space=pl.ANY)] * (count + extra),
-            out_specs=pl.BlockSpec(memory_space=pl.ANY),
+            out_specs=pl.BlockSpec((count * rows, width), lambda i, w: (0, 0)),
             scratch_shapes=[pltpu.SemaphoreType.DMA((count,))],
         ),
         out_shape=shape((count * rows, width), bf16),
-        compiler_params=pltpu.CompilerParams(vmem_limit_bytes=4 << 20),
-        cost_estimate=pl.CostEstimate(flops=10 ** 9, bytes_accessed=1, transcendentals=0),
+        compiler_params=pltpu.CompilerParams(vmem_limit_bytes=56 << 20),
+        cost_estimate=pl.CostEstimate(flops=STEP, bytes_accessed=1, transcendentals=0),
         name="assemble",
     )(where, *pieces, *after)
 
@@ -541,73 +655,73 @@
 def back_rows(name, where, steps, group, share, own_terms, pair_terms, model, dtypes, adds=(), unit=None, after=()):
     half = model // 2
     count = len(steps)
-    turn = lambda m: sum(jnp.where(m == k, s, 0) for k, s in enumerate(steps))
-    member = lambda m, w: lax.rem(w[MEMBER] + turn(m), group)
-    side = lambda i, w: lax.rem(w[CORE] + i, 2)
-    ins = []
-
-    def put(array, block, at):
-        ins.append((array, block, at))
-        return len(ins) - 1
-
-    rows_at = lambda i, m, w: (member(m, w), 0)
-    own_plan = [
-        ([put(x, (share, x.shape[1]), rows_at) for x in xs],
-         [put(a, (half, a.shape[1]), lambda i, m, w: (side(i, w), 0)) for a in weights])
-        for xs, weights in own_terms
-    ]
-    known = {}
-    pair_plan = []
+    member = lambda w, k: lax.rem(w[MEMBER] + steps[k], group)
+    parts, xs_at, weights_at = [], {}, {}
+
+    def x_parts(xs):
+        for x in xs:
+            for k in range(count):
+                if (id(x), k) not in xs_at:
+                    xs_at[id(x), k] = len(parts)
+                    parts.append(Part(x, share, lambda w, k=k: member(w, k) * share))
+
+    def w_part(a):
+        if id(a) not in weights_at:
+            weights_at[id(a)] = len(parts)
+            parts.append(Part(a))
+
+    for xs, weights in own_terms:
+        x_parts(xs)
+        for a in weights:
+            w_part(a)
     for xs, mine, theirs, lo in pair_terms:
-        for a in (mine, theirs):
-            if id(a) not in known:
-                known[id(a)] = put(a, a.shape, lambda i, m, w: (0, 0))
-        pair_plan.append(([put(x, (share, x.shape[1]), rows_at) for x in xs],
-                          known[id(mine)], known[id(theirs)], lo, sum(x.shape[1] for x in xs)))
-    first_add = len(ins)
+        x_parts(xs)
+        w_part(mine)
+    for xs, mine, theirs, lo in pair_terms:
+        w_part(theirs)
+    add_at = len(parts)
     for a, kind in adds:
-        ins.append((a, (share, half), (lambda i, m, w: (w[MEMBER], side(i, w))) if kind == "row"
-                    else (lambda i, m, w: (0, side(i, w)))))
+        parts.append(Part(a, share, (lambda w: w[MEMBER] * share) if kind == "row" else None))
+    unit_at = len(parts)
     if unit is not None:
-        values, base, inverse = unit
-        ins.append((values, (share, half), lambda i, m, w: (w[ROW] * base + member(m, w), side(i, w))))
-        ins.append((inverse, (share, 1), rows_at))
-
-    def body(w, ins_, outs, scratch):
-        wide = lambda refs: ins_[refs[0]][...] if len(refs) == 1 else jnp.concatenate([ins_[r][...] for r in refs], axis=1)
-        at = pl.program_id(1)
-        total = 0.0
-        for xs, weights in own_plan:
-            total = total + last(wide(xs), wide(weights))
-        scratch[0][...] = total
+        for k in range(count):
+            parts.append(Part(unit[0], share, lambda w, k=k: member(w, k) * share))
+        parts.append(Part(unit[1]))
+
+    def body(w, get, ready, put, rest):
+        wide = lambda xs, k: (get(xs_at[id(xs[0]), k])[...] if len(xs) == 1 else
+                              jnp.concatenate([get(xs_at[id(x), k])[...] for x in xs], axis=1))
         for which in (0, 1):
-            @pl.when(pl.program_id(0) == which)
-            def _():
-                part = 0.0
-                for xs, mine, theirs, lo, n in pair_plan:
-                    part = part + last(wide(xs), ins_[(mine, theirs)[which]][:, lo:lo + n])
-                scratch[0][...] += part
-        if unit is not None:
-            u = ins_[-2][...].astype(f32) * ins_[-1][...]
-            gained = jnp.sum(scratch[0][...] * u, axis=0, keepdims=True)
-            outs[count][...] = jnp.where(at == 0, 0.0, outs[count][...]) + gained
-        for k in range(count):
-            @pl.when(at == k)
-            def _():
-                total = scratch[0][...]
+            core = lax.rem(w[CORE] + which, 2)
+            at = pl.multiple_of(core * half, 128)
+            for k in range(count):
+                total = 0.0
+                for xs, weights in own_terms:
+                    rows = [get(weights_at[id(a)])[pl.ds(at, half), :] for a in weights]
+                    total = total + last(wide(xs, k), rows[0] if len(rows) == 1 else jnp.concatenate(rows, axis=1))
+                for xs, mine, theirs, lo in pair_terms:
+                    ref = get(weights_at[id((mine, theirs)[which])])
+                    total = total + last(wide(xs, k), ref[:, lo:lo + sum(x.shape[1] for x in xs)])
+                if unit is not None:
+                    u = get(unit_at + k)[:, pl.ds(at, half)].astype(f32)
+                    gained = jnp.sum(total * u, axis=0, keepdims=True) / get(unit_at + count)[:, pl.ds(at, half)]
+                    gain = ready[count]
+                    gain[:, pl.ds(at, half)] = gained if k == 0 else gain[:, pl.ds(at, half)] + gained
                 if k == count - 1:
                     for a in range(len(adds)):
-                        total = total + ins_[first_add + a][...].astype(f32)
-                outs[k][...] = total.astype(dtypes[k])
-
-    outs = [(shape((share, model), d), (share, half), lambda i, m, w: (0, side(i, w))) for d in dtypes]
+                        total = total + get(add_at + a)[:, pl.ds(at, half)].astype(f32)
+                ready[k][:, pl.ds(at, half)] = total.astype(dtypes[k])
+                put(k, col=at, cols=half)
+        if unit is not None:
+            put(count)
+
+    outs = [shape((share, model), d) for d in dtypes]
     if unit is not None:
-        outs.append((shape((1, model), f32), (1, half), lambda i, m, w: (0, side(i, w))))
-    flops = 2 * share * model * count * sum(x.shape[1] for t in tuple(own_terms) + tuple(pair_terms) for x in t[0])
-    return run(name, body, where, (2, count), ins, outs, [pltpu.VMEM((share, half), f32)], after, flops)
-
-
-def close_feed_forward(where, share, group, pieces, part, got, hidden_row, inverse, gain, cotangent,
+        outs.append(shape((1, model), f32))
+    return stream(name, body, where, parts, outs, (), after)
+
+
+def close_feed_forward(where, share, group, part, got, hidden_row, inverse, gain, cotangent,
                        out_own, out_mine, out_theirs, after=()):
     model = part.shape[1]
     half = model // 2
@@ -617,8 +731,8 @@
 
     def body(w, ins, outs, scratch):
         p_ref, h_ref, i_ref, gain_ref, e_ref, own_ref, m_ref, t_ref = ins[:8]
-        dh_ref, send_ref, keep_ref, mine_out, peer_out = outs
-        total = p_ref[...]
+        dh_ref, low_ref, mine_out, peer_out = outs
+        total = p_ref[...].astype(f32)
         for r in ins[8:]:
             total = total + r[...].astype(f32)
         unit = h_ref[...] * i_ref[...]
@@ -626,10 +740,9 @@
         dh = e_ref[...].astype(f32) + i_ref[...] * (scaled - unit * jnp.mean(scaled * unit, axis=1, keepdims=True))
         dh_ref[...] = dh
         d = low(dh)
-        send_ref[...], keep_ref[...] = halves(d, pieces, w[CORE])
-        scratch[0][...] = d
+        low_ref[...] = d
         dz = 0.0
-        for d_half, ref, core in zip(core_halves(scratch[0], w, half), (m_ref, t_ref), (w[CORE], 1 - w[CORE])):
+        for d_half, ref, core in zip(core_halves(low_ref, w, half), (m_ref, t_ref), (w[CORE], 1 - w[CORE])):
             own = own_ref[pl.ds(pl.multiple_of(core * half, 128), half), :]
             dz = dz + mm(d_half, jnp.concatenate([own, ref[...]], axis=1))
         mine_out[...] = low(dz[:, :own_slots])
@@ -637,16 +750,15 @@
 
     whole = lambda i, w: (0, 0)
     mine = lambda i, w: (w[MEMBER], 0)
-    side = (shape((share, half), bf16), (share, half), whole)
     return run(
         "close_feed_forward", body, where, (1,),
         [fixed(part), (hidden_row, (share, model), mine), (inverse, (share, 1), mine), fixed(gain),
          (cotangent, (share, model), lambda i, w: (w[ROW] * group + w[MEMBER], 0)),
          fixed(out_own), fixed(out_mine), fixed(out_theirs)] + [fixed(a) for a in got],
-        [(shape((share, model), f32), (share, model), whole), side, side,
+        [(shape((share, model), f32), (share, model), whole), (shape((share, model), bf16), (share, model), whole),
          (shape((share, own_slots), bf16), (share, own_slots), whole),
          (shape((share, filled - own_slots), bf16), (share, filled - own_slots), whole)],
-        [pltpu.VMEM((share, model), bf16)], after, 2 * share * model * filled,
+        (), after, 2 * share * model * filled,
     )
 
 
@@ -658,7 +770,7 @@
 
     def body(w, ins, outs, scratch):
         p_ref, x_ref, i_ref, gain_ref, dh_ref = ins[:5]
-        total = p_ref[...]
+        total = p_ref[...].astype(f32)
         for r in ins[5:]:
             total = total + r[...].astype(f32)
         unit = x_ref[...].astype(f32) * i_ref[...]
@@ -721,13 +833,6 @@
 
     def swap(self, value, bit):
         return lax.ppermute(value, "dp", [(i, i ^ bit) for i in range(self.dp)])
-
-    def sum_rest(self, value):
-        for bit in self.bits[1:]:
-            value = value + self.swap(value, bit)
-        for bit in [1 << b for b in range(self.tensor.bit_length() - 1)]:
-            value = value + lax.ppermute(value, "tensor", [(i, i ^ bit) for i in range(self.tensor)])
-        return value
 
 
 class Chain:
@@ -837,10 +942,10 @@
     attn_piece = go(collect, [w_query, w_key, w_value, w_outgate, w_forget], pieces, 256)
     attn_got = [here.fetch(attn_piece, 0, j) for j in turns]
     bias_got = [here.fetch(forget_bias, 0, j) for j in turns]
-    own = go(project_own, length, pieces, inputs, gain_attn,
+    own = go(project_own, length, inputs, gain_attn,
              [w_query, w_key, w_value, w_outgate, w_forget], forget_bias[None])
-    normed, norm_send, norm_keep, inverse_attn = own[:4]
-    mixed = {0: own[4:]}
+    normed, inverse_attn = own[:2]
+    mixed = {0: own[2:]}
     gated = {}
     logs = {}
 
@@ -851,15 +956,18 @@
         for s in range(1, group):
             gated[s, j] = here.fetch(z, s, 0)
 
+    def wait_gated(j):
+        arrived = go.sync(*[gated[s, j] for s in range(1, group)])
+        for s in range(1, group):
+            gated[s, j] = arrived[s - 1]
+
     attend(0)
     arrived = go.sync(*attn_got, *bias_got)
     attn_got, bias_got = arrived[:rows - 1], arrived[rows - 1:]
     attn_gather = [Gather(p, False) for p in attn_got]
     out_piece = go(collect, [w_out], pieces)
     out_got = [here.fetch(out_piece, 0, j) for j in turns]
-    gate_piece = go(collect, [w_gate, w_up], pieces)
-    gate_got = [here.fetch(gate_piece, 0, j) for j in turns]
-    cot_sides = go(split_rows, length, pieces, cotangent)
+    wait_gated(0)
     for gather in attn_gather:
         gather.hop()
     out_got = go.sync(*out_got)
@@ -868,58 +976,57 @@
     attn_w = [gather.close() for gather in attn_gather]
     out_peers = go.sync(*out_peers)
     out_gather = Gather(jnp.concatenate([*out_got, *out_peers], axis=1), True)
+    gate_piece = go(collect, [w_gate, w_up], pieces)
+    gate_got = [here.fetch(gate_piece, 0, j) for j in turns]
     for j in turns:
         mixed[j] = go(project_other, normed, *attn_w[j - 1], width, heads, bias_got[j - 1][None])
-    down_piece = go(collect, [w_down], pieces)
+    out_gather.hop()
+    for j in turns:
+        attend(j)
+    out_mine, out_theirs = out_gather.close()
     gate_got = go.sync(*gate_got)
     gate_gather = [Gather(p, False) for p in gate_got]
     for j in turns:
-        attend(j)
+        wait_gated(j)
+    down_piece = go(collect, [w_down], pieces)
     down_got = [here.fetch(down_piece, 0, j) for j in turns]
-    out_gather.hop()
+    out_theirs = go.sync(out_theirs)[0]
     for gather in gate_gather:
         gather.hop()
-    out_mine, out_theirs = out_gather.close()
-    gate_w = [gather.close() for gather in gate_gather]
-    hidden_row, mlp_normed, mlp_send, mlp_keep, inverse_mlp = go(
-        close_attention, length, pieces, inputs, [gated[slot] for slot in slots], w_out, out_mine, out_theirs, gain_mlp
+    hidden_row, mlp_normed, inverse_mlp = go(
+        close_attention, length, inputs, [gated[slot] for slot in slots], w_out, out_mine, out_theirs, gain_mlp
     )
     down_got = go.sync(*down_got)
     down_gather = [Gather(p, True) for p in down_got]
 
-    ffn = {0: go(feed_forward, mlp_normed, cotangent, [w_gate, w_up, w_down], hidden)}
+    def ffn(weights, before, final):
+        return go(feed_forward, mlp_normed, cotangent, weights, hidden, gain_mlp, group, pieces, before, final)
+
+    wide = BLK if hidden % BLK == 0 else hidden
+    mlp_sums = {}
+    send, keep, *carried = ffn([w_gate, w_up, w_down], [], False)
+    gate_w = [gather.close() for gather in gate_gather]
     for gather in down_gather:
         gather.hop()
-
-    def mlp_grads(j):
-        m, du, dw = ffn[j]
-        sides = [(mlp_send, mlp_keep), cot_sides]
-        send, keep = go(lambda w, after: weight_grads(
-            "mlp_grads", w, sides, [(0, [du]), (0, [dw]), (1, [m])], after=after))
-        return Reduce(send, keep, both_ways)
-
-    mlp_sums = {0: mlp_grads(0)}
+    down_w = [gather.close() for gather in down_gather]
+    mlp_sums[0] = Reduce(send, keep, both_ways)
     mlp_w = {}
     for j in turns:
-        mlp_w[j] = gate_w[j - 1] + down_gather[j - 1].close()
-        gm, gt, dm, dt = mlp_w[j]
-        ffn[j] = go(feed_forward, mlp_normed, cotangent, [gm, gt, dm, dt], hidden)
+        mlp_w[j] = gate_w[j - 1] + down_w[j - 1]
+        if j < rows - 1:
+            send, keep, *carried = ffn(mlp_w[j], carried, False)
+            mlp_sums[j] = Reduce(send, keep, both_ways)
+    mlp_sums[0].hop()
+    du, dw, m, *made = ffn(mlp_w[rows - 1], carried, True)
     peers = list(range(1, group))
-    own_terms = [([ffn[0][1]], [w_gate]), ([ffn[0][2]], [w_up])]
-    pair_terms = [([ffn[j][1], ffn[j][2]], *mlp_w[j][:2], 0) for j in turns]
-    made = go(lambda w, after: back_rows(
-        "mlp_back", w, peers + [0], group, share, own_terms, pair_terms, model, [bf16] * len(peers) + [f32],
-        (), (hidden_row, 0, inverse_mlp), after))
-    part, gain_mlp_part = made[-2:]
+    part, out_part_own, gain_mlp_part = made[group - 1], made[2 * group - 1], made[2 * group]
+    out_send = made[group:2 * group - 1]
     got = [to_member(v, s) for v, s in zip(made, peers)]
     mlp_sums[0].hop()
-    for j in turns:
-        mlp_sums[j] = mlp_grads(j)
-    mlp_sums[0].hop()
-    for j in turns:
-        mlp_sums[j].hop()
-    dh, dh_send, dh_keep, dz_mine, dz_peers = go(
-        close_feed_forward, share, group, pieces, part, got, hidden_row, inverse_mlp, gain_mlp, cotangent,
+    mlp_sums[rows - 1] = Reduce(*go(lambda w, after: weight_grads(
+        "mlp_grads", w, [mlp_normed, cotangent], [(0, [du]), (0, [dw]), (1, [m])], pieces, row_of=(1,), mixed=wide, after=after)), both_ways)
+    dh, dh_low, dz_mine, dz_peers = go(
+        close_feed_forward, share, group, part, got, hidden_row, inverse_mlp, gain_mlp, cotangent,
         w_out, out_mine, out_theirs,
     )
     dz_parts = [dz_mine]
@@ -927,19 +1034,12 @@
     for s in peers:
         lo = (group - s - 1) * own_slots
         dz_parts.append(here.fetch(dz_peers if group == 2 else dz_peers[:, lo:lo + own_slots], s, 0))
-
-    def mlp_out(steps, dtypes, adds):
-        own_terms = [([ffn[0][0]], [w_down])]
-        pair_terms = [([ffn[j][0]], *mlp_w[j][2:], 0) for j in turns]
-        return go(lambda w, after: back_rows(
-            "mlp_out", w, steps, group, share, own_terms, pair_terms, model, dtypes, adds, None, after))
-
-    out_send = mlp_out(peers, [bf16] * len(peers), ())
-    out_sum = Reduce(*go(lambda w, after: weight_grads(
-        "out_grads", w, [(dh_send, dh_keep)], [(0, [gated[slot] for slot in slots])], True, after)), both_ways)
+    mlp_sums[0].wait()
+    mlp_own = mlp_sums[0].close()
     for j in turns:
         mlp_sums[j].hop()
-    mlp_own = mlp_sums[0].close()
+    out_sum = Reduce(*go(lambda w, after: weight_grads(
+        "out_grads", w, [dh_low], [(0, [gated[slot] for slot in slots])], pieces, True, after=after)), both_ways[:1])
 
     back = {}
     attn_sums = {}
@@ -952,59 +1052,90 @@
             parts = [(a[:, o * per_step:(o + 1) * per_step], 0) for a, o in parts]
         back[j] = go(attend_backward, q, k, v, g, gated[0, j], parts, logs[j], ccol, forget, scol, srow)
 
-    def attn_grads(j):
+    def attn_grads(j, orders):
         attn_sums[j] = Reduce(*go(lambda w, after: weight_grads(
-            "attn_grads", w, [(norm_send, norm_keep)], [(0, back[j][:5])], False, after)), both_ways)
-
-    dz_parts[1:] = go.sync(*dz_parts[1:])
+            "attn_grads", w, [normed], [(0, back[j][:5])], pieces, after=after)), orders)
+
+    arrived = go.sync(*dz_parts[1:], *out_send)
+    dz_parts[1:], out_send = arrived[:group - 1], arrived[group - 1:]
     out_got = [to_member(v, s) for v, s in zip(out_send, peers)]
     for j in turns:
         attend_back(j)
+        attn_grads(j, both_ways)
+    for j in turns:
+        mlp_sums[j].hop()
     out_sum.hop()
+    out_got = go.sync(*out_got)
+    for j in turns:
+        attn_sums[j].hop()
     for j in turns:
         mlp_sums[j].wait()
     mlp_other = [here.deliver(low(mlp_sums[j].close()), 0, j) for j in turns]
-    for j in turns:
-        attn_grads(j)
-    out_got = go.sync(*out_got)
     attend_back(0)
     out_sum.hop()
     for j in turns:
         attn_sums[j].hop()
-    attn_grads(0)
+    attn_grads(0, both_ways)
     mlp_other = go.sync(*mlp_other)
+    for j in turns:
+        attn_sums[j].wait()
+    attn_other = [here.deliver(low(attn_sums[j].close()), 0, j) for j in turns]
+    out_sum.wait()
+    out_part = out_sum.close().reshape(-1, group, rows, width)
+    out_turned = [here.deliver(low(out_part[:, :, j]).reshape(-1, group * width), 0, j) for j in turns]
     own_terms = [(back[0][:5], [w_query, w_key, w_value, w_outgate, w_forget])]
     pair_terms = [(back[j][:5], *attn_w[j - 1], 0) for j in turns]
-    made = go(lambda w, after: back_rows(
-        "attn_back", w, peers + [0], group, share, own_terms, pair_terms, model, [bf16] * len(peers) + [f32],
-        (), (inputs, group, inverse_attn), after))
-    part, gain_attn_part = made[-2:]
+
+    def attn_back(name, steps):
+        return go(lambda w, after: back_rows(
+            name, w, steps, group, share, own_terms, pair_terms, model, [bf16] * len(steps), (), (normed, gain_attn), after))
+
+    made = attn_back("attn_back_send", peers)
     got = [to_member(v, s) for v, s in zip(made, peers)]
+    arrived = go.sync(*attn_other, *out_turned)
+    attn_other, out_turned = arrived[:rows - 1], arrived[rows - 1:]
+    attn_sums[0].hop()
+    part, gained = attn_back("attn_back_own", [0])
     bias_full = jnp.zeros((here.tensor, heads), f32)
     for j in range(rows):
         bias_full = lax.dynamic_update_slice(bias_full, back[j][5], (here.owner(here.at, 0, j), 0))
-    small = jnp.concatenate([gain_attn_part, gain_mlp_part, bias_full.reshape(1, -1)], axis=1)
-    small = go.sync(small + here.swap(small, 1))[0]
+    small = jnp.concatenate([made[-1] + gained, gain_mlp_part, bias_full.reshape(1, -1)], axis=1)
+    small_hops = [lambda v, b=b: here.swap(v, b) for b in [1] + here.bits] + [
+        lambda v, b=b: lax.ppermute(v, "tensor", [(i, i ^ b) for i in range(here.tensor)])
+        for b in [1 << k for k in range(here.tensor.bit_length() - 1)]]
+    flying = small_hops.pop(0)(small)
+
+    def small_step():
+        arrived = go.sync(flying)[0]
+        total = small + arrived
+        return total, (small_hops.pop(0)(total) if small_hops else None)
+
     attn_sums[0].hop()
-    small = small + here.swap(small, here.bits[0])
-    for j in turns:
-        attn_sums[j].hop()
-    small = go.sync(small)[0]
-    small = here.sum_rest(small)
-    out_sum.wait()
-    out_part = out_sum.close()
+    small, flying = small_step()
+    out_part = out_part[:, :, 0].reshape(-1, group * width) + sum(v.astype(f32) for v in out_turned)
     grad_out = out_part[:, :width]
-    out_rest = [here.deliver(low(out_part[:, (i + 1) * width:(i + 2) * width]), s, j) for i, (s, j) in enumerate(slots[1:])]
-    attn_other = [here.deliver(low(attn_sums[j].close()), 0, j) for j in turns]
-    output = mlp_out([0], [f32], [(hidden_row, "row")] + [(v, "own") for v in out_got])[0]
-    attn_sums[0].hop()
+    out_rest = [here.deliver(low(out_part[:, s * width:(s + 1) * width]), s, 0) for s in peers]
+    out_own, *arrived = go.sync(out_part_own, *out_got)
+    output = lax.dynamic_slice_in_dim(hidden_row, member * share, share, 0) + out_own.astype(f32)
+    for v in arrived:
+        output = output + v.astype(f32)
+    small, flying = small_step()
+    mlp_own, *mlp_other = go.sync(mlp_own, *mlp_other)
+    attn_sums[0].wait()
+    attn = attn_sums[0].close()
+    while flying is not None:
+        small, flying = small_step()
+    out_rest = go.sync(*out_rest)
     grad_inputs = go(close_block, share, group, part, got, inputs, inverse_attn, gain_attn, dh)
     mlp = mlp_own
     for v in mlp_other:
         mlp = mlp + v.astype(f32)
+
+    def columns(kind):
+        return jnp.concatenate([mlp[:, b + kind * wide:b + (kind + 1) * wide] for b in range(0, 3 * hidden, 3 * wide)], axis=1)
+
     for v in out_rest:
         grad_out = grad_out + v.astype(f32)
-    attn = attn_sums[0].close()
     for v in attn_other:
         attn = attn + v.astype(f32)
     bias_own = lax.dynamic_slice_in_dim(small[0, 2 * model:], here.at * heads, heads, 0)
@@ -1020,9 +1151,9 @@
         bias_own,
         grad_out,
         small[0, model:2 * model],
-        mlp[:, :hidden],
-        mlp[:, hidden:2 * hidden],
-        mlp[:, 2 * hidden:],
+        columns(0),
+        columns(1),
+        columns(2),
     )
 
 

time: 682 us -> 571 us (0.84)
  waiting for transfers between devices: 208 us -> 99.1 us
  Pallas kernels: 358 us -> 345 us
  other arithmetic: 8.15 us -> 20.1 us
    ppermute x44 -> x42, waiting for transfers between devices: 149 us -> 25.3 us  [swap(): return lax.ppermute(value, 'dp', [(i, i ^ bit) for i in range(self.dp)])]
    pallas_call x35 -> x25, Pallas kernels: 351 us -> 251 us  [run(): pl.pallas_call(kernel, grid_spec=pltpu.PrefetchScalarGridSpec(num_scalar_...]
    pallas_call x0 -> x6, Pallas kernels: none -> 79.1 us  [stream(): pl.pallas_call(kernel, grid_spec=pltpu.PrefetchScalarGridSpec(num_scalar_...]
    ppermute x3, waiting for transfers between devices: 0.01 us -> 11.6 us  [to_member(): lax.ppermute(value, 'tensor', [(i, i // group * group + (i % group + step...]
    pallas_call x4, Pallas kernels: 6.74 us -> 14.7 us  [assemble(): pl.pallas_call(kernel, grid_spec=pltpu.PrefetchScalarGridSpec(num_scalar_...]
    ppermute x9, waiting for transfers between devices: 30.8 us -> 38.3 us  [fetch(): return lax.ppermute(value, 'tensor', pairs)]
    unnamed x139 -> x92, local copies, waits for them, and re-layouts: 24.2 us -> 19.1 us
    ppermute x44 -> x42, starting transfers between devices: 39.2 us -> 34.9 us  [swap(): return lax.ppermute(value, 'dp', [(i, i ^ bit) for i in range(self.dp)])]
  transfers between devices with their start and end apart: 63 -> 60, of which waited for: 27 -> 16; matrix products, arithmetic and copies ran while one was open for 2% -> 6% of each run, Pallas kernels for 44% -> 60%
where the time goes in v3:
time: 571 us; the launch traced here: 562 us
  Pallas kernels  345 us (60%)
  waiting for transfers between devices  99.1 us (17%)
  starting transfers between devices  64.8 us (11%)
  local copies, waits for them, and re-layouts  30.9 us (5%)
  other arithmetic  20.1 us (4%)
    pallas_call x25, Pallas kernels, run(): pl.pallas_call(kernel, grid_spec=pltpu.PrefetchScalarGridSpec(num_scalar_...  251 us
    pallas_call x6, Pallas kernels, stream(): pl.pallas_call(kernel, grid_spec=pltpu.PrefetchScalarGridSpec(num_scalar_...  79.1 us
    ppermute x9, waiting for transfers between devices, fetch(): return lax.ppermute(value, 'tensor', pairs)  38.3 us
    ppermute x42, starting transfers between devices, swap(): return lax.ppermute(value, 'dp', [(i, i ^ bit) for i in range(self.dp)])  34.9 us
    ppermute x42, waiting for transfers between devices, swap(): return lax.ppermute(value, 'dp', [(i, i ^ bit) for i in range(self.dp)])  25.3 us
    ppermute x4, waiting for transfers between devices, deliver(): return lax.ppermute(value, 'tensor', pairs)  22.3 us
    unnamed x92, local copies, waits for them, and re-layouts  19.1 us
    ppermute x9, starting transfers between devices, fetch(): return lax.ppermute(value, 'tensor', pairs)  16.2 us
  transfers between devices with their start and end apart: 60, of which 16 were waited for; matrix products, arithmetic and copies ran while one was open for 6% of the time, Pallas kernels for 60%

profile of v3, /device:TPU:0, one launch (start us, length us, event | category | flops | bytes accessed | tf_op | source)
XLA Modules:
  0.0 561.8 jit_solution(16382762713027956186)
XLA Ops:
  3.0 2.8 collect.4.refs_8_
  5.8 4.0 collective-permute-start
  12.2 12.7 %project_own.1 = (bf16[1024,1536]{1,0:T(8,128)(2,1)}, f32[1024,1]{1,0:T(8,128)}, bf16[1024,384]{1,0:T(8,128)(2,1)}, bf16[1024,384]{1,0:T(8,128)(2,1)}, bf16[1024...) custom-call(s32[5]{0:T(128)} %stack.23.where_ref.w, ...), custom_call_target="tpu_custom_call" | custom-call | flops 115000000512 | bytes 1 | tf_op jit(solution)/shard_map/project_own/pallas_call | solution.py:51
  24.9 13.7 %attend_forward.2 = (bf16[1024,384]{1,0:T(8,128)(2,1)}, f32[3,2,1024]{2,1,0:T(2,128)}) custom-call(s32[5]{0:T(128)} %stack.23.where_ref.w, bf16[1024,384]{1,0:T(8,128)(2,1)} %get-tuple-element.192.refs_0_, bf16[1024,384]{1,0:T(8,128)(2,1)} %get-tuple-element.193.refs_1_, bf16[1024,384]{1,0:T(8,128)(2,1)} %get-tuple-element.194.refs_2_, ...), custom_call_target="tpu_custom_call" | custom-call | flops 115000000512 | bytes 1 | tf_op jit(solution)/shard_map/attend_forward/pallas_call | solution.py:51
  45.8 12.0 %collective-permute-done.4.refs_7_.refs_3_ = bf16[1024,384]{1,0:T(8,128)(2,1)S(1)} collective-permute-done((bf16[1024,384]{1,0:T(8,128)(2,1)}, bf16[1024,384]{1,0:T(8,128)(2,1)S(1)}, u32[]{:S(2)}, u32[]{:S(2)}) %collective-permute-start.4) | collective-permute-done | bytes 786464 | tf_op jit(solution)/shard_map/ppermute | solution.py:828
  59.4 2.6 collective-permute-start.2
  62.6 5.2 collective-permute-done.2
  70.0 3.9 collective-permute-done.7.refs_3_
  74.7 4.0 assemble.4.refs_2_.refs_1_.refs_15_
  82.3 2.7 collect.6.refs_4_
  85.0 2.6 collective-permute-start.14
  89.2 11.7 %project_other.1 = (bf16[1024,384]{1,0:T(8,128)(2,1)}, bf16[1024,384]{1,0:T(8,128)(2,1)}, bf16[1024,384]{1,0:T(8,128)(2,1)}, bf16[1024,384]{1,0:T(8,128)(2,1)}, ...) custom-call(s32[5]{0:T(128)} %stack.23.where_ref.w, ...), custom_call_target="tpu_custom_call" | custom-call | flops 115000000512 | bytes 1 | tf_op jit(solution)/shard_map/project_other/pallas_call | solution.py:51
  101.5 13.9 %attend_forward.3 = (bf16[1024,384]{1,0:T(8,128)(2,1)}, f32[3,2,1024]{2,1,0:T(2,128)}) custom-call(s32[5]{0:T(128)} %stack.23.where_ref.w, bf16[1024,384]{1,0:T(8,128)(2,1)} %get-tuple-element.216.refs_0_, bf16[1024,384]{1,0:T(8,128)(2,1)} %get-tuple-element.217.refs_1_, bf16[1024,384]{1,0:T(8,128)(2,1)} %get-tuple-element.218.refs_2_, ...), custom_call_target="tpu_custom_call" | custom-call | flops 115000000512 | bytes 1 | tf_op jit(solution)/shard_map/attend_forward/pallas_call | solution.py:51
  118.5 3.3 assemble.5.refs_1_.refs_2_.refs_6_
  124.1 15.1 %collective-permute-done.13.refs_8_.refs_4_ = bf16[1024,384]{1,0:T(8,128)(2,1)S(1)} collective-permute-done((bf16[1024,384]{1,0:T(8,128)(2,1)}, bf16[1024,384]{1,0:T(8,128)(2,1)S(1)}, u32[]{:S(2)}, u32[]{:S(2)}) %collective-permute-start.13) | collective-permute-done | bytes 786464 | tf_op jit(solution)/shard_map/ppermute | solution.py:828
  139.2 2.5 collect.7.refs_9_
  144.6 12.5 %close_attention.1 = (f32[1024,1536]{1,0:T(8,128)}, bf16[1024,1536]{1,0:T(8,128)(2,1)}, f32[1024,1]{1,0:T(8,128)}) custom-call(s32[5]{0:T(128)} %stack.23.where_ref.w, bf16[2048,1536]{1,0:T(8,128)(2,1)} %refs_1_.11, bf16[1536,384]{1,0:T(8,128)(2,1)} %refs_5_.7, bf16[768,1152]{1,0:T(8,128)(2,1)} %assemble.5.refs_1_.refs_2_.refs_6_, ...), custom_call_target="tpu_custom_call" | custom-call | flops 115000000512 | bytes 1 | tf_op jit(solution)/shard_map/close_attention/pallas_call | solution.py:51
  157.1 5.4 collective-permute-done.18.refs_0_
  165.0 40.0 %feed_forward.2 = (bf16[768,3072]{1,0:T(8,128)(2,1)}, bf16[768,3072]{1,0:T(8,128)(2,1)}, bf16[1024,1536]{1,0:T(8,128)(2,1)}, bf16[1024,1536]{1,0:T(8,128)(2,1)}) custom-call(s32[5]{0:T(128)} %stack.23.where_ref.w, bf16[1024,1536]{1,0:T(8,128)(2,1)} %get-tuple-element.236.refs_0_, bf16[2048,1536]{1,0:T(8,128)(2,1)} %refs_4_.6, ...), custom_call_target="tpu_custom_call" | custom-call | flops 115000000512 | bytes 1 | tf_op jit(solution)/shard_map/feed_forward/pallas_call | solution.py:51
  206.0 4.2 assemble.6.refs_4_.refs_3_
  212.3 7.6 %collective-permute-done.21.refs_3_ = bf16[192,1024]{1,0:T(8,128)(2,1)S(1)} collective-permute-done((bf16[192,1024]{1,0:T(8,128)(2,1)}, bf16[192,1024]{1,0:T(8,128)(2,1)S(1)}, u32[]{:S(2)}, u32[]{:S(2)}) %collective-permute-start.21) | collective-permute-done | bytes 393248 | tf_op jit(solution)/shard_map/ppermute | solution.py:835
  220.7 3.2 assemble.7.refs_8_.refs_5_
  226.7 7.0 %fold.10 = (bf16[384,1536]{1,0:T(8,128)(2,1)}, bf16[384,1536]{1,0:T(8,128)(2,1)}, bf16[384,1536]{1,0:T(8,128)(2,1)}, bf16[384,1536]{1,0:T(8,128)(2,1)}) custom-call(s32[5]{0:T(128)} %stack.23.where_ref.w, bf16[768,3072]{1,0:T(8,128)(2,1)} %get-tuple-element.251.refs_0_.refs_2_.refs_4_.refs_6_, bf16[768,3072]{1,0:T(8,128)(2,1)} %copy-done.24, ...), custom_call_target="tpu_custom_call" | custom-call | flops 115000000512 | bytes 1 | tf_op jit(solution)/shard_map/fold/pallas_call | solution.py:51
  236.5 34.1 %feed_forward.3 = (bf16[1024,1024]{1,0:T(8,128)(2,1)}, bf16[1024,1024]{1,0:T(8,128)(2,1)}, bf16[1024,1024]{1,0:T(8,128)(2,1)}, bf16[512,1536]{1,0:T(8,128)(2,1)}...) custom-call(s32[5]{0:T(128)} %stack.23.where_ref.w, ...), custom_call_target="tpu_custom_call" | custom-call | flops 115000000512 | bytes 1 | tf_op jit(solution)/shard_map/feed_forward/pallas_call | solution.py:51
  272.6 4.4 fold.11
  279.1 16.5 %mlp_grads.1 = (bf16[768,3072]{1,0:T(8,128)(2,1)}, bf16[768,3072]{1,0:T(8,128)(2,1)}) custom-call(s32[5]{0:T(128)} %stack.23.where_ref.w, bf16[1024,1536]{1,0:T(8,128)(2,1)} %get-tuple-element.236.refs_0_, bf16[1024,1024]{1,0:T(8,128)(2,1)} %get-tuple-element.257.refs_1_, bf16[1024,1024]{1,0:T(8,128)(2,1)} %get-tuple-element.258.refs_2_, ...), custom_call_target="tpu_custom_call" | custom-call | flops 115000000512 | bytes 1 | tf_op jit(solution)/shard_map/mlp_grads/pallas_call | solution.py:119
  295.7 11.6 %collective-permute-done.25.refs_8_ = bf16[512,1536]{1,0:T(8,128)(2,1)} collective-permute-done((bf16[512,1536]{1,0:T(8,128)(2,1)}, bf16[512,1536]{1,0:T(8,128)(2,1)}, u32[]{:S(2)}, u32[]{:S(2)}) %collective-permute-start.25) | collective-permute-done | bytes 1572896 | tf_op jit(solution)/shard_map/ppermute | solution.py:876
  307.3 11.1 %close_feed_forward.1 = (f32[512,1536]{1,0:T(8,128)}, bf16[512,1536]{1,0:T(8,128)(2,1)}, bf16[512,768]{1,0:T(8,128)(2,1)}, bf16[512,768]{1,0:T(8,128)(2,1)}) custom-call(s32[5]{0:T(128)} %stack.23.where_ref.w, bf16[512,1536]{1,0:T(8,128)(2,1)} %get-tuple-element.255.refs_0_, f32[1024,1536]{1,0:T(8,128)} %get-tuple-element.235.refs_1_, ...), custom_call_target="tpu_custom_call" | custom-call | flops 115000000512 | bytes 1 | tf_op jit(solution)/shard_map/close_feed_forward/pallas_call | solution.py:51
  324.3 6.9 %fold.12 = (bf16[384,1536]{1,0:T(8,128)(2,1)}, bf16[384,1536]{1,0:T(8,128)(2,1)}, bf16[384,1536]{1,0:T(8,128)(2,1)}, bf16[384,1536]{1,0:T(8,128)(2,1)}) custom-call(s32[5]{0:T(128)} %stack.23.where_ref.w, bf16[768,3072]{1,0:T(8,128)(2,1)} %get-tuple-element.269.refs_0_.refs_2_.refs_4_.refs_6_, bf16[768,3072]{1,0:T(8,128)(2,1)} %copy-done.23, ...), custom_call_target="tpu_custom_call" | custom-call | flops 115000000512 | bytes 1 | tf_op jit(solution)/shard_map/fold/pallas_call | solution.py:51
  332.1 7.6 %out_grads.1 = (bf16[768,1536]{1,0:T(8,128)(2,1)}, bf16[768,1536]{1,0:T(8,128)(2,1)}) custom-call(s32[5]{0:T(128)} %stack.23.where_ref.w, bf16[512,1536]{1,0:T(8,128)(2,1)} %get-tuple-element.268.refs_0_, bf16[1024,384]{1,0:T(8,128)(2,1)} %get-tuple-element.201.refs_5_.refs_1_.refs_4_, bf16[1024,384]{1,0:T(8,128)(2,1)} %get-tuple-element.226.refs_6_.refs_2_.refs_4_, ...), custom_call_target="tpu_custom_call" | custom-call | flops 115000000512 | bytes 1 | tf_op jit(solution)/shard_map/out_grads/pallas_call | solution.py:119
  342.7 18.8 %attend_backward.2 = (bf16[1024,384]{1,0:T(8,128)(2,1)}, bf16[1024,384]{1,0:T(8,128)(2,1)}, bf16[1024,384]{1,0:T(8,128)(2,1)}, bf16[1024,384]{1,0:T(8,128)(2,1)}...) custom-call(s32[5]{0:T(128)} %stack.23.where_ref.w, bf16[1024,384]{1,0:T(8,128)(2,1)} %get-tuple-element.216.refs_0_, ...), custom_call_target="tpu_custom_call" | custom-call | flops 115000000512 | bytes 1 | tf_op jit(solution)/shard_map/attend_backward/pallas_call | solution.py:51
  361.5 12.2 %attn_grads.2 = (bf16[768,1792]{1,0:T(8,128)(2,1)}, bf16[768,1792]{1,0:T(8,128)(2,1)}) custom-call(s32[5]{0:T(128)} %stack.23.where_ref.w, bf16[1024,1536]{1,0:T(8,128)(2,1)} %get-tuple-element.211.refs_0_.refs_17_, bf16[1024,384]{1,0:T(8,128)(2,1)} %get-tuple-element.283.refs_1_.refs_10_, bf16[1024,384]{1,0:T(8,128)(2,1)} %get-tuple-element.284.refs_2_.refs_11_, ...), custom_call_target="tpu_custom_call" | custom-call | flops 115000000512 | bytes 1 | tf_op jit(solution)/shard_map/attn_grads/pallas_call | solution.py:119
  373.9 4.3 fold.13
  380.2 5.1 fold.14
  386.3 4.7 fold.15
  401.4 18.5 %attend_backward.3 = (bf16[1024,384]{1,0:T(8,128)(2,1)}, bf16[1024,384]{1,0:T(8,128)(2,1)}, bf16[1024,384]{1,0:T(8,128)(2,1)}, bf16[1024,384]{1,0:T(8,128)(2,1)}...) custom-call(s32[5]{0:T(128)} %stack.23.where_ref.w, bf16[1024,384]{1,0:T(8,128)(2,1)} %get-tuple-element.192.refs_0_, ...), custom_call_target="tpu_custom_call" | custom-call | flops 115000000512 | bytes 1 | tf_op jit(solution)/shard_map/attend_backward/pallas_call | solution.py:51
  421.2 3.3 fold.16
  425.4 9.5 %collective-permute-done.41.refs_1_.refs_3_ = bf16[384,896]{1,0:T(8,128)(2,1)} collective-permute-done((bf16[384,896]{1,0:T(8,128)(2,1)}, bf16[384,896]{1,0:T(8,128)(2,1)}, u32[]{:S(2)}, u32[]{:S(2)}) %collective-permute-start.41) | collective-permute-done | bytes 688160 | tf_op jit(solution)/shard_map/ppermute | solution.py:835
  434.9 3.5 fold.17
  441.0 12.4 %attn_grads.3 = (bf16[768,1792]{1,0:T(8,128)(2,1)}, bf16[768,1792]{1,0:T(8,128)(2,1)}) custom-call(s32[5]{0:T(128)} %stack.23.where_ref.w, bf16[1024,1536]{1,0:T(8,128)(2,1)} %get-tuple-element.211.refs_0_.refs_17_, bf16[1024,384]{1,0:T(8,128)(2,1)} %get-tuple-element.300.refs_1_.refs_0_, bf16[1024,384]{1,0:T(8,128)(2,1)} %get-tuple-element.301.refs_2_.refs_1_, ...), custom_call_target="tpu_custom_call" | custom-call | flops 115000000512 | bytes 1 | tf_op jit(solution)/shard_map/attn_grads/pallas_call | solution.py:119
  460.5 15.3 %attn_back_send.1 = (bf16[512,1536]{1,0:T(8,128)(2,1)}, f32[1,1536]{1,0:T(1,128)}) custom-call(s32[5]{0:T(128)} %stack.23.where_ref.w, bf16[1024,384]{1,0:T(8,128)(2,1)} %get-tuple-element.300.refs_1_.refs_0_, bf16[1024,384]{1,0:T(8,128)(2,1)} %get-tuple-element.301.refs_2_.refs_1_, bf16[1024,384]{1,0:T(8,128)(2,1)} %get-tuple-element.302.refs_3_.refs_2_, ...), custom_call_target="tpu_custom_call" | custom-call | flops 115000000512 | bytes 1 | tf_op jit(solution)/shard_map/attn_back_send/pallas_call | solution.py:119
  478.6 22.3 %collective-permute-done.48 = bf16[192,768]{1,0:T(8,128)(2,1)S(1)} collective-permute-done((bf16[192,768]{1,0:T(8,128)(2,1)S(1)}, bf16[192,768]{1,0:T(8,128)(2,1)S(1)}, u32[]{:S(2)}, u32[]{:S(2)}) %collective-permute-start.48) | collective-permute-done | bytes 294944 | tf_op jit(solution)/shard_map/ppermute | solution.py:832
  502.7 4.6 fold.18
  508.7 15.1 %attn_back_own.1 = (bf16[512,1536]{1,0:T(8,128)(2,1)}, f32[1,1536]{1,0:T(1,128)}) custom-call(s32[5]{0:T(128)} %stack.23.where_ref.w, bf16[1024,384]{1,0:T(8,128)(2,1)} %get-tuple-element.300.refs_1_.refs_0_, bf16[1024,384]{1,0:T(8,128)(2,1)} %get-tuple-element.301.refs_2_.refs_1_, bf16[1024,384]{1,0:T(8,128)(2,1)} %get-tuple-element.302.refs_3_.refs_2_, ...), custom_call_target="tpu_custom_call" | custom-call | flops 115000000512 | bytes 1 | tf_op jit(solution)/shard_map/attn_back_own/pallas_call | solution.py:119
  526.4 4.0 fold.19
  533.7 3.8 convert_add_fusion
  547.1 3.5 collective-permute-start.59
  555.2 6.2 %close_block.1 = f32[512,1536]{1,0:T(8,128)} custom-call(s32[5]{0:T(128)} %stack.23.where_ref.w, bf16[512,1536]{1,0:T(8,128)(2,1)} %get-tuple-element.339.refs_0_, bf16[2048,1536]{1,0:T(8,128)(2,1)} %refs_1_.11, f32[1024,1]{1,0:T(8,128)} %get-tuple-element.197.refs_7_.refs_2_, f32[1,1536]{1,0:T(1,128)} %broadcast_in_dim.16.refs_1_.refs_18_.refs_3_, ...), custom_call_target="tpu_custom_call" | custom-call | flops 115000000512 | bytes 1 | tf_op jit(solution)/shard_map/close_block/pallas_call | solution.py:51
  (247 shorter events, 107.9 us)
Async XLA Ops:
  5.8 34.6 %collective-permute-start = (bf16[192,1792]{1,0:T(8,128)(2,1)}, bf16[192,1792]{1,0:T(8,128)(2,1)}, u32[]{:S(2)}, u32[]{:S(2)}) collective-permute-start(bf16[192,1792]{1,0:T(8,128)(2,1)} %collect.4.refs_8_), channel_id=1, source_target_pairs={{2,0},{3,1},{0,2},{1,3},{6,4},{7,5},{4,6},{5,7},{10,8},{11,9},{8,1... | collective-permute-start | bytes 2064392 | tf_op jit(solution)/shard_map/ppermute | solution.py:828
  9.9 30.6 %collective-permute-start.1 = (f32[6]{0:T(128)}, f32[6]{0:T(128)}, u32[]{:S(2)}, u32[]{:S(2)}) collective-permute-start(f32[6]{0:T(128)} %param.22), channel_id=1, source_target_pairs={{2,0},{3,1},{0,2},{1,3},{6,4},{7,5},{4,6},{5,7},{10,8},{11,9},{8,1... | collective-permute-start | bytes 80 | tf_op jit(solution)/shard_map/ppermute | solution.py:828
  38.6 19.2 %collective-permute-start.4 = (bf16[1024,384]{1,0:T(8,128)(2,1)}, bf16[1024,384]{1,0:T(8,128)(2,1)S(1)}, u32[]{:S(2)}, u32[]{:S(2)}) collective-permute-start(bf16[1024,384]{1,0:T(8,128)(2,1)} %get-tuple-element.201.refs_5_.refs_1_.refs_4_), channel_id=1, source_target_pairs={{1,0},{0,1},{3,2},{2,3},{5,4},{4,5},{7,6},{6,7},{9,8},{8,9},{11,10... | collective-permute-start | bytes 2359304 | tf_op jit(solution)/shard_map/ppermute | solution.py:828
  40.5 17.3 %collective-permute-start.3 = (bf16[192,1792]{1,0:T(8,128)(2,1)}, bf16[192,1792]{1,0:T(8,128)(2,1)S(1)}, u32[]{:S(2)}, u32[]{:S(2)}) collective-permute-start(bf16[192,1792]{1,0:T(8,128)(2,1)} %collective-permute-done.refs_0_), channel_id=1, source_target_pairs={{0,16},{4,20},{8,24},{12,28},{16,0},{20,4},{24,8},{28,12},{1,17},{... | collective-permute-start | bytes 2064392 | tf_op jit(solution)/shard_map/ppermute | solution.py:835
  42.1 27.9 %collective-permute-start.6 = (bf16[192,1792]{1,0:T(8,128)(2,1)}, bf16[192,1792]{1,0:T(8,128)(2,1)S(1)}, u32[]{:S(2)}, u32[]{:S(2)}) collective-permute-start(bf16[192,1792]{1,0:T(8,128)(2,1)} %collective-permute-done.refs_0_), channel_id=1, source_target_pairs={{0,8},{4,12},{8,0},{12,4},{16,24},{20,28},{24,16},{28,20},{1,9},{5... | collective-permute-start | bytes 2064392 | tf_op jit(solution)/shard_map/ppermute | solution.py:835
  57.8 16.0 %collective-permute-start.7 = (bf16[192,1792]{1,0:T(8,128)(2,1)S(1)}, bf16[192,1792]{1,0:T(8,128)(2,1)S(1)}, u32[]{:S(2)}, u32[]{:S(2)}) collective-permute-start(bf16[192,1792]{1,0:T(8,128)(2,1)S(1)} %collective-permute-done.3.refs_1_), channel_id=1, source_target_pairs={{0,8},{4,12},{8,0},{12,4},{16,24},{20,28},{24,16},{28,20},{1,9},{5... | collective-permute-start | bytes 2064392 | tf_op jit(solution)/shard_map/ppermute | solution.py:835
  79.6 21.3 %collective-permute-start.8 = (bf16[192,1152]{1,0:T(8,128)(2,1)}, bf16[192,1152]{1,0:T(8,128)(2,1)}, u32[]{:S(2)}, u32[]{:S(2)}) collective-permute-start(bf16[192,1152]{1,0:T(8,128)(2,1)} %constant_dynamic-update-slice_fusion.refs_0_), channel_id=1, source_target_pairs={{0,8},{4,12},{8,0},{12,4},{16,24},{20,28},{24,16},{28,20},{1,9},{5... | collective-permute-start | bytes 1327112 | tf_op jit(solution)/shard_map/ppermute | solution.py:835
  80.8 37.0 %collective-permute-start.10 = (bf16[192,1152]{1,0:T(8,128)(2,1)}, bf16[192,1152]{1,0:T(8,128)(2,1)}, u32[]{:S(2)}, u32[]{:S(2)}) collective-permute-start(bf16[192,1152]{1,0:T(8,128)(2,1)} %constant_dynamic-update-slice_fusion.refs_0_), channel_id=1, source_target_pairs={{0,16},{4,20},{8,24},{12,28},{16,0},{20,4},{24,8},{28,12},{1,17},{... | collective-permute-start | bytes 1327112 | tf_op jit(solution)/shard_map/ppermute | solution.py:835
  85.0 37.5 %collective-permute-start.14 = (bf16[192,2048]{1,0:T(8,128)(2,1)}, bf16[192,2048]{1,0:T(8,128)(2,1)}, u32[]{:S(2)}, u32[]{:S(2)}) collective-permute-start(bf16[192,2048]{1,0:T(8,128)(2,1)} %collect.6.refs_4_), channel_id=1, source_target_pairs={{2,0},{3,1},{0,2},{1,3},{6,4},{7,5},{4,6},{5,7},{10,8},{11,9},{8,1... | collective-permute-start | bytes 2359304 | tf_op jit(solution)/shard_map/ppermute | solution.py:828
  100.9 16.9 %collective-permute-start.11 = (bf16[192,1152]{1,0:T(8,128)(2,1)}, bf16[192,1152]{1,0:T(8,128)(2,1)S(1)}, u32[]{:S(2)}, u32[]{:S(2)}) collective-permute-start(bf16[192,1152]{1,0:T(8,128)(2,1)} %collective-permute-done.8.refs_1_), channel_id=1, source_target_pairs={{0,16},{4,20},{8,24},{12,28},{16,0},{20,4},{24,8},{28,12},{1,17},{... | collective-permute-start | bytes 1327112 | tf_op jit(solution)/shard_map/ppermute | solution.py:835
  115.4 23.9 %collective-permute-start.13 = (bf16[1024,384]{1,0:T(8,128)(2,1)}, bf16[1024,384]{1,0:T(8,128)(2,1)S(1)}, u32[]{:S(2)}, u32[]{:S(2)}) collective-permute-start(bf16[1024,384]{1,0:T(8,128)(2,1)} %get-tuple-element.226.refs_6_.refs_2_.refs_4_), channel_id=1, source_target_pairs={{1,0},{0,1},{3,2},{2,3},{5,4},{4,5},{7,6},{6,7},{9,8},{8,9},{11,10... | collective-permute-start | bytes 2359304 | tf_op jit(solution)/shard_map/ppermute | solution.py:828
  121.9 21.5 %collective-permute-start.12 = (bf16[768,1152]{1,0:T(8,128)(2,1)}, bf16[768,1152]{1,0:T(8,128)(2,1)S(1)}, u32[]{:S(2)}, u32[]{:S(2)}) collective-permute-start(bf16[768,1152]{1,0:T(8,128)(2,1)} %assemble.5.refs_1_.refs_2_.refs_6_), channel_id=1, source_target_pairs={{0,4},{4,0},{8,12},{12,8},{16,20},{20,16},{24,28},{28,24},{1,5},{5... | collective-permute-start | bytes 5308424 | tf_op jit(solution)/shard_map/ppermute | solution.py:835
  122.6 20.8 %collective-permute-start.15 = (bf16[192,2048]{1,0:T(8,128)(2,1)}, bf16[192,2048]{1,0:T(8,128)(2,1)S(1)}, u32[]{:S(2)}, u32[]{:S(2)}) collective-permute-start(bf16[192,2048]{1,0:T(8,128)(2,1)} %collective-permute-done.14.refs_0_), channel_id=1, source_target_pairs={{0,16},{4,20},{8,24},{12,28},{16,0},{20,4},{24,8},{28,12},{1,17},{... | collective-permute-start | bytes 2359304 | tf_op jit(solution)/shard_map/ppermute | solution.py:835
  123.5 81.5 %collective-permute-start.16 = (bf16[192,2048]{1,0:T(8,128)(2,1)}, bf16[192,2048]{1,0:T(8,128)(2,1)}, u32[]{:S(2)}, u32[]{:S(2)}) collective-permute-start(bf16[192,2048]{1,0:T(8,128)(2,1)} %collective-permute-done.14.refs_0_), channel_id=1, source_target_pairs={{0,8},{4,12},{8,0},{12,4},{16,24},{20,28},{24,16},{28,20},{1,9},{5... | collective-permute-start | bytes 2359304 | tf_op jit(solution)/shard_map/ppermute | solution.py:835
  141.7 20.8 %collective-permute-start.18 = (bf16[192,1024]{1,0:T(8,128)(2,1)}, bf16[192,1024]{1,0:T(8,128)(2,1)}, u32[]{:S(2)}, u32[]{:S(2)}) collective-permute-start(bf16[192,1024]{1,0:T(8,128)(2,1)} %collect.7.refs_9_), channel_id=1, source_target_pairs={{2,0},{3,1},{0,2},{1,3},{6,4},{7,5},{4,6},{5,7},{10,8},{11,9},{8,1... | collective-permute-start | bytes 1179656 | tf_op jit(solution)/shard_map/ppermute | solution.py:828
  162.5 47.7 %collective-permute-start.19 = (bf16[192,1024]{1,0:T(8,128)(2,1)}, bf16[192,1024]{1,0:T(8,128)(2,1)}, u32[]{:S(2)}, u32[]{:S(2)}) collective-permute-start(bf16[192,1024]{1,0:T(8,128)(2,1)} %collective-permute-done.18.refs_0_), channel_id=1, source_target_pairs={{0,8},{4,12},{8,0},{12,4},{16,24},{20,28},{24,16},{28,20},{1,9},{5... | collective-permute-start | bytes 1179656 | tf_op jit(solution)/shard_map/ppermute | solution.py:835
  163.0 49.3 %collective-permute-start.20 = (bf16[192,1024]{1,0:T(8,128)(2,1)}, bf16[192,1024]{1,0:T(8,128)(2,1)}, u32[]{:S(2)}, u32[]{:S(2)}) collective-permute-start(bf16[192,1024]{1,0:T(8,128)(2,1)} %collective-permute-done.18.refs_0_), channel_id=1, source_target_pairs={{0,16},{4,20},{8,24},{12,28},{16,0},{20,4},{24,8},{28,12},{1,17},{... | collective-permute-start | bytes 1179656 | tf_op jit(solution)/shard_map/ppermute | solution.py:835
  163.8 41.3 %collective-permute-start.17 = (bf16[192,2048]{1,0:T(8,128)(2,1)S(1)}, bf16[192,2048]{1,0:T(8,128)(2,1)S(1)}, u32[]{:S(2)}, u32[]{:S(2)}) collective-permute-start(bf16[192,2048]{1,0:T(8,128)(2,1)S(1)} %collective-permute-done.15.refs_1_), channel_id=1, source_target_pairs={{0,8},{4,12},{8,0},{12,4},{16,24},{20,28},{24,16},{28,20},{1,9},{5... | collective-permute-start | bytes 2359304 | tf_op jit(solution)/shard_map/ppermute | solution.py:835
  211.8 12.6 %collective-permute-start.24 = (bf16[768,3072]{1,0:T(8,128)(2,1)}, bf16[768,3072]{1,0:T(8,128)(2,1)S(1)}, u32[]{:S(2)}, u32[]{:S(2)}) collective-permute-start(bf16[768,3072]{1,0:T(8,128)(2,1)} %get-tuple-element.252), channel_id=1, source_target_pairs={{0,4},{4,0},{8,12},{12,8},{16,20},{20,16},{24,28},{28,24},{1,5},{5... | collective-permute-start | bytes 14155784 | tf_op jit(solution)/shard_map/ppermute | solution.py:835
  211.8 23.6 %collective-permute-start.22 = (bf16[768,2048]{1,0:T(8,128)(2,1)}, bf16[768,2048]{1,0:T(8,128)(2,1)}, u32[]{:S(2)}, u32[]{:S(2)}) collective-permute-start(bf16[768,2048]{1,0:T(8,128)(2,1)} %assemble.6.refs_4_.refs_3_), channel_id=1, source_target_pairs={{0,4},{4,0},{8,12},{12,8},{16,20},{20,16},{24,28},{28,24},{1,5},{5... | collective-permute-start | bytes 9437192 | tf_op jit(solution)/shard_map/ppermute | solution.py:835
  233.7 37.4 %collective-permute-start.26 = (bf16[384,1536]{1,0:T(8,128)(2,1)}, bf16[384,1536]{1,0:T(8,128)(2,1)S(1)}, u32[]{:S(2)}, u32[]{:S(2)}) collective-permute-start(bf16[384,1536]{1,0:T(8,128)(2,1)} %get-tuple-element.253.refs_11_), channel_id=1, source_target_pairs={{0,16},{4,20},{8,24},{12,28},{16,0},{20,4},{24,8},{28,12},{1,17},{... | collective-permute-start | bytes 3538952 | tf_op jit(solution)/shard_map/ppermute | solution.py:835
  234.8 36.3 %collective-permute-start.27 = (bf16[384,1536]{1,0:T(8,128)(2,1)}, bf16[384,1536]{1,0:T(8,128)(2,1)S(1)}, u32[]{:S(2)}, u32[]{:S(2)}) collective-permute-start(bf16[384,1536]{1,0:T(8,128)(2,1)} %get-tuple-element.262), channel_id=1, source_target_pairs={{0,8},{4,12},{8,0},{12,4},{16,24},{20,28},{24,16},{28,20},{1,9},{5... | collective-permute-start | bytes 3538952 | tf_op jit(solution)/shard_map/ppermute | solution.py:835
  270.6 36.7 %collective-permute-start.25 = (bf16[512,1536]{1,0:T(8,128)(2,1)}, bf16[512,1536]{1,0:T(8,128)(2,1)}, u32[]{:S(2)}, u32[]{:S(2)}) collective-permute-start(bf16[512,1536]{1,0:T(8,128)(2,1)} %get-tuple-element.256), channel_id=1, source_target_pairs={{0,1},{1,0},{2,3},{3,2},{4,5},{5,4},{6,7},{7,6},{8,9},{9,8},{10,11... | collective-permute-start | bytes 4718600 | tf_op jit(solution)/shard_map/ppermute | solution.py:876
  277.0 41.8 %collective-permute-start.30 = (bf16[192,1536]{1,0:T(8,128)(2,1)}, bf16[192,1536]{1,0:T(8,128)(2,1)}, u32[]{:S(2)}, u32[]{:S(2)}) collective-permute-start(bf16[192,1536]{1,0:T(8,128)(2,1)} %get-tuple-element.264.refs_5_), channel_id=1, source_target_pairs={{0,8},{4,12},{8,0},{12,4},{16,24},{20,28},{24,16},{28,20},{1,9},{5... | collective-permute-start | bytes 1769480 | tf_op jit(solution)/shard_map/ppermute | solution.py:835
  278.5 40.3 %collective-permute-start.31 = (bf16[192,1536]{1,0:T(8,128)(2,1)}, bf16[192,1536]{1,0:T(8,128)(2,1)}, u32[]{:S(2)}, u32[]{:S(2)}) collective-permute-start(bf16[192,1536]{1,0:T(8,128)(2,1)} %get-tuple-element.270), channel_id=1, source_target_pairs={{0,16},{4,20},{8,24},{12,28},{16,0},{20,4},{24,8},{28,12},{1,17},{... | collective-permute-start | bytes 1769480 | tf_op jit(solution)/shard_map/ppermute | solution.py:835
  295.6 26.4 %collective-permute-start.29 = (bf16[768,3072]{1,0:T(8,128)(2,1)}, bf16[768,3072]{1,0:T(8,128)(2,1)S(1)}, u32[]{:S(2)}, u32[]{:S(2)}) collective-permute-start(bf16[768,3072]{1,0:T(8,128)(2,1)} %get-tuple-element.265.refs_9_), channel_id=1, source_target_pairs={{0,4},{4,0},{8,12},{12,8},{16,20},{20,16},{24,28},{28,24},{1,5},{5... | collective-permute-start | bytes 14155784 | tf_op jit(solution)/shard_map/ppermute | solution.py:835
  318.4 21.4 %collective-permute-start.28 = (bf16[512,768]{1,0:T(8,128)(2,1)}, bf16[512,768]{1,0:T(8,128)(2,1)}, u32[]{:S(2)}, u32[]{:S(2)}) collective-permute-start(bf16[512,768]{1,0:T(8,128)(2,1)} %get-tuple-element.266), channel_id=1, source_target_pairs={{1,0},{0,1},{3,2},{2,3},{5,4},{4,5},{7,6},{6,7},{9,8},{8,9},{11,10... | collective-permute-start | bytes 2359304 | tf_op jit(solution)/shard_map/ppermute | solution.py:828
  331.2 42.7 %collective-permute-start.34 = (bf16[384,1536]{1,0:T(8,128)(2,1)}, bf16[384,1536]{1,0:T(8,128)(2,1)}, u32[]{:S(2)}, u32[]{:S(2)}) collective-permute-start(bf16[384,1536]{1,0:T(8,128)(2,1)} %get-tuple-element.273.refs_5_), channel_id=1, source_target_pairs={{0,16},{4,20},{8,24},{12,28},{16,0},{20,4},{24,8},{28,12},{1,17},{... | collective-permute-start | bytes 3538952 | tf_op jit(solution)/shard_map/ppermute | solution.py:835
  339.7 40.5 %collective-permute-start.33 = (bf16[768,1536]{1,0:T(8,128)(2,1)}, bf16[768,1536]{1,0:T(8,128)(2,1)}, u32[]{:S(2)}, u32[]{:S(2)}) collective-permute-start(bf16[768,1536]{1,0:T(8,128)(2,1)} %get-tuple-element.282.refs_12_), channel_id=1, source_target_pairs={{0,4},{4,0},{8,12},{12,8},{16,20},{20,16},{24,28},{28,24},{1,5},{5... | collective-permute-start | bytes 7077896 | tf_op jit(solution)/shard_map/ppermute | solution.py:835
  339.8 34.1 %collective-permute-start.35 = (bf16[384,1536]{1,0:T(8,128)(2,1)}, bf16[384,1536]{1,0:T(8,128)(2,1)}, u32[]{:S(2)}, u32[]{:S(2)}) collective-permute-start(bf16[384,1536]{1,0:T(8,128)(2,1)} %get-tuple-element.279), channel_id=1, source_target_pairs={{0,8},{4,12},{8,0},{12,4},{16,24},{20,28},{24,16},{28,20},{1,9},{5... | collective-permute-start | bytes 3538952 | tf_op jit(solution)/shard_map/ppermute | solution.py:835
  341.0 45.2 %collective-permute-start.32 = (bf16[512,1536]{1,0:T(8,128)(2,1)}, bf16[512,1536]{1,0:T(8,128)(2,1)}, u32[]{:S(2)}, u32[]{:S(2)}) collective-permute-start(bf16[512,1536]{1,0:T(8,128)(2,1)} %get-tuple-element.275), channel_id=1, source_target_pairs={{0,1},{1,0},{2,3},{3,2},{4,5},{5,4},{6,7},{7,6},{8,9},{9,8},{10,11... | collective-permute-start | bytes 4718600 | tf_op jit(solution)/shard_map/ppermute | solution.py:876
  378.2 16.1 %collective-permute-start.36 = (bf16[192,1536]{1,0:T(8,128)(2,1)}, bf16[192,1536]{1,0:T(8,128)(2,1)}, u32[]{:S(2)}, u32[]{:S(2)}) collective-permute-start(bf16[192,1536]{1,0:T(8,128)(2,1)} %get-tuple-element.290.refs_4_), channel_id=1, source_target_pairs={{0,8},{4,12},{8,0},{12,4},{16,24},{20,28},{24,16},{28,20},{1,9},{5... | collective-permute-start | bytes 1769480 | tf_op jit(solution)/shard_map/ppermute | solution.py:835
  379.1 16.5 %collective-permute-start.37 = (bf16[192,1536]{1,0:T(8,128)(2,1)}, bf16[192,1536]{1,0:T(8,128)(2,1)}, u32[]{:S(2)}, u32[]{:S(2)}) collective-permute-start(bf16[192,1536]{1,0:T(8,128)(2,1)} %get-tuple-element.295), channel_id=1, source_target_pairs={{0,16},{4,20},{8,24},{12,28},{16,0},{20,4},{24,8},{28,12},{1,17},{... | collective-permute-start | bytes 1769480 | tf_op jit(solution)/shard_map/ppermute | solution.py:835
  385.3 35.9 %collective-permute-start.39 = (bf16[384,1536]{1,0:T(8,128)(2,1)}, bf16[384,1536]{1,0:T(8,128)(2,1)}, u32[]{:S(2)}, u32[]{:S(2)}) collective-permute-start(bf16[384,1536]{1,0:T(8,128)(2,1)} %get-tuple-element.297.refs_8_), channel_id=1, source_target_pairs={{0,16},{4,20},{8,24},{12,28},{16,0},{20,4},{24,8},{28,12},{1,17},{... | collective-permute-start | bytes 3538952 | tf_op jit(solution)/shard_map/ppermute | solution.py:835
  391.0 43.9 %collective-permute-start.41 = (bf16[384,896]{1,0:T(8,128)(2,1)}, bf16[384,896]{1,0:T(8,128)(2,1)}, u32[]{:S(2)}, u32[]{:S(2)}) collective-permute-start(bf16[384,896]{1,0:T(8,128)(2,1)} %get-tuple-element.299.refs_12_), channel_id=1, source_target_pairs={{0,16},{4,20},{8,24},{12,28},{16,0},{20,4},{24,8},{28,12},{1,17},{... | collective-permute-start | bytes 2064392 | tf_op jit(solution)/shard_map/ppermute | solution.py:835
  395.6 39.3 %collective-permute-start.42 = (bf16[384,896]{1,0:T(8,128)(2,1)}, bf16[384,896]{1,0:T(8,128)(2,1)}, u32[]{:S(2)}, u32[]{:S(2)}) collective-permute-start(bf16[384,896]{1,0:T(8,128)(2,1)} %get-tuple-element.310), channel_id=1, source_target_pairs={{0,8},{4,12},{8,0},{12,4},{16,24},{20,28},{24,16},{28,20},{1,9},{5... | collective-permute-start | bytes 2064392 | tf_op jit(solution)/shard_map/ppermute | solution.py:835
  399.4 54.0 %collective-permute-start.45 = (bf16[192,3072]{1,0:T(8,128)(2,1)}, bf16[192,3072]{1,0:T(8,128)(2,1)}, u32[]{:S(2)}, u32[]{:S(2)}) collective-permute-start(bf16[192,3072]{1,0:T(8,128)(2,1)} %pad_maximum_fusion.1), channel_id=1, source_target_pairs={{0,2},{1,3},{2,0},{3,1},{4,6},{5,7},{6,4},{7,5},{8,10},{9,11},{10,... | collective-permute-start | bytes 3538952 | tf_op jit(solution)/shard_map/ppermute | solution.py:832
  424.5 32.1 %collective-permute-start.40 = (bf16[192,1536]{1,0:T(8,128)(2,1)}, bf16[192,1536]{1,0:T(8,128)(2,1)}, u32[]{:S(2)}, u32[]{:S(2)}) collective-permute-start(bf16[192,1536]{1,0:T(8,128)(2,1)} %get-tuple-element.307.refs_8_), channel_id=1, source_target_pairs={{0,8},{4,12},{8,0},{12,4},{16,24},{20,28},{24,16},{28,20},{1,9},{5... | collective-permute-start | bytes 1769480 | tf_op jit(solution)/shard_map/ppermute | solution.py:835
  438.4 15.1 %collective-permute-start.43 = (bf16[192,896]{1,0:T(8,128)(2,1)}, bf16[192,896]{1,0:T(8,128)(2,1)S(1)}, u32[]{:S(2)}, u32[]{:S(2)}) collective-permute-start(bf16[192,896]{1,0:T(8,128)(2,1)} %get-tuple-element.311.refs_6_), channel_id=1, source_target_pairs={{0,8},{4,12},{8,0},{12,4},{16,24},{20,28},{24,16},{28,20},{1,9},{5... | collective-permute-start | bytes 1032200 | tf_op jit(solution)/shard_map/ppermute | solution.py:835
  439.5 13.9 %collective-permute-start.44 = (bf16[192,896]{1,0:T(8,128)(2,1)}, bf16[192,896]{1,0:T(8,128)(2,1)S(1)}, u32[]{:S(2)}, u32[]{:S(2)}) collective-permute-start(bf16[192,896]{1,0:T(8,128)(2,1)} %get-tuple-element.312), channel_id=1, source_target_pairs={{0,16},{4,20},{8,24},{12,28},{16,0},{20,4},{24,8},{28,12},{1,17},{... | collective-permute-start | bytes 1032200 | tf_op jit(solution)/shard_map/ppermute | solution.py:835
  453.3 49.4 %collective-permute-start.46 = (bf16[768,1792]{1,0:T(8,128)(2,1)}, bf16[768,1792]{1,0:T(8,128)(2,1)}, u32[]{:S(2)}, u32[]{:S(2)}) collective-permute-start(bf16[768,1792]{1,0:T(8,128)(2,1)} %get-tuple-element.320.refs_19_), channel_id=1, source_target_pairs={{0,4},{4,0},{8,12},{12,8},{16,20},{20,16},{24,28},{28,24},{1,5},{5... | collective-permute-start | bytes 8257544 | tf_op jit(solution)/shard_map/ppermute | solution.py:835
  454.6 46.4 %collective-permute-start.47 = (bf16[192,1792]{1,0:T(8,128)(2,1)}, bf16[192,1792]{1,0:T(8,128)(2,1)S(1)}, u32[]{:S(2)}, u32[]{:S(2)}) collective-permute-start(bf16[192,1792]{1,0:T(8,128)(2,1)} %pad_maximum_fusion.5), channel_id=1, source_target_pairs={{0,2},{1,3},{2,0},{3,1},{4,6},{5,7},{6,4},{7,5},{8,10},{9,11},{10,... | collective-permute-start | bytes 2064392 | tf_op jit(solution)/shard_map/ppermute | solution.py:832
  459.6 41.4 %collective-permute-start.48 = (bf16[192,768]{1,0:T(8,128)(2,1)S(1)}, bf16[192,768]{1,0:T(8,128)(2,1)S(1)}, u32[]{:S(2)}, u32[]{:S(2)}) collective-permute-start(bf16[192,768]{1,0:T(8,128)(2,1)S(1)} %bitcast.22), channel_id=1, source_target_pairs={{0,2},{1,3},{2,0},{3,1},{4,6},{5,7},{6,4},{7,5},{8,10},{9,11},{10,... | collective-permute-start | bytes 884744 | tf_op jit(solution)/shard_map/ppermute | solution.py:832
  477.7 77.5 %collective-permute-start.52 = (bf16[512,1536]{1,0:T(8,128)(2,1)}, bf16[512,1536]{1,0:T(8,128)(2,1)}, u32[]{:S(2)}, u32[]{:S(2)}) collective-permute-start(bf16[512,1536]{1,0:T(8,128)(2,1)} %get-tuple-element.341), channel_id=1, source_target_pairs={{0,1},{1,0},{2,3},{3,2},{4,5},{5,4},{6,7},{7,6},{8,9},{9,8},{10,11... | collective-permute-start | bytes 4718600 | tf_op jit(solution)/shard_map/ppermute | solution.py:876
  502.6 49.7 %collective-permute-start.53 = (bf16[192,384]{1,0:T(8,128)(2,1)}, bf16[192,384]{1,0:T(8,128)(2,1)}, u32[]{:S(2)}, u32[]{:S(2)}) collective-permute-start(bf16[192,384]{1,0:T(8,128)(2,1)} %slice.127), channel_id=1, source_target_pairs={{0,1},{1,0},{2,3},{3,2},{4,5},{5,4},{6,7},{7,6},{8,9},{9,8},{10,11... | collective-permute-start | bytes 442376 | tf_op jit(solution)/shard_map/ppermute | solution.py:832
  507.3 17.4 %collective-permute-start.50 = (bf16[384,896]{1,0:T(8,128)(2,1)}, bf16[384,896]{1,0:T(8,128)(2,1)S(1)}, u32[]{:S(2)}, u32[]{:S(2)}) collective-permute-start(bf16[384,896]{1,0:T(8,128)(2,1)} %get-tuple-element.330.refs_19_), channel_id=1, source_target_pairs={{0,16},{4,20},{8,24},{12,28},{16,0},{20,4},{24,8},{28,12},{1,17},{... | collective-permute-start | bytes 2064392 | tf_op jit(solution)/shard_map/ppermute | solution.py:835
  507.9 17.0 %collective-permute-start.51 = (bf16[384,896]{1,0:T(8,128)(2,1)}, bf16[384,896]{1,0:T(8,128)(2,1)S(1)}, u32[]{:S(2)}, u32[]{:S(2)}) collective-permute-start(bf16[384,896]{1,0:T(8,128)(2,1)} %get-tuple-element.334), channel_id=1, source_target_pairs={{0,8},{4,12},{8,0},{12,4},{16,24},{20,28},{24,16},{28,20},{1,9},{5... | collective-permute-start | bytes 2064392 | tf_op jit(solution)/shard_map/ppermute | solution.py:835
  530.4 12.7 %collective-permute-start.56 = (bf16[192,896]{1,0:T(8,128)(2,1)}, bf16[192,896]{1,0:T(8,128)(2,1)S(1)}, u32[]{:S(2)}, u32[]{:S(2)}) collective-permute-start(bf16[192,896]{1,0:T(8,128)(2,1)} %get-tuple-element.360.refs_6_), channel_id=1, source_target_pairs={{0,8},{4,12},{8,0},{12,4},{16,24},{20,28},{24,16},{28,20},{1,9},{5... | collective-permute-start | bytes 1032200 | tf_op jit(solution)/shard_map/ppermute | solution.py:835
  (55 other events, 395.2 us)

commit v4 on v3

--- a/solution.py
+++ b/solution.py
@@ -65,11 +65,12 @@
 
 
 class Part:
-    def __init__(self, array, rows=None, row_at=None, cols=None, col_at=None):
+    def __init__(self, array, rows=None, row_at=None, cols=None, col_at=None, into=None):
         self.array = array
         self.rows = array.shape[0] if rows is None else rows
         self.cols = array.shape[1] if cols is None else cols
         self.row_at, self.col_at = row_at, col_at
+        self.into = into
 
     def view(self, ref, w):
         if self.row_at is None and self.col_at is None:
@@ -79,18 +80,24 @@
         return ref.at[pl.ds(row, self.rows), pl.ds(col, self.cols)]
 
 
-def stream(name, body, where, parts, outs, scratch=(), after=()):
+def stream(name, body, where, parts, outs, scratch=(), after=(), buffers=()):
     count, extra, made = len(parts), len(after), len(outs)
+    single = [p for p in parts if p.into is None]
     chunks = 16
 
     def kernel(w, *refs):
         sources = refs[:count]
         targets = refs[count + extra:count + extra + made]
         at = count + extra + made
-        held = refs[at:at + count]
-        ready = refs[at + count:at + count + made]
-        in_sems, out_sems = refs[at + count + made:at + count + made + 2]
-        rest = refs[at + count + made + 2:]
+        shared = refs[at:at + len(buffers)]
+        at += len(buffers)
+        alone = iter(refs[at:at + len(single)])
+        held = [next(alone) if p.into is None else shared[p.into[0]].at[
+            pl.ds(p.into[1](w) if callable(p.into[1]) else p.into[1], p.rows), pl.ds(p.into[2], p.cols)] for p in parts]
+        at += len(single)
+        ready = refs[at:at + made]
+        in_sems, out_sems = refs[at + made:at + made + 2]
+        rest = shared + refs[at + made + 2:]
         loads = []
         for k, part in enumerate(parts):
             copy = pltpu.make_async_copy(part.view(sources[k], w), held[k], in_sems.at[k])
@@ -122,7 +129,8 @@
             num_scalar_prefetch=1, grid=(),
             in_specs=[pl.BlockSpec(memory_space=pl.ANY)] * (count + extra),
             out_specs=[pl.BlockSpec(memory_space=pl.ANY)] * made,
-            scratch_shapes=[pltpu.VMEM((p.rows, p.cols), p.array.dtype) for p in parts]
+            scratch_shapes=[pltpu.VMEM(b, bf16) for b in buffers]
+            + [pltpu.VMEM((p.rows, p.cols), p.array.dtype) for p in single]
             + [pltpu.VMEM(o.shape, o.dtype) for o in outs]
             + [pltpu.SemaphoreType.DMA((count,)), pltpu.SemaphoreType.DMA((made, chunks))] + list(scratch),
         ),
@@ -241,19 +249,19 @@
             ref[:, pl.ds(pl.multiple_of((1 - w[CORE]) * half, 128), half)])
 
 
-def project_other(where, normed, mine, theirs, width, heads, bias, after=()):
+def project_other(where, normed, gathered, counts, width, heads, bias, after=()):
     length, model = normed.shape
     half = model // 2
 
     def body(w, ins, outs, scratch):
-        a_ref, m_ref, t_ref, b_ref = ins
+        a_ref, b_ref = ins[:2]
         am, at = core_halves(a_ref, w, half)
-        mixed = mm(am, m_ref[...]) + mm(at, t_ref[...])
-        project_tail(pl.program_id(0), mixed, width, b_ref[...], outs, scratch[0])
+        mixed = [mm(am, ins[2 + 2 * k][:, :n]) + mm(at, ins[3 + 2 * k][:, :n]) for k, n in enumerate(counts)]
+        project_tail(pl.program_id(0), jnp.concatenate(mixed, axis=1), width, b_ref[...], outs, scratch[0])
 
     return run(
         "project_other", body, where, (length // TOK,),
-        [(normed, (TOK, model), lambda i, w: (i, 0)), fixed(mine), fixed(theirs), fixed(bias)],
+        [(normed, (TOK, model), lambda i, w: (i, 0)), fixed(bias)] + [fixed(a) for pair in gathered for a in pair],
         project_outs(length, width, heads),
         [pltpu.VMEM((8, 128), f32)], after, 2 * length * model * (4 * width + heads),
     )
@@ -556,7 +564,8 @@
     length = groups[0][1][0].shape[0] if not rows_of else lefts[0].shape[0]
     half = lefts[0].shape[1] // 2
     widths = [sum(r.shape[1] for r in rights) for _, rights in groups]
-    padded = [-(-n // 256) * 256 for n in widths]
+    padded = [-(-n // 128) * 128 for n in widths]
+    padded[-1] += -sum(padded) % 256
     parts, plan, loaded = [], [], {}
     row_at = (lambda w: w[MEMBER] * length) if rows_of else None
     for k, (s, rights) in enumerate(groups):
@@ -652,73 +661,73 @@
     )(where, *pieces, *after)
 
 
-def back_rows(name, where, steps, group, share, own_terms, pair_terms, model, dtypes, adds=(), unit=None, after=()):
+def back_rows(name, where, step, group, own_x, own_w, pair_terms, normed, gain, after=()):
+    length, model = normed.shape
     half = model // 2
-    count = len(steps)
-    member = lambda w, k: lax.rem(w[MEMBER] + steps[k], group)
-    parts, xs_at, weights_at = [], {}, {}
-
-    def x_parts(xs):
-        for x in xs:
-            for k in range(count):
-                if (id(x), k) not in xs_at:
-                    xs_at[id(x), k] = len(parts)
-                    parts.append(Part(x, share, lambda w, k=k: member(w, k) * share))
-
-    def w_part(a):
-        if id(a) not in weights_at:
-            weights_at[id(a)] = len(parts)
-            parts.append(Part(a))
-
-    for xs, weights in own_terms:
-        x_parts(xs)
-        for a in weights:
-            w_part(a)
-    for xs, mine, theirs, lo in pair_terms:
-        x_parts(xs)
-        w_part(mine)
-    for xs, mine, theirs, lo in pair_terms:
-        w_part(theirs)
-    add_at = len(parts)
-    for a, kind in adds:
-        parts.append(Part(a, share, (lambda w: w[MEMBER] * share) if kind == "row" else None))
+    share = length // group
+    member = lambda w: lax.rem(w[MEMBER] + step, group)
+    row_at = lambda w: member(w) * share
+    parts, tails, cuts = [], [], []
+    col = 0
+
+    def lay(arrays, buffer, narrow):
+        at = col
+        for a in arrays:
+            n = a.shape[1]
+            rows, pick = (share, row_at) if buffer == 0 else (a.shape[0], None)
+            if n % 128 == 0 and at % 128 == 0:
+                parts.append(Part(a, rows, pick, n, None, (buffer, 0, at)))
+            else:
+                tails.append((len(parts), buffer, at, n))
+                parts.append(Part(a, rows, pick, n))
+            at += n
+        return at
+
+    if any(a.shape[1] % 128 for a in own_x[:-1]):
+        own_x, own_w = [jnp.concatenate(own_x, axis=1)], [jnp.concatenate(own_w, axis=1)]
+        pair_terms = [([jnp.concatenate(xs, axis=1)], mine, theirs) for xs, mine, theirs in pair_terms]
+    lay(own_x, 0, True)
+    end = lay(own_w, 1, True)
+    full = -(-end // 128) * 128
+    cuts.append((0, len(parts), 0, full))
+    col = full
+    for xs, mine, theirs in pair_terms:
+        first_part = len(parts)
+        lay(xs, 0, True)
+        n = mine.shape[1]
+        parts.append(Part(mine, into=(1, lambda w: pl.multiple_of(w[CORE] * half, half), col)))
+        parts.append(Part(theirs, into=(1, lambda w: pl.multiple_of((1 - w[CORE]) * half, half), col)))
+        cuts.append((first_part, len(parts), col, n))
+        col += n
     unit_at = len(parts)
-    if unit is not None:
-        for k in range(count):
-            parts.append(Part(unit[0], share, lambda w, k=k: member(w, k) * share))
-        parts.append(Part(unit[1]))
+    parts.append(Part(normed, share, row_at))
+    parts.append(Part(gain))
 
     def body(w, get, ready, put, rest):
-        wide = lambda xs, k: (get(xs_at[id(xs[0]), k])[...] if len(xs) == 1 else
-                              jnp.concatenate([get(xs_at[id(x), k])[...] for x in xs], axis=1))
-        for which in (0, 1):
-            core = lax.rem(w[CORE] + which, 2)
-            at = pl.multiple_of(core * half, 128)
-            for k in range(count):
-                total = 0.0
-                for xs, weights in own_terms:
-                    rows = [get(weights_at[id(a)])[pl.ds(at, half), :] for a in weights]
-                    total = total + last(wide(xs, k), rows[0] if len(rows) == 1 else jnp.concatenate(rows, axis=1))
-                for xs, mine, theirs, lo in pair_terms:
-                    ref = get(weights_at[id((mine, theirs)[which])])
-                    total = total + last(wide(xs, k), ref[:, lo:lo + sum(x.shape[1] for x in xs)])
-                if unit is not None:
-                    u = get(unit_at + k)[:, pl.ds(at, half)].astype(f32)
-                    gained = jnp.sum(total * u, axis=0, keepdims=True) / get(unit_at + count)[:, pl.ds(at, half)]
-                    gain = ready[count]
-                    gain[:, pl.ds(at, half)] = gained if k == 0 else gain[:, pl.ds(at, half)] + gained
-                if k == count - 1:
-                    for a in range(len(adds)):
-                        total = total + get(add_at + a)[:, pl.ds(at, half)].astype(f32)
-                ready[k][:, pl.ds(at, half)] = total.astype(dtypes[k])
-                put(k, col=at, cols=half)
-        if unit is not None:
-            put(count)
-
-    outs = [shape((share, model), d) for d in dtypes]
-    if unit is not None:
-        outs.append(shape((1, model), f32))
-    return stream(name, body, where, parts, outs, (), after)
+        x_all, w_all = rest[:2]
+        for low_part, high_part, at, n in cuts:
+            for k in range(low_part, high_part):
+                get(k)
+            for k, buffer, spot, count in tails:
+                if low_part <= k < high_part:
+                    target = (x_all, w_all)[buffer]
+                    last_col = at + n if spot + count <= at + n else spot + count
+                    value = get(k)[...]
+                    fill = jnp.zeros((value.shape[0], last_col - spot - count), bf16)
+                    target[:, spot:last_col] = jnp.concatenate([value, fill], axis=1) if last_col > spot + count else value
+            part = last(x_all[:, at:at + n], w_all[:, at:at + n])
+            rest[2][...] = part if at == 0 else rest[2][...] + part
+        total = rest[2][...]
+        ready[0][...] = low(total)
+        put(0)
+        u = get(unit_at)[...].astype(f32)
+        ready[1][...] = jnp.sum(total * u, axis=0, keepdims=True) / get(unit_at + 1)[...]
+        put(1)
+
+    return stream(
+        name, body, where, parts, [shape((share, model), bf16), shape((1, model), f32)],
+        [pltpu.VMEM((share, model), f32)], after, [(share, col), (model, col)],
+    )
 
 
 def close_feed_forward(where, share, group, part, got, hidden_row, inverse, gain, cotangent,
@@ -877,28 +886,15 @@
             (i, (i // group) * group + (i % group + step) % group) for i in range(here.tensor)])
 
     class Gather:
-        def __init__(self, piece, flip):
-            self.held, self.masks = [piece], [0]
-            self.left = here.bits[::-1] if flip else list(here.bits)
-            self.sent = {}
-            self.send()
-
-        def send(self):
-            for bit in self.left:
-                for i, p in enumerate(self.held):
-                    if (bit, i) not in self.sent:
-                        self.sent[bit, i] = here.swap(p, bit)
-
-        def hop(self):
-            bit = self.left.pop(0)
-            got = go.sync(*[self.sent[bit, i] for i in range(len(self.held))])
-            self.masks = self.masks + [k ^ (bit >> 1) for k in self.masks]
-            self.held = self.held + list(got)
-            self.send()
+        def __init__(self, piece):
+            others = range(1, here.dp // 2)
+            self.masks = [0] + sorted(others, key=lambda k: bin(k).count("1"))
+            self.held = [piece] + [here.swap(piece, 2 * k) for k in self.masks[1:]]
+
+        def wait(self):
+            self.held[1:] = go.sync(*self.held[1:])
 
         def close(self):
-            while self.left:
-                self.hop()
             self.mine = go(assemble, self.held, self.masks)
             self.theirs = here.swap(self.mine, 1)
             return self.mine, self.theirs
@@ -939,8 +935,10 @@
 
     both_ways = [here.bits, here.bits[::-1]]
 
-    attn_piece = go(collect, [w_query, w_key, w_value, w_outgate, w_forget], pieces, 256)
-    attn_got = [here.fetch(attn_piece, 0, j) for j in turns]
+    attn_cut = [[w_query, w_key], [w_value, w_outgate, w_forget]]
+    attn_counts = [sum(a.shape[1] for a in cut) for cut in attn_cut]
+    attn_pieces = [go(collect, cut, pieces, 128) for cut in attn_cut]
+    attn_got = [here.fetch(attn_pieces[0], 0, j) for j in turns]
     bias_got = [here.fetch(forget_bias, 0, j) for j in turns]
     own = go(project_own, length, inputs, gain_attn,
              [w_query, w_key, w_value, w_outgate, w_forget], forget_bias[None])
@@ -961,43 +959,50 @@
         for s in range(1, group):
             gated[s, j] = arrived[s - 1]
 
+    arrived = go.sync(*attn_got, *bias_got, attn_pieces[1])
+    attn_got, bias_got = arrived[:rows - 1], arrived[rows - 1:-1]
+    attn_later = [here.fetch(arrived[-1], 0, j) for j in turns]
+    attn_gather = [[Gather(p)] for p in attn_got]
     attend(0)
-    arrived = go.sync(*attn_got, *bias_got)
-    attn_got, bias_got = arrived[:rows - 1], arrived[rows - 1:]
-    attn_gather = [Gather(p, False) for p in attn_got]
+    for gathers, p in zip(attn_gather, go.sync(*attn_later)):
+        gathers[0].wait()
+        gathers.append(Gather(p))
     out_piece = go(collect, [w_out], pieces)
+    attn_w = [[gathers[0].close()] for gathers in attn_gather]
     out_got = [here.fetch(out_piece, 0, j) for j in turns]
+    gate_piece = go(collect, [w_gate, w_up], pieces)
     wait_gated(0)
-    for gather in attn_gather:
-        gather.hop()
+    for gathers in attn_gather:
+        gathers[1].wait()
+    for done, gathers in zip(attn_w, attn_gather):
+        done.append(gathers[1].close())
     out_got = go.sync(*out_got)
     out_own = jnp.concatenate([out_piece, *out_got], axis=1)
     out_peers = [here.fetch(out_own, s, 0) for s in range(1, group)]
-    attn_w = [gather.close() for gather in attn_gather]
-    out_peers = go.sync(*out_peers)
-    out_gather = Gather(jnp.concatenate([*out_got, *out_peers], axis=1), True)
-    gate_piece = go(collect, [w_gate, w_up], pieces)
+    gate_piece = go.sync(gate_piece)[0]
     gate_got = [here.fetch(gate_piece, 0, j) for j in turns]
     for j in turns:
-        mixed[j] = go(project_other, normed, *attn_w[j - 1], width, heads, bias_got[j - 1][None])
-    out_gather.hop()
+        mixed[j] = go(project_other, normed, attn_w[j - 1], attn_counts, width, heads, bias_got[j - 1][None])
+    out_peers = go.sync(*out_peers)
+    out_gather = Gather(jnp.concatenate([*out_got, *out_peers], axis=1))
     for j in turns:
         attend(j)
+    out_gather.wait()
     out_mine, out_theirs = out_gather.close()
     gate_got = go.sync(*gate_got)
-    gate_gather = [Gather(p, False) for p in gate_got]
+    gate_gather = [Gather(p) for p in gate_got]
+    down_piece = go(collect, [w_down], pieces)
     for j in turns:
         wait_gated(j)
-    down_piece = go(collect, [w_down], pieces)
+    down_piece, out_theirs = go.sync(down_piece, out_theirs)
     down_got = [here.fetch(down_piece, 0, j) for j in turns]
-    out_theirs = go.sync(out_theirs)[0]
-    for gather in gate_gather:
-        gather.hop()
     hidden_row, mlp_normed, inverse_mlp = go(
         close_attention, length, inputs, [gated[slot] for slot in slots], w_out, out_mine, out_theirs, gain_mlp
     )
+    for gather in gate_gather:
+        gather.wait()
     down_got = go.sync(*down_got)
-    down_gather = [Gather(p, True) for p in down_got]
+    down_gather = [Gather(p) for p in down_got]
 
     def ffn(weights, before, final):
         return go(feed_forward, mlp_normed, cotangent, weights, hidden, gain_mlp, group, pieces, before, final)
@@ -1006,8 +1011,6 @@
     mlp_sums = {}
     send, keep, *carried = ffn([w_gate, w_up, w_down], [], False)
     gate_w = [gather.close() for gather in gate_gather]
-    for gather in down_gather:
-        gather.hop()
     down_w = [gather.close() for gather in down_gather]
     mlp_sums[0] = Reduce(send, keep, both_ways)
     mlp_w = {}
@@ -1039,7 +1042,7 @@
     for j in turns:
         mlp_sums[j].hop()
     out_sum = Reduce(*go(lambda w, after: weight_grads(
-        "out_grads", w, [dh_low], [(0, [gated[slot] for slot in slots])], pieces, True, after=after)), both_ways[:1])
+        "out_grads", w, [dh_low], [(0, [gated[slot] for slot in slots])], pieces, True, after=after)), both_ways)
 
     back = {}
     attn_sums = {}
@@ -1054,7 +1057,7 @@
 
     def attn_grads(j, orders):
         attn_sums[j] = Reduce(*go(lambda w, after: weight_grads(
-            "attn_grads", w, [normed], [(0, back[j][:5])], pieces, after=after)), orders)
+            "attn_grads", w, [normed], [(0, back[j][:2]), (0, back[j][2:5])], pieces, after=after)), orders)
 
     arrived = go.sync(*dz_parts[1:], *out_send)
     dz_parts[1:], out_send = arrived[:group - 1], arrived[group - 1:]
@@ -1076,25 +1079,29 @@
     for j in turns:
         attn_sums[j].hop()
     attn_grads(0, both_ways)
+    own_w = [w_query, w_key, w_value, w_outgate, w_forget]
+    pair_terms = [
+        (list(back[j][lo:hi]), *attn_w[j - 1][k]) for j in turns for k, (lo, hi) in enumerate(((0, 2), (2, 5)))
+    ]
+
+    def attn_back(name, steps):
+        outs = []
+        for s in steps:
+            outs.append(go(lambda w, after: back_rows(
+                name, w, s, group, list(back[0][:5]), own_w, pair_terms, normed, gain_attn, after)))
+        return [o[0] for o in outs] + [sum(o[1] for o in outs)]
+
+    made = attn_back("attn_back_send", peers)
+    got = [to_member(v, s) for v, s in zip(made, peers)]
     mlp_other = go.sync(*mlp_other)
     for j in turns:
         attn_sums[j].wait()
     attn_other = [here.deliver(low(attn_sums[j].close()), 0, j) for j in turns]
     out_sum.wait()
+    attn_sums[0].hop()
     out_part = out_sum.close().reshape(-1, group, rows, width)
+    out_part = go.sync(out_part)[0]
     out_turned = [here.deliver(low(out_part[:, :, j]).reshape(-1, group * width), 0, j) for j in turns]
-    own_terms = [(back[0][:5], [w_query, w_key, w_value, w_outgate, w_forget])]
-    pair_terms = [(back[j][:5], *attn_w[j - 1], 0) for j in turns]
-
-    def attn_back(name, steps):
-        return go(lambda w, after: back_rows(
-            name, w, steps, group, share, own_terms, pair_terms, model, [bf16] * len(steps), (), (normed, gain_attn), after))
-
-    made = attn_back("attn_back_send", peers)
-    got = [to_member(v, s) for v, s in zip(made, peers)]
-    arrived = go.sync(*attn_other, *out_turned)
-    attn_other, out_turned = arrived[:rows - 1], arrived[rows - 1:]
-    attn_sums[0].hop()
     part, gained = attn_back("attn_back_own", [0])
     bias_full = jnp.zeros((here.tensor, heads), f32)
     for j in range(rows):
@@ -1110,15 +1117,18 @@
         total = small + arrived
         return total, (small_hops.pop(0)(total) if small_hops else None)
 
+    attn_other = go.sync(*attn_other)
     attn_sums[0].hop()
     small, flying = small_step()
-    out_part = out_part[:, :, 0].reshape(-1, group * width) + sum(v.astype(f32) for v in out_turned)
-    grad_out = out_part[:, :width]
-    out_rest = [here.deliver(low(out_part[:, s * width:(s + 1) * width]), s, 0) for s in peers]
     out_own, *arrived = go.sync(out_part_own, *out_got)
     output = lax.dynamic_slice_in_dim(hidden_row, member * share, share, 0) + out_own.astype(f32)
     for v in arrived:
         output = output + v.astype(f32)
+    out_turned = go.sync(*out_turned, output)
+    output = out_turned[-1]
+    out_part = out_part[:, :, 0].reshape(-1, group * width) + sum(v.astype(f32) for v in out_turned[:-1])
+    grad_out = out_part[:, :width]
+    out_rest = [here.deliver(low(out_part[:, s * width:(s + 1) * width]), s, 0) for s in peers]
     small, flying = small_step()
     mlp_own, *mlp_other = go.sync(mlp_own, *mlp_other)
     attn_sums[0].wait()

time: 571 us -> 541 us (0.947)
  waiting for transfers between devices: 99.1 us -> 81.2 us
  local copies, waits for them, and re-layouts: 30.9 us -> 23.1 us
  Pallas kernels: 345 us -> 339 us
    ppermute x9 -> x10, waiting for transfers between devices: 38.3 us -> 20.1 us  [fetch(): return lax.ppermute(value, 'tensor', pairs)]
    pallas_call x6, Pallas kernels: 79.1 us -> 70.1 us  [stream(): pl.pallas_call(kernel, grid_spec=pltpu.PrefetchScalarGridSpec(num_scalar_...]
    unnamed x92 -> x89, local copies, waits for them, and re-layouts: 19.1 us -> 10.8 us
    ppermute x42 -> x48, starting transfers between devices: 34.9 us -> 42.4 us  [swap(): return lax.ppermute(value, 'dp', [(i, i ^ bit) for i in range(self.dp)])]
    ppermute x9 -> x10, starting transfers between devices: 16.2 us -> 11.8 us  [fetch(): return lax.ppermute(value, 'tensor', pairs)]
    pallas_call x4 -> x5, Pallas kernels: 14.7 us -> 16.8 us  [assemble(): pl.pallas_call(kernel, grid_spec=pltpu.PrefetchScalarGridSpec(num_scalar_...]
    pallas_call x25 -> x26, Pallas kernels: 251 us -> 252 us  [run(): pl.pallas_call(kernel, grid_spec=pltpu.PrefetchScalarGridSpec(num_scalar_...]
    ppermute x42 -> x48, waiting for transfers between devices: 25.3 us -> 25.2 us  [swap(): return lax.ppermute(value, 'dp', [(i, i ^ bit) for i in range(self.dp)])]
  transfers between devices with their start and end apart: 60 -> 67, of which waited for: 16 -> 17; matrix products, arithmetic and copies ran while one was open for 6% -> 7% of each run, Pallas kernels for 60% -> 61%
where the time goes in v4:
time: 541 us; the launch traced here: 532 us
  Pallas kernels  339 us (63%)
  waiting for transfers between devices  81.2 us (15%)
  starting transfers between devices  64.6 us (12%)
  local copies, waits for them, and re-layouts  23.1 us (4%)
  other arithmetic  22.4 us (4%)
    pallas_call x26, Pallas kernels, run(): pl.pallas_call(kernel, grid_spec=pltpu.PrefetchScalarGridSpec(num_scalar_...  252 us
    pallas_call x6, Pallas kernels, stream(): pl.pallas_call(kernel, grid_spec=pltpu.PrefetchScalarGridSpec(num_scalar_...  70.1 us
    ppermute x48, starting transfers between devices, swap(): return lax.ppermute(value, 'dp', [(i, i ^ bit) for i in range(self.dp)])  42.4 us
    ppermute x48, waiting for transfers between devices, swap(): return lax.ppermute(value, 'dp', [(i, i ^ bit) for i in range(self.dp)])  25.2 us
    ppermute x4, waiting for transfers between devices, deliver(): return lax.ppermute(value, 'tensor', pairs)  20.5 us
    ppermute x10, waiting for transfers between devices, fetch(): return lax.ppermute(value, 'tensor', pairs)  20.1 us
    pallas_call x5, Pallas kernels, assemble(): pl.pallas_call(kernel, grid_spec=pltpu.PrefetchScalarGridSpec(num_scalar_...  16.8 us
    ppermute x10, starting transfers between devices, fetch(): return lax.ppermute(value, 'tensor', pairs)  11.8 us
  transfers between devices with their start and end apart: 67, of which 17 were waited for; matrix products, arithmetic and copies ran while one was open for 7% of the time, Pallas kernels for 61%

profile of v4, /device:TPU:0, one launch (start us, length us, event | category | flops | bytes accessed | tf_op | source)
XLA Modules:
  0.0 532.1 jit_solution(7476725152869212475)
XLA Ops:
  1.4 2.5 collect.5.refs_3_
  3.9 4.0 collective-permute-start
  11.9 12.9 %project_own.1 = (bf16[1024,1536]{1,0:T(8,128)(2,1)}, f32[1024,1]{1,0:T(8,128)}, bf16[1024,384]{1,0:T(8,128)(2,1)}, bf16[1024,384]{1,0:T(8,128)(2,1)}, bf16[1024...) custom-call(s32[5]{0:T(128)} %stack.23.where_ref.w, ...), custom_call_target="tpu_custom_call" | custom-call | flops 115000000512 | bytes 1 | tf_op jit(solution)/shard_map/project_own/pallas_call | solution.py:51
  30.0 2.9 collective-permute-start.5
  32.9 13.7 %attend_forward.2 = (bf16[1024,384]{1,0:T(8,128)(2,1)}, f32[3,2,1024]{2,1,0:T(2,128)}) custom-call(s32[5]{0:T(128)} %stack.23.where_ref.w, bf16[1024,384]{1,0:T(8,128)(2,1)} %get-tuple-element.206.refs_0_, bf16[1024,384]{1,0:T(8,128)(2,1)} %get-tuple-element.207.refs_1_, bf16[1024,384]{1,0:T(8,128)(2,1)} %get-tuple-element.208.refs_2_, ...), custom_call_target="tpu_custom_call" | custom-call | flops 115000000512 | bytes 1 | tf_op jit(solution)/shard_map/attend_forward/pallas_call | solution.py:51
  53.9 2.9 assemble.5.refs_2_.refs_12_
  56.9 2.7 collect.8.refs_4_
  59.6 4.9 collective-permute-done.10.refs_7_.refs_3_
  64.9 3.1 assemble.6.refs_4_.refs_6_.refs_17_
  69.8 8.7 %collective-permute-done.6 = bf16[192,384]{1,0:T(8,128)(2,1)S(1)} collective-permute-done((bf16[192,384]{1,0:T(8,128)(2,1)S(1)}, bf16[192,384]{1,0:T(8,128)(2,1)S(1)}, u32[]{:S(2)}, u32[]{:S(2)}) %collective-permute-start.6) | collective-permute-done | bytes 147488 | tf_op jit(solution)/shard_map/ppermute | solution.py:837
  81.8 11.5 %project_other.1 = (bf16[1024,384]{1,0:T(8,128)(2,1)}, bf16[1024,384]{1,0:T(8,128)(2,1)}, bf16[1024,384]{1,0:T(8,128)(2,1)}, bf16[1024,384]{1,0:T(8,128)(2,1)}, ...) custom-call(s32[5]{0:T(128)} %stack.23.where_ref.w, ...), custom_call_target="tpu_custom_call" | custom-call | flops 115000000512 | bytes 1 | tf_op jit(solution)/shard_map/project_other/pallas_call | solution.py:51
  96.9 13.8 %attend_forward.3 = (bf16[1024,384]{1,0:T(8,128)(2,1)}, f32[3,2,1024]{2,1,0:T(2,128)}) custom-call(s32[5]{0:T(128)} %stack.23.where_ref.w, bf16[1024,384]{1,0:T(8,128)(2,1)} %get-tuple-element.232.refs_0_, bf16[1024,384]{1,0:T(8,128)(2,1)} %get-tuple-element.233.refs_1_, bf16[1024,384]{1,0:T(8,128)(2,1)} %get-tuple-element.234.refs_2_, ...), custom_call_target="tpu_custom_call" | custom-call | flops 115000000512 | bytes 1 | tf_op jit(solution)/shard_map/attend_forward/pallas_call | solution.py:51
  110.9 4.5 collective-permute-done.15.refs_2_
  116.4 3.3 assemble.7.refs_1_.refs_2_.refs_6_
  123.3 2.4 collect.9.refs_9_
  125.8 6.5 %collective-permute-done.19.refs_8_.refs_4_ = bf16[1024,384]{1,0:T(8,128)(2,1)} collective-permute-done((bf16[1024,384]{1,0:T(8,128)(2,1)}, bf16[1024,384]{1,0:T(8,128)(2,1)}, u32[]{:S(2)}, u32[]{:S(2)}) %collective-permute-start.19) | collective-permute-done | bytes 786464 | tf_op jit(solution)/shard_map/ppermute | solution.py:837
  133.5 12.5 %close_attention.1 = (f32[1024,1536]{1,0:T(8,128)}, bf16[1024,1536]{1,0:T(8,128)(2,1)}, f32[1024,1]{1,0:T(8,128)}) custom-call(s32[5]{0:T(128)} %stack.23.where_ref.w, bf16[2048,1536]{1,0:T(8,128)(2,1)} %refs_1_.13, bf16[1536,384]{1,0:T(8,128)(2,1)} %refs_5_.7, bf16[768,1152]{1,0:T(8,128)(2,1)} %assemble.7.refs_1_.refs_2_.refs_6_, ...), custom_call_target="tpu_custom_call" | custom-call | flops 115000000512 | bytes 1 | tf_op jit(solution)/shard_map/close_attention/pallas_call | solution.py:51
  146.0 10.3 %collective-permute-done.21.refs_2_ = bf16[192,2048]{1,0:T(8,128)(2,1)} collective-permute-done((bf16[192,2048]{1,0:T(8,128)(2,1)}, bf16[192,2048]{1,0:T(8,128)(2,1)}, u32[]{:S(2)}, u32[]{:S(2)}) %collective-permute-start.21) | collective-permute-done | bytes 786464 | tf_op jit(solution)/shard_map/ppermute | solution.py:844
  161.6 40.1 %feed_forward.2 = (bf16[768,3072]{1,0:T(8,128)(2,1)}, bf16[768,3072]{1,0:T(8,128)(2,1)}, bf16[1024,1536]{1,0:T(8,128)(2,1)}, bf16[1024,1536]{1,0:T(8,128)(2,1)}) custom-call(s32[5]{0:T(128)} %stack.23.where_ref.w, bf16[1024,1536]{1,0:T(8,128)(2,1)} %get-tuple-element.251.refs_0_, bf16[2048,1536]{1,0:T(8,128)(2,1)} %refs_4_.5, ...), custom_call_target="tpu_custom_call" | custom-call | flops 115000000512 | bytes 1 | tf_op jit(solution)/shard_map/feed_forward/pallas_call | solution.py:51
  201.7 4.2 assemble.8.refs_4_.refs_3_
  206.5 3.3 assemble.9.refs_8_.refs_5_
  210.0 7.0 %fold.10 = (bf16[384,1536]{1,0:T(8,128)(2,1)}, bf16[384,1536]{1,0:T(8,128)(2,1)}, bf16[384,1536]{1,0:T(8,128)(2,1)}, bf16[384,1536]{1,0:T(8,128)(2,1)}) custom-call(s32[5]{0:T(128)} %stack.23.where_ref.w, bf16[768,3072]{1,0:T(8,128)(2,1)} %get-tuple-element.263.refs_0_.refs_2_.refs_4_.refs_6_, ...), custom_call_target="tpu_custom_call" | custom-call | flops 115000000512 | bytes 1 | tf_op jit(solution)/shard_map/fold/pallas_call | solution.py:51
  220.5 34.1 %feed_forward.3 = (bf16[1024,1024]{1,0:T(8,128)(2,1)}, bf16[1024,1024]{1,0:T(8,128)(2,1)}, bf16[1024,1024]{1,0:T(8,128)(2,1)}, bf16[512,1536]{1,0:T(8,128)(2,1)}...) custom-call(s32[5]{0:T(128)} %stack.23.where_ref.w, ...), custom_call_target="tpu_custom_call" | custom-call | flops 115000000512 | bytes 1 | tf_op jit(solution)/shard_map/feed_forward/pallas_call | solution.py:51
  256.5 4.4 fold.11
  262.7 16.5 %mlp_grads.1 = (bf16[768,3072]{1,0:T(8,128)(2,1)}, bf16[768,3072]{1,0:T(8,128)(2,1)}) custom-call(s32[5]{0:T(128)} %stack.23.where_ref.w, bf16[1024,1536]{1,0:T(8,128)(2,1)} %get-tuple-element.251.refs_0_, bf16[1024,1024]{1,0:T(8,128)(2,1)} %get-tuple-element.269.refs_1_, bf16[1024,1024]{1,0:T(8,128)(2,1)} %get-tuple-element.270.refs_2_, ...), custom_call_target="tpu_custom_call" | custom-call | flops 115000000512 | bytes 1 | tf_op jit(solution)/shard_map/mlp_grads/pallas_call | solution.py:126
  279.3 11.6 %collective-permute-done.30.refs_8_ = bf16[512,1536]{1,0:T(8,128)(2,1)} collective-permute-done((bf16[512,1536]{1,0:T(8,128)(2,1)}, bf16[512,1536]{1,0:T(8,128)(2,1)}, u32[]{:S(2)}, u32[]{:S(2)}) %collective-permute-start.30) | collective-permute-done | bytes 1572896 | tf_op jit(solution)/shard_map/ppermute | solution.py:885
  290.9 11.3 %close_feed_forward.1 = (f32[512,1536]{1,0:T(8,128)}, bf16[512,1536]{1,0:T(8,128)(2,1)}, bf16[512,768]{1,0:T(8,128)(2,1)}, bf16[512,768]{1,0:T(8,128)(2,1)}) custom-call(s32[5]{0:T(128)} %stack.23.where_ref.w, bf16[512,1536]{1,0:T(8,128)(2,1)} %get-tuple-element.266.refs_0_, f32[1024,1536]{1,0:T(8,128)} %get-tuple-element.267.refs_1_, ...), custom_call_target="tpu_custom_call" | custom-call | flops 115000000512 | bytes 1 | tf_op jit(solution)/shard_map/close_feed_forward/pallas_call | solution.py:51
  307.9 6.9 %fold.12 = (bf16[384,1536]{1,0:T(8,128)(2,1)}, bf16[384,1536]{1,0:T(8,128)(2,1)}, bf16[384,1536]{1,0:T(8,128)(2,1)}, bf16[384,1536]{1,0:T(8,128)(2,1)}) custom-call(s32[5]{0:T(128)} %stack.23.where_ref.w, bf16[768,3072]{1,0:T(8,128)(2,1)} %get-tuple-element.279.refs_0_.refs_2_.refs_4_.refs_6_, bf16[768,3072]{1,0:T(8,128)(2,1)} %copy-done.24, ...), custom_call_target="tpu_custom_call" | custom-call | flops 115000000512 | bytes 1 | tf_op jit(solution)/shard_map/fold/pallas_call | solution.py:51
  315.2 7.6 %out_grads.1 = (bf16[768,1536]{1,0:T(8,128)(2,1)}, bf16[768,1536]{1,0:T(8,128)(2,1)}) custom-call(s32[5]{0:T(128)} %stack.23.where_ref.w, bf16[512,1536]{1,0:T(8,128)(2,1)} %get-tuple-element.278.refs_0_, bf16[1024,384]{1,0:T(8,128)(2,1)} %get-tuple-element.216.refs_5_.refs_1_.refs_4_, bf16[1024,384]{1,0:T(8,128)(2,1)} %get-tuple-element.245.refs_6_.refs_2_.refs_4_, ...), custom_call_target="tpu_custom_call" | custom-call | flops 115000000512 | bytes 1 | tf_op jit(solution)/shard_map/out_grads/pallas_call | solution.py:126
  326.0 18.6 %attend_backward.2 = (bf16[1024,384]{1,0:T(8,128)(2,1)}, bf16[1024,384]{1,0:T(8,128)(2,1)}, bf16[1024,384]{1,0:T(8,128)(2,1)}, bf16[1024,384]{1,0:T(8,128)(2,1)}...) custom-call(s32[5]{0:T(128)} %stack.23.where_ref.w, bf16[1024,384]{1,0:T(8,128)(2,1)} %get-tuple-element.232.refs_0_, ...), custom_call_target="tpu_custom_call" | custom-call | flops 115000000512 | bytes 1 | tf_op jit(solution)/shard_map/attend_backward/pallas_call | solution.py:51
  344.6 11.5 %attn_grads.2 = (bf16[768,1792]{1,0:T(8,128)(2,1)}, bf16[768,1792]{1,0:T(8,128)(2,1)}) custom-call(s32[5]{0:T(128)} %stack.23.where_ref.w, bf16[1024,1536]{1,0:T(8,128)(2,1)} %get-tuple-element.226.refs_0_.refs_19_, bf16[1024,384]{1,0:T(8,128)(2,1)} %get-tuple-element.294.refs_1_.refs_10_, bf16[1024,384]{1,0:T(8,128)(2,1)} %get-tuple-element.295.refs_2_.refs_11_, ...), custom_call_target="tpu_custom_call" | custom-call | flops 115000000512 | bytes 1 | tf_op jit(solution)/shard_map/attn_grads/pallas_call | solution.py:126
  356.2 4.3 fold.13
  362.8 4.3 fold.14
  368.9 4.7 fold.15
  374.3 2.6 collective-permute-done.42
  382.1 18.6 %attend_backward.3 = (bf16[1024,384]{1,0:T(8,128)(2,1)}, bf16[1024,384]{1,0:T(8,128)(2,1)}, bf16[1024,384]{1,0:T(8,128)(2,1)}, bf16[1024,384]{1,0:T(8,128)(2,1)}...) custom-call(s32[5]{0:T(128)} %stack.23.where_ref.w, bf16[1024,384]{1,0:T(8,128)(2,1)} %get-tuple-element.206.refs_0_, ...), custom_call_target="tpu_custom_call" | custom-call | flops 115000000512 | bytes 1 | tf_op jit(solution)/shard_map/attend_backward/pallas_call | solution.py:51
  402.4 3.3 fold.16
  406.4 3.5 fold.17
  412.2 11.5 %attn_grads.3 = (bf16[768,1792]{1,0:T(8,128)(2,1)}, bf16[768,1792]{1,0:T(8,128)(2,1)}) custom-call(s32[5]{0:T(128)} %stack.23.where_ref.w, bf16[1024,1536]{1,0:T(8,128)(2,1)} %get-tuple-element.226.refs_0_.refs_19_, bf16[1024,384]{1,0:T(8,128)(2,1)} %get-tuple-element.327.refs_1_.refs_0_, bf16[1024,384]{1,0:T(8,128)(2,1)} %get-tuple-element.328.refs_2_.refs_1_, ...), custom_call_target="tpu_custom_call" | custom-call | flops 115000000512 | bytes 1 | tf_op jit(solution)/shard_map/attn_grads/pallas_call | solution.py:126
  423.8 11.6 %attn_back_send.1 = (bf16[512,1536]{1,0:T(8,128)(2,1)}, f32[1,1536]{1,0:T(1,128)}) custom-call(s32[5]{0:T(128)} %stack.23.where_ref.w, bf16[1024,384]{1,0:T(8,128)(2,1)} %get-tuple-element.327.refs_1_.refs_0_, bf16[1024,384]{1,0:T(8,128)(2,1)} %get-tuple-element.328.refs_2_.refs_1_, bf16[1024,384]{1,0:T(8,128)(2,1)} %get-tuple-element.329.refs_3_.refs_2_, ...), custom_call_target="tpu_custom_call" | custom-call | flops 115000000512 | bytes 1 | tf_op jit(solution)/shard_map/attn_back_send/pallas_call | solution.py:126
  448.0 4.6 fold.18
  454.4 11.4 %attn_back_own.1 = (bf16[512,1536]{1,0:T(8,128)(2,1)}, f32[1,1536]{1,0:T(1,128)}) custom-call(s32[5]{0:T(128)} %stack.23.where_ref.w, bf16[1024,384]{1,0:T(8,128)(2,1)} %get-tuple-element.327.refs_1_.refs_0_, bf16[1024,384]{1,0:T(8,128)(2,1)} %get-tuple-element.328.refs_2_.refs_1_, bf16[1024,384]{1,0:T(8,128)(2,1)} %get-tuple-element.329.refs_3_.refs_2_, ...), custom_call_target="tpu_custom_call" | custom-call | flops 115000000512 | bytes 1 | tf_op jit(solution)/shard_map/attn_back_own/pallas_call | solution.py:126
  466.6 20.3 %collective-permute-done.58 = bf16[192,1792]{1,0:T(8,128)(2,1)} collective-permute-done((bf16[192,1792]{1,0:T(8,128)(2,1)}, bf16[192,1792]{1,0:T(8,128)(2,1)}, u32[]{:S(2)}, u32[]{:S(2)}) %collective-permute-start.58) | collective-permute-done | bytes 688160 | tf_op jit(solution)/shard_map/ppermute | solution.py:841
  487.9 3.4 collective-permute-start.54
  494.3 3.6 fold.19
  500.3 4.8 convert_add_fusion
  512.5 2.7 collective-permute-done.64
  525.6 6.2 %close_block.1 = f32[512,1536]{1,0:T(8,128)} custom-call(s32[5]{0:T(128)} %stack.23.where_ref.w, bf16[512,1536]{1,0:T(8,128)(2,1)} %get-tuple-element.361.refs_0_, bf16[2048,1536]{1,0:T(8,128)(2,1)} %refs_1_.13, f32[1024,1]{1,0:T(8,128)} %get-tuple-element.211.refs_7_.refs_2_, f32[1,1536]{1,0:T(1,128)} %broadcast_in_dim.16.refs_1_.refs_20_.refs_3_, ...), custom_call_target="tpu_custom_call" | custom-call | flops 115000000512 | bytes 1 | tf_op jit(solution)/shard_map/close_block/pallas_call | solution.py:51
  (262 shorter events, 108.7 us)
Async XLA Ops:
  3.9 22.6 %collective-permute-start = (bf16[192,768]{1,0:T(8,128)(2,1)}, bf16[192,768]{1,0:T(8,128)(2,1)}, u32[]{:S(2)}, u32[]{:S(2)}) collective-permute-start(bf16[192,768]{1,0:T(8,128)(2,1)} %collect.5.refs_3_), channel_id=1, source_target_pairs={{2,0},{3,1},{0,2},{1,3},{6,4},{7,5},{4,6},{5,7},{10,8},{11,9},{8,1... | collective-permute-start | bytes 884744 | tf_op jit(solution)/shard_map/ppermute | solution.py:837
  7.9 18.6 %collective-permute-start.1 = (f32[6]{0:T(128)}, f32[6]{0:T(128)}, u32[]{:S(2)}, u32[]{:S(2)}) collective-permute-start(f32[6]{0:T(128)} %param.22), channel_id=1, source_target_pairs={{2,0},{3,1},{0,2},{1,3},{6,4},{7,5},{4,6},{5,7},{10,8},{11,9},{8,1... | collective-permute-start | bytes 80 | tf_op jit(solution)/shard_map/ppermute | solution.py:837
  26.5 23.1 %collective-permute-start.2 = (bf16[192,768]{1,0:T(8,128)(2,1)}, bf16[192,768]{1,0:T(8,128)(2,1)S(1)}, u32[]{:S(2)}, u32[]{:S(2)}) collective-permute-start(bf16[192,768]{1,0:T(8,128)(2,1)} %collective-permute-done.refs_0_), channel_id=1, source_target_pairs={{0,8},{4,12},{8,0},{12,4},{16,24},{20,28},{24,16},{28,20},{1,9},{5... | collective-permute-start | bytes 884744 | tf_op jit(solution)/shard_map/ppermute | solution.py:844
  28.3 22.9 %collective-permute-start.3 = (bf16[192,768]{1,0:T(8,128)(2,1)}, bf16[192,768]{1,0:T(8,128)(2,1)S(1)}, u32[]{:S(2)}, u32[]{:S(2)}) collective-permute-start(bf16[192,768]{1,0:T(8,128)(2,1)} %collective-permute-done.refs_0_), channel_id=1, source_target_pairs={{0,16},{4,20},{8,24},{12,28},{16,0},{20,4},{24,8},{28,12},{1,17},{... | collective-permute-start | bytes 884744 | tf_op jit(solution)/shard_map/ppermute | solution.py:844
  29.8 21.8 %collective-permute-start.4 = (bf16[192,768]{1,0:T(8,128)(2,1)}, bf16[192,768]{1,0:T(8,128)(2,1)S(1)}, u32[]{:S(2)}, u32[]{:S(2)}) collective-permute-start(bf16[192,768]{1,0:T(8,128)(2,1)} %collective-permute-done.refs_0_), channel_id=1, source_target_pairs={{0,24},{4,28},{8,16},{12,20},{16,8},{20,12},{24,0},{28,4},{1,25},{... | collective-permute-start | bytes 884744 | tf_op jit(solution)/shard_map/ppermute | solution.py:844
  30.0 18.1 %collective-permute-start.5 = (bf16[192,896]{1,0:T(8,128)(2,1)S(1)}, bf16[192,896]{1,0:T(8,128)(2,1)}, u32[]{:S(2)}, u32[]{:S(2)}) collective-permute-start(bf16[192,896]{1,0:T(8,128)(2,1)S(1)} %copy-done.37), channel_id=1, source_target_pairs={{2,0},{3,1},{0,2},{1,3},{6,4},{7,5},{4,6},{5,7},{10,8},{11,9},{8,1... | collective-permute-start | bytes 1032200 | tf_op jit(solution)/shard_map/ppermute | solution.py:837
  46.5 17.9 %collective-permute-start.10 = (bf16[1024,384]{1,0:T(8,128)(2,1)}, bf16[1024,384]{1,0:T(8,128)(2,1)}, u32[]{:S(2)}, u32[]{:S(2)}) collective-permute-start(bf16[1024,384]{1,0:T(8,128)(2,1)} %get-tuple-element.216.refs_5_.refs_1_.refs_4_), channel_id=1, source_target_pairs={{1,0},{0,1},{3,2},{2,3},{5,4},{4,5},{7,6},{6,7},{9,8},{8,9},{11,10... | collective-permute-start | bytes 2359304 | tf_op jit(solution)/shard_map/ppermute | solution.py:837
  48.1 16.3 %collective-permute-start.7 = (bf16[192,896]{1,0:T(8,128)(2,1)}, bf16[192,896]{1,0:T(8,128)(2,1)}, u32[]{:S(2)}, u32[]{:S(2)}) collective-permute-start(bf16[192,896]{1,0:T(8,128)(2,1)} %collective-permute-done.5.refs_0_), channel_id=1, source_target_pairs={{0,8},{4,12},{8,0},{12,4},{16,24},{20,28},{24,16},{28,20},{1,9},{5... | collective-permute-start | bytes 1032200 | tf_op jit(solution)/shard_map/ppermute | solution.py:844
  78.6 41.2 %collective-permute-start.17 = (bf16[192,2048]{1,0:T(8,128)(2,1)}, bf16[192,2048]{1,0:T(8,128)(2,1)}, u32[]{:S(2)}, u32[]{:S(2)}) collective-permute-start(bf16[192,2048]{1,0:T(8,128)(2,1)} %collect.8.refs_4_), channel_id=1, source_target_pairs={{2,0},{3,1},{0,2},{1,3},{6,4},{7,5},{4,6},{5,7},{10,8},{11,9},{8,1... | collective-permute-start | bytes 2359304 | tf_op jit(solution)/shard_map/ppermute | solution.py:837
  93.3 17.6 %collective-permute-start.14 = (bf16[192,1152]{1,0:T(8,128)(2,1)S(1)}, bf16[192,1152]{1,0:T(8,128)(2,1)S(1)}, u32[]{:S(2)}, u32[]{:S(2)}) collective-permute-start(bf16[192,1152]{1,0:T(8,128)(2,1)S(1)} %constant_dynamic-update-slice_fusion.refs_0_), channel_id=1, source_target_pairs={{0,8},{4,12},{8,0},{12,4},{16,24},{20,28},{24,16},{28,20},{1,9},{5... | collective-permute-start | bytes 1327112 | tf_op jit(solution)/shard_map/ppermute | solution.py:844
  94.9 20.5 %collective-permute-start.15 = (bf16[192,1152]{1,0:T(8,128)(2,1)S(1)}, bf16[192,1152]{1,0:T(8,128)(2,1)S(1)}, u32[]{:S(2)}, u32[]{:S(2)}) collective-permute-start(bf16[192,1152]{1,0:T(8,128)(2,1)S(1)} %constant_dynamic-update-slice_fusion.refs_0_), channel_id=1, source_target_pairs={{0,16},{4,20},{8,24},{12,28},{16,0},{20,4},{24,8},{28,12},{1,17},{... | collective-permute-start | bytes 1327112 | tf_op jit(solution)/shard_map/ppermute | solution.py:844
  96.4 19.0 %collective-permute-start.16 = (bf16[192,1152]{1,0:T(8,128)(2,1)S(1)}, bf16[192,1152]{1,0:T(8,128)(2,1)S(1)}, u32[]{:S(2)}, u32[]{:S(2)}) collective-permute-start(bf16[192,1152]{1,0:T(8,128)(2,1)S(1)} %constant_dynamic-update-slice_fusion.refs_0_), channel_id=1, source_target_pairs={{0,24},{4,28},{8,16},{12,20},{16,8},{20,12},{24,0},{28,4},{1,25},{... | collective-permute-start | bytes 1327112 | tf_op jit(solution)/shard_map/ppermute | solution.py:844
  110.7 21.6 %collective-permute-start.19 = (bf16[1024,384]{1,0:T(8,128)(2,1)}, bf16[1024,384]{1,0:T(8,128)(2,1)}, u32[]{:S(2)}, u32[]{:S(2)}) collective-permute-start(bf16[1024,384]{1,0:T(8,128)(2,1)} %get-tuple-element.245.refs_6_.refs_2_.refs_4_), channel_id=1, source_target_pairs={{1,0},{0,1},{3,2},{2,3},{5,4},{4,5},{7,6},{6,7},{9,8},{8,9},{11,10... | collective-permute-start | bytes 2359304 | tf_op jit(solution)/shard_map/ppermute | solution.py:837
  119.8 26.2 %collective-permute-start.20 = (bf16[192,2048]{1,0:T(8,128)(2,1)}, bf16[192,2048]{1,0:T(8,128)(2,1)}, u32[]{:S(2)}, u32[]{:S(2)}) collective-permute-start(bf16[192,2048]{1,0:T(8,128)(2,1)} %collective-permute-done.17.refs_0_), channel_id=1, source_target_pairs={{0,8},{4,12},{8,0},{12,4},{16,24},{20,28},{24,16},{28,20},{1,9},{5... | collective-permute-start | bytes 2359304 | tf_op jit(solution)/shard_map/ppermute | solution.py:844
  121.2 35.1 %collective-permute-start.21 = (bf16[192,2048]{1,0:T(8,128)(2,1)}, bf16[192,2048]{1,0:T(8,128)(2,1)}, u32[]{:S(2)}, u32[]{:S(2)}) collective-permute-start(bf16[192,2048]{1,0:T(8,128)(2,1)} %collective-permute-done.17.refs_0_), channel_id=1, source_target_pairs={{0,16},{4,20},{8,24},{12,28},{16,0},{20,4},{24,8},{28,12},{1,17},{... | collective-permute-start | bytes 2359304 | tf_op jit(solution)/shard_map/ppermute | solution.py:844
  122.0 36.1 %collective-permute-start.22 = (bf16[192,2048]{1,0:T(8,128)(2,1)}, bf16[192,2048]{1,0:T(8,128)(2,1)}, u32[]{:S(2)}, u32[]{:S(2)}) collective-permute-start(bf16[192,2048]{1,0:T(8,128)(2,1)} %collective-permute-done.17.refs_0_), channel_id=1, source_target_pairs={{0,24},{4,28},{8,16},{12,20},{16,8},{20,12},{24,0},{28,4},{1,25},{... | collective-permute-start | bytes 2359304 | tf_op jit(solution)/shard_map/ppermute | solution.py:844
  132.3 25.8 %collective-permute-start.23 = (bf16[192,1024]{1,0:T(8,128)(2,1)}, bf16[192,1024]{1,0:T(8,128)(2,1)}, u32[]{:S(2)}, u32[]{:S(2)}) collective-permute-start(bf16[192,1024]{1,0:T(8,128)(2,1)} %collect.9.refs_9_), channel_id=1, source_target_pairs={{2,0},{3,1},{0,2},{1,3},{6,4},{7,5},{4,6},{5,7},{10,8},{11,9},{8,1... | collective-permute-start | bytes 1179656 | tf_op jit(solution)/shard_map/ppermute | solution.py:837
  158.1 48.4 %collective-permute-start.24 = (bf16[192,1024]{1,0:T(8,128)(2,1)}, bf16[192,1024]{1,0:T(8,128)(2,1)}, u32[]{:S(2)}, u32[]{:S(2)}) collective-permute-start(bf16[192,1024]{1,0:T(8,128)(2,1)} %collective-permute-done.23.refs_0_), channel_id=1, source_target_pairs={{0,8},{4,12},{8,0},{12,4},{16,24},{20,28},{24,16},{28,20},{1,9},{5... | collective-permute-start | bytes 1179656 | tf_op jit(solution)/shard_map/ppermute | solution.py:844
  158.7 47.8 %collective-permute-start.25 = (bf16[192,1024]{1,0:T(8,128)(2,1)}, bf16[192,1024]{1,0:T(8,128)(2,1)}, u32[]{:S(2)}, u32[]{:S(2)}) collective-permute-start(bf16[192,1024]{1,0:T(8,128)(2,1)} %collective-permute-done.23.refs_0_), channel_id=1, source_target_pairs={{0,16},{4,20},{8,24},{12,28},{16,0},{20,4},{24,8},{28,12},{1,17},{... | collective-permute-start | bytes 1179656 | tf_op jit(solution)/shard_map/ppermute | solution.py:844
  160.4 46.1 %collective-permute-start.26 = (bf16[192,1024]{1,0:T(8,128)(2,1)}, bf16[192,1024]{1,0:T(8,128)(2,1)}, u32[]{:S(2)}, u32[]{:S(2)}) collective-permute-start(bf16[192,1024]{1,0:T(8,128)(2,1)} %collective-permute-done.23.refs_0_), channel_id=1, source_target_pairs={{0,24},{4,28},{8,16},{12,20},{16,8},{20,12},{24,0},{28,4},{1,25},{... | collective-permute-start | bytes 1179656 | tf_op jit(solution)/shard_map/ppermute | solution.py:844
  217.0 38.1 %collective-permute-start.31 = (bf16[384,1536]{1,0:T(8,128)(2,1)}, bf16[384,1536]{1,0:T(8,128)(2,1)S(1)}, u32[]{:S(2)}, u32[]{:S(2)}) collective-permute-start(bf16[384,1536]{1,0:T(8,128)(2,1)} %get-tuple-element.265.refs_11_), channel_id=1, source_target_pairs={{0,16},{4,20},{8,24},{12,28},{16,0},{20,4},{24,8},{28,12},{1,17},{... | collective-permute-start | bytes 3538952 | tf_op jit(solution)/shard_map/ppermute | solution.py:844
  217.7 37.4 %collective-permute-start.32 = (bf16[384,1536]{1,0:T(8,128)(2,1)}, bf16[384,1536]{1,0:T(8,128)(2,1)S(1)}, u32[]{:S(2)}, u32[]{:S(2)}) collective-permute-start(bf16[384,1536]{1,0:T(8,128)(2,1)} %get-tuple-element.274), channel_id=1, source_target_pairs={{0,8},{4,12},{8,0},{12,4},{16,24},{20,28},{24,16},{28,20},{1,9},{5... | collective-permute-start | bytes 3538952 | tf_op jit(solution)/shard_map/ppermute | solution.py:844
  254.6 36.3 %collective-permute-start.30 = (bf16[512,1536]{1,0:T(8,128)(2,1)}, bf16[512,1536]{1,0:T(8,128)(2,1)}, u32[]{:S(2)}, u32[]{:S(2)}) collective-permute-start(bf16[512,1536]{1,0:T(8,128)(2,1)} %get-tuple-element.268), channel_id=1, source_target_pairs={{0,1},{1,0},{2,3},{3,2},{4,5},{5,4},{6,7},{7,6},{8,9},{9,8},{10,11... | collective-permute-start | bytes 4718600 | tf_op jit(solution)/shard_map/ppermute | solution.py:885
  260.9 41.7 %collective-permute-start.34 = (bf16[192,1536]{1,0:T(8,128)(2,1)}, bf16[192,1536]{1,0:T(8,128)(2,1)}, u32[]{:S(2)}, u32[]{:S(2)}) collective-permute-start(bf16[192,1536]{1,0:T(8,128)(2,1)} %get-tuple-element.276.refs_5_), channel_id=1, source_target_pairs={{0,8},{4,12},{8,0},{12,4},{16,24},{20,28},{24,16},{28,20},{1,9},{5... | collective-permute-start | bytes 1769480 | tf_op jit(solution)/shard_map/ppermute | solution.py:844
  261.3 41.2 %collective-permute-start.35 = (bf16[192,1536]{1,0:T(8,128)(2,1)}, bf16[192,1536]{1,0:T(8,128)(2,1)}, u32[]{:S(2)}, u32[]{:S(2)}) collective-permute-start(bf16[192,1536]{1,0:T(8,128)(2,1)} %get-tuple-element.280), channel_id=1, source_target_pairs={{0,16},{4,20},{8,24},{12,28},{16,0},{20,4},{24,8},{28,12},{1,17},{... | collective-permute-start | bytes 1769480 | tf_op jit(solution)/shard_map/ppermute | solution.py:844
  279.2 26.5 %collective-permute-start.33 = (bf16[768,3072]{1,0:T(8,128)(2,1)}, bf16[768,3072]{1,0:T(8,128)(2,1)S(1)}, u32[]{:S(2)}, u32[]{:S(2)}) collective-permute-start(bf16[768,3072]{1,0:T(8,128)(2,1)} %get-tuple-element.277.refs_9_), channel_id=1, source_target_pairs={{0,4},{4,0},{8,12},{12,8},{16,20},{20,16},{24,28},{28,24},{1,5},{5... | collective-permute-start | bytes 14155784 | tf_op jit(solution)/shard_map/ppermute | solution.py:844
  302.2 20.7 %collective-permute-start.39 = (bf16[512,768]{1,0:T(8,128)(2,1)}, bf16[512,768]{1,0:T(8,128)(2,1)}, u32[]{:S(2)}, u32[]{:S(2)}) collective-permute-start(bf16[512,768]{1,0:T(8,128)(2,1)} %get-tuple-element.289), channel_id=1, source_target_pairs={{1,0},{0,1},{3,2},{2,3},{5,4},{4,5},{7,6},{6,7},{9,8},{8,9},{11,10... | collective-permute-start | bytes 2359304 | tf_op jit(solution)/shard_map/ppermute | solution.py:837
  314.8 41.4 %collective-permute-start.37 = (bf16[384,1536]{1,0:T(8,128)(2,1)}, bf16[384,1536]{1,0:T(8,128)(2,1)}, u32[]{:S(2)}, u32[]{:S(2)}) collective-permute-start(bf16[384,1536]{1,0:T(8,128)(2,1)} %get-tuple-element.283.refs_5_), channel_id=1, source_target_pairs={{0,16},{4,20},{8,24},{12,28},{16,0},{20,4},{24,8},{28,12},{1,17},{... | collective-permute-start | bytes 3538952 | tf_op jit(solution)/shard_map/ppermute | solution.py:844
  322.8 40.0 %collective-permute-start.36 = (bf16[768,1536]{1,0:T(8,128)(2,1)}, bf16[768,1536]{1,0:T(8,128)(2,1)}, u32[]{:S(2)}, u32[]{:S(2)}) collective-permute-start(bf16[768,1536]{1,0:T(8,128)(2,1)} %get-tuple-element.293.refs_12_), channel_id=1, source_target_pairs={{0,4},{4,0},{8,12},{12,8},{16,20},{20,16},{24,28},{28,24},{1,5},{5... | collective-permute-start | bytes 7077896 | tf_op jit(solution)/shard_map/ppermute | solution.py:844
  322.9 33.3 %collective-permute-start.38 = (bf16[384,1536]{1,0:T(8,128)(2,1)}, bf16[384,1536]{1,0:T(8,128)(2,1)}, u32[]{:S(2)}, u32[]{:S(2)}) collective-permute-start(bf16[384,1536]{1,0:T(8,128)(2,1)} %get-tuple-element.288), channel_id=1, source_target_pairs={{0,8},{4,12},{8,0},{12,4},{16,24},{20,28},{24,16},{28,20},{1,9},{5... | collective-permute-start | bytes 3538952 | tf_op jit(solution)/shard_map/ppermute | solution.py:844
  324.3 43.2 %collective-permute-start.45 = (bf16[512,1536]{1,0:T(8,128)(2,1)}, bf16[512,1536]{1,0:T(8,128)(2,1)}, u32[]{:S(2)}, u32[]{:S(2)}) collective-permute-start(bf16[512,1536]{1,0:T(8,128)(2,1)} %get-tuple-element.310), channel_id=1, source_target_pairs={{0,1},{1,0},{2,3},{3,2},{4,5},{5,4},{6,7},{7,6},{8,9},{9,8},{10,11... | collective-permute-start | bytes 4718600 | tf_op jit(solution)/shard_map/ppermute | solution.py:885
  360.4 16.5 %collective-permute-start.42 = (bf16[192,1536]{1,0:T(8,128)(2,1)}, bf16[192,1536]{1,0:T(8,128)(2,1)}, u32[]{:S(2)}, u32[]{:S(2)}) collective-permute-start(bf16[192,1536]{1,0:T(8,128)(2,1)} %get-tuple-element.301.refs_8_), channel_id=1, source_target_pairs={{0,8},{4,12},{8,0},{12,4},{16,24},{20,28},{24,16},{28,20},{1,9},{5... | collective-permute-start | bytes 1769480 | tf_op jit(solution)/shard_map/ppermute | solution.py:844
  361.1 16.5 %collective-permute-start.43 = (bf16[192,1536]{1,0:T(8,128)(2,1)}, bf16[192,1536]{1,0:T(8,128)(2,1)}, u32[]{:S(2)}, u32[]{:S(2)}) collective-permute-start(bf16[192,1536]{1,0:T(8,128)(2,1)} %get-tuple-element.308), channel_id=1, source_target_pairs={{0,16},{4,20},{8,24},{12,28},{16,0},{20,4},{24,8},{28,12},{1,17},{... | collective-permute-start | bytes 1769480 | tf_op jit(solution)/shard_map/ppermute | solution.py:844
  367.1 35.3 %collective-permute-start.40 = (bf16[384,768]{1,0:T(8,128)(2,1)}, bf16[384,768]{1,0:T(8,128)(2,1)}, u32[]{:S(2)}, u32[]{:S(2)}) collective-permute-start(bf16[384,768]{1,0:T(8,128)(2,1)} %get-tuple-element.311.refs_8_), channel_id=1, source_target_pairs={{0,16},{4,20},{8,24},{12,28},{16,0},{20,4},{24,8},{28,12},{1,17},{... | collective-permute-start | bytes 1769480 | tf_op jit(solution)/shard_map/ppermute | solution.py:844
  367.5 34.9 %collective-permute-start.41 = (bf16[384,768]{1,0:T(8,128)(2,1)}, bf16[384,768]{1,0:T(8,128)(2,1)}, u32[]{:S(2)}, u32[]{:S(2)}) collective-permute-start(bf16[384,768]{1,0:T(8,128)(2,1)} %get-tuple-element.305), channel_id=1, source_target_pairs={{0,8},{4,12},{8,0},{12,4},{16,24},{20,28},{24,16},{28,20},{1,9},{5... | collective-permute-start | bytes 1769480 | tf_op jit(solution)/shard_map/ppermute | solution.py:844
  373.6 32.8 %collective-permute-start.48 = (bf16[384,896]{1,0:T(8,128)(2,1)}, bf16[384,896]{1,0:T(8,128)(2,1)}, u32[]{:S(2)}, u32[]{:S(2)}) collective-permute-start(bf16[384,896]{1,0:T(8,128)(2,1)} %get-tuple-element.313.refs_12_), channel_id=1, source_target_pairs={{0,16},{4,20},{8,24},{12,28},{16,0},{20,4},{24,8},{28,12},{1,17},{... | collective-permute-start | bytes 2064392 | tf_op jit(solution)/shard_map/ppermute | solution.py:844
  377.6 28.7 %collective-permute-start.49 = (bf16[384,896]{1,0:T(8,128)(2,1)}, bf16[384,896]{1,0:T(8,128)(2,1)}, u32[]{:S(2)}, u32[]{:S(2)}) collective-permute-start(bf16[384,896]{1,0:T(8,128)(2,1)} %get-tuple-element.320), channel_id=1, source_target_pairs={{0,8},{4,12},{8,0},{12,4},{16,24},{20,28},{24,16},{28,20},{1,9},{5... | collective-permute-start | bytes 2064392 | tf_op jit(solution)/shard_map/ppermute | solution.py:844
  381.7 53.7 %collective-permute-start.52 = (bf16[192,3072]{1,0:T(8,128)(2,1)}, bf16[192,3072]{1,0:T(8,128)(2,1)}, u32[]{:S(2)}, u32[]{:S(2)}) collective-permute-start(bf16[192,3072]{1,0:T(8,128)(2,1)} %pad_maximum_fusion.1), channel_id=1, source_target_pairs={{0,2},{1,3},{2,0},{3,1},{4,6},{5,7},{6,4},{7,5},{8,10},{9,11},{10,... | collective-permute-start | bytes 3538952 | tf_op jit(solution)/shard_map/ppermute | solution.py:841
  405.7 37.0 %collective-permute-start.46 = (bf16[192,768]{1,0:T(8,128)(2,1)}, bf16[192,768]{1,0:T(8,128)(2,1)}, u32[]{:S(2)}, u32[]{:S(2)}) collective-permute-start(bf16[192,768]{1,0:T(8,128)(2,1)} %get-tuple-element.316.refs_8_), channel_id=1, source_target_pairs={{0,8},{4,12},{8,0},{12,4},{16,24},{20,28},{24,16},{28,20},{1,9},{5... | collective-permute-start | bytes 884744 | tf_op jit(solution)/shard_map/ppermute | solution.py:844
  409.9 26.7 %collective-permute-start.50 = (bf16[192,896]{1,0:T(8,128)(2,1)}, bf16[192,896]{1,0:T(8,128)(2,1)}, u32[]{:S(2)}, u32[]{:S(2)}) collective-permute-start(bf16[192,896]{1,0:T(8,128)(2,1)} %get-tuple-element.321.refs_6_), channel_id=1, source_target_pairs={{0,8},{4,12},{8,0},{12,4},{16,24},{20,28},{24,16},{28,20},{1,9},{5... | collective-permute-start | bytes 1032200 | tf_op jit(solution)/shard_map/ppermute | solution.py:844
  411.2 26.7 %collective-permute-start.51 = (bf16[192,896]{1,0:T(8,128)(2,1)}, bf16[192,896]{1,0:T(8,128)(2,1)}, u32[]{:S(2)}, u32[]{:S(2)}) collective-permute-start(bf16[192,896]{1,0:T(8,128)(2,1)} %get-tuple-element.322), channel_id=1, source_target_pairs={{0,16},{4,20},{8,24},{12,28},{16,0},{20,4},{24,8},{28,12},{1,17},{... | collective-permute-start | bytes 1032200 | tf_op jit(solution)/shard_map/ppermute | solution.py:844
  423.7 24.2 %collective-permute-start.53 = (bf16[768,1792]{1,0:T(8,128)(2,1)}, bf16[768,1792]{1,0:T(8,128)(2,1)}, u32[]{:S(2)}, u32[]{:S(2)}) collective-permute-start(bf16[768,1792]{1,0:T(8,128)(2,1)} %get-tuple-element.332.refs_21_), channel_id=1, source_target_pairs={{0,4},{4,0},{8,12},{12,8},{16,20},{20,16},{24,28},{28,24},{1,5},{5... | collective-permute-start | bytes 8257544 | tf_op jit(solution)/shard_map/ppermute | solution.py:844
  436.6 89.0 %collective-permute-start.59 = (bf16[512,1536]{1,0:T(8,128)(2,1)}, bf16[512,1536]{1,0:T(8,128)(2,1)}, u32[]{:S(2)}, u32[]{:S(2)}) collective-permute-start(bf16[512,1536]{1,0:T(8,128)(2,1)} %get-tuple-element.363), channel_id=1, source_target_pairs={{0,1},{1,0},{2,3},{3,2},{4,5},{5,4},{6,7},{7,6},{8,9},{9,8},{10,11... | collective-permute-start | bytes 4718600 | tf_op jit(solution)/shard_map/ppermute | solution.py:885
  441.2 45.7 %collective-permute-start.58 = (bf16[192,1792]{1,0:T(8,128)(2,1)}, bf16[192,1792]{1,0:T(8,128)(2,1)}, u32[]{:S(2)}, u32[]{:S(2)}) collective-permute-start(bf16[192,1792]{1,0:T(8,128)(2,1)} %pad_maximum_fusion.6), channel_id=1, source_target_pairs={{0,2},{1,3},{2,0},{3,1},{4,6},{5,7},{6,4},{7,5},{8,10},{9,11},{10,... | collective-permute-start | bytes 2064392 | tf_op jit(solution)/shard_map/ppermute | solution.py:841
  452.5 40.6 %collective-permute-start.56 = (bf16[384,896]{1,0:T(8,128)(2,1)}, bf16[384,896]{1,0:T(8,128)(2,1)S(1)}, u32[]{:S(2)}, u32[]{:S(2)}) collective-permute-start(bf16[384,896]{1,0:T(8,128)(2,1)} %get-tuple-element.345.refs_21_), channel_id=1, source_target_pairs={{0,16},{4,20},{8,24},{12,28},{16,0},{20,4},{24,8},{28,12},{1,17},{... | collective-permute-start | bytes 2064392 | tf_op jit(solution)/shard_map/ppermute | solution.py:844
  453.7 39.5 %collective-permute-start.57 = (bf16[384,896]{1,0:T(8,128)(2,1)}, bf16[384,896]{1,0:T(8,128)(2,1)S(1)}, u32[]{:S(2)}, u32[]{:S(2)}) collective-permute-start(bf16[384,896]{1,0:T(8,128)(2,1)} %get-tuple-element.349), channel_id=1, source_target_pairs={{0,8},{4,12},{8,0},{12,4},{16,24},{20,28},{24,16},{28,20},{1,9},{5... | collective-permute-start | bytes 2064392 | tf_op jit(solution)/shard_map/ppermute | solution.py:844
  487.9 17.4 %collective-permute-start.54 = (bf16[192,768]{1,0:T(8,128)(2,1)S(1)}, bf16[192,768]{1,0:T(8,128)(2,1)S(1)}, u32[]{:S(2)}, u32[]{:S(2)}) collective-permute-start(bf16[192,768]{1,0:T(8,128)(2,1)S(1)} %bitcast.20), channel_id=1, source_target_pairs={{0,2},{1,3},{2,0},{3,1},{4,6},{5,7},{6,4},{7,5},{8,10},{9,11},{10,... | collective-permute-start | bytes 884744 | tf_op jit(solution)/shard_map/ppermute | solution.py:841
  506.6 17.1 %collective-permute-start.60 = (bf16[192,384]{1,0:T(8,128)(2,1)S(1)}, bf16[192,384]{1,0:T(8,128)(2,1)S(1)}, u32[]{:S(2)}, u32[]{:S(2)}) collective-permute-start(bf16[192,384]{1,0:T(8,128)(2,1)S(1)} %slice.128), channel_id=1, source_target_pairs={{0,1},{1,0},{2,3},{3,2},{4,5},{5,4},{6,7},{7,6},{8,9},{9,8},{10,11... | collective-permute-start | bytes 442376 | tf_op jit(solution)/shard_map/ppermute | solution.py:841
  (61 other events, 593.0 us)

commit v5 on v4

--- a/solution.py
+++ b/solution.py
@@ -280,6 +280,7 @@
         lane1 = lax.broadcasted_iota(jnp.int32, (BLK, 128), 1)
         tri = lax.broadcasted_iota(jnp.int32, (BLK, BLK), 0) >= lax.broadcasted_iota(jnp.int32, (BLK, BLK), 1)
         crows = crow_ref[0]
+        v_wide = jnp.concatenate([v_ref[...], jnp.ones((length, 128), bf16)], axis=1)
         for i in range(length // BLK):
             rows = pl.ds(i * BLK, BLK)
             reach = (i + 1) * BLK
@@ -289,17 +290,21 @@
                 allowed = jnp.concatenate([same[:, :reach - BLK], same[:, reach - BLK:] & tri], axis=1)
             else:
                 allowed = same & tri
+            scores = last(jnp.concatenate([jnp.where(lane == h, q, 0) for h in range(hp)], axis=0), k_ref[:reach, :])
+            tops, grown = [], []
+            for h in range(hp):
+                s = jnp.where(allowed, scores[h * BLK:(h + 1) * BLK] - crows[h:h + 1, :reach], -1e30)
+                top = jnp.max(s, axis=1, keepdims=True)
+                tops.append(top)
+                grown.append(low(jnp.exp2(s - top)))
+            parts = mm(jnp.concatenate(grown, axis=0), v_wide[:reach, :])
             out = jnp.zeros((BLK, width), f32)
             stats = jnp.zeros((BLK, 128), f32)
             for h in range(hp):
-                s = last(jnp.where(lane == h, q, 0), k_ref[:reach, :])
-                s = jnp.where(allowed, s - crows[h:h + 1, :reach], -1e30)
-                top = jnp.max(s, axis=1, keepdims=True)
-                e = jnp.exp2(s - top)
-                total = jnp.sum(e, axis=1, keepdims=True)
-                part = mm(low(e), v_ref[:reach, :])
-                out = jnp.where(lane == h, part * (1.0 / total), out)
-                stats = jnp.where(lane1 == h, top + jnp.log2(total), stats)
+                part = parts[h * BLK:(h + 1) * BLK]
+                total = part[:, width:width + 1]
+                out = jnp.where(lane == h, part[:, :width] * (1.0 / total), out)
+                stats = jnp.where(lane1 == h, tops[h] + jnp.log2(total), stats)
             z_ref[rows, :] = low(out * jax.nn.sigmoid(g_ref[rows, :].astype(f32)))
             lse_ref[0, :, i * BLK:(i + 1) * BLK] = stats.T[:hp, :]
 
@@ -328,7 +333,7 @@
         dz_refs = ins[5:5 + group]
         lse_ref, ccol_ref, f_ref, scol_ref, srow_ref = ins[5 + group:]
         dq_ref, dk_ref, dv_ref, dg_ref, df_ref, db_ref = outs
-        dqacc, dkacc, rates, dzfull = scratch
+        dqacc, rates, dzfull = scratch
         step = pl.program_id(0)
         lane = lax.broadcasted_iota(jnp.int32, (1, width), 1) // HEAD
         lane1 = lax.broadcasted_iota(jnp.int32, (1, 128), 1)
@@ -350,48 +355,55 @@
         prod_hi = low(prod)
         prod_lo = low(prod - prod_hi.astype(f32))
         lses = lse_ref[0]
+        chosen = lax.broadcasted_iota(jnp.int32, (8, width), 0) == lax.broadcasted_iota(jnp.int32, (8, width), 1) // HEAD
+        chosen = jnp.where(chosen, 1.0, 0.0).astype(bf16)
+        centres = last(chosen, prod_hi) + last(chosen, prod_lo)
+        ones = jnp.ones((length, 128), bf16)
+        q_wide = jnp.concatenate([q_ref[...], ones], axis=1)
+        k_wide = jnp.concatenate([k_ref[...], ones], axis=1)
+        decays = [
+            jnp.sum(jnp.where(lane1[:, :heads] == step * hp + h, ccol_ref[...], 0.0), axis=1, keepdims=True)
+            for h in range(hp)
+        ]
+        dqacc[...] = jnp.zeros_like(dqacc)
+        for j in range(blocks):
+            keys = pl.ds(j * BLK, BLK)
+            lo = j * BLK
+            count = length - lo
+            keyed = lambda ref: jnp.concatenate([jnp.where(lane == h, ref[keys, :], 0) for h in range(hp)], axis=0)
+            scores = last(keyed(k_ref), q_ref[lo:, :])
+            dps = last(keyed(v_ref), dout[lo:, :])
+            same = scol_ref[keys, :] == srow_ref[:, lo:]
+            if j < blocks - 1:
+                allowed = jnp.concatenate([same[:, :BLK] & tri, same[:, BLK:]], axis=1)
+            else:
+                allowed = same & tri
+            ps, dss = [], []
+            for h in range(hp):
+                rows = slice(h * BLK, (h + 1) * BLK)
+                s = scores[rows] - decays[h][lo:lo + BLK, :] - lses[h:h + 1, lo:]
+                p = jnp.exp2(jnp.where(allowed, s, -1e30))
+                ps.append(low(p))
+                dss.append(low(p * (dps[rows] - centres[h:h + 1, lo:])))
+            dvs = mm(jnp.concatenate(ps, axis=0), dout[lo:, :])
+            dks = mm(jnp.concatenate(dss, axis=0), q_wide[lo:, :])
+            dqs = first(jnp.concatenate(dss, axis=1), k_wide[lo:lo + BLK, :])
+            dk = jnp.zeros((BLK, width), f32)
+            dv = jnp.zeros((BLK, width), f32)
+            for h in range(hp):
+                rows = slice(h * BLK, (h + 1) * BLK)
+                dk = jnp.where(lane == h, dks[rows, :width], dk)
+                dv = jnp.where(lane == h, dvs[rows], dv)
+                rates[keys, :] = jnp.where(lane1 == step * hp + h, -dks[rows, width:width + 1], rates[keys, :])
+                dqacc[h * length + lo:(h + 1) * length, :] += dqs[h * count:(h + 1) * count]
+            dk_ref[keys, :] = low(dk * LN2)
+            dv_ref[keys, :] = low(dv)
+        dq = jnp.zeros((length, width), f32)
         for h in range(hp):
-            head = lane == h
-            index = step * hp + h
-            decay = jnp.sum(jnp.where(lane1[:, :heads] == index, ccol_ref[...], 0.0), axis=1, keepdims=True)
-            ones = jnp.broadcast_to(jnp.where(head, 1.0, 0.0).astype(bf16), (8, width))
-            centre = (last(ones, prod_hi) + last(ones, prod_lo))[0:1, :]
-            q_one = jnp.where(head, q_ref[...], 1.0)
-            q_zero = jnp.where(head, q_ref[...], 0.0)
-            k_one = jnp.where(head, k_ref[...], 1.0)
-            d_zero = jnp.where(head, dout, 0.0)
-            dqacc[...] = jnp.zeros_like(dqacc)
-            for j in range(blocks):
-                keys = pl.ds(j * BLK, BLK)
-                lo = j * BLK
-                s = last(k_ref[keys, :], q_zero[lo:, :])
-                s = s - decay[lo:lo + BLK, :] - lses[h:h + 1, lo:]
-                same = scol_ref[keys, :] == srow_ref[:, lo:]
-                if j < blocks - 1:
-                    allowed = jnp.concatenate([same[:, :BLK] & tri, same[:, BLK:]], axis=1)
-                else:
-                    allowed = same & tri
-                p = jnp.exp2(jnp.where(allowed, s, -1e30))
-                dp = last(v_ref[keys, :], d_zero[lo:, :])
-                ds = low(p * (dp - centre[:, lo:]))
-                dv = mm(low(p), dout[lo:, :])
-                dk = mm(ds, q_one[lo:, :])
-                dqacc[lo:, :] += first(ds, k_one[lo:lo + BLK, :])
-                dkacc[keys, :] = dk
-                if h == 0:
-                    dk_ref[keys, :] = low(dk * LN2)
-                    dv_ref[keys, :] = low(dv)
-                else:
-                    dk_ref[keys, :] = jnp.where(head, low(dk * LN2), dk_ref[keys, :])
-                    dv_ref[keys, :] = jnp.where(head, low(dv), dv_ref[keys, :])
-            dq = dqacc[...]
-            if h == 0:
-                dq_ref[...] = low(dq * HEAD ** -0.5)
-            else:
-                dq_ref[...] = jnp.where(head, low(dq * HEAD ** -0.5), dq_ref[...])
-            spare = HEAD if h == 0 else 0
-            rate = (dq - dkacc[...])[:, spare:spare + 1]
-            rates[...] = jnp.where(lane1 == index, rate, rates[...])
+            part = dqacc[h * length:(h + 1) * length, :]
+            dq = jnp.where(lane == h, part[:, :width], dq)
+            rates[...] = jnp.where(lane1 == step * hp + h, rates[...] + part[:, width:width + 1], rates[...])
+        dq_ref[...] = low(dq * HEAD ** -0.5)
 
         @pl.when(step == steps - 1)
         def _():
@@ -415,8 +427,7 @@
         + [(a, (share, width), lambda i, w, off=off: (0, off + i)) for a, off in dz_parts]
         + [(lse, (1, hp, length), lambda i, w: (i, 0, 0))] + [fixed(a) for a in (ccol, forget, scol, srow)],
         [wide] * 4 + [fixed_out((length, heads), bf16), fixed_out((1, heads), f32)],
-        [pltpu.VMEM((length, width), f32), pltpu.VMEM((length, width), f32), pltpu.VMEM((length, 128), f32),
-         pltpu.VMEM((length, width), bf16)],
+        [pltpu.VMEM((hp * length, width + 128), f32), pltpu.VMEM((length, 128), f32), pltpu.VMEM((length, width), bf16)],
         after, heads * length * length * 1500,
     )
 
@@ -959,26 +970,26 @@
         for s in range(1, group):
             gated[s, j] = arrived[s - 1]
 
-    arrived = go.sync(*attn_got, *bias_got, attn_pieces[1])
-    attn_got, bias_got = arrived[:rows - 1], arrived[rows - 1:-1]
-    attn_later = [here.fetch(arrived[-1], 0, j) for j in turns]
+    out_piece = go(collect, [w_out], pieces)
+    arrived = go.sync(*attn_got, *bias_got, attn_pieces[1], out_piece)
+    attn_got, bias_got = arrived[:rows - 1], arrived[rows - 1:-2]
+    attn_later = [here.fetch(arrived[-2], 0, j) for j in turns]
     attn_gather = [[Gather(p)] for p in attn_got]
     attend(0)
+    out_got = [here.fetch(arrived[-1], 0, j) for j in turns]
     for gathers, p in zip(attn_gather, go.sync(*attn_later)):
         gathers[0].wait()
         gathers.append(Gather(p))
-    out_piece = go(collect, [w_out], pieces)
     attn_w = [[gathers[0].close()] for gathers in attn_gather]
-    out_got = [here.fetch(out_piece, 0, j) for j in turns]
     gate_piece = go(collect, [w_gate, w_up], pieces)
     wait_gated(0)
+    out_got = go.sync(*out_got)
+    out_own = jnp.concatenate([out_piece, *out_got], axis=1)
+    out_peers = [here.fetch(out_own, s, 0) for s in range(1, group)]
     for gathers in attn_gather:
         gathers[1].wait()
     for done, gathers in zip(attn_w, attn_gather):
         done.append(gathers[1].close())
-    out_got = go.sync(*out_got)
-    out_own = jnp.concatenate([out_piece, *out_got], axis=1)
-    out_peers = [here.fetch(out_own, s, 0) for s in range(1, group)]
     gate_piece = go.sync(gate_piece)[0]
     gate_got = [here.fetch(gate_piece, 0, j) for j in turns]
     for j in turns:
@@ -1091,13 +1102,13 @@
                 name, w, s, group, list(back[0][:5]), own_w, pair_terms, normed, gain_attn, after)))
         return [o[0] for o in outs] + [sum(o[1] for o in outs)]
 
-    made = attn_back("attn_back_send", peers)
-    got = [to_member(v, s) for v, s in zip(made, peers)]
     mlp_other = go.sync(*mlp_other)
     for j in turns:
         attn_sums[j].wait()
     attn_other = [here.deliver(low(attn_sums[j].close()), 0, j) for j in turns]
     out_sum.wait()
+    made = attn_back("attn_back_send", peers)
+    got = [to_member(v, s) for v, s in zip(made, peers)]
     attn_sums[0].hop()
     out_part = out_sum.close().reshape(-1, group, rows, width)
     out_part = go.sync(out_part)[0]

time: 541 us -> 532 us (0.983)
  waiting for transfers between devices: 81.2 us -> 74.1 us
    unnamed x89 -> x85, local copies, waits for them, and re-layouts: 10.8 us -> 11.8 us
  transfers between devices with their start and end apart: 67 -> 67, of which waited for: 17 -> 15; matrix products, arithmetic and copies ran while one was open for 7% -> 7% of each run, Pallas kernels for 61% -> 62%
where the time goes in v5:
time: 532 us; the launch traced here: 523 us
  Pallas kernels  334 us (63%)
  waiting for transfers between devices  74.1 us (14%)
  starting transfers between devices  67.1 us (13%)
  local copies, waits for them, and re-layouts  23.8 us (4%)
  other arithmetic  22.3 us (4%)
    pallas_call x26, Pallas kernels, run(): pl.pallas_call(kernel, grid_spec=pltpu.PrefetchScalarGridSpec(num_scalar_...  247 us
    pallas_call x6, Pallas kernels, stream(): pl.pallas_call(kernel, grid_spec=pltpu.PrefetchScalarGridSpec(num_scalar_...  70.4 us
    ppermute x48, starting transfers between devices, swap(): return lax.ppermute(value, 'dp', [(i, i ^ bit) for i in range(self.dp)])  42.2 us
    ppermute x48, waiting for transfers between devices, swap(): return lax.ppermute(value, 'dp', [(i, i ^ bit) for i in range(self.dp)])  21.7 us
    ppermute x10, waiting for transfers between devices, fetch(): return lax.ppermute(value, 'tensor', pairs)  17.4 us
    pallas_call x5, Pallas kernels, assemble(): pl.pallas_call(kernel, grid_spec=pltpu.PrefetchScalarGridSpec(num_scalar_...  16.8 us
    ppermute x4, waiting for transfers between devices, deliver(): return lax.ppermute(value, 'tensor', pairs)  16.6 us
    ppermute x10, starting transfers between devices, fetch(): return lax.ppermute(value, 'tensor', pairs)  13.5 us
  transfers between devices with their start and end apart: 67, of which 15 were waited for; matrix products, arithmetic and copies ran while one was open for 7% of the time, Pallas kernels for 62%

profile of v5, /device:TPU:0, one launch (start us, length us, event | category | flops | bytes accessed | tf_op | source)
XLA Modules:
  0.0 523.1 jit_solution(4971040911049402485)
XLA Ops:
  1.3 2.5 collect.5.refs_3_
  3.8 4.0 collective-permute-start
  11.9 12.8 %project_own.1 = (bf16[1024,1536]{1,0:T(8,128)(2,1)}, f32[1024,1]{1,0:T(8,128)}, bf16[1024,384]{1,0:T(8,128)(2,1)}, bf16[1024,384]{1,0:T(8,128)(2,1)}, bf16[1024...) custom-call(s32[5]{0:T(128)} %stack.23.where_ref.w, ...), custom_call_target="tpu_custom_call" | custom-call | flops 115000000512 | bytes 1 | tf_op jit(solution)/shard_map/project_own/pallas_call | solution.py:51
  32.2 2.9 collective-permute-start.7
  35.1 12.2 %attend_forward.2 = (bf16[1024,384]{1,0:T(8,128)(2,1)}, f32[3,2,1024]{2,1,0:T(2,128)}) custom-call(s32[5]{0:T(128)} %stack.23.where_ref.w, bf16[1024,384]{1,0:T(8,128)(2,1)} %get-tuple-element.206.refs_0_, bf16[1024,384]{1,0:T(8,128)(2,1)} %get-tuple-element.207.refs_1_, bf16[1024,384]{1,0:T(8,128)(2,1)} %get-tuple-element.208.refs_2_, ...), custom_call_target="tpu_custom_call" | custom-call | flops 115000000512 | bytes 1 | tf_op jit(solution)/shard_map/attend_forward/pallas_call | solution.py:51
  53.2 3.0 assemble.5.refs_2_.refs_12_
  56.2 2.7 collect.8.refs_4_
  58.9 10.4 %collective-permute-done.3.refs_7_.refs_3_ = bf16[1024,384]{1,0:T(8,128)(2,1)} collective-permute-done((bf16[1024,384]{1,0:T(8,128)(2,1)}, bf16[1024,384]{1,0:T(8,128)(2,1)}, u32[]{:S(2)}, u32[]{:S(2)}) %collective-permute-start.3) | collective-permute-done | bytes 786464 | tf_op jit(solution)/shard_map/ppermute | solution.py:848
  69.3 3.1 assemble.6.refs_4_.refs_6_.refs_17_
  74.6 2.8 collective-permute-start.8
  80.8 11.5 %project_other.1 = (bf16[1024,384]{1,0:T(8,128)(2,1)}, bf16[1024,384]{1,0:T(8,128)(2,1)}, bf16[1024,384]{1,0:T(8,128)(2,1)}, bf16[1024,384]{1,0:T(8,128)(2,1)}, ...) custom-call(s32[5]{0:T(128)} %stack.23.where_ref.w, ...), custom_call_target="tpu_custom_call" | custom-call | flops 115000000512 | bytes 1 | tf_op jit(solution)/shard_map/project_other/pallas_call | solution.py:51
  95.9 12.4 %attend_forward.3 = (bf16[1024,384]{1,0:T(8,128)(2,1)}, f32[3,2,1024]{2,1,0:T(2,128)}) custom-call(s32[5]{0:T(128)} %stack.23.where_ref.w, bf16[1024,384]{1,0:T(8,128)(2,1)} %get-tuple-element.234.refs_0_, bf16[1024,384]{1,0:T(8,128)(2,1)} %get-tuple-element.235.refs_1_, bf16[1024,384]{1,0:T(8,128)(2,1)} %get-tuple-element.236.refs_2_, ...), custom_call_target="tpu_custom_call" | custom-call | flops 115000000512 | bytes 1 | tf_op jit(solution)/shard_map/attend_forward/pallas_call | solution.py:51
  108.8 5.9 %collective-permute-done.15.refs_2_ = bf16[192,1152]{1,0:T(8,128)(2,1)S(1)} collective-permute-done((bf16[192,1152]{1,0:T(8,128)(2,1)S(1)}, bf16[192,1152]{1,0:T(8,128)(2,1)S(1)}, u32[]{:S(2)}, u32[]{:S(2)}) %collective-permute-start.15) | collective-permute-done | bytes 442400 | tf_op jit(solution)/shard_map/ppermute | solution.py:855
  115.6 3.4 assemble.7.refs_1_.refs_2_.refs_6_
  125.1 6.5 %collective-permute-done.19.refs_8_.refs_4_ = bf16[1024,384]{1,0:T(8,128)(2,1)} collective-permute-done((bf16[1024,384]{1,0:T(8,128)(2,1)}, bf16[1024,384]{1,0:T(8,128)(2,1)}, u32[]{:S(2)}, u32[]{:S(2)}) %collective-permute-start.19) | collective-permute-done | bytes 786464 | tf_op jit(solution)/shard_map/ppermute | solution.py:848
  132.8 12.5 %close_attention.1 = (f32[1024,1536]{1,0:T(8,128)}, bf16[1024,1536]{1,0:T(8,128)(2,1)}, f32[1024,1]{1,0:T(8,128)}) custom-call(s32[5]{0:T(128)} %stack.23.where_ref.w, bf16[2048,1536]{1,0:T(8,128)(2,1)} %refs_1_.13, bf16[1536,384]{1,0:T(8,128)(2,1)} %refs_5_.7, bf16[768,1152]{1,0:T(8,128)(2,1)} %assemble.7.refs_1_.refs_2_.refs_6_, ...), custom_call_target="tpu_custom_call" | custom-call | flops 115000000512 | bytes 1 | tf_op jit(solution)/shard_map/close_attention/pallas_call | solution.py:51
  145.3 10.3 %collective-permute-done.21.refs_2_ = bf16[192,2048]{1,0:T(8,128)(2,1)} collective-permute-done((bf16[192,2048]{1,0:T(8,128)(2,1)}, bf16[192,2048]{1,0:T(8,128)(2,1)}, u32[]{:S(2)}, u32[]{:S(2)}) %collective-permute-start.21) | collective-permute-done | bytes 786464 | tf_op jit(solution)/shard_map/ppermute | solution.py:855
  160.7 40.1 %feed_forward.2 = (bf16[768,3072]{1,0:T(8,128)(2,1)}, bf16[768,3072]{1,0:T(8,128)(2,1)}, bf16[1024,1536]{1,0:T(8,128)(2,1)}, bf16[1024,1536]{1,0:T(8,128)(2,1)}) custom-call(s32[5]{0:T(128)} %stack.23.where_ref.w, bf16[1024,1536]{1,0:T(8,128)(2,1)} %get-tuple-element.253.refs_0_, bf16[2048,1536]{1,0:T(8,128)(2,1)} %refs_4_.5, ...), custom_call_target="tpu_custom_call" | custom-call | flops 115000000512 | bytes 1 | tf_op jit(solution)/shard_map/feed_forward/pallas_call | solution.py:51
  200.9 4.2 assemble.8.refs_4_.refs_3_
  205.6 3.3 assemble.9.refs_8_.refs_5_
  209.1 7.0 %fold.10 = (bf16[384,1536]{1,0:T(8,128)(2,1)}, bf16[384,1536]{1,0:T(8,128)(2,1)}, bf16[384,1536]{1,0:T(8,128)(2,1)}, bf16[384,1536]{1,0:T(8,128)(2,1)}) custom-call(s32[5]{0:T(128)} %stack.23.where_ref.w, bf16[768,3072]{1,0:T(8,128)(2,1)} %get-tuple-element.265.refs_0_.refs_2_.refs_4_.refs_6_, ...), custom_call_target="tpu_custom_call" | custom-call | flops 115000000512 | bytes 1 | tf_op jit(solution)/shard_map/fold/pallas_call | solution.py:51
  219.6 34.1 %feed_forward.3 = (bf16[1024,1024]{1,0:T(8,128)(2,1)}, bf16[1024,1024]{1,0:T(8,128)(2,1)}, bf16[1024,1024]{1,0:T(8,128)(2,1)}, bf16[512,1536]{1,0:T(8,128)(2,1)}...) custom-call(s32[5]{0:T(128)} %stack.23.where_ref.w, ...), custom_call_target="tpu_custom_call" | custom-call | flops 115000000512 | bytes 1 | tf_op jit(solution)/shard_map/feed_forward/pallas_call | solution.py:51
  255.6 4.4 fold.11
  261.8 16.5 %mlp_grads.1 = (bf16[768,3072]{1,0:T(8,128)(2,1)}, bf16[768,3072]{1,0:T(8,128)(2,1)}) custom-call(s32[5]{0:T(128)} %stack.23.where_ref.w, bf16[1024,1536]{1,0:T(8,128)(2,1)} %get-tuple-element.253.refs_0_, bf16[1024,1024]{1,0:T(8,128)(2,1)} %get-tuple-element.271.refs_1_, bf16[1024,1024]{1,0:T(8,128)(2,1)} %get-tuple-element.272.refs_2_, ...), custom_call_target="tpu_custom_call" | custom-call | flops 115000000512 | bytes 1 | tf_op jit(solution)/shard_map/mlp_grads/pallas_call | solution.py:126
  278.5 11.5 %collective-permute-done.30.refs_8_ = bf16[512,1536]{1,0:T(8,128)(2,1)} collective-permute-done((bf16[512,1536]{1,0:T(8,128)(2,1)}, bf16[512,1536]{1,0:T(8,128)(2,1)}, u32[]{:S(2)}, u32[]{:S(2)}) %collective-permute-start.30) | collective-permute-done | bytes 1572896 | tf_op jit(solution)/shard_map/ppermute | solution.py:896
  290.0 11.1 %close_feed_forward.1 = (f32[512,1536]{1,0:T(8,128)}, bf16[512,1536]{1,0:T(8,128)(2,1)}, bf16[512,768]{1,0:T(8,128)(2,1)}, bf16[512,768]{1,0:T(8,128)(2,1)}) custom-call(s32[5]{0:T(128)} %stack.23.where_ref.w, bf16[512,1536]{1,0:T(8,128)(2,1)} %get-tuple-element.268.refs_0_, f32[1024,1536]{1,0:T(8,128)} %get-tuple-element.269.refs_1_, ...), custom_call_target="tpu_custom_call" | custom-call | flops 115000000512 | bytes 1 | tf_op jit(solution)/shard_map/close_feed_forward/pallas_call | solution.py:51
  306.8 6.9 %fold.12 = (bf16[384,1536]{1,0:T(8,128)(2,1)}, bf16[384,1536]{1,0:T(8,128)(2,1)}, bf16[384,1536]{1,0:T(8,128)(2,1)}, bf16[384,1536]{1,0:T(8,128)(2,1)}) custom-call(s32[5]{0:T(128)} %stack.23.where_ref.w, bf16[768,3072]{1,0:T(8,128)(2,1)} %get-tuple-element.281.refs_0_.refs_2_.refs_4_.refs_6_, bf16[768,3072]{1,0:T(8,128)(2,1)} %copy-done.23, ...), custom_call_target="tpu_custom_call" | custom-call | flops 115000000512 | bytes 1 | tf_op jit(solution)/shard_map/fold/pallas_call | solution.py:51
  314.7 7.6 %out_grads.1 = (bf16[768,1536]{1,0:T(8,128)(2,1)}, bf16[768,1536]{1,0:T(8,128)(2,1)}) custom-call(s32[5]{0:T(128)} %stack.23.where_ref.w, bf16[512,1536]{1,0:T(8,128)(2,1)} %get-tuple-element.280.refs_0_, bf16[1024,384]{1,0:T(8,128)(2,1)} %get-tuple-element.212.refs_5_.refs_1_.refs_4_, bf16[1024,384]{1,0:T(8,128)(2,1)} %get-tuple-element.247.refs_6_.refs_2_.refs_4_, ...), custom_call_target="tpu_custom_call" | custom-call | flops 115000000512 | bytes 1 | tf_op jit(solution)/shard_map/out_grads/pallas_call | solution.py:126
  324.9 17.6 %attend_backward.2 = (bf16[1024,384]{1,0:T(8,128)(2,1)}, bf16[1024,384]{1,0:T(8,128)(2,1)}, bf16[1024,384]{1,0:T(8,128)(2,1)}, bf16[1024,384]{1,0:T(8,128)(2,1)}...) custom-call(s32[5]{0:T(128)} %stack.23.where_ref.w, bf16[1024,384]{1,0:T(8,128)(2,1)} %get-tuple-element.234.refs_0_, ...), custom_call_target="tpu_custom_call" | custom-call | flops 115000000512 | bytes 1 | tf_op jit(solution)/shard_map/attend_backward/pallas_call | solution.py:51
  342.5 11.6 %attn_grads.2 = (bf16[768,1792]{1,0:T(8,128)(2,1)}, bf16[768,1792]{1,0:T(8,128)(2,1)}) custom-call(s32[5]{0:T(128)} %stack.23.where_ref.w, bf16[1024,1536]{1,0:T(8,128)(2,1)} %get-tuple-element.223.refs_0_.refs_19_, bf16[1024,384]{1,0:T(8,128)(2,1)} %get-tuple-element.296.refs_1_.refs_10_, bf16[1024,384]{1,0:T(8,128)(2,1)} %get-tuple-element.297.refs_2_.refs_11_, ...), custom_call_target="tpu_custom_call" | custom-call | flops 115000000512 | bytes 1 | tf_op jit(solution)/shard_map/attn_grads/pallas_call | solution.py:126
  354.2 4.3 fold.13
  360.9 4.2 fold.14
  367.0 4.7 fold.15
  380.7 17.4 %attend_backward.3 = (bf16[1024,384]{1,0:T(8,128)(2,1)}, bf16[1024,384]{1,0:T(8,128)(2,1)}, bf16[1024,384]{1,0:T(8,128)(2,1)}, bf16[1024,384]{1,0:T(8,128)(2,1)}...) custom-call(s32[5]{0:T(128)} %stack.23.where_ref.w, bf16[1024,384]{1,0:T(8,128)(2,1)} %get-tuple-element.206.refs_0_, ...), custom_call_target="tpu_custom_call" | custom-call | flops 115000000512 | bytes 1 | tf_op jit(solution)/shard_map/attend_backward/pallas_call | solution.py:51
  399.6 3.3 fold.16
  405.0 3.5 fold.17
  410.4 11.6 %attn_grads.3 = (bf16[768,1792]{1,0:T(8,128)(2,1)}, bf16[768,1792]{1,0:T(8,128)(2,1)}) custom-call(s32[5]{0:T(128)} %stack.23.where_ref.w, bf16[1024,1536]{1,0:T(8,128)(2,1)} %get-tuple-element.223.refs_0_.refs_19_, bf16[1024,384]{1,0:T(8,128)(2,1)} %get-tuple-element.329.refs_1_.refs_0_, bf16[1024,384]{1,0:T(8,128)(2,1)} %get-tuple-element.330.refs_2_.refs_1_, ...), custom_call_target="tpu_custom_call" | custom-call | flops 115000000512 | bytes 1 | tf_op jit(solution)/shard_map/attn_grads/pallas_call | solution.py:126
  422.1 10.3 %collective-permute-done.52 = bf16[192,3072]{1,0:T(8,128)(2,1)} collective-permute-done((bf16[192,3072]{1,0:T(8,128)(2,1)}, bf16[192,3072]{1,0:T(8,128)(2,1)}, u32[]{:S(2)}, u32[]{:S(2)}) %collective-permute-start.52) | collective-permute-done | bytes 1179680 | tf_op jit(solution)/shard_map/ppermute | solution.py:852
  433.5 11.6 %attn_back_send.1 = (bf16[512,1536]{1,0:T(8,128)(2,1)}, f32[1,1536]{1,0:T(1,128)}) custom-call(s32[5]{0:T(128)} %stack.23.where_ref.w, bf16[1024,384]{1,0:T(8,128)(2,1)} %get-tuple-element.329.refs_1_.refs_0_, bf16[1024,384]{1,0:T(8,128)(2,1)} %get-tuple-element.330.refs_2_.refs_1_, bf16[1024,384]{1,0:T(8,128)(2,1)} %get-tuple-element.331.refs_3_.refs_2_, ...), custom_call_target="tpu_custom_call" | custom-call | flops 115000000512 | bytes 1 | tf_op jit(solution)/shard_map/attn_back_send/pallas_call | solution.py:126
  451.7 4.6 fold.18
  458.5 11.4 %attn_back_own.1 = (bf16[512,1536]{1,0:T(8,128)(2,1)}, f32[1,1536]{1,0:T(1,128)}) custom-call(s32[5]{0:T(128)} %stack.23.where_ref.w, bf16[1024,384]{1,0:T(8,128)(2,1)} %get-tuple-element.329.refs_1_.refs_0_, bf16[1024,384]{1,0:T(8,128)(2,1)} %get-tuple-element.330.refs_2_.refs_1_, bf16[1024,384]{1,0:T(8,128)(2,1)} %get-tuple-element.331.refs_3_.refs_2_, ...), custom_call_target="tpu_custom_call" | custom-call | flops 115000000512 | bytes 1 | tf_op jit(solution)/shard_map/attn_back_own/pallas_call | solution.py:126
  475.4 3.6 fold.19
  481.1 4.8 convert_add_fusion
  485.9 6.4 %collective-permute-done.54 = bf16[192,768]{1,0:T(8,128)(2,1)S(1)} collective-permute-done((bf16[192,768]{1,0:T(8,128)(2,1)S(1)}, bf16[192,768]{1,0:T(8,128)(2,1)S(1)}, u32[]{:S(2)}, u32[]{:S(2)}) %collective-permute-start.54) | collective-permute-done | bytes 294944 | tf_op jit(solution)/shard_map/ppermute | solution.py:852
  493.3 3.0 collective-permute-start.60
  506.0 4.0 collective-permute-done.65
  511.7 2.9 collective-permute-done.66
  516.6 6.2 %close_block.1 = f32[512,1536]{1,0:T(8,128)} custom-call(s32[5]{0:T(128)} %stack.23.where_ref.w, bf16[512,1536]{1,0:T(8,128)(2,1)} %get-tuple-element.363.refs_0_, bf16[2048,1536]{1,0:T(8,128)(2,1)} %refs_1_.13, f32[1024,1]{1,0:T(8,128)} %get-tuple-element.204.refs_1_.refs_2_, f32[1,1536]{1,0:T(1,128)} %broadcast_in_dim.16.refs_1_.refs_20_.refs_3_, ...), custom_call_target="tpu_custom_call" | custom-call | flops 115000000512 | bytes 1 | tf_op jit(solution)/shard_map/close_block/pallas_call | solution.py:51
  (258 shorter events, 108.9 us)
Async XLA Ops:
  3.8 24.9 %collective-permute-start = (bf16[192,768]{1,0:T(8,128)(2,1)}, bf16[192,768]{1,0:T(8,128)(2,1)}, u32[]{:S(2)}, u32[]{:S(2)}) collective-permute-start(bf16[192,768]{1,0:T(8,128)(2,1)} %collect.5.refs_3_), channel_id=1, source_target_pairs={{2,0},{3,1},{0,2},{1,3},{6,4},{7,5},{4,6},{5,7},{10,8},{11,9},{8,1... | collective-permute-start | bytes 884744 | tf_op jit(solution)/shard_map/ppermute | solution.py:848
  7.9 20.8 %collective-permute-start.1 = (f32[6]{0:T(128)}, f32[6]{0:T(128)}, u32[]{:S(2)}, u32[]{:S(2)}) collective-permute-start(f32[6]{0:T(128)} %param.22), channel_id=1, source_target_pairs={{2,0},{3,1},{0,2},{1,3},{6,4},{7,5},{4,6},{5,7},{10,8},{11,9},{8,1... | collective-permute-start | bytes 80 | tf_op jit(solution)/shard_map/ppermute | solution.py:848
  28.7 20.6 %collective-permute-start.4 = (bf16[192,768]{1,0:T(8,128)(2,1)}, bf16[192,768]{1,0:T(8,128)(2,1)S(1)}, u32[]{:S(2)}, u32[]{:S(2)}) collective-permute-start(bf16[192,768]{1,0:T(8,128)(2,1)} %collective-permute-done.refs_0_), channel_id=1, source_target_pairs={{0,8},{4,12},{8,0},{12,4},{16,24},{20,28},{24,16},{28,20},{1,9},{5... | collective-permute-start | bytes 884744 | tf_op jit(solution)/shard_map/ppermute | solution.py:855
  30.5 20.4 %collective-permute-start.5 = (bf16[192,768]{1,0:T(8,128)(2,1)}, bf16[192,768]{1,0:T(8,128)(2,1)S(1)}, u32[]{:S(2)}, u32[]{:S(2)}) collective-permute-start(bf16[192,768]{1,0:T(8,128)(2,1)} %collective-permute-done.refs_0_), channel_id=1, source_target_pairs={{0,16},{4,20},{8,24},{12,28},{16,0},{20,4},{24,8},{28,12},{1,17},{... | collective-permute-start | bytes 884744 | tf_op jit(solution)/shard_map/ppermute | solution.py:855
  32.0 20.5 %collective-permute-start.6 = (bf16[192,768]{1,0:T(8,128)(2,1)}, bf16[192,768]{1,0:T(8,128)(2,1)S(1)}, u32[]{:S(2)}, u32[]{:S(2)}) collective-permute-start(bf16[192,768]{1,0:T(8,128)(2,1)} %collective-permute-done.refs_0_), channel_id=1, source_target_pairs={{0,24},{4,28},{8,16},{12,20},{16,8},{20,12},{24,0},{28,4},{1,25},{... | collective-permute-start | bytes 884744 | tf_op jit(solution)/shard_map/ppermute | solution.py:855
  47.3 22.0 %collective-permute-start.3 = (bf16[1024,384]{1,0:T(8,128)(2,1)}, bf16[1024,384]{1,0:T(8,128)(2,1)}, u32[]{:S(2)}, u32[]{:S(2)}) collective-permute-start(bf16[1024,384]{1,0:T(8,128)(2,1)} %get-tuple-element.212.refs_5_.refs_1_.refs_4_), channel_id=1, source_target_pairs={{1,0},{0,1},{3,2},{2,3},{5,4},{4,5},{7,6},{6,7},{9,8},{8,9},{11,10... | collective-permute-start | bytes 2359304 | tf_op jit(solution)/shard_map/ppermute | solution.py:848
  49.4 19.9 %collective-permute-start.2 = (bf16[192,384]{1,0:T(8,128)(2,1)}, bf16[192,384]{1,0:T(8,128)(2,1)}, u32[]{:S(2)}, u32[]{:S(2)}) collective-permute-start(bf16[192,384]{1,0:T(8,128)(2,1)} %collect.7.refs_7_), channel_id=1, source_target_pairs={{2,0},{3,1},{0,2},{1,3},{6,4},{7,5},{4,6},{5,7},{10,8},{11,9},{8,1... | collective-permute-start | bytes 442376 | tf_op jit(solution)/shard_map/ppermute | solution.py:848
  49.4 19.9 %collective-permute-start.10 = (bf16[192,896]{1,0:T(8,128)(2,1)}, bf16[192,896]{1,0:T(8,128)(2,1)}, u32[]{:S(2)}, u32[]{:S(2)}) collective-permute-start(bf16[192,896]{1,0:T(8,128)(2,1)} %collective-permute-done.7.refs_0_), channel_id=1, source_target_pairs={{0,8},{4,12},{8,0},{12,4},{16,24},{20,28},{24,16},{28,20},{1,9},{5... | collective-permute-start | bytes 1032200 | tf_op jit(solution)/shard_map/ppermute | solution.py:855
  51.0 18.3 %collective-permute-start.11 = (bf16[192,896]{1,0:T(8,128)(2,1)}, bf16[192,896]{1,0:T(8,128)(2,1)}, u32[]{:S(2)}, u32[]{:S(2)}) collective-permute-start(bf16[192,896]{1,0:T(8,128)(2,1)} %collective-permute-done.7.refs_0_), channel_id=1, source_target_pairs={{0,16},{4,20},{8,24},{12,28},{16,0},{20,4},{24,8},{28,12},{1,17},{... | collective-permute-start | bytes 1032200 | tf_op jit(solution)/shard_map/ppermute | solution.py:855
  74.6 17.7 %collective-permute-start.8 = (bf16[192,768]{1,0:T(8,128)(2,1)S(1)}, bf16[192,768]{1,0:T(8,128)(2,1)S(1)}, u32[]{:S(2)}, u32[]{:S(2)}) collective-permute-start(bf16[192,768]{1,0:T(8,128)(2,1)S(1)} %pad_maximum_fusion.7), channel_id=1, source_target_pairs={{1,0},{0,1},{3,2},{2,3},{5,4},{4,5},{7,6},{6,7},{9,8},{8,9},{11,10... | collective-permute-start | bytes 884744 | tf_op jit(solution)/shard_map/ppermute | solution.py:848
  77.3 41.7 %collective-permute-start.17 = (bf16[192,2048]{1,0:T(8,128)(2,1)}, bf16[192,2048]{1,0:T(8,128)(2,1)}, u32[]{:S(2)}, u32[]{:S(2)}) collective-permute-start(bf16[192,2048]{1,0:T(8,128)(2,1)} %collect.8.refs_4_), channel_id=1, source_target_pairs={{2,0},{3,1},{0,2},{1,3},{6,4},{7,5},{4,6},{5,7},{10,8},{11,9},{8,1... | collective-permute-start | bytes 2359304 | tf_op jit(solution)/shard_map/ppermute | solution.py:848
  93.9 20.8 %collective-permute-start.15 = (bf16[192,1152]{1,0:T(8,128)(2,1)S(1)}, bf16[192,1152]{1,0:T(8,128)(2,1)S(1)}, u32[]{:S(2)}, u32[]{:S(2)}) collective-permute-start(bf16[192,1152]{1,0:T(8,128)(2,1)S(1)} %constant_dynamic-update-slice_fusion.refs_0_), channel_id=1, source_target_pairs={{0,16},{4,20},{8,24},{12,28},{16,0},{20,4},{24,8},{28,12},{1,17},{... | collective-permute-start | bytes 1327112 | tf_op jit(solution)/shard_map/ppermute | solution.py:855
  95.4 19.3 %collective-permute-start.16 = (bf16[192,1152]{1,0:T(8,128)(2,1)S(1)}, bf16[192,1152]{1,0:T(8,128)(2,1)S(1)}, u32[]{:S(2)}, u32[]{:S(2)}) collective-permute-start(bf16[192,1152]{1,0:T(8,128)(2,1)S(1)} %constant_dynamic-update-slice_fusion.refs_0_), channel_id=1, source_target_pairs={{0,24},{4,28},{8,16},{12,20},{16,8},{20,12},{24,0},{28,4},{1,25},{... | collective-permute-start | bytes 1327112 | tf_op jit(solution)/shard_map/ppermute | solution.py:855
  108.3 23.3 %collective-permute-start.19 = (bf16[1024,384]{1,0:T(8,128)(2,1)}, bf16[1024,384]{1,0:T(8,128)(2,1)}, u32[]{:S(2)}, u32[]{:S(2)}) collective-permute-start(bf16[1024,384]{1,0:T(8,128)(2,1)} %get-tuple-element.247.refs_6_.refs_2_.refs_4_), channel_id=1, source_target_pairs={{1,0},{0,1},{3,2},{2,3},{5,4},{4,5},{7,6},{6,7},{9,8},{8,9},{11,10... | collective-permute-start | bytes 2359304 | tf_op jit(solution)/shard_map/ppermute | solution.py:848
  119.1 26.2 %collective-permute-start.20 = (bf16[192,2048]{1,0:T(8,128)(2,1)}, bf16[192,2048]{1,0:T(8,128)(2,1)}, u32[]{:S(2)}, u32[]{:S(2)}) collective-permute-start(bf16[192,2048]{1,0:T(8,128)(2,1)} %collective-permute-done.17.refs_0_), channel_id=1, source_target_pairs={{0,8},{4,12},{8,0},{12,4},{16,24},{20,28},{24,16},{28,20},{1,9},{5... | collective-permute-start | bytes 2359304 | tf_op jit(solution)/shard_map/ppermute | solution.py:855
  120.2 35.3 %collective-permute-start.21 = (bf16[192,2048]{1,0:T(8,128)(2,1)}, bf16[192,2048]{1,0:T(8,128)(2,1)}, u32[]{:S(2)}, u32[]{:S(2)}) collective-permute-start(bf16[192,2048]{1,0:T(8,128)(2,1)} %collective-permute-done.17.refs_0_), channel_id=1, source_target_pairs={{0,16},{4,20},{8,24},{12,28},{16,0},{20,4},{24,8},{28,12},{1,17},{... | collective-permute-start | bytes 2359304 | tf_op jit(solution)/shard_map/ppermute | solution.py:855
  121.2 36.0 %collective-permute-start.22 = (bf16[192,2048]{1,0:T(8,128)(2,1)}, bf16[192,2048]{1,0:T(8,128)(2,1)}, u32[]{:S(2)}, u32[]{:S(2)}) collective-permute-start(bf16[192,2048]{1,0:T(8,128)(2,1)} %collective-permute-done.17.refs_0_), channel_id=1, source_target_pairs={{0,24},{4,28},{8,16},{12,20},{16,8},{20,12},{24,0},{28,4},{1,25},{... | collective-permute-start | bytes 2359304 | tf_op jit(solution)/shard_map/ppermute | solution.py:855
  131.6 25.6 %collective-permute-start.23 = (bf16[192,1024]{1,0:T(8,128)(2,1)}, bf16[192,1024]{1,0:T(8,128)(2,1)}, u32[]{:S(2)}, u32[]{:S(2)}) collective-permute-start(bf16[192,1024]{1,0:T(8,128)(2,1)} %collect.9.refs_9_), channel_id=1, source_target_pairs={{2,0},{3,1},{0,2},{1,3},{6,4},{7,5},{4,6},{5,7},{10,8},{11,9},{8,1... | collective-permute-start | bytes 1179656 | tf_op jit(solution)/shard_map/ppermute | solution.py:848
  157.2 48.4 %collective-permute-start.24 = (bf16[192,1024]{1,0:T(8,128)(2,1)}, bf16[192,1024]{1,0:T(8,128)(2,1)}, u32[]{:S(2)}, u32[]{:S(2)}) collective-permute-start(bf16[192,1024]{1,0:T(8,128)(2,1)} %collective-permute-done.23.refs_0_), channel_id=1, source_target_pairs={{0,8},{4,12},{8,0},{12,4},{16,24},{20,28},{24,16},{28,20},{1,9},{5... | collective-permute-start | bytes 1179656 | tf_op jit(solution)/shard_map/ppermute | solution.py:855
  158.0 47.6 %collective-permute-start.25 = (bf16[192,1024]{1,0:T(8,128)(2,1)}, bf16[192,1024]{1,0:T(8,128)(2,1)}, u32[]{:S(2)}, u32[]{:S(2)}) collective-permute-start(bf16[192,1024]{1,0:T(8,128)(2,1)} %collective-permute-done.23.refs_0_), channel_id=1, source_target_pairs={{0,16},{4,20},{8,24},{12,28},{16,0},{20,4},{24,8},{28,12},{1,17},{... | collective-permute-start | bytes 1179656 | tf_op jit(solution)/shard_map/ppermute | solution.py:855
  159.5 46.1 %collective-permute-start.26 = (bf16[192,1024]{1,0:T(8,128)(2,1)}, bf16[192,1024]{1,0:T(8,128)(2,1)}, u32[]{:S(2)}, u32[]{:S(2)}) collective-permute-start(bf16[192,1024]{1,0:T(8,128)(2,1)} %collective-permute-done.23.refs_0_), channel_id=1, source_target_pairs={{0,24},{4,28},{8,16},{12,20},{16,8},{20,12},{24,0},{28,4},{1,25},{... | collective-permute-start | bytes 1179656 | tf_op jit(solution)/shard_map/ppermute | solution.py:855
  216.1 38.1 %collective-permute-start.31 = (bf16[384,1536]{1,0:T(8,128)(2,1)}, bf16[384,1536]{1,0:T(8,128)(2,1)S(1)}, u32[]{:S(2)}, u32[]{:S(2)}) collective-permute-start(bf16[384,1536]{1,0:T(8,128)(2,1)} %get-tuple-element.267.refs_11_), channel_id=1, source_target_pairs={{0,16},{4,20},{8,24},{12,28},{16,0},{20,4},{24,8},{28,12},{1,17},{... | collective-permute-start | bytes 3538952 | tf_op jit(solution)/shard_map/ppermute | solution.py:855
  217.0 37.2 %collective-permute-start.32 = (bf16[384,1536]{1,0:T(8,128)(2,1)}, bf16[384,1536]{1,0:T(8,128)(2,1)S(1)}, u32[]{:S(2)}, u32[]{:S(2)}) collective-permute-start(bf16[384,1536]{1,0:T(8,128)(2,1)} %get-tuple-element.276), channel_id=1, source_target_pairs={{0,8},{4,12},{8,0},{12,4},{16,24},{20,28},{24,16},{28,20},{1,9},{5... | collective-permute-start | bytes 3538952 | tf_op jit(solution)/shard_map/ppermute | solution.py:855
  253.7 36.3 %collective-permute-start.30 = (bf16[512,1536]{1,0:T(8,128)(2,1)}, bf16[512,1536]{1,0:T(8,128)(2,1)}, u32[]{:S(2)}, u32[]{:S(2)}) collective-permute-start(bf16[512,1536]{1,0:T(8,128)(2,1)} %get-tuple-element.270), channel_id=1, source_target_pairs={{0,1},{1,0},{2,3},{3,2},{4,5},{5,4},{6,7},{7,6},{8,9},{9,8},{10,11... | collective-permute-start | bytes 4718600 | tf_op jit(solution)/shard_map/ppermute | solution.py:896
  260.0 41.4 %collective-permute-start.34 = (bf16[192,1536]{1,0:T(8,128)(2,1)}, bf16[192,1536]{1,0:T(8,128)(2,1)}, u32[]{:S(2)}, u32[]{:S(2)}) collective-permute-start(bf16[192,1536]{1,0:T(8,128)(2,1)} %get-tuple-element.278.refs_5_), channel_id=1, source_target_pairs={{0,8},{4,12},{8,0},{12,4},{16,24},{20,28},{24,16},{28,20},{1,9},{5... | collective-permute-start | bytes 1769480 | tf_op jit(solution)/shard_map/ppermute | solution.py:855
  261.3 40.2 %collective-permute-start.35 = (bf16[192,1536]{1,0:T(8,128)(2,1)}, bf16[192,1536]{1,0:T(8,128)(2,1)}, u32[]{:S(2)}, u32[]{:S(2)}) collective-permute-start(bf16[192,1536]{1,0:T(8,128)(2,1)} %get-tuple-element.282), channel_id=1, source_target_pairs={{0,16},{4,20},{8,24},{12,28},{16,0},{20,4},{24,8},{28,12},{1,17},{... | collective-permute-start | bytes 1769480 | tf_op jit(solution)/shard_map/ppermute | solution.py:855
  278.4 26.3 %collective-permute-start.33 = (bf16[768,3072]{1,0:T(8,128)(2,1)}, bf16[768,3072]{1,0:T(8,128)(2,1)S(1)}, u32[]{:S(2)}, u32[]{:S(2)}) collective-permute-start(bf16[768,3072]{1,0:T(8,128)(2,1)} %get-tuple-element.279.refs_9_), channel_id=1, source_target_pairs={{0,4},{4,0},{8,12},{12,8},{16,20},{20,16},{24,28},{28,24},{1,5},{5... | collective-permute-start | bytes 14155784 | tf_op jit(solution)/shard_map/ppermute | solution.py:855
  301.1 21.3 %collective-permute-start.39 = (bf16[512,768]{1,0:T(8,128)(2,1)}, bf16[512,768]{1,0:T(8,128)(2,1)}, u32[]{:S(2)}, u32[]{:S(2)}) collective-permute-start(bf16[512,768]{1,0:T(8,128)(2,1)} %get-tuple-element.291), channel_id=1, source_target_pairs={{1,0},{0,1},{3,2},{2,3},{5,4},{4,5},{7,6},{6,7},{9,8},{8,9},{11,10... | collective-permute-start | bytes 2359304 | tf_op jit(solution)/shard_map/ppermute | solution.py:848
  313.7 40.5 %collective-permute-start.37 = (bf16[384,1536]{1,0:T(8,128)(2,1)}, bf16[384,1536]{1,0:T(8,128)(2,1)}, u32[]{:S(2)}, u32[]{:S(2)}) collective-permute-start(bf16[384,1536]{1,0:T(8,128)(2,1)} %get-tuple-element.285.refs_5_), channel_id=1, source_target_pairs={{0,16},{4,20},{8,24},{12,28},{16,0},{20,4},{24,8},{28,12},{1,17},{... | collective-permute-start | bytes 3538952 | tf_op jit(solution)/shard_map/ppermute | solution.py:855
  322.3 38.6 %collective-permute-start.36 = (bf16[768,1536]{1,0:T(8,128)(2,1)}, bf16[768,1536]{1,0:T(8,128)(2,1)}, u32[]{:S(2)}, u32[]{:S(2)}) collective-permute-start(bf16[768,1536]{1,0:T(8,128)(2,1)} %get-tuple-element.295.refs_12_), channel_id=1, source_target_pairs={{0,4},{4,0},{8,12},{12,8},{16,20},{20,16},{24,28},{28,24},{1,5},{5... | collective-permute-start | bytes 7077896 | tf_op jit(solution)/shard_map/ppermute | solution.py:855
  322.4 31.9 %collective-permute-start.38 = (bf16[384,1536]{1,0:T(8,128)(2,1)}, bf16[384,1536]{1,0:T(8,128)(2,1)}, u32[]{:S(2)}, u32[]{:S(2)}) collective-permute-start(bf16[384,1536]{1,0:T(8,128)(2,1)} %get-tuple-element.290), channel_id=1, source_target_pairs={{0,8},{4,12},{8,0},{12,4},{16,24},{20,28},{24,16},{28,20},{1,9},{5... | collective-permute-start | bytes 3538952 | tf_op jit(solution)/shard_map/ppermute | solution.py:855
  323.2 42.5 %collective-permute-start.45 = (bf16[512,1536]{1,0:T(8,128)(2,1)}, bf16[512,1536]{1,0:T(8,128)(2,1)}, u32[]{:S(2)}, u32[]{:S(2)}) collective-permute-start(bf16[512,1536]{1,0:T(8,128)(2,1)} %get-tuple-element.312), channel_id=1, source_target_pairs={{0,1},{1,0},{2,3},{3,2},{4,5},{5,4},{6,7},{7,6},{8,9},{9,8},{10,11... | collective-permute-start | bytes 4718600 | tf_op jit(solution)/shard_map/ppermute | solution.py:896
  365.2 34.4 %collective-permute-start.40 = (bf16[384,768]{1,0:T(8,128)(2,1)}, bf16[384,768]{1,0:T(8,128)(2,1)}, u32[]{:S(2)}, u32[]{:S(2)}) collective-permute-start(bf16[384,768]{1,0:T(8,128)(2,1)} %get-tuple-element.313.refs_8_), channel_id=1, source_target_pairs={{0,16},{4,20},{8,24},{12,28},{16,0},{20,4},{24,8},{28,12},{1,17},{... | collective-permute-start | bytes 1769480 | tf_op jit(solution)/shard_map/ppermute | solution.py:855
  365.7 33.8 %collective-permute-start.41 = (bf16[384,768]{1,0:T(8,128)(2,1)}, bf16[384,768]{1,0:T(8,128)(2,1)}, u32[]{:S(2)}, u32[]{:S(2)}) collective-permute-start(bf16[384,768]{1,0:T(8,128)(2,1)} %get-tuple-element.307), channel_id=1, source_target_pairs={{0,8},{4,12},{8,0},{12,4},{16,24},{20,28},{24,16},{28,20},{1,9},{5... | collective-permute-start | bytes 1769480 | tf_op jit(solution)/shard_map/ppermute | solution.py:855
  371.7 33.3 %collective-permute-start.48 = (bf16[384,896]{1,0:T(8,128)(2,1)}, bf16[384,896]{1,0:T(8,128)(2,1)}, u32[]{:S(2)}, u32[]{:S(2)}) collective-permute-start(bf16[384,896]{1,0:T(8,128)(2,1)} %get-tuple-element.315.refs_12_), channel_id=1, source_target_pairs={{0,16},{4,20},{8,24},{12,28},{16,0},{20,4},{24,8},{28,12},{1,17},{... | collective-permute-start | bytes 2064392 | tf_op jit(solution)/shard_map/ppermute | solution.py:855
  375.9 29.2 %collective-permute-start.49 = (bf16[384,896]{1,0:T(8,128)(2,1)}, bf16[384,896]{1,0:T(8,128)(2,1)}, u32[]{:S(2)}, u32[]{:S(2)}) collective-permute-start(bf16[384,896]{1,0:T(8,128)(2,1)} %get-tuple-element.322), channel_id=1, source_target_pairs={{0,8},{4,12},{8,0},{12,4},{16,24},{20,28},{24,16},{28,20},{1,9},{5... | collective-permute-start | bytes 2064392 | tf_op jit(solution)/shard_map/ppermute | solution.py:855
  379.8 52.5 %collective-permute-start.52 = (bf16[192,3072]{1,0:T(8,128)(2,1)}, bf16[192,3072]{1,0:T(8,128)(2,1)}, u32[]{:S(2)}, u32[]{:S(2)}) collective-permute-start(bf16[192,3072]{1,0:T(8,128)(2,1)} %pad_maximum_fusion.1), channel_id=1, source_target_pairs={{0,2},{1,3},{2,0},{3,1},{4,6},{5,7},{6,4},{7,5},{8,10},{9,11},{10,... | collective-permute-start | bytes 3538952 | tf_op jit(solution)/shard_map/ppermute | solution.py:852
  402.9 30.6 %collective-permute-start.46 = (bf16[192,768]{1,0:T(8,128)(2,1)}, bf16[192,768]{1,0:T(8,128)(2,1)}, u32[]{:S(2)}, u32[]{:S(2)}) collective-permute-start(bf16[192,768]{1,0:T(8,128)(2,1)} %get-tuple-element.318.refs_8_), channel_id=1, source_target_pairs={{0,8},{4,12},{8,0},{12,4},{16,24},{20,28},{24,16},{28,20},{1,9},{5... | collective-permute-start | bytes 884744 | tf_op jit(solution)/shard_map/ppermute | solution.py:855
  404.1 29.4 %collective-permute-start.47 = (bf16[192,768]{1,0:T(8,128)(2,1)}, bf16[192,768]{1,0:T(8,128)(2,1)}, u32[]{:S(2)}, u32[]{:S(2)}) collective-permute-start(bf16[192,768]{1,0:T(8,128)(2,1)} %get-tuple-element.319), channel_id=1, source_target_pairs={{0,16},{4,20},{8,24},{12,28},{16,0},{20,4},{24,8},{28,12},{1,17},{... | collective-permute-start | bytes 884744 | tf_op jit(solution)/shard_map/ppermute | solution.py:855
  408.5 23.9 %collective-permute-start.50 = (bf16[192,896]{1,0:T(8,128)(2,1)}, bf16[192,896]{1,0:T(8,128)(2,1)S(1)}, u32[]{:S(2)}, u32[]{:S(2)}) collective-permute-start(bf16[192,896]{1,0:T(8,128)(2,1)} %get-tuple-element.323.refs_6_), channel_id=1, source_target_pairs={{0,8},{4,12},{8,0},{12,4},{16,24},{20,28},{24,16},{28,20},{1,9},{5... | collective-permute-start | bytes 1032200 | tf_op jit(solution)/shard_map/ppermute | solution.py:855
  409.9 22.5 %collective-permute-start.51 = (bf16[192,896]{1,0:T(8,128)(2,1)}, bf16[192,896]{1,0:T(8,128)(2,1)S(1)}, u32[]{:S(2)}, u32[]{:S(2)}) collective-permute-start(bf16[192,896]{1,0:T(8,128)(2,1)} %get-tuple-element.324), channel_id=1, source_target_pairs={{0,16},{4,20},{8,24},{12,28},{16,0},{20,4},{24,8},{28,12},{1,17},{... | collective-permute-start | bytes 1032200 | tf_op jit(solution)/shard_map/ppermute | solution.py:855
  432.3 19.3 %collective-permute-start.53 = (bf16[768,1792]{1,0:T(8,128)(2,1)}, bf16[768,1792]{1,0:T(8,128)(2,1)}, u32[]{:S(2)}, u32[]{:S(2)}) collective-permute-start(bf16[768,1792]{1,0:T(8,128)(2,1)} %get-tuple-element.341.refs_21_), channel_id=1, source_target_pairs={{0,4},{4,0},{8,12},{12,8},{16,20},{20,16},{24,28},{28,24},{1,5},{5... | collective-permute-start | bytes 8257544 | tf_op jit(solution)/shard_map/ppermute | solution.py:855
  433.5 37.2 %collective-permute-start.58 = (bf16[192,1792]{1,0:T(8,128)(2,1)}, bf16[192,1792]{1,0:T(8,128)(2,1)}, u32[]{:S(2)}, u32[]{:S(2)}) collective-permute-start(bf16[192,1792]{1,0:T(8,128)(2,1)} %pad_maximum_fusion.6), channel_id=1, source_target_pairs={{0,2},{1,3},{2,0},{3,1},{4,6},{5,7},{6,4},{7,5},{8,10},{9,11},{10,... | collective-permute-start | bytes 2064392 | tf_op jit(solution)/shard_map/ppermute | solution.py:852
  449.3 67.3 %collective-permute-start.59 = (bf16[512,1536]{1,0:T(8,128)(2,1)}, bf16[512,1536]{1,0:T(8,128)(2,1)}, u32[]{:S(2)}, u32[]{:S(2)}) collective-permute-start(bf16[512,1536]{1,0:T(8,128)(2,1)} %get-tuple-element.365), channel_id=1, source_target_pairs={{0,1},{1,0},{2,3},{3,2},{4,5},{5,4},{6,7},{7,6},{8,9},{9,8},{10,11... | collective-permute-start | bytes 4718600 | tf_op jit(solution)/shard_map/ppermute | solution.py:896
  456.2 18.0 %collective-permute-start.56 = (bf16[384,896]{1,0:T(8,128)(2,1)}, bf16[384,896]{1,0:T(8,128)(2,1)S(1)}, u32[]{:S(2)}, u32[]{:S(2)}) collective-permute-start(bf16[384,896]{1,0:T(8,128)(2,1)} %get-tuple-element.347.refs_21_), channel_id=1, source_target_pairs={{0,16},{4,20},{8,24},{12,28},{16,0},{20,4},{24,8},{28,12},{1,17},{... | collective-permute-start | bytes 2064392 | tf_op jit(solution)/shard_map/ppermute | solution.py:855
  471.7 20.5 %collective-permute-start.54 = (bf16[192,768]{1,0:T(8,128)(2,1)S(1)}, bf16[192,768]{1,0:T(8,128)(2,1)S(1)}, u32[]{:S(2)}, u32[]{:S(2)}) collective-permute-start(bf16[192,768]{1,0:T(8,128)(2,1)S(1)} %bitcast.20), channel_id=1, source_target_pairs={{0,2},{1,3},{2,0},{3,1},{4,6},{5,7},{6,4},{7,5},{8,10},{9,11},{10,... | collective-permute-start | bytes 884744 | tf_op jit(solution)/shard_map/ppermute | solution.py:852
  479.1 23.3 %collective-permute-start.63 = (bf16[192,896]{1,0:T(8,128)(2,1)}, bf16[192,896]{1,0:T(8,128)(2,1)S(1)}, u32[]{:S(2)}, u32[]{:S(2)}) collective-permute-start(bf16[192,896]{1,0:T(8,128)(2,1)} %get-tuple-element.384.refs_6_), channel_id=1, source_target_pairs={{0,8},{4,12},{8,0},{12,4},{16,24},{20,28},{24,16},{28,20},{1,9},{5... | collective-permute-start | bytes 1032200 | tf_op jit(solution)/shard_map/ppermute | solution.py:855
  493.3 21.3 %collective-permute-start.60 = (bf16[192,384]{1,0:T(8,128)(2,1)S(1)}, bf16[192,384]{1,0:T(8,128)(2,1)S(1)}, u32[]{:S(2)}, u32[]{:S(2)}) collective-permute-start(bf16[192,384]{1,0:T(8,128)(2,1)S(1)} %slice.128), channel_id=1, source_target_pairs={{0,1},{1,0},{2,3},{3,2},{4,5},{5,4},{6,7},{7,6},{8,9},{9,8},{10,11... | collective-permute-start | bytes 442376 | tf_op jit(solution)/shard_map/ppermute | solution.py:852
  (59 other events, 567.8 us)

commit v6 on v5

--- a/solution.py
+++ b/solution.py
@@ -647,23 +647,26 @@
     rows, width = pieces[0].shape
 
     def kernel(w, *refs):
-        out, sems = refs[count + extra], refs[count + extra + 1]
-        copies = []
+        out, held, sems = refs[count + extra:]
+        loads = [pltpu.make_async_copy(refs[k], held.at[k], sems.at[0, k]) for k in range(count)]
+        for c in loads:
+            c.start()
+        stores = []
         for k in range(count):
+            loads[k].wait()
             at = pl.multiple_of(jnp.bitwise_xor(w[CHIP], masks[k]) * rows, rows)
-            copies.append(pltpu.make_async_copy(refs[k], out.at[pl.ds(at, rows), :], sems.at[k]))
-        for c in copies:
-            c.start()
-        for c in copies:
+            stores.append(pltpu.make_async_copy(held.at[k], out.at[pl.ds(at, rows), :], sems.at[1, k]))
+            stores[k].start()
+        for c in stores:
             c.wait()
 
     return pl.pallas_call(
         kernel,
         grid_spec=pltpu.PrefetchScalarGridSpec(
-            num_scalar_prefetch=1, grid=(1,),
+            num_scalar_prefetch=1, grid=(),
             in_specs=[pl.BlockSpec(memory_space=pl.ANY)] * (count + extra),
-            out_specs=pl.BlockSpec((count * rows, width), lambda i, w: (0, 0)),
-            scratch_shapes=[pltpu.SemaphoreType.DMA((count,))],
+            out_specs=pl.BlockSpec(memory_space=pl.ANY),
+            scratch_shapes=[pltpu.VMEM((count, rows, width), bf16), pltpu.SemaphoreType.DMA((2, count))],
         ),
         out_shape=shape((count * rows, width), bf16),
         compiler_params=pltpu.CompilerParams(vmem_limit_bytes=56 << 20),
@@ -1144,10 +1147,11 @@
     mlp_own, *mlp_other = go.sync(mlp_own, *mlp_other)
     attn_sums[0].wait()
     attn = attn_sums[0].close()
-    while flying is not None:
+    while small_hops:
         small, flying = small_step()
     out_rest = go.sync(*out_rest)
     grad_inputs = go(close_block, share, group, part, got, inputs, inverse_attn, gain_attn, dh)
+    small, flying = small_step()
     mlp = mlp_own
     for v in mlp_other:
         mlp = mlp + v.astype(f32)

time: 532 us -> 527 us (level)
  transfers between devices with their start and end apart: 67 -> 67, of which waited for: 15 -> 14; matrix products, arithmetic and copies ran while one was open for 7% -> 7% of each run, Pallas kernels for 62% -> 63%
where the time goes in v6:
time: 527 us; the launch traced here: 518 us
  Pallas kernels  332 us (63%)
  waiting for transfers between devices  70.4 us (13%)
  starting transfers between devices  67.1 us (13%)
  local copies, waits for them, and re-layouts  23.8 us (5%)
  other arithmetic  22.4 us (4%)
    pallas_call x26, Pallas kernels, run(): pl.pallas_call(kernel, grid_spec=pltpu.PrefetchScalarGridSpec(num_scalar_...  247 us
    pallas_call x6, Pallas kernels, stream(): pl.pallas_call(kernel, grid_spec=pltpu.PrefetchScalarGridSpec(num_scalar_...  70.5 us
    ppermute x48, starting transfers between devices, swap(): return lax.ppermute(value, 'dp', [(i, i ^ bit) for i in range(self.dp)])  42.2 us
    ppermute x48, waiting for transfers between devices, swap(): return lax.ppermute(value, 'dp', [(i, i ^ bit) for i in range(self.dp)])  22.4 us
    ppermute x10, waiting for transfers between devices, fetch(): return lax.ppermute(value, 'tensor', pairs)  18 us
    ppermute x4, waiting for transfers between devices, deliver(): return lax.ppermute(value, 'tensor', pairs)  16.6 us
    pallas_call x5, Pallas kernels, assemble(): pl.pallas_call(kernel, grid_spec=pltpu.PrefetchScalarGridSpec(num_scalar_...  14.9 us
    ppermute x10, starting transfers between devices, fetch(): return lax.ppermute(value, 'tensor', pairs)  13.5 us
  transfers between devices with their start and end apart: 67, of which 14 were waited for; matrix products, arithmetic and copies ran while one was open for 7% of the time, Pallas kernels for 63%

profile of v6, /device:TPU:0, one launch (start us, length us, event | category | flops | bytes accessed | tf_op | source)
XLA Modules:
  0.0 517.6 jit_solution(4684972852744503638)
XLA Ops:
  1.3 2.5 collect.5.refs_3_
  3.8 4.0 collective-permute-start
  11.9 12.8 %project_own.1 = (bf16[1024,1536]{1,0:T(8,128)(2,1)}, f32[1024,1]{1,0:T(8,128)}, bf16[1024,384]{1,0:T(8,128)(2,1)}, bf16[1024,384]{1,0:T(8,128)(2,1)}, bf16[1024...) custom-call(s32[5]{0:T(128)} %stack.23.where_ref.w, ...), custom_call_target="tpu_custom_call" | custom-call | flops 115000000512 | bytes 1 | tf_op jit(solution)/shard_map/project_own/pallas_call | solution.py:51
  32.2 2.9 collective-permute-start.7
  35.1 12.2 %attend_forward.2 = (bf16[1024,384]{1,0:T(8,128)(2,1)}, f32[3,2,1024]{2,1,0:T(2,128)}) custom-call(s32[5]{0:T(128)} %stack.23.where_ref.w, bf16[1024,384]{1,0:T(8,128)(2,1)} %get-tuple-element.205.refs_0_, bf16[1024,384]{1,0:T(8,128)(2,1)} %get-tuple-element.206.refs_1_, bf16[1024,384]{1,0:T(8,128)(2,1)} %get-tuple-element.207.refs_2_, ...), custom_call_target="tpu_custom_call" | custom-call | flops 115000000512 | bytes 1 | tf_op jit(solution)/shard_map/attend_forward/pallas_call | solution.py:51
  53.2 2.7 assemble.5.refs_2_.refs_12_
  55.9 2.7 collect.8.refs_4_
  58.6 10.6 %collective-permute-done.3.refs_7_.refs_3_ = bf16[1024,384]{1,0:T(8,128)(2,1)} collective-permute-done((bf16[1024,384]{1,0:T(8,128)(2,1)}, bf16[1024,384]{1,0:T(8,128)(2,1)}, u32[]{:S(2)}, u32[]{:S(2)}) %collective-permute-start.3) | collective-permute-done | bytes 786464 | tf_op jit(solution)/shard_map/ppermute | solution.py:851
  69.3 2.8 assemble.6.refs_4_.refs_6_.refs_17_
  74.3 2.8 collective-permute-start.8
  80.5 11.5 %project_other.1 = (bf16[1024,384]{1,0:T(8,128)(2,1)}, bf16[1024,384]{1,0:T(8,128)(2,1)}, bf16[1024,384]{1,0:T(8,128)(2,1)}, bf16[1024,384]{1,0:T(8,128)(2,1)}, ...) custom-call(s32[5]{0:T(128)} %stack.23.where_ref.w, ...), custom_call_target="tpu_custom_call" | custom-call | flops 115000000512 | bytes 1 | tf_op jit(solution)/shard_map/project_other/pallas_call | solution.py:51
  95.6 12.4 %attend_forward.3 = (bf16[1024,384]{1,0:T(8,128)(2,1)}, f32[3,2,1024]{2,1,0:T(2,128)}) custom-call(s32[5]{0:T(128)} %stack.23.where_ref.w, bf16[1024,384]{1,0:T(8,128)(2,1)} %get-tuple-element.233.refs_0_, bf16[1024,384]{1,0:T(8,128)(2,1)} %get-tuple-element.234.refs_1_, bf16[1024,384]{1,0:T(8,128)(2,1)} %get-tuple-element.235.refs_2_, ...), custom_call_target="tpu_custom_call" | custom-call | flops 115000000512 | bytes 1 | tf_op jit(solution)/shard_map/attend_forward/pallas_call | solution.py:51
  108.5 5.9 %collective-permute-done.15.refs_2_ = bf16[192,1152]{1,0:T(8,128)(2,1)S(1)} collective-permute-done((bf16[192,1152]{1,0:T(8,128)(2,1)S(1)}, bf16[192,1152]{1,0:T(8,128)(2,1)S(1)}, u32[]{:S(2)}, u32[]{:S(2)}) %collective-permute-start.15) | collective-permute-done | bytes 442400 | tf_op jit(solution)/shard_map/ppermute | solution.py:858
  115.4 3.0 assemble.7.refs_1_.refs_2_.refs_6_
  122.0 2.4 collect.9.refs_9_
  124.4 6.9 %collective-permute-done.19.refs_8_.refs_4_ = bf16[1024,384]{1,0:T(8,128)(2,1)} collective-permute-done((bf16[1024,384]{1,0:T(8,128)(2,1)}, bf16[1024,384]{1,0:T(8,128)(2,1)}, u32[]{:S(2)}, u32[]{:S(2)}) %collective-permute-start.19) | collective-permute-done | bytes 786464 | tf_op jit(solution)/shard_map/ppermute | solution.py:851
  132.5 12.5 %close_attention.1 = (f32[1024,1536]{1,0:T(8,128)}, bf16[1024,1536]{1,0:T(8,128)(2,1)}, f32[1024,1]{1,0:T(8,128)}) custom-call(s32[5]{0:T(128)} %stack.23.where_ref.w, bf16[2048,1536]{1,0:T(8,128)(2,1)} %refs_1_.13, bf16[1536,384]{1,0:T(8,128)(2,1)} %refs_5_.7, bf16[768,1152]{1,0:T(8,128)(2,1)} %assemble.7.refs_1_.refs_2_.refs_6_, ...), custom_call_target="tpu_custom_call" | custom-call | flops 115000000512 | bytes 1 | tf_op jit(solution)/shard_map/close_attention/pallas_call | solution.py:51
  145.0 9.9 %collective-permute-done.21.refs_2_ = bf16[192,2048]{1,0:T(8,128)(2,1)} collective-permute-done((bf16[192,2048]{1,0:T(8,128)(2,1)}, bf16[192,2048]{1,0:T(8,128)(2,1)}, u32[]{:S(2)}, u32[]{:S(2)}) %collective-permute-start.21) | collective-permute-done | bytes 786464 | tf_op jit(solution)/shard_map/ppermute | solution.py:858
  160.0 40.1 %feed_forward.2 = (bf16[768,3072]{1,0:T(8,128)(2,1)}, bf16[768,3072]{1,0:T(8,128)(2,1)}, bf16[1024,1536]{1,0:T(8,128)(2,1)}, bf16[1024,1536]{1,0:T(8,128)(2,1)}) custom-call(s32[5]{0:T(128)} %stack.23.where_ref.w, bf16[1024,1536]{1,0:T(8,128)(2,1)} %get-tuple-element.252.refs_0_, bf16[2048,1536]{1,0:T(8,128)(2,1)} %refs_4_.5, ...), custom_call_target="tpu_custom_call" | custom-call | flops 115000000512 | bytes 1 | tf_op jit(solution)/shard_map/feed_forward/pallas_call | solution.py:51
  200.2 3.5 assemble.8.refs_4_.refs_3_
  204.3 2.9 assemble.9.refs_8_.refs_5_
  208.4 7.0 %fold.10 = (bf16[384,1536]{1,0:T(8,128)(2,1)}, bf16[384,1536]{1,0:T(8,128)(2,1)}, bf16[384,1536]{1,0:T(8,128)(2,1)}, bf16[384,1536]{1,0:T(8,128)(2,1)}) custom-call(s32[5]{0:T(128)} %stack.23.where_ref.w, bf16[768,3072]{1,0:T(8,128)(2,1)} %get-tuple-element.264.refs_0_.refs_2_.refs_4_.refs_6_, ...), custom_call_target="tpu_custom_call" | custom-call | flops 115000000512 | bytes 1 | tf_op jit(solution)/shard_map/fold/pallas_call | solution.py:51
  218.9 34.1 %feed_forward.3 = (bf16[1024,1024]{1,0:T(8,128)(2,1)}, bf16[1024,1024]{1,0:T(8,128)(2,1)}, bf16[1024,1024]{1,0:T(8,128)(2,1)}, bf16[512,1536]{1,0:T(8,128)(2,1)}...) custom-call(s32[5]{0:T(128)} %stack.23.where_ref.w, ...), custom_call_target="tpu_custom_call" | custom-call | flops 115000000512 | bytes 1 | tf_op jit(solution)/shard_map/feed_forward/pallas_call | solution.py:51
  254.9 4.4 fold.11
  261.2 16.5 %mlp_grads.1 = (bf16[768,3072]{1,0:T(8,128)(2,1)}, bf16[768,3072]{1,0:T(8,128)(2,1)}) custom-call(s32[5]{0:T(128)} %stack.23.where_ref.w, bf16[1024,1536]{1,0:T(8,128)(2,1)} %get-tuple-element.252.refs_0_, bf16[1024,1024]{1,0:T(8,128)(2,1)} %get-tuple-element.270.refs_1_, bf16[1024,1024]{1,0:T(8,128)(2,1)} %get-tuple-element.271.refs_2_, ...), custom_call_target="tpu_custom_call" | custom-call | flops 115000000512 | bytes 1 | tf_op jit(solution)/shard_map/mlp_grads/pallas_call | solution.py:126
  277.8 11.3 %collective-permute-done.30.refs_8_ = bf16[512,1536]{1,0:T(8,128)(2,1)} collective-permute-done((bf16[512,1536]{1,0:T(8,128)(2,1)}, bf16[512,1536]{1,0:T(8,128)(2,1)}, u32[]{:S(2)}, u32[]{:S(2)}) %collective-permute-start.30) | collective-permute-done | bytes 1572896 | tf_op jit(solution)/shard_map/ppermute | solution.py:899
  289.1 11.1 %close_feed_forward.1 = (f32[512,1536]{1,0:T(8,128)}, bf16[512,1536]{1,0:T(8,128)(2,1)}, bf16[512,768]{1,0:T(8,128)(2,1)}, bf16[512,768]{1,0:T(8,128)(2,1)}) custom-call(s32[5]{0:T(128)} %stack.23.where_ref.w, bf16[512,1536]{1,0:T(8,128)(2,1)} %get-tuple-element.267.refs_0_, f32[1024,1536]{1,0:T(8,128)} %get-tuple-element.268.refs_1_, ...), custom_call_target="tpu_custom_call" | custom-call | flops 115000000512 | bytes 1 | tf_op jit(solution)/shard_map/close_feed_forward/pallas_call | solution.py:51
  305.9 6.9 %fold.12 = (bf16[384,1536]{1,0:T(8,128)(2,1)}, bf16[384,1536]{1,0:T(8,128)(2,1)}, bf16[384,1536]{1,0:T(8,128)(2,1)}, bf16[384,1536]{1,0:T(8,128)(2,1)}) custom-call(s32[5]{0:T(128)} %stack.23.where_ref.w, bf16[768,3072]{1,0:T(8,128)(2,1)} %get-tuple-element.280.refs_0_.refs_2_.refs_4_.refs_6_, bf16[768,3072]{1,0:T(8,128)(2,1)} %copy-done.23, ...), custom_call_target="tpu_custom_call" | custom-call | flops 115000000512 | bytes 1 | tf_op jit(solution)/shard_map/fold/pallas_call | solution.py:51
  313.8 7.6 %out_grads.1 = (bf16[768,1536]{1,0:T(8,128)(2,1)}, bf16[768,1536]{1,0:T(8,128)(2,1)}) custom-call(s32[5]{0:T(128)} %stack.23.where_ref.w, bf16[512,1536]{1,0:T(8,128)(2,1)} %get-tuple-element.279.refs_0_, bf16[1024,384]{1,0:T(8,128)(2,1)} %get-tuple-element.211.refs_5_.refs_1_.refs_4_, bf16[1024,384]{1,0:T(8,128)(2,1)} %get-tuple-element.246.refs_6_.refs_2_.refs_4_, ...), custom_call_target="tpu_custom_call" | custom-call | flops 115000000512 | bytes 1 | tf_op jit(solution)/shard_map/out_grads/pallas_call | solution.py:126
  324.1 17.6 %attend_backward.2 = (bf16[1024,384]{1,0:T(8,128)(2,1)}, bf16[1024,384]{1,0:T(8,128)(2,1)}, bf16[1024,384]{1,0:T(8,128)(2,1)}, bf16[1024,384]{1,0:T(8,128)(2,1)}...) custom-call(s32[5]{0:T(128)} %stack.23.where_ref.w, bf16[1024,384]{1,0:T(8,128)(2,1)} %get-tuple-element.233.refs_0_, ...), custom_call_target="tpu_custom_call" | custom-call | flops 115000000512 | bytes 1 | tf_op jit(solution)/shard_map/attend_backward/pallas_call | solution.py:51
  341.7 11.6 %attn_grads.2 = (bf16[768,1792]{1,0:T(8,128)(2,1)}, bf16[768,1792]{1,0:T(8,128)(2,1)}) custom-call(s32[5]{0:T(128)} %stack.23.where_ref.w, bf16[1024,1536]{1,0:T(8,128)(2,1)} %get-tuple-element.222.refs_0_.refs_19_, bf16[1024,384]{1,0:T(8,128)(2,1)} %get-tuple-element.295.refs_1_.refs_10_, bf16[1024,384]{1,0:T(8,128)(2,1)} %get-tuple-element.296.refs_2_.refs_11_, ...), custom_call_target="tpu_custom_call" | custom-call | flops 115000000512 | bytes 1 | tf_op jit(solution)/shard_map/attn_grads/pallas_call | solution.py:126
  353.4 4.3 fold.13
  360.1 4.2 fold.14
  366.1 4.7 fold.15
  371.7 2.5 collective-permute-done.42
  379.9 17.4 %attend_backward.3 = (bf16[1024,384]{1,0:T(8,128)(2,1)}, bf16[1024,384]{1,0:T(8,128)(2,1)}, bf16[1024,384]{1,0:T(8,128)(2,1)}, bf16[1024,384]{1,0:T(8,128)(2,1)}...) custom-call(s32[5]{0:T(128)} %stack.23.where_ref.w, bf16[1024,384]{1,0:T(8,128)(2,1)} %get-tuple-element.205.refs_0_, ...), custom_call_target="tpu_custom_call" | custom-call | flops 115000000512 | bytes 1 | tf_op jit(solution)/shard_map/attend_backward/pallas_call | solution.py:51
  398.8 3.3 fold.16
  404.2 3.5 fold.17
  409.7 11.7 %attn_grads.3 = (bf16[768,1792]{1,0:T(8,128)(2,1)}, bf16[768,1792]{1,0:T(8,128)(2,1)}) custom-call(s32[5]{0:T(128)} %stack.23.where_ref.w, bf16[1024,1536]{1,0:T(8,128)(2,1)} %get-tuple-element.222.refs_0_.refs_19_, bf16[1024,384]{1,0:T(8,128)(2,1)} %get-tuple-element.328.refs_1_.refs_0_, bf16[1024,384]{1,0:T(8,128)(2,1)} %get-tuple-element.329.refs_2_.refs_1_, ...), custom_call_target="tpu_custom_call" | custom-call | flops 115000000512 | bytes 1 | tf_op jit(solution)/shard_map/attn_grads/pallas_call | solution.py:126
  421.3 10.2 %collective-permute-done.52 = bf16[192,3072]{1,0:T(8,128)(2,1)} collective-permute-done((bf16[192,3072]{1,0:T(8,128)(2,1)}, bf16[192,3072]{1,0:T(8,128)(2,1)}, u32[]{:S(2)}, u32[]{:S(2)}) %collective-permute-start.52) | collective-permute-done | bytes 1179680 | tf_op jit(solution)/shard_map/ppermute | solution.py:855
  432.7 11.7 %attn_back_send.1 = (bf16[512,1536]{1,0:T(8,128)(2,1)}, f32[1,1536]{1,0:T(1,128)}) custom-call(s32[5]{0:T(128)} %stack.23.where_ref.w, bf16[1024,384]{1,0:T(8,128)(2,1)} %get-tuple-element.328.refs_1_.refs_0_, bf16[1024,384]{1,0:T(8,128)(2,1)} %get-tuple-element.329.refs_2_.refs_1_, bf16[1024,384]{1,0:T(8,128)(2,1)} %get-tuple-element.330.refs_3_.refs_2_, ...), custom_call_target="tpu_custom_call" | custom-call | flops 115000000512 | bytes 1 | tf_op jit(solution)/shard_map/attn_back_send/pallas_call | solution.py:126
  450.9 4.6 fold.18
  457.8 11.4 %attn_back_own.1 = (bf16[512,1536]{1,0:T(8,128)(2,1)}, f32[1,1536]{1,0:T(1,128)}) custom-call(s32[5]{0:T(128)} %stack.23.where_ref.w, bf16[1024,384]{1,0:T(8,128)(2,1)} %get-tuple-element.328.refs_1_.refs_0_, bf16[1024,384]{1,0:T(8,128)(2,1)} %get-tuple-element.329.refs_2_.refs_1_, bf16[1024,384]{1,0:T(8,128)(2,1)} %get-tuple-element.330.refs_3_.refs_2_, ...), custom_call_target="tpu_custom_call" | custom-call | flops 115000000512 | bytes 1 | tf_op jit(solution)/shard_map/attn_back_own/pallas_call | solution.py:126
  474.7 3.6 fold.19
  480.3 4.8 convert_add_fusion
  485.1 6.4 %collective-permute-done.54 = bf16[192,768]{1,0:T(8,128)(2,1)S(1)} collective-permute-done((bf16[192,768]{1,0:T(8,128)(2,1)S(1)}, bf16[192,768]{1,0:T(8,128)(2,1)S(1)}, u32[]{:S(2)}, u32[]{:S(2)}) %collective-permute-start.54) | collective-permute-done | bytes 294944 | tf_op jit(solution)/shard_map/ppermute | solution.py:855
  492.6 3.0 collective-permute-start.60
  509.3 6.1 %close_block.1 = f32[512,1536]{1,0:T(8,128)} custom-call(s32[5]{0:T(128)} %stack.23.where_ref.w, bf16[512,1536]{1,0:T(8,128)(2,1)} %get-tuple-element.362.refs_0_, bf16[2048,1536]{1,0:T(8,128)(2,1)} %refs_1_.13, f32[1024,1]{1,0:T(8,128)} %get-tuple-element.203.refs_1_.refs_2_, f32[1,1536]{1,0:T(1,128)} %broadcast_in_dim.16.refs_1_.refs_20_.refs_3_, ...), custom_call_target="tpu_custom_call" | custom-call | flops 115000000512 | bytes 1 | tf_op jit(solution)/shard_map/close_block/pallas_call | solution.py:51
  (258 shorter events, 107.2 us)
Async XLA Ops:
  3.8 24.9 %collective-permute-start = (bf16[192,768]{1,0:T(8,128)(2,1)}, bf16[192,768]{1,0:T(8,128)(2,1)}, u32[]{:S(2)}, u32[]{:S(2)}) collective-permute-start(bf16[192,768]{1,0:T(8,128)(2,1)} %collect.5.refs_3_), channel_id=1, source_target_pairs={{2,0},{3,1},{0,2},{1,3},{6,4},{7,5},{4,6},{5,7},{10,8},{11,9},{8,1... | collective-permute-start | bytes 884744 | tf_op jit(solution)/shard_map/ppermute | solution.py:851
  7.9 20.8 %collective-permute-start.1 = (f32[6]{0:T(128)}, f32[6]{0:T(128)}, u32[]{:S(2)}, u32[]{:S(2)}) collective-permute-start(f32[6]{0:T(128)} %param.22), channel_id=1, source_target_pairs={{2,0},{3,1},{0,2},{1,3},{6,4},{7,5},{4,6},{5,7},{10,8},{11,9},{8,1... | collective-permute-start | bytes 80 | tf_op jit(solution)/shard_map/ppermute | solution.py:851
  28.7 20.7 %collective-permute-start.4 = (bf16[192,768]{1,0:T(8,128)(2,1)}, bf16[192,768]{1,0:T(8,128)(2,1)S(1)}, u32[]{:S(2)}, u32[]{:S(2)}) collective-permute-start(bf16[192,768]{1,0:T(8,128)(2,1)} %collective-permute-done.refs_0_), channel_id=1, source_target_pairs={{0,8},{4,12},{8,0},{12,4},{16,24},{20,28},{24,16},{28,20},{1,9},{5... | collective-permute-start | bytes 884744 | tf_op jit(solution)/shard_map/ppermute | solution.py:858
  30.5 20.4 %collective-permute-start.5 = (bf16[192,768]{1,0:T(8,128)(2,1)}, bf16[192,768]{1,0:T(8,128)(2,1)S(1)}, u32[]{:S(2)}, u32[]{:S(2)}) collective-permute-start(bf16[192,768]{1,0:T(8,128)(2,1)} %collective-permute-done.refs_0_), channel_id=1, source_target_pairs={{0,16},{4,20},{8,24},{12,28},{16,0},{20,4},{24,8},{28,12},{1,17},{... | collective-permute-start | bytes 884744 | tf_op jit(solution)/shard_map/ppermute | solution.py:858
  32.0 20.5 %collective-permute-start.6 = (bf16[192,768]{1,0:T(8,128)(2,1)}, bf16[192,768]{1,0:T(8,128)(2,1)S(1)}, u32[]{:S(2)}, u32[]{:S(2)}) collective-permute-start(bf16[192,768]{1,0:T(8,128)(2,1)} %collective-permute-done.refs_0_), channel_id=1, source_target_pairs={{0,24},{4,28},{8,16},{12,20},{16,8},{20,12},{24,0},{28,4},{1,25},{... | collective-permute-start | bytes 884744 | tf_op jit(solution)/shard_map/ppermute | solution.py:858
  47.3 22.0 %collective-permute-start.3 = (bf16[1024,384]{1,0:T(8,128)(2,1)}, bf16[1024,384]{1,0:T(8,128)(2,1)}, u32[]{:S(2)}, u32[]{:S(2)}) collective-permute-start(bf16[1024,384]{1,0:T(8,128)(2,1)} %get-tuple-element.211.refs_5_.refs_1_.refs_4_), channel_id=1, source_target_pairs={{1,0},{0,1},{3,2},{2,3},{5,4},{4,5},{7,6},{6,7},{9,8},{8,9},{11,10... | collective-permute-start | bytes 2359304 | tf_op jit(solution)/shard_map/ppermute | solution.py:851
  49.4 19.9 %collective-permute-start.2 = (bf16[192,384]{1,0:T(8,128)(2,1)}, bf16[192,384]{1,0:T(8,128)(2,1)}, u32[]{:S(2)}, u32[]{:S(2)}) collective-permute-start(bf16[192,384]{1,0:T(8,128)(2,1)} %collect.7.refs_7_), channel_id=1, source_target_pairs={{2,0},{3,1},{0,2},{1,3},{6,4},{7,5},{4,6},{5,7},{10,8},{11,9},{8,1... | collective-permute-start | bytes 442376 | tf_op jit(solution)/shard_map/ppermute | solution.py:851
  49.4 19.9 %collective-permute-start.10 = (bf16[192,896]{1,0:T(8,128)(2,1)}, bf16[192,896]{1,0:T(8,128)(2,1)}, u32[]{:S(2)}, u32[]{:S(2)}) collective-permute-start(bf16[192,896]{1,0:T(8,128)(2,1)} %collective-permute-done.7.refs_0_), channel_id=1, source_target_pairs={{0,8},{4,12},{8,0},{12,4},{16,24},{20,28},{24,16},{28,20},{1,9},{5... | collective-permute-start | bytes 1032200 | tf_op jit(solution)/shard_map/ppermute | solution.py:858
  51.0 18.3 %collective-permute-start.11 = (bf16[192,896]{1,0:T(8,128)(2,1)}, bf16[192,896]{1,0:T(8,128)(2,1)}, u32[]{:S(2)}, u32[]{:S(2)}) collective-permute-start(bf16[192,896]{1,0:T(8,128)(2,1)} %collective-permute-done.7.refs_0_), channel_id=1, source_target_pairs={{0,16},{4,20},{8,24},{12,28},{16,0},{20,4},{24,8},{28,12},{1,17},{... | collective-permute-start | bytes 1032200 | tf_op jit(solution)/shard_map/ppermute | solution.py:858
  74.3 17.7 %collective-permute-start.8 = (bf16[192,768]{1,0:T(8,128)(2,1)S(1)}, bf16[192,768]{1,0:T(8,128)(2,1)S(1)}, u32[]{:S(2)}, u32[]{:S(2)}) collective-permute-start(bf16[192,768]{1,0:T(8,128)(2,1)S(1)} %pad_maximum_fusion.7), channel_id=1, source_target_pairs={{1,0},{0,1},{3,2},{2,3},{5,4},{4,5},{7,6},{6,7},{9,8},{8,9},{11,10... | collective-permute-start | bytes 884744 | tf_op jit(solution)/shard_map/ppermute | solution.py:851
  77.1 41.4 %collective-permute-start.17 = (bf16[192,2048]{1,0:T(8,128)(2,1)}, bf16[192,2048]{1,0:T(8,128)(2,1)}, u32[]{:S(2)}, u32[]{:S(2)}) collective-permute-start(bf16[192,2048]{1,0:T(8,128)(2,1)} %collect.8.refs_4_), channel_id=1, source_target_pairs={{2,0},{3,1},{0,2},{1,3},{6,4},{7,5},{4,6},{5,7},{10,8},{11,9},{8,1... | collective-permute-start | bytes 2359304 | tf_op jit(solution)/shard_map/ppermute | solution.py:851
  93.6 20.8 %collective-permute-start.15 = (bf16[192,1152]{1,0:T(8,128)(2,1)S(1)}, bf16[192,1152]{1,0:T(8,128)(2,1)S(1)}, u32[]{:S(2)}, u32[]{:S(2)}) collective-permute-start(bf16[192,1152]{1,0:T(8,128)(2,1)S(1)} %constant_dynamic-update-slice_fusion.refs_0_), channel_id=1, source_target_pairs={{0,16},{4,20},{8,24},{12,28},{16,0},{20,4},{24,8},{28,12},{1,17},{... | collective-permute-start | bytes 1327112 | tf_op jit(solution)/shard_map/ppermute | solution.py:858
  95.2 19.3 %collective-permute-start.16 = (bf16[192,1152]{1,0:T(8,128)(2,1)S(1)}, bf16[192,1152]{1,0:T(8,128)(2,1)S(1)}, u32[]{:S(2)}, u32[]{:S(2)}) collective-permute-start(bf16[192,1152]{1,0:T(8,128)(2,1)S(1)} %constant_dynamic-update-slice_fusion.refs_0_), channel_id=1, source_target_pairs={{0,24},{4,28},{8,16},{12,20},{16,8},{20,12},{24,0},{28,4},{1,25},{... | collective-permute-start | bytes 1327112 | tf_op jit(solution)/shard_map/ppermute | solution.py:858
  108.0 23.3 %collective-permute-start.19 = (bf16[1024,384]{1,0:T(8,128)(2,1)}, bf16[1024,384]{1,0:T(8,128)(2,1)}, u32[]{:S(2)}, u32[]{:S(2)}) collective-permute-start(bf16[1024,384]{1,0:T(8,128)(2,1)} %get-tuple-element.246.refs_6_.refs_2_.refs_4_), channel_id=1, source_target_pairs={{1,0},{0,1},{3,2},{2,3},{5,4},{4,5},{7,6},{6,7},{9,8},{8,9},{11,10... | collective-permute-start | bytes 2359304 | tf_op jit(solution)/shard_map/ppermute | solution.py:851
  118.4 26.6 %collective-permute-start.20 = (bf16[192,2048]{1,0:T(8,128)(2,1)}, bf16[192,2048]{1,0:T(8,128)(2,1)}, u32[]{:S(2)}, u32[]{:S(2)}) collective-permute-start(bf16[192,2048]{1,0:T(8,128)(2,1)} %collective-permute-done.17.refs_0_), channel_id=1, source_target_pairs={{0,8},{4,12},{8,0},{12,4},{16,24},{20,28},{24,16},{28,20},{1,9},{5... | collective-permute-start | bytes 2359304 | tf_op jit(solution)/shard_map/ppermute | solution.py:858
  119.6 35.3 %collective-permute-start.21 = (bf16[192,2048]{1,0:T(8,128)(2,1)}, bf16[192,2048]{1,0:T(8,128)(2,1)}, u32[]{:S(2)}, u32[]{:S(2)}) collective-permute-start(bf16[192,2048]{1,0:T(8,128)(2,1)} %collective-permute-done.17.refs_0_), channel_id=1, source_target_pairs={{0,16},{4,20},{8,24},{12,28},{16,0},{20,4},{24,8},{28,12},{1,17},{... | collective-permute-start | bytes 2359304 | tf_op jit(solution)/shard_map/ppermute | solution.py:858
  120.6 36.0 %collective-permute-start.22 = (bf16[192,2048]{1,0:T(8,128)(2,1)}, bf16[192,2048]{1,0:T(8,128)(2,1)}, u32[]{:S(2)}, u32[]{:S(2)}) collective-permute-start(bf16[192,2048]{1,0:T(8,128)(2,1)} %collective-permute-done.17.refs_0_), channel_id=1, source_target_pairs={{0,24},{4,28},{8,16},{12,20},{16,8},{20,12},{24,0},{28,4},{1,25},{... | collective-permute-start | bytes 2359304 | tf_op jit(solution)/shard_map/ppermute | solution.py:858
  131.3 25.2 %collective-permute-start.23 = (bf16[192,1024]{1,0:T(8,128)(2,1)}, bf16[192,1024]{1,0:T(8,128)(2,1)}, u32[]{:S(2)}, u32[]{:S(2)}) collective-permute-start(bf16[192,1024]{1,0:T(8,128)(2,1)} %collect.9.refs_9_), channel_id=1, source_target_pairs={{2,0},{3,1},{0,2},{1,3},{6,4},{7,5},{4,6},{5,7},{10,8},{11,9},{8,1... | collective-permute-start | bytes 1179656 | tf_op jit(solution)/shard_map/ppermute | solution.py:851
  156.5 47.7 %collective-permute-start.24 = (bf16[192,1024]{1,0:T(8,128)(2,1)}, bf16[192,1024]{1,0:T(8,128)(2,1)}, u32[]{:S(2)}, u32[]{:S(2)}) collective-permute-start(bf16[192,1024]{1,0:T(8,128)(2,1)} %collective-permute-done.23.refs_0_), channel_id=1, source_target_pairs={{0,8},{4,12},{8,0},{12,4},{16,24},{20,28},{24,16},{28,20},{1,9},{5... | collective-permute-start | bytes 1179656 | tf_op jit(solution)/shard_map/ppermute | solution.py:858
  157.3 47.0 %collective-permute-start.25 = (bf16[192,1024]{1,0:T(8,128)(2,1)}, bf16[192,1024]{1,0:T(8,128)(2,1)}, u32[]{:S(2)}, u32[]{:S(2)}) collective-permute-start(bf16[192,1024]{1,0:T(8,128)(2,1)} %collective-permute-done.23.refs_0_), channel_id=1, source_target_pairs={{0,16},{4,20},{8,24},{12,28},{16,0},{20,4},{24,8},{28,12},{1,17},{... | collective-permute-start | bytes 1179656 | tf_op jit(solution)/shard_map/ppermute | solution.py:858
  158.8 45.4 %collective-permute-start.26 = (bf16[192,1024]{1,0:T(8,128)(2,1)}, bf16[192,1024]{1,0:T(8,128)(2,1)}, u32[]{:S(2)}, u32[]{:S(2)}) collective-permute-start(bf16[192,1024]{1,0:T(8,128)(2,1)} %collective-permute-done.23.refs_0_), channel_id=1, source_target_pairs={{0,24},{4,28},{8,16},{12,20},{16,8},{20,12},{24,0},{28,4},{1,25},{... | collective-permute-start | bytes 1179656 | tf_op jit(solution)/shard_map/ppermute | solution.py:858
  215.4 38.1 %collective-permute-start.31 = (bf16[384,1536]{1,0:T(8,128)(2,1)}, bf16[384,1536]{1,0:T(8,128)(2,1)S(1)}, u32[]{:S(2)}, u32[]{:S(2)}) collective-permute-start(bf16[384,1536]{1,0:T(8,128)(2,1)} %get-tuple-element.266.refs_11_), channel_id=1, source_target_pairs={{0,16},{4,20},{8,24},{12,28},{16,0},{20,4},{24,8},{28,12},{1,17},{... | collective-permute-start | bytes 3538952 | tf_op jit(solution)/shard_map/ppermute | solution.py:858
  216.3 37.2 %collective-permute-start.32 = (bf16[384,1536]{1,0:T(8,128)(2,1)}, bf16[384,1536]{1,0:T(8,128)(2,1)S(1)}, u32[]{:S(2)}, u32[]{:S(2)}) collective-permute-start(bf16[384,1536]{1,0:T(8,128)(2,1)} %get-tuple-element.275), channel_id=1, source_target_pairs={{0,8},{4,12},{8,0},{12,4},{16,24},{20,28},{24,16},{28,20},{1,9},{5... | collective-permute-start | bytes 3538952 | tf_op jit(solution)/shard_map/ppermute | solution.py:858
  253.1 36.0 %collective-permute-start.30 = (bf16[512,1536]{1,0:T(8,128)(2,1)}, bf16[512,1536]{1,0:T(8,128)(2,1)}, u32[]{:S(2)}, u32[]{:S(2)}) collective-permute-start(bf16[512,1536]{1,0:T(8,128)(2,1)} %get-tuple-element.269), channel_id=1, source_target_pairs={{0,1},{1,0},{2,3},{3,2},{4,5},{5,4},{6,7},{7,6},{8,9},{9,8},{10,11... | collective-permute-start | bytes 4718600 | tf_op jit(solution)/shard_map/ppermute | solution.py:899
  259.4 41.2 %collective-permute-start.34 = (bf16[192,1536]{1,0:T(8,128)(2,1)}, bf16[192,1536]{1,0:T(8,128)(2,1)}, u32[]{:S(2)}, u32[]{:S(2)}) collective-permute-start(bf16[192,1536]{1,0:T(8,128)(2,1)} %get-tuple-element.277.refs_5_), channel_id=1, source_target_pairs={{0,8},{4,12},{8,0},{12,4},{16,24},{20,28},{24,16},{28,20},{1,9},{5... | collective-permute-start | bytes 1769480 | tf_op jit(solution)/shard_map/ppermute | solution.py:858
  260.7 39.9 %collective-permute-start.35 = (bf16[192,1536]{1,0:T(8,128)(2,1)}, bf16[192,1536]{1,0:T(8,128)(2,1)}, u32[]{:S(2)}, u32[]{:S(2)}) collective-permute-start(bf16[192,1536]{1,0:T(8,128)(2,1)} %get-tuple-element.281), channel_id=1, source_target_pairs={{0,16},{4,20},{8,24},{12,28},{16,0},{20,4},{24,8},{28,12},{1,17},{... | collective-permute-start | bytes 1769480 | tf_op jit(solution)/shard_map/ppermute | solution.py:858
  277.7 26.0 %collective-permute-start.33 = (bf16[768,3072]{1,0:T(8,128)(2,1)}, bf16[768,3072]{1,0:T(8,128)(2,1)S(1)}, u32[]{:S(2)}, u32[]{:S(2)}) collective-permute-start(bf16[768,3072]{1,0:T(8,128)(2,1)} %get-tuple-element.278.refs_9_), channel_id=1, source_target_pairs={{0,4},{4,0},{8,12},{12,8},{16,20},{20,16},{24,28},{28,24},{1,5},{5... | collective-permute-start | bytes 14155784 | tf_op jit(solution)/shard_map/ppermute | solution.py:858
  300.2 21.3 %collective-permute-start.39 = (bf16[512,768]{1,0:T(8,128)(2,1)}, bf16[512,768]{1,0:T(8,128)(2,1)}, u32[]{:S(2)}, u32[]{:S(2)}) collective-permute-start(bf16[512,768]{1,0:T(8,128)(2,1)} %get-tuple-element.290), channel_id=1, source_target_pairs={{1,0},{0,1},{3,2},{2,3},{5,4},{4,5},{7,6},{6,7},{9,8},{8,9},{11,10... | collective-permute-start | bytes 2359304 | tf_op jit(solution)/shard_map/ppermute | solution.py:851
  312.8 40.6 %collective-permute-start.37 = (bf16[384,1536]{1,0:T(8,128)(2,1)}, bf16[384,1536]{1,0:T(8,128)(2,1)}, u32[]{:S(2)}, u32[]{:S(2)}) collective-permute-start(bf16[384,1536]{1,0:T(8,128)(2,1)} %get-tuple-element.284.refs_5_), channel_id=1, source_target_pairs={{0,16},{4,20},{8,24},{12,28},{16,0},{20,4},{24,8},{28,12},{1,17},{... | collective-permute-start | bytes 3538952 | tf_op jit(solution)/shard_map/ppermute | solution.py:858
  321.5 38.6 %collective-permute-start.36 = (bf16[768,1536]{1,0:T(8,128)(2,1)}, bf16[768,1536]{1,0:T(8,128)(2,1)}, u32[]{:S(2)}, u32[]{:S(2)}) collective-permute-start(bf16[768,1536]{1,0:T(8,128)(2,1)} %get-tuple-element.294.refs_12_), channel_id=1, source_target_pairs={{0,4},{4,0},{8,12},{12,8},{16,20},{20,16},{24,28},{28,24},{1,5},{5... | collective-permute-start | bytes 7077896 | tf_op jit(solution)/shard_map/ppermute | solution.py:858
  321.6 31.9 %collective-permute-start.38 = (bf16[384,1536]{1,0:T(8,128)(2,1)}, bf16[384,1536]{1,0:T(8,128)(2,1)}, u32[]{:S(2)}, u32[]{:S(2)}) collective-permute-start(bf16[384,1536]{1,0:T(8,128)(2,1)} %get-tuple-element.289), channel_id=1, source_target_pairs={{0,8},{4,12},{8,0},{12,4},{16,24},{20,28},{24,16},{28,20},{1,9},{5... | collective-permute-start | bytes 3538952 | tf_op jit(solution)/shard_map/ppermute | solution.py:858
  322.4 42.4 %collective-permute-start.45 = (bf16[512,1536]{1,0:T(8,128)(2,1)}, bf16[512,1536]{1,0:T(8,128)(2,1)}, u32[]{:S(2)}, u32[]{:S(2)}) collective-permute-start(bf16[512,1536]{1,0:T(8,128)(2,1)} %get-tuple-element.311), channel_id=1, source_target_pairs={{0,1},{1,0},{2,3},{3,2},{4,5},{5,4},{6,7},{7,6},{8,9},{9,8},{10,11... | collective-permute-start | bytes 4718600 | tf_op jit(solution)/shard_map/ppermute | solution.py:899
  364.3 34.5 %collective-permute-start.40 = (bf16[384,768]{1,0:T(8,128)(2,1)}, bf16[384,768]{1,0:T(8,128)(2,1)}, u32[]{:S(2)}, u32[]{:S(2)}) collective-permute-start(bf16[384,768]{1,0:T(8,128)(2,1)} %get-tuple-element.312.refs_8_), channel_id=1, source_target_pairs={{0,16},{4,20},{8,24},{12,28},{16,0},{20,4},{24,8},{28,12},{1,17},{... | collective-permute-start | bytes 1769480 | tf_op jit(solution)/shard_map/ppermute | solution.py:858
  364.8 33.9 %collective-permute-start.41 = (bf16[384,768]{1,0:T(8,128)(2,1)}, bf16[384,768]{1,0:T(8,128)(2,1)}, u32[]{:S(2)}, u32[]{:S(2)}) collective-permute-start(bf16[384,768]{1,0:T(8,128)(2,1)} %get-tuple-element.306), channel_id=1, source_target_pairs={{0,8},{4,12},{8,0},{12,4},{16,24},{20,28},{24,16},{28,20},{1,9},{5... | collective-permute-start | bytes 1769480 | tf_op jit(solution)/shard_map/ppermute | solution.py:858
  370.8 33.4 %collective-permute-start.48 = (bf16[384,896]{1,0:T(8,128)(2,1)}, bf16[384,896]{1,0:T(8,128)(2,1)}, u32[]{:S(2)}, u32[]{:S(2)}) collective-permute-start(bf16[384,896]{1,0:T(8,128)(2,1)} %get-tuple-element.314.refs_12_), channel_id=1, source_target_pairs={{0,16},{4,20},{8,24},{12,28},{16,0},{20,4},{24,8},{28,12},{1,17},{... | collective-permute-start | bytes 2064392 | tf_op jit(solution)/shard_map/ppermute | solution.py:858
  375.0 29.2 %collective-permute-start.49 = (bf16[384,896]{1,0:T(8,128)(2,1)}, bf16[384,896]{1,0:T(8,128)(2,1)}, u32[]{:S(2)}, u32[]{:S(2)}) collective-permute-start(bf16[384,896]{1,0:T(8,128)(2,1)} %get-tuple-element.321), channel_id=1, source_target_pairs={{0,8},{4,12},{8,0},{12,4},{16,24},{20,28},{24,16},{28,20},{1,9},{5... | collective-permute-start | bytes 2064392 | tf_op jit(solution)/shard_map/ppermute | solution.py:858
  379.0 52.5 %collective-permute-start.52 = (bf16[192,3072]{1,0:T(8,128)(2,1)}, bf16[192,3072]{1,0:T(8,128)(2,1)}, u32[]{:S(2)}, u32[]{:S(2)}) collective-permute-start(bf16[192,3072]{1,0:T(8,128)(2,1)} %pad_maximum_fusion.1), channel_id=1, source_target_pairs={{0,2},{1,3},{2,0},{3,1},{4,6},{5,7},{6,4},{7,5},{8,10},{9,11},{10,... | collective-permute-start | bytes 3538952 | tf_op jit(solution)/shard_map/ppermute | solution.py:855
  402.1 30.6 %collective-permute-start.46 = (bf16[192,768]{1,0:T(8,128)(2,1)}, bf16[192,768]{1,0:T(8,128)(2,1)}, u32[]{:S(2)}, u32[]{:S(2)}) collective-permute-start(bf16[192,768]{1,0:T(8,128)(2,1)} %get-tuple-element.317.refs_8_), channel_id=1, source_target_pairs={{0,8},{4,12},{8,0},{12,4},{16,24},{20,28},{24,16},{28,20},{1,9},{5... | collective-permute-start | bytes 884744 | tf_op jit(solution)/shard_map/ppermute | solution.py:858
  403.3 29.4 %collective-permute-start.47 = (bf16[192,768]{1,0:T(8,128)(2,1)}, bf16[192,768]{1,0:T(8,128)(2,1)}, u32[]{:S(2)}, u32[]{:S(2)}) collective-permute-start(bf16[192,768]{1,0:T(8,128)(2,1)} %get-tuple-element.318), channel_id=1, source_target_pairs={{0,16},{4,20},{8,24},{12,28},{16,0},{20,4},{24,8},{28,12},{1,17},{... | collective-permute-start | bytes 884744 | tf_op jit(solution)/shard_map/ppermute | solution.py:858
  407.7 23.8 %collective-permute-start.50 = (bf16[192,896]{1,0:T(8,128)(2,1)}, bf16[192,896]{1,0:T(8,128)(2,1)S(1)}, u32[]{:S(2)}, u32[]{:S(2)}) collective-permute-start(bf16[192,896]{1,0:T(8,128)(2,1)} %get-tuple-element.322.refs_6_), channel_id=1, source_target_pairs={{0,8},{4,12},{8,0},{12,4},{16,24},{20,28},{24,16},{28,20},{1,9},{5... | collective-permute-start | bytes 1032200 | tf_op jit(solution)/shard_map/ppermute | solution.py:858
  409.1 22.4 %collective-permute-start.51 = (bf16[192,896]{1,0:T(8,128)(2,1)}, bf16[192,896]{1,0:T(8,128)(2,1)S(1)}, u32[]{:S(2)}, u32[]{:S(2)}) collective-permute-start(bf16[192,896]{1,0:T(8,128)(2,1)} %get-tuple-element.323), channel_id=1, source_target_pairs={{0,16},{4,20},{8,24},{12,28},{16,0},{20,4},{24,8},{28,12},{1,17},{... | collective-permute-start | bytes 1032200 | tf_op jit(solution)/shard_map/ppermute | solution.py:858
  431.6 19.4 %collective-permute-start.53 = (bf16[768,1792]{1,0:T(8,128)(2,1)}, bf16[768,1792]{1,0:T(8,128)(2,1)}, u32[]{:S(2)}, u32[]{:S(2)}) collective-permute-start(bf16[768,1792]{1,0:T(8,128)(2,1)} %get-tuple-element.340.refs_21_), channel_id=1, source_target_pairs={{0,4},{4,0},{8,12},{12,8},{16,20},{20,16},{24,28},{28,24},{1,5},{5... | collective-permute-start | bytes 8257544 | tf_op jit(solution)/shard_map/ppermute | solution.py:858
  432.7 37.3 %collective-permute-start.58 = (bf16[192,1792]{1,0:T(8,128)(2,1)}, bf16[192,1792]{1,0:T(8,128)(2,1)}, u32[]{:S(2)}, u32[]{:S(2)}) collective-permute-start(bf16[192,1792]{1,0:T(8,128)(2,1)} %pad_maximum_fusion.6), channel_id=1, source_target_pairs={{0,2},{1,3},{2,0},{3,1},{4,6},{5,7},{6,4},{7,5},{8,10},{9,11},{10,... | collective-permute-start | bytes 2064392 | tf_op jit(solution)/shard_map/ppermute | solution.py:855
  448.6 60.7 %collective-permute-start.59 = (bf16[512,1536]{1,0:T(8,128)(2,1)}, bf16[512,1536]{1,0:T(8,128)(2,1)}, u32[]{:S(2)}, u32[]{:S(2)}) collective-permute-start(bf16[512,1536]{1,0:T(8,128)(2,1)} %get-tuple-element.364), channel_id=1, source_target_pairs={{0,1},{1,0},{2,3},{3,2},{4,5},{5,4},{6,7},{7,6},{8,9},{9,8},{10,11... | collective-permute-start | bytes 4718600 | tf_op jit(solution)/shard_map/ppermute | solution.py:899
  455.5 17.9 %collective-permute-start.56 = (bf16[384,896]{1,0:T(8,128)(2,1)}, bf16[384,896]{1,0:T(8,128)(2,1)S(1)}, u32[]{:S(2)}, u32[]{:S(2)}) collective-permute-start(bf16[384,896]{1,0:T(8,128)(2,1)} %get-tuple-element.346.refs_21_), channel_id=1, source_target_pairs={{0,16},{4,20},{8,24},{12,28},{16,0},{20,4},{24,8},{28,12},{1,17},{... | collective-permute-start | bytes 2064392 | tf_op jit(solution)/shard_map/ppermute | solution.py:858
  456.6 17.3 %collective-permute-start.57 = (bf16[384,896]{1,0:T(8,128)(2,1)}, bf16[384,896]{1,0:T(8,128)(2,1)S(1)}, u32[]{:S(2)}, u32[]{:S(2)}) collective-permute-start(bf16[384,896]{1,0:T(8,128)(2,1)} %get-tuple-element.350), channel_id=1, source_target_pairs={{0,8},{4,12},{8,0},{12,4},{16,24},{20,28},{24,16},{28,20},{1,9},{5... | collective-permute-start | bytes 2064392 | tf_op jit(solution)/shard_map/ppermute | solution.py:858
  470.9 20.6 %collective-permute-start.54 = (bf16[192,768]{1,0:T(8,128)(2,1)S(1)}, bf16[192,768]{1,0:T(8,128)(2,1)S(1)}, u32[]{:S(2)}, u32[]{:S(2)}) collective-permute-start(bf16[192,768]{1,0:T(8,128)(2,1)S(1)} %bitcast.20), channel_id=1, source_target_pairs={{0,2},{1,3},{2,0},{3,1},{4,6},{5,7},{6,4},{7,5},{8,10},{9,11},{10,... | collective-permute-start | bytes 884744 | tf_op jit(solution)/shard_map/ppermute | solution.py:855
  478.3 23.3 %collective-permute-start.63 = (bf16[192,896]{1,0:T(8,128)(2,1)}, bf16[192,896]{1,0:T(8,128)(2,1)S(1)}, u32[]{:S(2)}, u32[]{:S(2)}) collective-permute-start(bf16[192,896]{1,0:T(8,128)(2,1)} %get-tuple-element.381.refs_6_), channel_id=1, source_target_pairs={{0,8},{4,12},{8,0},{12,4},{16,24},{20,28},{24,16},{28,20},{1,9},{5... | collective-permute-start | bytes 1032200 | tf_op jit(solution)/shard_map/ppermute | solution.py:858
  (59 other events, 573.2 us)

commit v7 on v6

--- a/solution.py
+++ b/solution.py
@@ -1078,16 +1078,17 @@
     out_got = [to_member(v, s) for v, s in zip(out_send, peers)]
     for j in turns:
         attend_back(j)
-        attn_grads(j, both_ways)
     for j in turns:
         mlp_sums[j].hop()
+    for j in turns:
+        attn_grads(j, both_ways)
+    out_got = go.sync(*out_got)
     out_sum.hop()
-    out_got = go.sync(*out_got)
-    for j in turns:
-        attn_sums[j].hop()
     for j in turns:
         mlp_sums[j].wait()
     mlp_other = [here.deliver(low(mlp_sums[j].close()), 0, j) for j in turns]
+    for j in turns:
+        attn_sums[j].hop()
     attend_back(0)
     out_sum.hop()
     for j in turns:

time: 527 us -> 528 us (level)
    ppermute x4, waiting for transfers between devices: 16.6 us -> 9.97 us  [deliver(): return lax.ppermute(value, 'tensor', pairs)]
    unnamed x85 -> x93, local copies, waits for them, and re-layouts: 11.8 us -> 14.3 us
  transfers between devices with their start and end apart: 67 -> 67, of which waited for: 14 -> 13; matrix products, arithmetic and copies ran while one was open for 7% -> 7% of each run, Pallas kernels for 63% -> 63%
where the time goes in v7:
time: 528 us; the launch traced here: 519 us
  Pallas kernels  332 us (63%)
  waiting for transfers between devices  69.1 us (13%)
  starting transfers between devices  67.8 us (13%)
  local copies, waits for them, and re-layouts  25.7 us (5%)
  other arithmetic  22.3 us (4%)
    pallas_call x26, Pallas kernels, run(): pl.pallas_call(kernel, grid_spec=pltpu.PrefetchScalarGridSpec(num_scalar_...  247 us
    pallas_call x6, Pallas kernels, stream(): pl.pallas_call(kernel, grid_spec=pltpu.PrefetchScalarGridSpec(num_scalar_...  70.5 us
    ppermute x48, starting transfers between devices, swap(): return lax.ppermute(value, 'dp', [(i, i ^ bit) for i in range(self.dp)])  42.3 us
    ppermute x48, waiting for transfers between devices, swap(): return lax.ppermute(value, 'dp', [(i, i ^ bit) for i in range(self.dp)])  27.5 us
    ppermute x10, waiting for transfers between devices, fetch(): return lax.ppermute(value, 'tensor', pairs)  18 us
    pallas_call x5, Pallas kernels, assemble(): pl.pallas_call(kernel, grid_spec=pltpu.PrefetchScalarGridSpec(num_scalar_...  15 us
    unnamed x93, local copies, waits for them, and re-layouts  14.3 us
    ppermute x10, starting transfers between devices, fetch(): return lax.ppermute(value, 'tensor', pairs)  13.5 us
  transfers between devices with their start and end apart: 67, of which 13 were waited for; matrix products, arithmetic and copies ran while one was open for 7% of the time, Pallas kernels for 63%

profile of v7, /device:TPU:0, one launch (start us, length us, event | category | flops | bytes accessed | tf_op | source)
XLA Modules:
  0.0 519.1 jit_solution(2322207504919091960)
XLA Ops:
  1.3 2.5 collect.5.refs_3_
  3.8 4.0 collective-permute-start
  11.9 12.8 %project_own.1 = (bf16[1024,1536]{1,0:T(8,128)(2,1)}, f32[1024,1]{1,0:T(8,128)}, bf16[1024,384]{1,0:T(8,128)(2,1)}, bf16[1024,384]{1,0:T(8,128)(2,1)}, bf16[1024...) custom-call(s32[5]{0:T(128)} %stack.23.where_ref.w, ...), custom_call_target="tpu_custom_call" | custom-call | flops 115000000512 | bytes 1 | tf_op jit(solution)/shard_map/project_own/pallas_call | solution.py:51
  32.2 2.9 collective-permute-start.7
  35.1 12.2 %attend_forward.2 = (bf16[1024,384]{1,0:T(8,128)(2,1)}, f32[3,2,1024]{2,1,0:T(2,128)}) custom-call(s32[5]{0:T(128)} %stack.23.where_ref.w, bf16[1024,384]{1,0:T(8,128)(2,1)} %get-tuple-element.205.refs_0_, bf16[1024,384]{1,0:T(8,128)(2,1)} %get-tuple-element.206.refs_1_, bf16[1024,384]{1,0:T(8,128)(2,1)} %get-tuple-element.207.refs_2_, ...), custom_call_target="tpu_custom_call" | custom-call | flops 115000000512 | bytes 1 | tf_op jit(solution)/shard_map/attend_forward/pallas_call | solution.py:51
  53.2 2.7 assemble.5.refs_2_.refs_12_
  55.9 2.7 collect.8.refs_4_
  58.6 10.6 %collective-permute-done.3.refs_7_.refs_3_ = bf16[1024,384]{1,0:T(8,128)(2,1)} collective-permute-done((bf16[1024,384]{1,0:T(8,128)(2,1)}, bf16[1024,384]{1,0:T(8,128)(2,1)}, u32[]{:S(2)}, u32[]{:S(2)}) %collective-permute-start.3) | collective-permute-done | bytes 786464 | tf_op jit(solution)/shard_map/ppermute | solution.py:851
  69.3 2.8 assemble.6.refs_4_.refs_6_.refs_17_
  74.3 2.8 collective-permute-start.8
  80.5 11.5 %project_other.1 = (bf16[1024,384]{1,0:T(8,128)(2,1)}, bf16[1024,384]{1,0:T(8,128)(2,1)}, bf16[1024,384]{1,0:T(8,128)(2,1)}, bf16[1024,384]{1,0:T(8,128)(2,1)}, ...) custom-call(s32[5]{0:T(128)} %stack.23.where_ref.w, ...), custom_call_target="tpu_custom_call" | custom-call | flops 115000000512 | bytes 1 | tf_op jit(solution)/shard_map/project_other/pallas_call | solution.py:51
  95.6 12.4 %attend_forward.3 = (bf16[1024,384]{1,0:T(8,128)(2,1)}, f32[3,2,1024]{2,1,0:T(2,128)}) custom-call(s32[5]{0:T(128)} %stack.23.where_ref.w, bf16[1024,384]{1,0:T(8,128)(2,1)} %get-tuple-element.233.refs_0_, bf16[1024,384]{1,0:T(8,128)(2,1)} %get-tuple-element.234.refs_1_, bf16[1024,384]{1,0:T(8,128)(2,1)} %get-tuple-element.235.refs_2_, ...), custom_call_target="tpu_custom_call" | custom-call | flops 115000000512 | bytes 1 | tf_op jit(solution)/shard_map/attend_forward/pallas_call | solution.py:51
  108.5 5.9 %collective-permute-done.15.refs_2_ = bf16[192,1152]{1,0:T(8,128)(2,1)S(1)} collective-permute-done((bf16[192,1152]{1,0:T(8,128)(2,1)S(1)}, bf16[192,1152]{1,0:T(8,128)(2,1)S(1)}, u32[]{:S(2)}, u32[]{:S(2)}) %collective-permute-start.15) | collective-permute-done | bytes 442400 | tf_op jit(solution)/shard_map/ppermute | solution.py:858
  115.3 3.0 assemble.7.refs_1_.refs_2_.refs_6_
  121.9 2.4 collect.9.refs_9_
  124.4 6.9 %collective-permute-done.19.refs_8_.refs_4_ = bf16[1024,384]{1,0:T(8,128)(2,1)} collective-permute-done((bf16[1024,384]{1,0:T(8,128)(2,1)}, bf16[1024,384]{1,0:T(8,128)(2,1)}, u32[]{:S(2)}, u32[]{:S(2)}) %collective-permute-start.19) | collective-permute-done | bytes 786464 | tf_op jit(solution)/shard_map/ppermute | solution.py:851
  132.5 12.5 %close_attention.1 = (f32[1024,1536]{1,0:T(8,128)}, bf16[1024,1536]{1,0:T(8,128)(2,1)}, f32[1024,1]{1,0:T(8,128)}) custom-call(s32[5]{0:T(128)} %stack.23.where_ref.w, bf16[2048,1536]{1,0:T(8,128)(2,1)} %refs_1_.13, bf16[1536,384]{1,0:T(8,128)(2,1)} %refs_5_.7, bf16[768,1152]{1,0:T(8,128)(2,1)} %assemble.7.refs_1_.refs_2_.refs_6_, ...), custom_call_target="tpu_custom_call" | custom-call | flops 115000000512 | bytes 1 | tf_op jit(solution)/shard_map/close_attention/pallas_call | solution.py:51
  145.0 9.8 %collective-permute-done.21.refs_2_ = bf16[192,2048]{1,0:T(8,128)(2,1)} collective-permute-done((bf16[192,2048]{1,0:T(8,128)(2,1)}, bf16[192,2048]{1,0:T(8,128)(2,1)}, u32[]{:S(2)}, u32[]{:S(2)}) %collective-permute-start.21) | collective-permute-done | bytes 786464 | tf_op jit(solution)/shard_map/ppermute | solution.py:858
  160.0 40.1 %feed_forward.2 = (bf16[768,3072]{1,0:T(8,128)(2,1)}, bf16[768,3072]{1,0:T(8,128)(2,1)}, bf16[1024,1536]{1,0:T(8,128)(2,1)}, bf16[1024,1536]{1,0:T(8,128)(2,1)}) custom-call(s32[5]{0:T(128)} %stack.23.where_ref.w, bf16[1024,1536]{1,0:T(8,128)(2,1)} %get-tuple-element.252.refs_0_, bf16[2048,1536]{1,0:T(8,128)(2,1)} %refs_4_.5, ...), custom_call_target="tpu_custom_call" | custom-call | flops 115000000512 | bytes 1 | tf_op jit(solution)/shard_map/feed_forward/pallas_call | solution.py:51
  200.2 3.5 assemble.8.refs_4_.refs_3_
  204.2 3.0 assemble.9.refs_8_.refs_5_
  208.4 7.0 %fold.10 = (bf16[384,1536]{1,0:T(8,128)(2,1)}, bf16[384,1536]{1,0:T(8,128)(2,1)}, bf16[384,1536]{1,0:T(8,128)(2,1)}, bf16[384,1536]{1,0:T(8,128)(2,1)}) custom-call(s32[5]{0:T(128)} %stack.23.where_ref.w, bf16[768,3072]{1,0:T(8,128)(2,1)} %get-tuple-element.264.refs_0_.refs_2_.refs_4_.refs_6_, ...), custom_call_target="tpu_custom_call" | custom-call | flops 115000000512 | bytes 1 | tf_op jit(solution)/shard_map/fold/pallas_call | solution.py:51
  218.9 34.2 %feed_forward.3 = (bf16[1024,1024]{1,0:T(8,128)(2,1)}, bf16[1024,1024]{1,0:T(8,128)(2,1)}, bf16[1024,1024]{1,0:T(8,128)(2,1)}, bf16[512,1536]{1,0:T(8,128)(2,1)}...) custom-call(s32[5]{0:T(128)} %stack.23.where_ref.w, ...), custom_call_target="tpu_custom_call" | custom-call | flops 115000000512 | bytes 1 | tf_op jit(solution)/shard_map/feed_forward/pallas_call | solution.py:51
  254.9 4.4 fold.11
  261.2 16.5 %mlp_grads.1 = (bf16[768,3072]{1,0:T(8,128)(2,1)}, bf16[768,3072]{1,0:T(8,128)(2,1)}) custom-call(s32[5]{0:T(128)} %stack.23.where_ref.w, bf16[1024,1536]{1,0:T(8,128)(2,1)} %get-tuple-element.252.refs_0_, bf16[1024,1024]{1,0:T(8,128)(2,1)} %get-tuple-element.270.refs_1_, bf16[1024,1024]{1,0:T(8,128)(2,1)} %get-tuple-element.271.refs_2_, ...), custom_call_target="tpu_custom_call" | custom-call | flops 115000000512 | bytes 1 | tf_op jit(solution)/shard_map/mlp_grads/pallas_call | solution.py:126
  277.8 11.4 %collective-permute-done.30.refs_8_ = bf16[512,1536]{1,0:T(8,128)(2,1)} collective-permute-done((bf16[512,1536]{1,0:T(8,128)(2,1)}, bf16[512,1536]{1,0:T(8,128)(2,1)}, u32[]{:S(2)}, u32[]{:S(2)}) %collective-permute-start.30) | collective-permute-done | bytes 1572896 | tf_op jit(solution)/shard_map/ppermute | solution.py:899
  289.1 11.1 %close_feed_forward.1 = (f32[512,1536]{1,0:T(8,128)}, bf16[512,1536]{1,0:T(8,128)(2,1)}, bf16[512,768]{1,0:T(8,128)(2,1)}, bf16[512,768]{1,0:T(8,128)(2,1)}) custom-call(s32[5]{0:T(128)} %stack.23.where_ref.w, bf16[512,1536]{1,0:T(8,128)(2,1)} %get-tuple-element.267.refs_0_, f32[1024,1536]{1,0:T(8,128)} %get-tuple-element.268.refs_1_, ...), custom_call_target="tpu_custom_call" | custom-call | flops 115000000512 | bytes 1 | tf_op jit(solution)/shard_map/close_feed_forward/pallas_call | solution.py:51
  305.9 7.0 %fold.12 = (bf16[384,1536]{1,0:T(8,128)(2,1)}, bf16[384,1536]{1,0:T(8,128)(2,1)}, bf16[384,1536]{1,0:T(8,128)(2,1)}, bf16[384,1536]{1,0:T(8,128)(2,1)}) custom-call(s32[5]{0:T(128)} %stack.23.where_ref.w, bf16[768,3072]{1,0:T(8,128)(2,1)} %get-tuple-element.280.refs_0_.refs_2_.refs_4_.refs_6_, bf16[768,3072]{1,0:T(8,128)(2,1)} %copy-done.24, ...), custom_call_target="tpu_custom_call" | custom-call | flops 115000000512 | bytes 1 | tf_op jit(solution)/shard_map/fold/pallas_call | solution.py:51
  313.8 7.7 %out_grads.1 = (bf16[768,1536]{1,0:T(8,128)(2,1)}, bf16[768,1536]{1,0:T(8,128)(2,1)}) custom-call(s32[5]{0:T(128)} %stack.23.where_ref.w, bf16[512,1536]{1,0:T(8,128)(2,1)} %get-tuple-element.279.refs_0_, bf16[1024,384]{1,0:T(8,128)(2,1)} %get-tuple-element.211.refs_5_.refs_1_.refs_4_, bf16[1024,384]{1,0:T(8,128)(2,1)} %get-tuple-element.246.refs_6_.refs_2_.refs_4_, ...), custom_call_target="tpu_custom_call" | custom-call | flops 115000000512 | bytes 1 | tf_op jit(solution)/shard_map/out_grads/pallas_call | solution.py:126
  324.2 17.2 %attend_backward.2 = (bf16[1024,384]{1,0:T(8,128)(2,1)}, bf16[1024,384]{1,0:T(8,128)(2,1)}, bf16[1024,384]{1,0:T(8,128)(2,1)}, bf16[1024,384]{1,0:T(8,128)(2,1)}...) custom-call(s32[5]{0:T(128)} %stack.23.where_ref.w, bf16[1024,384]{1,0:T(8,128)(2,1)} %get-tuple-element.233.refs_0_, ...), custom_call_target="tpu_custom_call" | custom-call | flops 115000000512 | bytes 1 | tf_op jit(solution)/shard_map/attend_backward/pallas_call | solution.py:51
  341.5 8.6 %collective-permute-done.40.refs_5_.refs_7_ = bf16[384,1536]{1,0:T(8,128)(2,1)S(1)} collective-permute-done((bf16[384,1536]{1,0:T(8,128)(2,1)S(1)}, bf16[384,1536]{1,0:T(8,128)(2,1)S(1)}, u32[]{:S(2)}, u32[]{:S(2)}) %collective-permute-start.40) | collective-permute-done | bytes 1179680 | tf_op jit(solution)/shard_map/ppermute | solution.py:858
  351.1 4.7 fold.13
  358.1 11.6 %attn_grads.2 = (bf16[768,1792]{1,0:T(8,128)(2,1)}, bf16[768,1792]{1,0:T(8,128)(2,1)}) custom-call(s32[5]{0:T(128)} %stack.23.where_ref.w, bf16[1024,1536]{1,0:T(8,128)(2,1)} %get-tuple-element.222.refs_0_.refs_19_, bf16[1024,384]{1,0:T(8,128)(2,1)} %get-tuple-element.293.refs_1_.refs_10_, bf16[1024,384]{1,0:T(8,128)(2,1)} %get-tuple-element.294.refs_2_.refs_11_, ...), custom_call_target="tpu_custom_call" | custom-call | flops 115000000512 | bytes 1 | tf_op jit(solution)/shard_map/attn_grads/pallas_call | solution.py:126
  369.8 4.4 fold.14
  381.9 4.6 fold.15
  388.6 17.3 %attend_backward.3 = (bf16[1024,384]{1,0:T(8,128)(2,1)}, bf16[1024,384]{1,0:T(8,128)(2,1)}, bf16[1024,384]{1,0:T(8,128)(2,1)}, bf16[1024,384]{1,0:T(8,128)(2,1)}...) custom-call(s32[5]{0:T(128)} %stack.23.where_ref.w, bf16[1024,384]{1,0:T(8,128)(2,1)} %get-tuple-element.205.refs_0_, ...), custom_call_target="tpu_custom_call" | custom-call | flops 115000000512 | bytes 1 | tf_op jit(solution)/shard_map/attend_backward/pallas_call | solution.py:51
  406.0 3.4 fold.16
  412.3 3.5 fold.17
  417.8 11.6 %attn_grads.3 = (bf16[768,1792]{1,0:T(8,128)(2,1)}, bf16[768,1792]{1,0:T(8,128)(2,1)}) custom-call(s32[5]{0:T(128)} %stack.23.where_ref.w, bf16[1024,1536]{1,0:T(8,128)(2,1)} %get-tuple-element.222.refs_0_.refs_19_, bf16[1024,384]{1,0:T(8,128)(2,1)} %get-tuple-element.328.refs_1_.refs_0_, bf16[1024,384]{1,0:T(8,128)(2,1)} %get-tuple-element.329.refs_2_.refs_1_, ...), custom_call_target="tpu_custom_call" | custom-call | flops 115000000512 | bytes 1 | tf_op jit(solution)/shard_map/attn_grads/pallas_call | solution.py:126
  429.5 3.5 collective-permute-done.52
  434.2 11.6 %attn_back_send.1 = (bf16[512,1536]{1,0:T(8,128)(2,1)}, f32[1,1536]{1,0:T(1,128)}) custom-call(s32[5]{0:T(128)} %stack.23.where_ref.w, bf16[1024,384]{1,0:T(8,128)(2,1)} %get-tuple-element.328.refs_1_.refs_0_, bf16[1024,384]{1,0:T(8,128)(2,1)} %get-tuple-element.329.refs_2_.refs_1_, bf16[1024,384]{1,0:T(8,128)(2,1)} %get-tuple-element.330.refs_3_.refs_2_, ...), custom_call_target="tpu_custom_call" | custom-call | flops 115000000512 | bytes 1 | tf_op jit(solution)/shard_map/attn_back_send/pallas_call | solution.py:126
  452.4 4.6 fold.18
  459.4 11.4 %attn_back_own.1 = (bf16[512,1536]{1,0:T(8,128)(2,1)}, f32[1,1536]{1,0:T(1,128)}) custom-call(s32[5]{0:T(128)} %stack.23.where_ref.w, bf16[1024,384]{1,0:T(8,128)(2,1)} %get-tuple-element.328.refs_1_.refs_0_, bf16[1024,384]{1,0:T(8,128)(2,1)} %get-tuple-element.329.refs_2_.refs_1_, bf16[1024,384]{1,0:T(8,128)(2,1)} %get-tuple-element.330.refs_3_.refs_2_, ...), custom_call_target="tpu_custom_call" | custom-call | flops 115000000512 | bytes 1 | tf_op jit(solution)/shard_map/attn_back_own/pallas_call | solution.py:126
  476.1 3.6 fold.19
  481.7 4.8 convert_add_fusion
  486.5 6.5 %collective-permute-done.54 = bf16[192,768]{1,0:T(8,128)(2,1)S(1)} collective-permute-done((bf16[192,768]{1,0:T(8,128)(2,1)S(1)}, bf16[192,768]{1,0:T(8,128)(2,1)S(1)}, u32[]{:S(2)}, u32[]{:S(2)}) %collective-permute-start.54) | collective-permute-done | bytes 294944 | tf_op jit(solution)/shard_map/ppermute | solution.py:855
  494.0 3.1 collective-permute-start.60
  510.8 6.1 %close_block.1 = f32[512,1536]{1,0:T(8,128)} custom-call(s32[5]{0:T(128)} %stack.23.where_ref.w, bf16[512,1536]{1,0:T(8,128)(2,1)} %get-tuple-element.362.refs_0_, bf16[2048,1536]{1,0:T(8,128)(2,1)} %refs_1_.13, f32[1024,1]{1,0:T(8,128)} %get-tuple-element.203.refs_1_.refs_2_, f32[1,1536]{1,0:T(1,128)} %broadcast_in_dim.16.refs_1_.refs_20_.refs_3_, ...), custom_call_target="tpu_custom_call" | custom-call | flops 115000000512 | bytes 1 | tf_op jit(solution)/shard_map/close_block/pallas_call | solution.py:51
  (266 shorter events, 108.9 us)
Async XLA Ops:
  3.8 24.9 %collective-permute-start = (bf16[192,768]{1,0:T(8,128)(2,1)}, bf16[192,768]{1,0:T(8,128)(2,1)}, u32[]{:S(2)}, u32[]{:S(2)}) collective-permute-start(bf16[192,768]{1,0:T(8,128)(2,1)} %collect.5.refs_3_), channel_id=1, source_target_pairs={{2,0},{3,1},{0,2},{1,3},{6,4},{7,5},{4,6},{5,7},{10,8},{11,9},{8,1... | collective-permute-start | bytes 884744 | tf_op jit(solution)/shard_map/ppermute | solution.py:851
  7.9 20.9 %collective-permute-start.1 = (f32[6]{0:T(128)}, f32[6]{0:T(128)}, u32[]{:S(2)}, u32[]{:S(2)}) collective-permute-start(f32[6]{0:T(128)} %param.22), channel_id=1, source_target_pairs={{2,0},{3,1},{0,2},{1,3},{6,4},{7,5},{4,6},{5,7},{10,8},{11,9},{8,1... | collective-permute-start | bytes 80 | tf_op jit(solution)/shard_map/ppermute | solution.py:851
  28.7 20.6 %collective-permute-start.4 = (bf16[192,768]{1,0:T(8,128)(2,1)}, bf16[192,768]{1,0:T(8,128)(2,1)S(1)}, u32[]{:S(2)}, u32[]{:S(2)}) collective-permute-start(bf16[192,768]{1,0:T(8,128)(2,1)} %collective-permute-done.refs_0_), channel_id=1, source_target_pairs={{0,8},{4,12},{8,0},{12,4},{16,24},{20,28},{24,16},{28,20},{1,9},{5... | collective-permute-start | bytes 884744 | tf_op jit(solution)/shard_map/ppermute | solution.py:858
  30.5 20.4 %collective-permute-start.5 = (bf16[192,768]{1,0:T(8,128)(2,1)}, bf16[192,768]{1,0:T(8,128)(2,1)S(1)}, u32[]{:S(2)}, u32[]{:S(2)}) collective-permute-start(bf16[192,768]{1,0:T(8,128)(2,1)} %collective-permute-done.refs_0_), channel_id=1, source_target_pairs={{0,16},{4,20},{8,24},{12,28},{16,0},{20,4},{24,8},{28,12},{1,17},{... | collective-permute-start | bytes 884744 | tf_op jit(solution)/shard_map/ppermute | solution.py:858
  32.0 20.5 %collective-permute-start.6 = (bf16[192,768]{1,0:T(8,128)(2,1)}, bf16[192,768]{1,0:T(8,128)(2,1)S(1)}, u32[]{:S(2)}, u32[]{:S(2)}) collective-permute-start(bf16[192,768]{1,0:T(8,128)(2,1)} %collective-permute-done.refs_0_), channel_id=1, source_target_pairs={{0,24},{4,28},{8,16},{12,20},{16,8},{20,12},{24,0},{28,4},{1,25},{... | collective-permute-start | bytes 884744 | tf_op jit(solution)/shard_map/ppermute | solution.py:858
  47.3 22.0 %collective-permute-start.3 = (bf16[1024,384]{1,0:T(8,128)(2,1)}, bf16[1024,384]{1,0:T(8,128)(2,1)}, u32[]{:S(2)}, u32[]{:S(2)}) collective-permute-start(bf16[1024,384]{1,0:T(8,128)(2,1)} %get-tuple-element.211.refs_5_.refs_1_.refs_4_), channel_id=1, source_target_pairs={{1,0},{0,1},{3,2},{2,3},{5,4},{4,5},{7,6},{6,7},{9,8},{8,9},{11,10... | collective-permute-start | bytes 2359304 | tf_op jit(solution)/shard_map/ppermute | solution.py:851
  49.3 19.9 %collective-permute-start.2 = (bf16[192,384]{1,0:T(8,128)(2,1)}, bf16[192,384]{1,0:T(8,128)(2,1)}, u32[]{:S(2)}, u32[]{:S(2)}) collective-permute-start(bf16[192,384]{1,0:T(8,128)(2,1)} %collect.7.refs_7_), channel_id=1, source_target_pairs={{2,0},{3,1},{0,2},{1,3},{6,4},{7,5},{4,6},{5,7},{10,8},{11,9},{8,1... | collective-permute-start | bytes 442376 | tf_op jit(solution)/shard_map/ppermute | solution.py:851
  49.4 19.9 %collective-permute-start.10 = (bf16[192,896]{1,0:T(8,128)(2,1)}, bf16[192,896]{1,0:T(8,128)(2,1)}, u32[]{:S(2)}, u32[]{:S(2)}) collective-permute-start(bf16[192,896]{1,0:T(8,128)(2,1)} %collective-permute-done.7.refs_0_), channel_id=1, source_target_pairs={{0,8},{4,12},{8,0},{12,4},{16,24},{20,28},{24,16},{28,20},{1,9},{5... | collective-permute-start | bytes 1032200 | tf_op jit(solution)/shard_map/ppermute | solution.py:858
  51.0 18.3 %collective-permute-start.11 = (bf16[192,896]{1,0:T(8,128)(2,1)}, bf16[192,896]{1,0:T(8,128)(2,1)}, u32[]{:S(2)}, u32[]{:S(2)}) collective-permute-start(bf16[192,896]{1,0:T(8,128)(2,1)} %collective-permute-done.7.refs_0_), channel_id=1, source_target_pairs={{0,16},{4,20},{8,24},{12,28},{16,0},{20,4},{24,8},{28,12},{1,17},{... | collective-permute-start | bytes 1032200 | tf_op jit(solution)/shard_map/ppermute | solution.py:858
  74.3 17.7 %collective-permute-start.8 = (bf16[192,768]{1,0:T(8,128)(2,1)S(1)}, bf16[192,768]{1,0:T(8,128)(2,1)S(1)}, u32[]{:S(2)}, u32[]{:S(2)}) collective-permute-start(bf16[192,768]{1,0:T(8,128)(2,1)S(1)} %pad_maximum_fusion.7), channel_id=1, source_target_pairs={{1,0},{0,1},{3,2},{2,3},{5,4},{4,5},{7,6},{6,7},{9,8},{8,9},{11,10... | collective-permute-start | bytes 884744 | tf_op jit(solution)/shard_map/ppermute | solution.py:851
  77.1 41.3 %collective-permute-start.17 = (bf16[192,2048]{1,0:T(8,128)(2,1)}, bf16[192,2048]{1,0:T(8,128)(2,1)}, u32[]{:S(2)}, u32[]{:S(2)}) collective-permute-start(bf16[192,2048]{1,0:T(8,128)(2,1)} %collect.8.refs_4_), channel_id=1, source_target_pairs={{2,0},{3,1},{0,2},{1,3},{6,4},{7,5},{4,6},{5,7},{10,8},{11,9},{8,1... | collective-permute-start | bytes 2359304 | tf_op jit(solution)/shard_map/ppermute | solution.py:851
  93.6 20.8 %collective-permute-start.15 = (bf16[192,1152]{1,0:T(8,128)(2,1)S(1)}, bf16[192,1152]{1,0:T(8,128)(2,1)S(1)}, u32[]{:S(2)}, u32[]{:S(2)}) collective-permute-start(bf16[192,1152]{1,0:T(8,128)(2,1)S(1)} %constant_dynamic-update-slice_fusion.refs_0_), channel_id=1, source_target_pairs={{0,16},{4,20},{8,24},{12,28},{16,0},{20,4},{24,8},{28,12},{1,17},{... | collective-permute-start | bytes 1327112 | tf_op jit(solution)/shard_map/ppermute | solution.py:858
  95.1 19.3 %collective-permute-start.16 = (bf16[192,1152]{1,0:T(8,128)(2,1)S(1)}, bf16[192,1152]{1,0:T(8,128)(2,1)S(1)}, u32[]{:S(2)}, u32[]{:S(2)}) collective-permute-start(bf16[192,1152]{1,0:T(8,128)(2,1)S(1)} %constant_dynamic-update-slice_fusion.refs_0_), channel_id=1, source_target_pairs={{0,24},{4,28},{8,16},{12,20},{16,8},{20,12},{24,0},{28,4},{1,25},{... | collective-permute-start | bytes 1327112 | tf_op jit(solution)/shard_map/ppermute | solution.py:858
  108.0 23.3 %collective-permute-start.19 = (bf16[1024,384]{1,0:T(8,128)(2,1)}, bf16[1024,384]{1,0:T(8,128)(2,1)}, u32[]{:S(2)}, u32[]{:S(2)}) collective-permute-start(bf16[1024,384]{1,0:T(8,128)(2,1)} %get-tuple-element.246.refs_6_.refs_2_.refs_4_), channel_id=1, source_target_pairs={{1,0},{0,1},{3,2},{2,3},{5,4},{4,5},{7,6},{6,7},{9,8},{8,9},{11,10... | collective-permute-start | bytes 2359304 | tf_op jit(solution)/shard_map/ppermute | solution.py:851
  118.4 26.6 %collective-permute-start.20 = (bf16[192,2048]{1,0:T(8,128)(2,1)}, bf16[192,2048]{1,0:T(8,128)(2,1)}, u32[]{:S(2)}, u32[]{:S(2)}) collective-permute-start(bf16[192,2048]{1,0:T(8,128)(2,1)} %collective-permute-done.17.refs_0_), channel_id=1, source_target_pairs={{0,8},{4,12},{8,0},{12,4},{16,24},{20,28},{24,16},{28,20},{1,9},{5... | collective-permute-start | bytes 2359304 | tf_op jit(solution)/shard_map/ppermute | solution.py:858
  119.5 35.3 %collective-permute-start.21 = (bf16[192,2048]{1,0:T(8,128)(2,1)}, bf16[192,2048]{1,0:T(8,128)(2,1)}, u32[]{:S(2)}, u32[]{:S(2)}) collective-permute-start(bf16[192,2048]{1,0:T(8,128)(2,1)} %collective-permute-done.17.refs_0_), channel_id=1, source_target_pairs={{0,16},{4,20},{8,24},{12,28},{16,0},{20,4},{24,8},{28,12},{1,17},{... | collective-permute-start | bytes 2359304 | tf_op jit(solution)/shard_map/ppermute | solution.py:858
  120.5 36.0 %collective-permute-start.22 = (bf16[192,2048]{1,0:T(8,128)(2,1)}, bf16[192,2048]{1,0:T(8,128)(2,1)}, u32[]{:S(2)}, u32[]{:S(2)}) collective-permute-start(bf16[192,2048]{1,0:T(8,128)(2,1)} %collective-permute-done.17.refs_0_), channel_id=1, source_target_pairs={{0,24},{4,28},{8,16},{12,20},{16,8},{20,12},{24,0},{28,4},{1,25},{... | collective-permute-start | bytes 2359304 | tf_op jit(solution)/shard_map/ppermute | solution.py:858
  131.3 25.2 %collective-permute-start.23 = (bf16[192,1024]{1,0:T(8,128)(2,1)}, bf16[192,1024]{1,0:T(8,128)(2,1)}, u32[]{:S(2)}, u32[]{:S(2)}) collective-permute-start(bf16[192,1024]{1,0:T(8,128)(2,1)} %collect.9.refs_9_), channel_id=1, source_target_pairs={{2,0},{3,1},{0,2},{1,3},{6,4},{7,5},{4,6},{5,7},{10,8},{11,9},{8,1... | collective-permute-start | bytes 1179656 | tf_op jit(solution)/shard_map/ppermute | solution.py:851
  156.5 47.7 %collective-permute-start.24 = (bf16[192,1024]{1,0:T(8,128)(2,1)}, bf16[192,1024]{1,0:T(8,128)(2,1)}, u32[]{:S(2)}, u32[]{:S(2)}) collective-permute-start(bf16[192,1024]{1,0:T(8,128)(2,1)} %collective-permute-done.23.refs_0_), channel_id=1, source_target_pairs={{0,8},{4,12},{8,0},{12,4},{16,24},{20,28},{24,16},{28,20},{1,9},{5... | collective-permute-start | bytes 1179656 | tf_op jit(solution)/shard_map/ppermute | solution.py:858
  157.3 46.9 %collective-permute-start.25 = (bf16[192,1024]{1,0:T(8,128)(2,1)}, bf16[192,1024]{1,0:T(8,128)(2,1)}, u32[]{:S(2)}, u32[]{:S(2)}) collective-permute-start(bf16[192,1024]{1,0:T(8,128)(2,1)} %collective-permute-done.23.refs_0_), channel_id=1, source_target_pairs={{0,16},{4,20},{8,24},{12,28},{16,0},{20,4},{24,8},{28,12},{1,17},{... | collective-permute-start | bytes 1179656 | tf_op jit(solution)/shard_map/ppermute | solution.py:858
  158.8 45.4 %collective-permute-start.26 = (bf16[192,1024]{1,0:T(8,128)(2,1)}, bf16[192,1024]{1,0:T(8,128)(2,1)}, u32[]{:S(2)}, u32[]{:S(2)}) collective-permute-start(bf16[192,1024]{1,0:T(8,128)(2,1)} %collective-permute-done.23.refs_0_), channel_id=1, source_target_pairs={{0,24},{4,28},{8,16},{12,20},{16,8},{20,12},{24,0},{28,4},{1,25},{... | collective-permute-start | bytes 1179656 | tf_op jit(solution)/shard_map/ppermute | solution.py:858
  215.4 38.1 %collective-permute-start.31 = (bf16[384,1536]{1,0:T(8,128)(2,1)}, bf16[384,1536]{1,0:T(8,128)(2,1)S(1)}, u32[]{:S(2)}, u32[]{:S(2)}) collective-permute-start(bf16[384,1536]{1,0:T(8,128)(2,1)} %get-tuple-element.266.refs_11_), channel_id=1, source_target_pairs={{0,16},{4,20},{8,24},{12,28},{16,0},{20,4},{24,8},{28,12},{1,17},{... | collective-permute-start | bytes 3538952 | tf_op jit(solution)/shard_map/ppermute | solution.py:858
  216.2 37.3 %collective-permute-start.32 = (bf16[384,1536]{1,0:T(8,128)(2,1)}, bf16[384,1536]{1,0:T(8,128)(2,1)S(1)}, u32[]{:S(2)}, u32[]{:S(2)}) collective-permute-start(bf16[384,1536]{1,0:T(8,128)(2,1)} %get-tuple-element.275), channel_id=1, source_target_pairs={{0,8},{4,12},{8,0},{12,4},{16,24},{20,28},{24,16},{28,20},{1,9},{5... | collective-permute-start | bytes 3538952 | tf_op jit(solution)/shard_map/ppermute | solution.py:858
  253.1 36.0 %collective-permute-start.30 = (bf16[512,1536]{1,0:T(8,128)(2,1)}, bf16[512,1536]{1,0:T(8,128)(2,1)}, u32[]{:S(2)}, u32[]{:S(2)}) collective-permute-start(bf16[512,1536]{1,0:T(8,128)(2,1)} %get-tuple-element.269), channel_id=1, source_target_pairs={{0,1},{1,0},{2,3},{3,2},{4,5},{5,4},{6,7},{7,6},{8,9},{9,8},{10,11... | collective-permute-start | bytes 4718600 | tf_op jit(solution)/shard_map/ppermute | solution.py:899
  259.4 41.2 %collective-permute-start.34 = (bf16[192,1536]{1,0:T(8,128)(2,1)}, bf16[192,1536]{1,0:T(8,128)(2,1)}, u32[]{:S(2)}, u32[]{:S(2)}) collective-permute-start(bf16[192,1536]{1,0:T(8,128)(2,1)} %get-tuple-element.277.refs_5_), channel_id=1, source_target_pairs={{0,8},{4,12},{8,0},{12,4},{16,24},{20,28},{24,16},{28,20},{1,9},{5... | collective-permute-start | bytes 1769480 | tf_op jit(solution)/shard_map/ppermute | solution.py:858
  260.7 39.9 %collective-permute-start.35 = (bf16[192,1536]{1,0:T(8,128)(2,1)}, bf16[192,1536]{1,0:T(8,128)(2,1)}, u32[]{:S(2)}, u32[]{:S(2)}) collective-permute-start(bf16[192,1536]{1,0:T(8,128)(2,1)} %get-tuple-element.281), channel_id=1, source_target_pairs={{0,16},{4,20},{8,24},{12,28},{16,0},{20,4},{24,8},{28,12},{1,17},{... | collective-permute-start | bytes 1769480 | tf_op jit(solution)/shard_map/ppermute | solution.py:858
  277.7 26.1 %collective-permute-start.33 = (bf16[768,3072]{1,0:T(8,128)(2,1)}, bf16[768,3072]{1,0:T(8,128)(2,1)S(1)}, u32[]{:S(2)}, u32[]{:S(2)}) collective-permute-start(bf16[768,3072]{1,0:T(8,128)(2,1)} %get-tuple-element.278.refs_9_), channel_id=1, source_target_pairs={{0,4},{4,0},{8,12},{12,8},{16,20},{20,16},{24,28},{28,24},{1,5},{5... | collective-permute-start | bytes 14155784 | tf_op jit(solution)/shard_map/ppermute | solution.py:858
  300.2 21.4 %collective-permute-start.37 = (bf16[512,768]{1,0:T(8,128)(2,1)}, bf16[512,768]{1,0:T(8,128)(2,1)}, u32[]{:S(2)}, u32[]{:S(2)}) collective-permute-start(bf16[512,768]{1,0:T(8,128)(2,1)} %get-tuple-element.287), channel_id=1, source_target_pairs={{1,0},{0,1},{3,2},{2,3},{5,4},{4,5},{7,6},{6,7},{9,8},{8,9},{11,10... | collective-permute-start | bytes 2359304 | tf_op jit(solution)/shard_map/ppermute | solution.py:851
  312.9 28.6 %collective-permute-start.39 = (bf16[384,1536]{1,0:T(8,128)(2,1)}, bf16[384,1536]{1,0:T(8,128)(2,1)}, u32[]{:S(2)}, u32[]{:S(2)}) collective-permute-start(bf16[384,1536]{1,0:T(8,128)(2,1)} %get-tuple-element.284.refs_5_), channel_id=1, source_target_pairs={{0,16},{4,20},{8,24},{12,28},{16,0},{20,4},{24,8},{28,12},{1,17},{... | collective-permute-start | bytes 3538952 | tf_op jit(solution)/shard_map/ppermute | solution.py:858
  321.6 48.2 %collective-permute-start.36 = (bf16[768,1536]{1,0:T(8,128)(2,1)}, bf16[768,1536]{1,0:T(8,128)(2,1)}, u32[]{:S(2)}, u32[]{:S(2)}) collective-permute-start(bf16[768,1536]{1,0:T(8,128)(2,1)} %get-tuple-element.292.refs_12_), channel_id=1, source_target_pairs={{0,4},{4,0},{8,12},{12,8},{16,20},{20,16},{24,28},{28,24},{1,5},{5... | collective-permute-start | bytes 7077896 | tf_op jit(solution)/shard_map/ppermute | solution.py:858
  321.7 28.4 %collective-permute-start.40 = (bf16[384,1536]{1,0:T(8,128)(2,1)S(1)}, bf16[384,1536]{1,0:T(8,128)(2,1)S(1)}, u32[]{:S(2)}, u32[]{:S(2)}) collective-permute-start(bf16[384,1536]{1,0:T(8,128)(2,1)S(1)} %copy-done.30), channel_id=1, source_target_pairs={{0,8},{4,12},{8,0},{12,4},{16,24},{20,28},{24,16},{28,20},{1,9},{5... | collective-permute-start | bytes 3538952 | tf_op jit(solution)/shard_map/ppermute | solution.py:858
  322.6 47.2 %collective-permute-start.38 = (bf16[512,1536]{1,0:T(8,128)(2,1)}, bf16[512,1536]{1,0:T(8,128)(2,1)}, u32[]{:S(2)}, u32[]{:S(2)}) collective-permute-start(bf16[512,1536]{1,0:T(8,128)(2,1)} %get-tuple-element.289), channel_id=1, source_target_pairs={{0,1},{1,0},{2,3},{3,2},{4,5},{5,4},{6,7},{7,6},{8,9},{9,8},{10,11... | collective-permute-start | bytes 4718600 | tf_op jit(solution)/shard_map/ppermute | solution.py:899
  355.7 19.1 %collective-permute-start.44 = (bf16[192,1536]{1,0:T(8,128)(2,1)}, bf16[192,1536]{1,0:T(8,128)(2,1)}, u32[]{:S(2)}, u32[]{:S(2)}) collective-permute-start(bf16[192,1536]{1,0:T(8,128)(2,1)} %get-tuple-element.302.refs_6_), channel_id=1, source_target_pairs={{0,8},{4,12},{8,0},{12,4},{16,24},{20,28},{24,16},{28,20},{1,9},{5... | collective-permute-start | bytes 1769480 | tf_op jit(solution)/shard_map/ppermute | solution.py:858
  356.6 18.2 %collective-permute-start.45 = (bf16[192,1536]{1,0:T(8,128)(2,1)}, bf16[192,1536]{1,0:T(8,128)(2,1)}, u32[]{:S(2)}, u32[]{:S(2)}) collective-permute-start(bf16[192,1536]{1,0:T(8,128)(2,1)} %get-tuple-element.312), channel_id=1, source_target_pairs={{0,16},{4,20},{8,24},{12,28},{16,0},{20,4},{24,8},{28,12},{1,17},{... | collective-permute-start | bytes 1769480 | tf_op jit(solution)/shard_map/ppermute | solution.py:858
  374.2 31.8 %collective-permute-start.41 = (bf16[384,768]{1,0:T(8,128)(2,1)}, bf16[384,768]{1,0:T(8,128)(2,1)}, u32[]{:S(2)}, u32[]{:S(2)}) collective-permute-start(bf16[384,768]{1,0:T(8,128)(2,1)} %get-tuple-element.313.refs_8_), channel_id=1, source_target_pairs={{0,16},{4,20},{8,24},{12,28},{16,0},{20,4},{24,8},{28,12},{1,17},{... | collective-permute-start | bytes 1769480 | tf_op jit(solution)/shard_map/ppermute | solution.py:858
  374.8 31.2 %collective-permute-start.42 = (bf16[384,768]{1,0:T(8,128)(2,1)}, bf16[384,768]{1,0:T(8,128)(2,1)}, u32[]{:S(2)}, u32[]{:S(2)}) collective-permute-start(bf16[384,768]{1,0:T(8,128)(2,1)} %get-tuple-element.308), channel_id=1, source_target_pairs={{0,8},{4,12},{8,0},{12,4},{16,24},{20,28},{24,16},{28,20},{1,9},{5... | collective-permute-start | bytes 1769480 | tf_op jit(solution)/shard_map/ppermute | solution.py:858
  378.7 54.3 %collective-permute-start.52 = (bf16[192,3072]{1,0:T(8,128)(2,1)}, bf16[192,3072]{1,0:T(8,128)(2,1)}, u32[]{:S(2)}, u32[]{:S(2)}) collective-permute-start(bf16[192,3072]{1,0:T(8,128)(2,1)} %pad_maximum_fusion.1), channel_id=1, source_target_pairs={{0,2},{1,3},{2,0},{3,1},{4,6},{5,7},{6,4},{7,5},{8,10},{9,11},{10,... | collective-permute-start | bytes 3538952 | tf_op jit(solution)/shard_map/ppermute | solution.py:855
  386.5 25.8 %collective-permute-start.48 = (bf16[384,896]{1,0:T(8,128)(2,1)}, bf16[384,896]{1,0:T(8,128)(2,1)}, u32[]{:S(2)}, u32[]{:S(2)}) collective-permute-start(bf16[384,896]{1,0:T(8,128)(2,1)} %get-tuple-element.314.refs_12_), channel_id=1, source_target_pairs={{0,16},{4,20},{8,24},{12,28},{16,0},{20,4},{24,8},{28,12},{1,17},{... | collective-permute-start | bytes 2064392 | tf_op jit(solution)/shard_map/ppermute | solution.py:858
  388.1 24.2 %collective-permute-start.49 = (bf16[384,896]{1,0:T(8,128)(2,1)}, bf16[384,896]{1,0:T(8,128)(2,1)}, u32[]{:S(2)}, u32[]{:S(2)}) collective-permute-start(bf16[384,896]{1,0:T(8,128)(2,1)} %get-tuple-element.321), channel_id=1, source_target_pairs={{0,8},{4,12},{8,0},{12,4},{16,24},{20,28},{24,16},{28,20},{1,9},{5... | collective-permute-start | bytes 2064392 | tf_op jit(solution)/shard_map/ppermute | solution.py:858
  409.5 24.7 %collective-permute-start.46 = (bf16[192,768]{1,0:T(8,128)(2,1)}, bf16[192,768]{1,0:T(8,128)(2,1)}, u32[]{:S(2)}, u32[]{:S(2)}) collective-permute-start(bf16[192,768]{1,0:T(8,128)(2,1)} %get-tuple-element.317.refs_8_), channel_id=1, source_target_pairs={{0,8},{4,12},{8,0},{12,4},{16,24},{20,28},{24,16},{28,20},{1,9},{5... | collective-permute-start | bytes 884744 | tf_op jit(solution)/shard_map/ppermute | solution.py:858
  411.0 23.2 %collective-permute-start.47 = (bf16[192,768]{1,0:T(8,128)(2,1)}, bf16[192,768]{1,0:T(8,128)(2,1)}, u32[]{:S(2)}, u32[]{:S(2)}) collective-permute-start(bf16[192,768]{1,0:T(8,128)(2,1)} %get-tuple-element.318), channel_id=1, source_target_pairs={{0,16},{4,20},{8,24},{12,28},{16,0},{20,4},{24,8},{28,12},{1,17},{... | collective-permute-start | bytes 884744 | tf_op jit(solution)/shard_map/ppermute | solution.py:858
  433.0 19.4 %collective-permute-start.53 = (bf16[768,1792]{1,0:T(8,128)(2,1)}, bf16[768,1792]{1,0:T(8,128)(2,1)}, u32[]{:S(2)}, u32[]{:S(2)}) collective-permute-start(bf16[768,1792]{1,0:T(8,128)(2,1)} %get-tuple-element.340.refs_21_), channel_id=1, source_target_pairs={{0,4},{4,0},{8,12},{12,8},{16,20},{20,16},{24,28},{28,24},{1,5},{5... | collective-permute-start | bytes 8257544 | tf_op jit(solution)/shard_map/ppermute | solution.py:858
  434.2 37.4 %collective-permute-start.58 = (bf16[192,1792]{1,0:T(8,128)(2,1)}, bf16[192,1792]{1,0:T(8,128)(2,1)}, u32[]{:S(2)}, u32[]{:S(2)}) collective-permute-start(bf16[192,1792]{1,0:T(8,128)(2,1)} %pad_maximum_fusion.6), channel_id=1, source_target_pairs={{0,2},{1,3},{2,0},{3,1},{4,6},{5,7},{6,4},{7,5},{8,10},{9,11},{10,... | collective-permute-start | bytes 2064392 | tf_op jit(solution)/shard_map/ppermute | solution.py:855
  450.0 60.7 %collective-permute-start.59 = (bf16[512,1536]{1,0:T(8,128)(2,1)}, bf16[512,1536]{1,0:T(8,128)(2,1)}, u32[]{:S(2)}, u32[]{:S(2)}) collective-permute-start(bf16[512,1536]{1,0:T(8,128)(2,1)} %get-tuple-element.364), channel_id=1, source_target_pairs={{0,1},{1,0},{2,3},{3,2},{4,5},{5,4},{6,7},{7,6},{8,9},{9,8},{10,11... | collective-permute-start | bytes 4718600 | tf_op jit(solution)/shard_map/ppermute | solution.py:899
  456.9 17.9 %collective-permute-start.56 = (bf16[384,896]{1,0:T(8,128)(2,1)}, bf16[384,896]{1,0:T(8,128)(2,1)S(1)}, u32[]{:S(2)}, u32[]{:S(2)}) collective-permute-start(bf16[384,896]{1,0:T(8,128)(2,1)} %get-tuple-element.346.refs_21_), channel_id=1, source_target_pairs={{0,16},{4,20},{8,24},{12,28},{16,0},{20,4},{24,8},{28,12},{1,17},{... | collective-permute-start | bytes 2064392 | tf_op jit(solution)/shard_map/ppermute | solution.py:858
  457.9 17.3 %collective-permute-start.57 = (bf16[384,896]{1,0:T(8,128)(2,1)}, bf16[384,896]{1,0:T(8,128)(2,1)S(1)}, u32[]{:S(2)}, u32[]{:S(2)}) collective-permute-start(bf16[384,896]{1,0:T(8,128)(2,1)} %get-tuple-element.350), channel_id=1, source_target_pairs={{0,8},{4,12},{8,0},{12,4},{16,24},{20,28},{24,16},{28,20},{1,9},{5... | collective-permute-start | bytes 2064392 | tf_op jit(solution)/shard_map/ppermute | solution.py:858
  472.6 20.4 %collective-permute-start.54 = (bf16[192,768]{1,0:T(8,128)(2,1)S(1)}, bf16[192,768]{1,0:T(8,128)(2,1)S(1)}, u32[]{:S(2)}, u32[]{:S(2)}) collective-permute-start(bf16[192,768]{1,0:T(8,128)(2,1)S(1)} %bitcast.20), channel_id=1, source_target_pairs={{0,2},{1,3},{2,0},{3,1},{4,6},{5,7},{6,4},{7,5},{8,10},{9,11},{10,... | collective-permute-start | bytes 884744 | tf_op jit(solution)/shard_map/ppermute | solution.py:855
  479.7 23.3 %collective-permute-start.63 = (bf16[192,896]{1,0:T(8,128)(2,1)}, bf16[192,896]{1,0:T(8,128)(2,1)S(1)}, u32[]{:S(2)}, u32[]{:S(2)}) collective-permute-start(bf16[192,896]{1,0:T(8,128)(2,1)} %get-tuple-element.381.refs_6_), channel_id=1, source_target_pairs={{0,8},{4,12},{8,0},{12,4},{16,24},{20,28},{24,16},{28,20},{1,9},{5... | collective-permute-start | bytes 1032200 | tf_op jit(solution)/shard_map/ppermute | solution.py:858
  (63 other events, 554.2 us)
